TPU v7x, 32 devices: a whole 2x2x4 slice. The times are simulated.
32 devices in a mesh: grp: 2 (over y), comp: 8 (over z, x), tile: 2 (over core).
Axes of the slice: x: 2, y: 2, z: 4, core: 2. Of those that a mesh axis runs over, the one named last changes fastest.
Arguments:
- energy: float32 [1152, 512, 256], P('comp', ('grp', 'tile')), parts along dimension 1, may hold values from 0.2 to 2
- sea_mask: int32 [512, 256], P('grp'), parts along dimension 0, may hold values from 0 to 1, as said below
- current_u: float32 [512, 256], P('grp'), parts along dimension 0, may hold values from -0.15 to 0.15
- current_v: float32 [512, 256], P('grp'), parts along dimension 0, may hold values from -0.15 to 0.15
- wind_forcing: float32 [512, 256], P('grp'), parts along dimension 0, may hold values from 0.3 to 3
- refraction: float32 [512, 256], P('grp'), parts along dimension 0, may hold values from -0.3 to 0.3
- group_speed: float32 [32], replicated, may hold values from 0.15 to 0.35
- growth: float32 [1152], replicated, may hold values from 0.03 to 0.3
- damping: float32 [1152], replicated, may hold values from 0.03 to 0.3
- coupling: float32 [1152], replicated, may hold values from 0.01 to 0.1
- dia_index: int32 [4, 1152], replicated, may hold values from 0 to 1151, as said below
Outputs:
- energy_out: float32 [1152, 512, 256], P('comp', ('grp', 'tile')), parts along dimension 1
There are 2 independent parts, one for each index of `grp`. A program takes and returns all parts, laid end to end along the dimension named above; an argument that names none is the same for every part. Nothing has to cross between parts.
Inputs may be any that keep to these rules, and one draw needn't show every extreme that they name: `sea_mask`: each tile's block of 128 x 256 cells holds at most 16384 sea cells, and one tile holds exactly that many. `dia_index`: partners of a component lie one or two frequency bins above (plus) or below (minus), clamped to the range, with direction offsets that depend only on the frequency.
All inputs are finite; a program needn't handle non-finite values.
Results may differ from a plain program's by a relative error of at most 0.0025.
Values sent between devices are 32-bit elements; how exact they have to be, the bound alone decides.
No kernel may reach another device: no remote copies, remote signals or barrier semaphores. Data moves between devices by JAX's collectives and lax.ppermute only.
A program may use at most 320 MiB of HBM per device.

v0:
```python
import math

import jax
import jax.numpy as jnp
from jax import lax
from jax.sharding import PartitionSpec as P

NTH = 36
NF = 32


weight_plus = 0.4096
weight_minus = 3.1605
weight_cross = 1.2945


def with_halo(block, sides, width):
    for axis, dim in sides:
        count = lax.axis_size(axis)
        forward = [(i, i + 1) for i in range(count - 1)]
        backward = [(target, source) for source, target in forward]
        low = lax.ppermute(
            lax.slice_in_dim(block, block.shape[dim] - width, None, axis=dim), axis, forward
        )
        high = lax.ppermute(lax.slice_in_dim(block, 0, width, axis=dim), axis, backward)
        block = jnp.concatenate([low, block, high], axis=dim)
    return block


def quick_flux(far_left, left_cell, right_cell, far_right, courant):
    centre = 0.5 * (left_cell + right_cell) - 0.5 * courant * (right_cell - left_cell)
    curvature = (1.0 - courant * courant) / 6.0
    upward = centre - curvature * (right_cell - 2.0 * left_cell + far_left)
    downward = centre - curvature * (left_cell - 2.0 * right_cell + far_right)
    return courant * jnp.where(courant > 0.0, upward, downward)


def flux_change(padded, speed, current, sea_pad, axis):
    cell_count = padded.shape[axis] - 4

    def take_part(source, first, which_axis):
        return lax.slice_in_dim(source, first, first + cell_count + 1, axis=which_axis)

    face_current = 0.5 * (take_part(current, 0, axis - 1) + take_part(current, 1, axis - 1))
    courant = speed[:, None, None] + face_current[None]
    open_face = (take_part(sea_pad, 0, axis - 1) * take_part(sea_pad, 1, axis - 1))[None]
    face_flux = (
        quick_flux(
            take_part(padded, 0, axis),
            take_part(padded, 1, axis),
            take_part(padded, 2, axis),
            take_part(padded, 3, axis),
            courant,
        )
        * open_face
    )
    return lax.slice_in_dim(face_flux, 1, cell_count + 1, axis=axis) - lax.slice_in_dim(
        face_flux, 0, cell_count, axis=axis
    )


def source_terms(energy_block, wind, turning, growth, damping, coupling, lookup, spread):
    cell_count = energy_block.shape[1]
    spectrum = energy_block.reshape(NF, NTH, cell_count)
    turn_rate = turning[None, None, :]
    next_dir = jnp.roll(spectrum, -1, axis=1)
    forward = jnp.maximum(turn_rate, 0.0)
    backward = jnp.minimum(turn_rate, 0.0)
    upper_flux = forward * spectrum + backward * next_dir
    lower_flux = jnp.roll(upper_flux, 1, axis=1)
    turned = (spectrum - upper_flux + lower_flux).reshape(energy_block.shape)
    rounded = turned.astype(jnp.bfloat16)
    plus_first, minus_first, plus_second, minus_second = lookup(rounded)
    couple_rate = coupling[:, None]
    delta_first = couple_rate * (
        turned * turned * (weight_plus * plus_first + weight_minus * minus_first)
        - 2.0 * weight_cross * turned * plus_first * minus_first
    )
    delta_second = couple_rate * (
        turned * turned * (weight_plus * plus_second + weight_minus * minus_second)
        - 2.0 * weight_cross * turned * plus_second * minus_second
    )
    moved = spread(delta_first.astype(jnp.bfloat16), delta_second.astype(jnp.bfloat16))
    mean_level = jnp.sum(turned, axis=0) / energy_block.shape[0]
    return (
        turned
        + growth[:, None] * wind[None] * turned
        - damping[:, None] * mean_level[None] * turned
        - 2.0 * (delta_first + delta_second)
        + moved
    )


def shards(
    energy,
    sea_mask,
    current_u,
    current_v,
    wind_forcing,
    refraction,
    group_speed,
    growth,
    damping,
    coupling,
    dia_index,
):
    comp_count = lax.axis_size("comp")
    comp_pos = lax.axis_index("comp")
    tile_pos = lax.axis_index("tile")
    local_comps, row_count, col_count = energy.shape
    first_row = tile_pos * row_count
    first_comp = comp_pos * local_comps
    comp_total = NTH * NF
    angles = 2.0 * math.pi / NTH * (jnp.arange(comp_total) % NTH).astype(jnp.float32)
    speeds = jnp.repeat(group_speed, NTH)
    speed_east = lax.dynamic_slice_in_dim(speeds * jnp.cos(angles), first_comp, local_comps)
    speed_north = lax.dynamic_slice_in_dim(speeds * jnp.sin(angles), first_comp, local_comps)
    window = (row_count + 2, col_count + 2)
    sea_pad = lax.dynamic_slice(jnp.pad(sea_mask.astype(jnp.float32), 1), (first_row, 0), window)
    east_pad = lax.dynamic_slice(jnp.pad(current_u, 1), (first_row, 0), window)
    north_pad = lax.dynamic_slice(jnp.pad(current_v, 1), (first_row, 0), window)
    sea_tile = sea_pad[1:-1, 1:-1]
    masked = energy * sea_tile[None]
    padded_east = with_halo(masked, (("tile", 1),), 2)
    along_east = flux_change(padded_east, speed_east, east_pad[:, 1:-1], sea_pad[:, 1:-1], 1)
    along_north = flux_change(
        jnp.pad(masked, ((0, 0), (0, 0), (2, 2))),
        speed_north,
        north_pad[1:-1, :],
        sea_pad[1:-1, :],
        2,
    )
    propagated = (sea_tile[None] * (masked - along_east - along_north)).reshape(
        local_comps, row_count * col_count
    )
    tile_wind = lax.dynamic_slice(wind_forcing, (first_row, 0), (row_count, col_count)).reshape(-1)
    tile_turn = lax.dynamic_slice(refraction, (first_row, 0), (row_count, col_count)).reshape(-1)
    comp_ids = jnp.arange(comp_total)
    tables = [
        (dia_index[slot_row][:, None] == comp_ids[None, :]).astype(jnp.bfloat16)
        for slot_row in range(4)
    ]

    def lookup(rounded):
        return tuple(
            (
                jnp.dot(tables[slot_row], rounded, preferred_element_type=jnp.float32)
                for slot_row in range(4)
            )
        )

    def scatter_back(table, terms):
        return lax.dot_general(
            table, terms, (((0,), (0,)), ((), ())), preferred_element_type=jnp.float32
        )

    def spread(first_terms, second_terms):
        return (
            scatter_back(tables[0], first_terms)
            + scatter_back(tables[1], first_terms)
            + scatter_back(tables[2], second_terms)
            + scatter_back(tables[3], second_terms)
        )

    share_size = row_count * col_count // comp_count
    point_field = lax.all_to_all(propagated, "comp", split_axis=1, concat_axis=0, tiled=True)
    first_point = comp_pos * share_size
    own_wind = lax.dynamic_slice_in_dim(tile_wind, first_point, share_size)
    own_turn = lax.dynamic_slice_in_dim(tile_turn, first_point, share_size)
    result = source_terms(
        point_field, own_wind, own_turn, growth, damping, coupling, lookup, spread
    )
    returned_field = lax.all_to_all(result, "comp", split_axis=0, concat_axis=1, tiled=True)
    return returned_field.reshape(local_comps, row_count, col_count)


def solution(mesh):
    placed = (
        P("comp", ("grp", "tile"), None),
        P("grp", None),
        P("grp", None),
        P("grp", None),
        P("grp", None),
        P("grp", None),
        P(),
        P(),
        P(),
        P(),
        P(),
    )
    return jax.shard_map(
        shards,
        mesh=mesh,
        in_specs=placed,
        out_specs=P("comp", ("grp", "tile"), None),
        check_vma=False,
    )
```

profile of v0, /device:TPU:0, one launch (start us, length us, event | category | flops | bytes accessed | tf_op | source)
XLA Modules:
  0.0 1488.2 jit_solution(4127246700077183608)
XLA Ops:
  31.4 43.5 %fusion.11 = f32[144,128,257]{2,0,1:T(8,128)} fusion(f32[144,128,256]{2,0,1:T(8,128)} %copy-done, f32[128,257]{1,0:T(8,128)S(1)} %get-tuple-element.22, f32[128,257]{1,0:T(8,128)S(1)} %get-tuple-element.21, f32[144]{0:T(256)S(1)} %get-tuple-element.18), kind=kLoop, calls=%fused_computation.23 | loop fusion | flops 113688576 | bytes 38086208 | tf_op jit(solution)/shard_map/mul | solution.py:48
  75.2 30.0 %fusion.25 = f32[144,129,256]{2,0,1:T(8,128)} fusion(f32[144,2,256]{2,0,1:T(8,128)S(1)} %collective-permute-done.1, f32[144,128,256]{2,0,1:T(8,128)S(1)} %bitcast.29, f32[144,2,256]{2,0,1:T(8,128)S(1)} %collective-permute-done, f32[129,256]{1,0:T(8,128)S(1)} %get-tuple-element.20, f32[129,256]{1,0:T(8,128)S(1)} %get-tuple-element.19, ...), kind=kLoop, calls=%fused_computation.47 | loop fusion | flops 133152768 | bytes 38750784 | tf_op jit(solution)/shard_map/mul | solution.py:48
  105.1 41.2 %fusion.30 = f32[144,128,256]{2,0,1:T(8,128)} fusion(f32[144,128,257]{2,0,1:T(8,128)} %fusion.11, f32[144,129,256]{2,0,1:T(8,128)} %fusion.25, f32[128,256]{1,0:T(8,128)S(1)} %pad_dynamic-slice_fusion.3, f32[144,128,256]{2,1,0:T(8,128)} %param.11), kind=kLoop, calls=%fused_computation.56 | loop fusion | flops 28311552 | bytes 113377280 | tf_op jit(solution)/shard_map/mul | solution.py:133
  146.4 18.6 %copy.21 = f32[144,128,256]{2,1,0:T(8,128)} copy(f32[144,128,256]{2,0,1:T(8,128)} %fusion.30) | data formatting | bytes 37748736 | tf_op jit(solution)/shard_map/mul | solution.py:133
  165.0 20.4 %all_to_all.24 = f32[144,8,4096]{2,1,0:T(8,128)} reshape(f32[144,128,256]{2,1,0:T(8,128)} %copy.21) | data formatting | bytes 37748736 | tf_op jit(solution)/shard_map/all_to_all | solution.py:166
  185.4 19.7 %copy.22 = f32[144,8,4096]{2,0,1:T(8,128)} copy(f32[144,8,4096]{2,1,0:T(8,128)} %all_to_all.24) | data formatting | bytes 37748736 | tf_op jit(solution)/shard_map/all_to_all | solution.py:166
  213.4 408.2 %all-to-all-done = f32[144,8,4096]{2,0,1:T(8,128)} async-done(((f32[144,8,4096]{2,0,1:T(8,128)}), f32[144,8,4096]{2,0,1:T(8,128)}, u32[]{:S(2)}, u32[]{:S(2)}) %all-to-all-start) | async-done | bytes 18874400 | tf_op jit(solution)/shard_map/all_to_all | solution.py:166
  621.6 19.1 %reshape.67 = f32[32,36,4096]{2,1,0:T(8,128)} reshape(f32[8,144,4096]{2,1,0:T(8,128)} %bitcast) | data formatting | bytes 37748736 | tf_op jit(solution)/shard_map/reshape | solution.py:64
  663.4 24.1 %multiply_add_fusion.1 = (f32[32,36,4096]{2,1,0:T(8,128)}, f32[32,36,4096]{2,1,0:T(8,128)}) fusion(f32[32,36,4096]{2,1,0:T(8,128)S(1)} %bitcast.27, f32[4096]{0:T(1024)S(1)} %get-tuple-element.16, f32[4096]{0:T(1024)S(1)} %get-tuple-element.15, f32[32,1,4096]{2,1,0:T(1,128)} %slice.155, f32[32,35,4096]{2,1,0:T(8,128)} %slice.154), kind=kLoop, calls=%fused_computation.27 | loop fusion | flops 18874368 | bytes 75530240 | tf_op jit(solution)/shard_map/add | solution.py:69
  706.6 19.3 %concatenate.32 = f32[8,144,4096]{2,1,0:T(8,128)} reshape(f32[32,36,4096]{2,1,0:T(8,128)} %pad_maximum_fusion.1) | data formatting | bytes 37748736 | tf_op jit(solution)/shard_map/jit(_roll_static)/concatenate | solution.py:70
  725.9 19.3 %concatenate.30 = f32[1152,4096]{1,0:T(8,128)} reshape(f32[32,36,4096]{2,1,0:T(8,128)} %pad_maximum_fusion.1) | data formatting | bytes 37748736 | tf_op jit(solution)/shard_map/jit(_roll_static)/concatenate | solution.py:70
  745.2 19.3 %concatenate.31 = f32[8,144,4096]{2,1,0:T(8,128)} reshape(f32[32,36,4096]{2,1,0:T(8,128)} %get-tuple-element.12) | data formatting | bytes 37748736 | tf_op jit(solution)/shard_map/jit(_roll_static)/concatenate | solution.py:66
  764.6 19.3 %concatenate.28 = f32[1152,4096]{1,0:T(8,128)} reshape(f32[32,36,4096]{2,1,0:T(8,128)} %get-tuple-element.12) | data formatting | bytes 37748736 | tf_op jit(solution)/shard_map/jit(_roll_static)/concatenate | solution.py:66
  806.5 24.1 %fusion.62 = (bf16[1152,4096]{1,0:T(8,128)(2,1)}, f32[1152,4096]{1,0:T(8,128)}) fusion(f32[1152,4096]{1,0:T(8,128)} %concatenate.30, f32[1152,4096]{1,0:T(8,128)S(1)} %copy-done.1, f32[4096]{0:T(1024)S(1)} %get-tuple-element.16, f32[4096]{0:T(1024)S(1)} %get-tuple-element.15, f32[144,8,4096]{2,0,1:T(8,128)} %all-to-all-done), kind=kLoop, calls=%fused_computation.121 | loop fusion | flops 28311552 | bytes 84967424 | tf_op jit(solution)/shard_map/convert_element_type | solution.py:72
  830.6 18.8 %fusion.35 = f32[1152,4096]{1,0:T(8,128)} fusion(bf16[1152,4096]{1,0:T(8,128)(2,1)} %get-tuple-element.9, s32[1152]{0:T(1024)S(1)} %get-tuple-element.8), kind=kOutput, calls=%fused_computation.70 | convolution fusion | flops 10872963072 | bytes 28316160 | tf_op jit(solution)/shard_map/dot_general | solution.py:147
  865.8 28.7 %subtract_multiply_fusion.1 = f32[1152,4096]{1,0:T(8,128)} fusion(f32[1152,4096]{1,0:T(8,128)} %fusion.38, f32[1152,4096]{1,0:T(8,128)} %get-tuple-element.10, f32[1152]{0:T(1024)S(1)} %copy-done.13, bf16[1152,4096]{1,0:T(8,128)(2,1)} %get-tuple-element.9, s32[1152]{0:T(1024)S(1)} %copy-done.10), kind=kOutput, calls=%fused_computation.65 | convolution fusion | flops 10920148992 | bytes 66069504 | tf_op jit(solution)/shard_map/dot_general | solution.py:147
  894.5 20.5 %fusion.37 = f32[1152,4096]{1,0:T(8,128)} fusion(f32[1152,4096]{1,0:T(8,128)} %subtract_multiply_fusion.1, s32[1152]{0:T(1024)S(1)} %copy-done.11), kind=kOutput, calls=%fused_computation.74 | convolution fusion | flops 10877681664 | bytes 37753344 | tf_op jit(solution)/shard_map/dot_general | solution.py:153
  915.0 24.6 %convolution_add_fusion.2 = f32[1152,4096]{1,0:T(8,128)} fusion(f32[1152,4096]{1,0:T(8,128)} %fusion.37, f32[1152,4096]{1,0:T(8,128)} %subtract_multiply_fusion.1, s32[1152]{0:T(1024)S(1)} %copy-done.10), kind=kOutput, calls=%fused_computation.51 | convolution fusion | flops 10882400256 | bytes 56627712 | tf_op jit(solution)/shard_map/dot_general | solution.py:153
  939.6 28.8 %subtract_multiply_fusion = f32[1152,4096]{1,0:T(8,128)} fusion(f32[1152,4096]{1,0:T(8,128)} %fusion.35, f32[1152,4096]{1,0:T(8,128)} %get-tuple-element.10, f32[1152]{0:T(1024)S(1)} %copy-done.13, bf16[1152,4096]{1,0:T(8,128)(2,1)} %get-tuple-element.9, s32[1152]{0:T(1024)S(1)} %copy-done.9), kind=kOutput, calls=%fused_computation.64 | convolution fusion | flops 10920148992 | bytes 66069504 | tf_op jit(solution)/shard_map/dot_general | solution.py:147
  968.4 24.7 %convolution_add_fusion.1 = f32[1152,4096]{1,0:T(8,128)} fusion(f32[1152,4096]{1,0:T(8,128)} %convolution_add_fusion.2, f32[1152,4096]{1,0:T(8,128)} %subtract_multiply_fusion, s32[1152]{0:T(1024)S(1)} %get-tuple-element.8), kind=kOutput, calls=%fused_computation.50 | convolution fusion | flops 10882400256 | bytes 56627712 | tf_op jit(solution)/shard_map/dot_general | solution.py:153
  993.1 40.5 %fusion.26 = f32[1152,4096]{1,0:T(8,128)} fusion(f32[1152,4096]{1,0:T(8,128)} %convolution_add_fusion.1, f32[1152,4096]{1,0:T(8,128)} %get-tuple-element.10, f32[1152,4096]{1,0:T(8,128)} %subtract_multiply_fusion.1, f32[1152,4096]{1,0:T(8,128)} %subtract_multiply_fusion, f32[4096]{0:T(1024)S(1)} %copy-done.8, f32[1152]{0:T(1024)S(1)} %copy-done.14, ...), kind=kOutput, calls=%fused_computation.49 | convolution fusion | flops 10929586176 | bytes 94418432 | tf_op jit(solution)/shard_map/dot_general | solution.py:153
  1033.6 412.5 %all_to_all.32 = f32[8,144,4096]{2,1,0:T(8,128)S(1)} all-to-all(f32[8,144,4096]{2,1,0:T(8,128)} %bitcast.32), channel_id=1, replica_groups=mesh['grp'=2,'comp'=8,'tile'=2] {'comp'}, dimensions={0} | all-to-all | bytes 37748736 | tf_op jit(solution)/shard_map/all_to_all | solution.py:173
  1446.1 21.7 %copy.23 = f32[144,8,4096]{2,1,0:T(8,128)} copy(f32[144,8,4096]{2,0,1:T(8,128)S(1)} %bitcast.31) | data formatting | bytes 37748736 | tf_op jit(solution)/shard_map/all_to_all | solution.py:173
  1467.8 20.2 %reshape.69 = f32[144,128,256]{2,1,0:T(8,128)} reshape(f32[144,8,4096]{2,1,0:T(8,128)} %copy.23) | data formatting | bytes 37748736 | tf_op jit(solution)/shard_map/reshape | solution.py:174
  (82 shorter events, 120.4 us)
Async XLA Ops:
  1.1 28.5 %copy-start.12 = (f32[32]{0:T(128)S(1)}, f32[32]{0:T(128)}, u32[]{:S(2)}) copy-start(f32[32]{0:T(128)} %param.17) | copy-start | bytes 388
  25.9 49.2 %collective-permute-start = (f32[144,2,256]{2,0,1:T(8,128)}, f32[144,2,256]{2,0,1:T(8,128)S(1)}, u32[]{:S(2)}, u32[]{:S(2)}) collective-permute-start(f32[144,2,256]{2,0,1:T(8,128)} %get-tuple-element.13), channel_id=1, source_target_pairs={{0,1},{2,3},{4,5},{6,7},{8,9},{10,11},{12,13},{14,15},{16,17},{18,... | collective-permute-start | bytes 884744 | tf_op jit(solution)/shard_map/ppermute | solution.py:22
  28.2 46.9 %collective-permute-start.1 = (f32[144,2,256]{2,0,1:T(8,128)}, f32[144,2,256]{2,0,1:T(8,128)S(1)}, u32[]{:S(2)}, u32[]{:S(2)}) collective-permute-start(f32[144,2,256]{2,0,1:T(8,128)} %get-tuple-element.14), channel_id=1, source_target_pairs={{1,0},{3,2},{5,4},{7,6},{9,8},{11,10},{13,12},{15,14},{17,16},{19,... | collective-permute-start | bytes 884744 | tf_op jit(solution)/shard_map/ppermute | solution.py:25
  29.8 45.4 %slice-start.5 = ((s8[18874368]{0:T(1024)(128)(4,1)}), s8[2097152]{0:T(1024)(128)(4,1)S(1)}, s32[]{:S(2)}) async-start(s8[18874368]{0:T(1024)(128)(4,1)} %bitcast.28), calls=%async_computation.7 | async-start | bytes 4194304
  31.3 43.6 %copy-start.3 = (f32[256,256]{1,0:T(8,128)S(1)}, f32[256,256]{1,0:T(8,128)}, u32[]{:S(2)}) copy-start(f32[256,256]{1,0:T(8,128)} %param.13) | copy-start | bytes 786436
  31.3 43.8 %slice-start.6 = ((s8[18874368]{0:T(1024)(128)(4,1)}), s8[4194304]{0:T(1024)(128)(4,1)S(1)}, s32[]{:S(2)}) async-start(s8[18874368]{0:T(1024)(128)(4,1)} %bitcast.28), calls=%async_computation.8 | async-start | bytes 8388608
  31.3 43.8 %slice-start.7 = ((s8[18874368]{0:T(1024)(128)(4,1)}), s8[4194304]{0:T(1024)(128)(4,1)S(1)}, s32[]{:S(2)}) async-start(s8[18874368]{0:T(1024)(128)(4,1)} %bitcast.28), calls=%async_computation.9 | async-start | bytes 8388608
  31.3 43.8 %slice-start.8 = ((s8[18874368]{0:T(1024)(128)(4,1)}), s8[4194304]{0:T(1024)(128)(4,1)S(1)}, s32[]{:S(2)}) async-start(s8[18874368]{0:T(1024)(128)(4,1)} %bitcast.28), calls=%async_computation.10 | async-start | bytes 8388608
  31.4 43.8 %slice-start.9 = ((s8[18874368]{0:T(1024)(128)(4,1)}), s8[4194304]{0:T(1024)(128)(4,1)S(1)}, s32[]{:S(2)}) async-start(s8[18874368]{0:T(1024)(128)(4,1)} %bitcast.28), calls=%async_computation.11 | async-start | bytes 8388608
  205.1 416.5 %all-to-all-start = ((f32[144,8,4096]{2,0,1:T(8,128)}), f32[144,8,4096]{2,0,1:T(8,128)}, u32[]{:S(2)}, u32[]{:S(2)}) async-start(f32[144,8,4096]{2,0,1:T(8,128)} %copy.22), calls=%async_computation | async-start | bytes 37748736 | tf_op jit(solution)/shard_map/all_to_all | solution.py:166
  640.7 21.9 %slice-start = ((s8[20971520]{0:T(1024)(128)(4,1)}), s8[4194304]{0:T(1024)(128)(4,1)S(1)}, s32[]{:S(2)}) async-start(s8[20971520]{0:T(1024)(128)(4,1)} %bitcast.26), calls=%async_computation.2 | async-start | bytes 8388608
  644.2 18.4 %slice-start.1 = ((s8[20971520]{0:T(1024)(128)(4,1)}), s8[4194304]{0:T(1024)(128)(4,1)S(1)}, s32[]{:S(2)}) async-start(s8[20971520]{0:T(1024)(128)(4,1)} %bitcast.26), calls=%async_computation.3 | async-start | bytes 8388608
  644.2 18.4 %slice-start.2 = ((s8[20971520]{0:T(1024)(128)(4,1)}), s8[4194304]{0:T(1024)(128)(4,1)S(1)}, s32[]{:S(2)}) async-start(s8[20971520]{0:T(1024)(128)(4,1)} %bitcast.26), calls=%async_computation.4 | async-start | bytes 8388608
  644.2 18.4 %slice-start.3 = ((s8[20971520]{0:T(1024)(128)(4,1)}), s8[4194304]{0:T(1024)(128)(4,1)S(1)}, s32[]{:S(2)}) async-start(s8[20971520]{0:T(1024)(128)(4,1)} %bitcast.26), calls=%async_computation.5 | async-start | bytes 8388608
  644.2 19.2 %slice-start.4 = ((s8[20971520]{0:T(1024)(128)(4,1)}), s8[4194304]{0:T(1024)(128)(4,1)S(1)}, s32[]{:S(2)}) async-start(s8[20971520]{0:T(1024)(128)(4,1)} %bitcast.26), calls=%async_computation.6 | async-start | bytes 8388608
  783.9 22.6 %copy-start.1 = (f32[1152,4096]{1,0:T(8,128)S(1)}, f32[1152,4096]{1,0:T(8,128)}, u32[]{:S(2)}) copy-start(f32[1152,4096]{1,0:T(8,128)} %concatenate.28) | copy-start | bytes 56623108
  830.6 18.8 %copy-start.2 = (bf16[1152,4096]{1,0:T(8,128)(2,1)S(1)}, bf16[1152,4096]{1,0:T(8,128)(2,1)}, u32[]{:S(2)}) copy-start(bf16[1152,4096]{1,0:T(8,128)(2,1)} %get-tuple-element.9) | copy-start | bytes 28311556
  830.6 18.8 %copy-start.11 = (s32[1152]{0:T(1024)S(1)}, s32[1152]{0:T(1024)}, u32[]{:S(2)}) copy-start(s32[1152]{0:T(1024)} %get-tuple-element.7) | copy-start | bytes 13828
  849.4 16.4 %copy-start.10 = (s32[1152]{0:T(1024)S(1)}, s32[1152]{0:T(1024)}, u32[]{:S(2)}) copy-start(s32[1152]{0:T(1024)} %get-tuple-element.6) | copy-start | bytes 13828
  915.0 24.6 %copy-start.9 = (s32[1152]{0:T(1024)S(1)}, s32[1152]{0:T(1024)}, u32[]{:S(2)}) copy-start(s32[1152]{0:T(1024)} %get-tuple-element.5) | copy-start | bytes 13828
  968.3 24.7 %copy-start.7 = (f32[4096]{0:T(1024)S(1)}, f32[4096]{0:T(1024)}, u32[]{:S(2)}) copy-start(f32[4096]{0:T(1024)} %dynamic_slice.35) | copy-start | bytes 49156
  968.4 24.7 %copy-start.8 = (f32[4096]{0:T(1024)S(1)}, f32[4096]{0:T(1024)}, u32[]{:S(2)}) copy-start(f32[4096]{0:T(1024)} %broadcast_multiply_fusion) | copy-start | bytes 49156
  968.4 24.7 %copy-start.14 = (f32[1152]{0:T(1024)S(1)}, f32[1152]{0:T(1024)}, u32[]{:S(2)}) copy-start(f32[1152]{0:T(1024)} %param.19) | copy-start | bytes 13828
  968.4 24.7 %copy-start.15 = (f32[1152]{0:T(1024)S(1)}, f32[1152]{0:T(1024)}, u32[]{:S(2)}) copy-start(f32[1152]{0:T(1024)} %param.18) | copy-start | bytes 13828
  (5 other events, 44.4 us)
where the time goes:
time: 1500 us; the launch traced here: 1490 us
  blocking collectives  413 us (28%)
  waiting for transfers between devices  408 us (27%)
  local copies, waits for them, and re-layouts  236 us (16%)
  other arithmetic  218 us (15%)
  matrix products  203 us (14%)
    all_to_all x1, blocking collectives, shards(): lax.all_to_all(result, 'comp', split_axis=0, concat_axis=1, tiled=True)  413 us
    all_to_all x1, waiting for transfers between devices, shards(): lax.all_to_all(propagated, 'comp', split_axis=1, concat_axis=0, tiled=True)  408 us
    dot_general x4, matrix products, scatter_back(): lax.dot_general(table, terms, (((0,), (0,)), ((), ())), preferred_element...  110 us
    dot_general x4, matrix products, lookup(): jnp.dot(tables[slot_row], rounded, preferred_element_type=jnp.float32)  92.6 us
    mul x2, other arithmetic, flux_change(): quick_flux(take_part(padded, 0, axis), take_part(padded, 1, axis), take_p...  73.5 us
    mul x1, other arithmetic, shards(): sea_tile[None] * (masked - along_east - along_north)  41.2 us
    all_to_all x2, local copies, waits for them, and re-layouts, shards(): lax.all_to_all(propagated, 'comp', split_axis=1, concat_axis=0, tiled=True)  40.1 us
    concatenate x2, local copies, waits for them, and re-layouts, source_terms(): next_dir = jnp.roll(spectrum, -1, axis=1)  38.6 us
  transfers between devices with their start and end apart: 3, of which 1 were waited for; matrix products, arithmetic and copies ran while one was open for 3% of the time, Pallas kernels for 0%

commit v1 on v0

--- a/solution.py
+++ b/solution.py
@@ -1,8 +1,11 @@
+import functools
 import math
 
 import jax
 import jax.numpy as jnp
 from jax import lax
+from jax.experimental import pallas as pl
+from jax.experimental.pallas import tpu as pltpu
 from jax.sharding import PartitionSpec as P
 
 NTH = 36
@@ -174,6 +177,474 @@
     return returned_field.reshape(local_comps, row_count, col_count)
 
 
+BLOCK = 128
+GROUP = 24
+CELL_CHUNKS = 4
+MIB = 1024 * 1024
+
+
+def row_of(ref, row):
+    return ref[row : row + 1, :]
+
+
+def upwind(courant, here, ahead, slope_here, bend_here, bend_ahead):
+    square = courant * courant
+    bend = jnp.where(courant > 0.0, bend_here, bend_ahead)
+    return courant * ((here + ahead) - courant * slope_here - (1.0 / 3.0 - square * (1.0 / 3.0)) * bend)
+
+
+def pack_block(block, index, offset, spill, tile, out_ref, rows, held):
+    lanes = lax.broadcasted_iota(jnp.int32, block.shape, 1)
+    moved = jnp.take_along_axis(block, jnp.broadcast_to(index, block.shape), axis=1)
+    merged = jnp.where(lanes >= offset, moved, held)
+    out_ref[rows, pl.ds(pl.multiple_of(tile * BLOCK, BLOCK), BLOCK)] = merged
+    return jnp.where(spill > 0, moved, merged)
+
+
+def pack_fields_kernel(row_count, table_ref, fields_ref, index_ref, out_ref, wide_ref):
+    halves = fields_ref.shape[2] // BLOCK
+    group = 8 // halves
+
+    def step(i, held):
+        index_rows = index_ref[pl.ds(pl.multiple_of(8 * i, 8), 8), :]
+        for r in range(group):
+            row = fields_ref[i * group + r]
+            for h in range(halves):
+                at = r * halves + h
+                b = i * 8 + at
+                held = pack_block(
+                    row[:, h * BLOCK : (h + 1) * BLOCK], index_rows[at : at + 1, :],
+                    table_ref[1, b], table_ref[2, b], table_ref[0, b], wide_ref, slice(None), held,
+                )
+        return held
+
+    held = lax.fori_loop(0, row_count // group, step, jnp.zeros((8, BLOCK), jnp.float32))
+    last = table_ref[0, row_count * halves]
+    wide_ref[:, pl.ds(pl.multiple_of(last * BLOCK, BLOCK), BLOCK)] = held
+    out_ref[...] = wide_ref[:, : out_ref.shape[1]]
+
+
+def propagate_kernel(steps, table_ref, energy_ref, low_ref, high_ref, coef_ref, index_ref, east_ref, north_ref,
+                     fields_ref, *refs):
+    wide_ref, sum_ref, outs = refs[-1], refs[-2], refs[:-2]
+    step_id = pl.program_id(0)
+    row_count, col_count = energy_ref.shape[1:]
+    halves = col_count // BLOCK
+    lane = lax.broadcasted_iota(jnp.int32, (8, col_count), 1)
+    first_lane, last_lane = lane == 0, lane == col_count - 1
+
+    def cell_row(at, coef, index_rows, first, fresh, state, east, north, rows):
+        here, ahead, bend_here, flux_low, held = state
+        new = fresh * row_of(coef, 0)
+        slope = ahead - here
+        bend_ahead = (new - ahead) - slope
+        flux = upwind(east * row_of(coef, 1) + row_of(coef, 2), here, ahead, slope, bend_here, bend_ahead)
+        right = jnp.where(last_lane, 0.0, pltpu.roll(here, col_count - 1, 1))
+        left = jnp.where(first_lane, 0.0, pltpu.roll(here, 1, 1))
+        slope_right = right - here
+        bend = slope_right - (here - left)
+        cross = upwind(north * row_of(coef, 3) + row_of(coef, 4), here, right, slope_right, bend,
+                       pltpu.roll(bend, col_count - 1, 1))
+        moved = row_of(coef, 5) * ((here + here) - (flux - flux_low) - (cross - pltpu.roll(cross, 1, 1)))
+        for h in range(halves):
+            b = first + at * halves + h
+            held = pack_block(
+                moved[:, h * BLOCK : (h + 1) * BLOCK], index_rows[at * halves + h],
+                table_ref[1, b], table_ref[2, b], table_ref[0, b], wide_ref, rows, held,
+            )
+        return ahead, new, bend_ahead, flux, held
+
+    @pl.loop(0, GROUP // 8)
+    def _(g):
+        local = pl.ds(pl.multiple_of(g * 8, 8), 8)
+        rows = pl.ds(pl.multiple_of(step_id * GROUP + g * 8, 8), 8)
+        east = jnp.broadcast_to(east_ref[local, :], (8, col_count))
+        north = jnp.broadcast_to(north_ref[local, :], (8, col_count))
+        here = low_ref[0, local, :] * coef_ref[row_count + 2, 0:1, :]
+        ahead = low_ref[1, local, :] * coef_ref[row_count + 3, 0:1, :]
+        zero = jnp.zeros_like(here)
+        state = (here, ahead, zero, zero, jnp.zeros((8, BLOCK), jnp.float32))
+
+        def eight(i, state):
+            fresh = jnp.swapaxes(energy_ref[local, pl.ds(pl.multiple_of(8 * i, 8), 8), :], 0, 1)
+            picks = index_ref[pl.ds(pl.multiple_of(8 * halves * i, 8), 8 * halves), :]
+            index_rows = [picks[b : b + 1, :] for b in range(8 * halves)]
+            for at in range(8):
+                state = cell_row(at, coef_ref.at[8 * i + at], index_rows, 8 * halves * i, fresh[at], state,
+                                 east, north, rows)
+            return state
+
+        state = lax.fori_loop(0, row_count // 8, eight, state)
+        first = row_count * halves
+        index_rows = [index_ref[first + b : first + b + 1, :] for b in range(2 * halves)]
+        for at in range(2):
+            state = cell_row(at, coef_ref.at[row_count + at], index_rows, first, high_ref[at, local, :], state,
+                             east, north, rows)
+        last = table_ref[0, first + 2 * halves]
+        wide_ref[rows, pl.ds(pl.multiple_of(last * BLOCK, BLOCK), BLOCK)] = state[-1]
+
+    @pl.when(step_id == steps - 1)
+    def _():
+        comps, width = outs[0].shape
+        tile_width = 2 * BLOCK
+        comp_row = lax.broadcasted_iota(jnp.int32, (comps, tile_width), 0)
+        circle_row = comp_row % NTH
+        for o, out_ref in enumerate(outs):
+
+            @pl.loop(0, width // tile_width)
+            def _(i):
+                source = pl.ds(pl.multiple_of(o * width + i * tile_width, tile_width), tile_width)
+                target = pl.ds(pl.multiple_of(i * tile_width, tile_width), tile_width)
+                level = wide_ref[:, source]
+                rate = fields_ref[1:2, source]
+                forward = jnp.maximum(rate, 0.0)
+                backward = jnp.minimum(rate, 0.0)
+                after = pltpu.roll(level, comps - 1, 0)
+                before = pltpu.roll(level, 1, 0)
+                for start in range(0, comps, NTH):
+                    end = start + NTH - 1
+                    after = jnp.where(comp_row == end, level[start : start + 1, :], after)
+                    before = jnp.where(comp_row == start, level[end : end + 1, :], before)
+                turned = (1.0 - forward + backward) * level - backward * after + forward * before
+                out_ref[:, target] = turned
+                sum_ref[:, source] = jnp.sum(turned, axis=0, keepdims=True)
+
+
+def interact_kernel(table_ref, spread_ref, coupling_ref, *refs):
+    window, own_ref, back_ref, delta_ref = refs[:8], refs[8], refs[9], refs[10]
+    comps = window[0].shape[0]
+    kept = []
+    for j in range(1, 7):
+        level = window[j][...]
+        around = jnp.concatenate([window[j - 1][...], level, window[j + 1][...]], axis=0).astype(jnp.bfloat16)
+        partner = jnp.dot(table_ref[j - 1], around, preferred_element_type=jnp.float32)
+        rate = coupling_ref[(j - 1) * comps : j * comps, :] * level
+        plus_part = weight_plus * level
+        minus_part = weight_minus * level
+        deltas = []
+        for pair in range(2):
+            plus = partner[2 * pair * comps : (2 * pair + 1) * comps, :]
+            minus = partner[(2 * pair + 1) * comps : (2 * pair + 2) * comps, :]
+            deltas.append(rate * (plus * (plus_part - (2.0 * weight_cross) * minus) + minus_part * minus))
+        both = jnp.concatenate(deltas, axis=0).astype(jnp.bfloat16)
+        delta_ref[(j - 1) * 2 * comps : j * 2 * comps, :] = both
+        if 2 <= j <= 5:
+            part = -2.0 * (deltas[0] + deltas[1])
+            target = own_ref if j <= 3 else back_ref
+            at = (j % 2) * comps
+            target[at : at + comps, :] = part
+    spread = jnp.dot(spread_ref[...], delta_ref[...], preferred_element_type=jnp.float32)
+    own_ref[...] += spread[: 2 * comps, :]
+    back_ref[...] += spread[2 * comps :, :]
+
+
+def finish_kernel(chunks, table_ref, place_ref, mean_ref, fields_ref, growth_ref, damping_ref, *refs):
+    turned, own, back = refs[: 2 * chunks], refs[2 * chunks : 3 * chunks], refs[3 * chunks : 4 * chunks]
+    out_ref, wide_ref = refs[-2], refs[-1]
+    width = own[0].shape[1]
+    col_count = out_ref.shape[2]
+    halves = col_count // BLOCK
+    tile_width = 2 * BLOCK
+    for o in range(2 * chunks):
+        extra = own[o] if o < chunks else back[o - chunks]
+
+        @pl.loop(0, width // tile_width)
+        def _(i):
+            source = pl.ds(pl.multiple_of(i * tile_width, tile_width), tile_width)
+            target = pl.ds(pl.multiple_of(o * width + i * tile_width, tile_width), tile_width)
+            scale = 1.0 + growth_ref[...] * fields_ref[0:1, target] - damping_ref[...] * mean_ref[0:1, target]
+            wide_ref[:, target] = turned[o][:, source] * scale + extra[:, source]
+
+    @pl.loop(0, GROUP // 8)
+    def _(g):
+        local = pl.ds(pl.multiple_of(g * 8, 8), 8)
+
+        @pl.loop(0, out_ref.shape[1] // 8)
+        def _(i):
+            places = place_ref[pl.ds(pl.multiple_of(8 * halves * i, 8), 8 * halves), :]
+            grid_rows = []
+            for r in range(8):
+                parts = []
+                for h in range(halves):
+                    at = r * halves + h
+                    b = 8 * halves * i + at
+                    place = jnp.broadcast_to(places[at : at + 1, :], (8, BLOCK))
+                    lane = jnp.bitwise_and(place, BLOCK - 1)
+                    low = wide_ref[local, pl.ds(pl.multiple_of(table_ref[1, b] * BLOCK, BLOCK), BLOCK)]
+                    high = wide_ref[local, pl.ds(pl.multiple_of(table_ref[2, b] * BLOCK, BLOCK), BLOCK)]
+                    low = jnp.take_along_axis(low, lane, axis=1)
+                    high = jnp.take_along_axis(high, lane, axis=1)
+                    parts.append(jnp.where(place >= BLOCK, high, jnp.where(place >= 0, low, 0.0)))
+                grid_rows.append(jnp.concatenate(parts, axis=1))
+            out_ref[local, pl.ds(pl.multiple_of(8 * i, 8), 8), :] = jnp.swapaxes(jnp.stack(grid_rows), 0, 1)
+
+
+def params(limit):
+    return pltpu.CompilerParams(vmem_limit_bytes=limit * MIB)
+
+
+def packed_shards(energy, sea_mask, current_u, current_v, wind_forcing, refraction, group_speed, growth, damping,
+                  coupling, dia_index):
+    comp_count = lax.axis_size("comp")
+    comp_pos = lax.axis_index("comp")
+    tile_pos = lax.axis_index("tile")
+    odd = lax.rem(comp_pos, 2)
+    pair_pos = comp_pos // 2
+    local_comps, row_count, col_count = energy.shape
+    comps = local_comps // 2
+    comp_total = NTH * NF
+    first_row = tile_pos * row_count
+    first_comp = comp_pos * local_comps
+    cells = row_count * col_count // 2
+    half = cells // 2
+    width = half // CELL_CHUNKS
+    halves = col_count // BLOCK
+    blocks = row_count * halves
+    tiles = cells // BLOCK
+    f32, i32 = jnp.float32, jnp.int32
+
+    low, high = [], []
+    tile_count = lax.axis_size("tile")
+    forward = [(i, i + 1) for i in range(tile_count - 1)]
+    backward = [(target, source) for source, target in forward]
+    low = lax.ppermute(jnp.swapaxes(energy[:, -2:, :], 0, 1), "tile", forward)
+    high = lax.ppermute(jnp.swapaxes(energy[:, :2, :], 0, 1), "tile", backward)
+
+    window = (row_count + 4, col_count)
+
+    def rows_of(field):
+        return lax.dynamic_slice(jnp.pad(field, ((2, 2), (0, 0))), (first_row, 0), window)
+
+    sea = rows_of(sea_mask.astype(f32))
+    east = rows_of(current_u)
+    north = rows_of(current_v)
+    sea_up = jnp.pad(sea[1:], ((0, 1), (0, 0)))
+    east_up = jnp.pad(east[1:], ((0, 1), (0, 0)))
+    open_east = sea * sea_up
+    flow_east = open_east * (0.5 * (east + east_up))
+    open_north = sea * jnp.pad(sea[:, 1:], ((0, 0), (0, 1)))
+    flow_north = open_north * (0.5 * (north + jnp.pad(north[:, 1:], ((0, 0), (0, 1)))))
+    sea_new = jnp.concatenate([sea[2:], sea[:2]], axis=0)
+    coef = jnp.stack([sea_new, open_east, flow_east, open_north, flow_north, 0.5 * sea, sea, sea], axis=1)
+
+    sea_blocks = sea[2:-2].reshape(blocks, BLOCK)
+    lane = jnp.arange(BLOCK)
+    earlier = (lane[:, None] < lane[None, :]).astype(jnp.bfloat16)
+    rank = jnp.dot(sea_blocks.astype(jnp.bfloat16), earlier, preferred_element_type=f32).astype(i32)
+    number = jnp.sum(sea_blocks, axis=1).astype(i32)
+    block_ids = jnp.arange(blocks + 1)
+    start = jnp.sum(jnp.where(block_ids[None, :blocks] < block_ids[:, None], number[None, :], 0), axis=1)
+    offset = start % BLOCK
+    tile_of = start // BLOCK
+    is_sea = sea_blocks > 0.0
+    place = jnp.where(is_sea, rank + offset[:blocks, None], -1)
+    slot = jnp.where(is_sea, place % BLOCK, -1)
+    index = jnp.sum(jnp.where(slot[:, :, None] == lane[None, None, :], lane[None, :, None], 0), axis=1)
+
+    def turned_tile(tile):
+        return jnp.where(tile >= tiles, tiles, (tile + odd * (tiles // 2)) % tiles)
+
+    put = turned_tile(tile_of)
+    put = put.at[blocks].set(jnp.where(offset[blocks] == 0, tiles, put[blocks]))
+    spill = (offset[:blocks] + number >= BLOCK).astype(i32)
+    get_low = jnp.minimum(put[:blocks], tiles - 1)
+    get_high = jnp.minimum(turned_tile(tile_of[:blocks] + 1), tiles - 1)
+    table = jnp.stack([put, offset, jnp.pad(spill, (0, 1))])
+    edge = 2 * halves
+    table_wide = jnp.concatenate(
+        [jnp.broadcast_to(jnp.array([[tiles], [0], [0]], i32), (3, edge)), table], axis=1
+    )
+    index_wide = jnp.pad(index, ((edge, edge), (0, 0)))
+    table_back = jnp.stack([put[:blocks], get_low, get_high])
+
+    tile_wind = lax.dynamic_slice(wind_forcing, (first_row, 0), (row_count, col_count))
+    tile_turn = lax.dynamic_slice(refraction, (first_row, 0), (row_count, col_count))
+    fields = jnp.stack([tile_wind, tile_turn] * 4, axis=1)
+    packed_fields = pl.pallas_call(
+        functools.partial(pack_fields_kernel, row_count),
+        grid_spec=pltpu.PrefetchScalarGridSpec(
+            num_scalar_prefetch=1,
+            grid=(),
+            in_specs=[pl.BlockSpec(memory_space=pltpu.VMEM)] * 2,
+            out_specs=pl.BlockSpec(memory_space=pltpu.VMEM),
+            scratch_shapes=[pltpu.VMEM((8, cells + BLOCK), f32)],
+        ),
+        out_shape=jax.ShapeDtypeStruct((8, cells), f32),
+        name="pack_fields",
+        compiler_params=params(16),
+    )(table, fields, index)
+
+    angles = (2.0 * math.pi / NTH) * (jnp.arange(comp_total) % NTH).astype(f32)
+    speeds = jnp.repeat(group_speed, NTH)
+    speed_east = lax.dynamic_slice_in_dim(speeds * jnp.cos(angles), first_comp, local_comps)[:, None]
+    speed_north = lax.dynamic_slice_in_dim(speeds * jnp.sin(angles), first_comp, local_comps)[:, None]
+    own_growth = lax.dynamic_slice_in_dim(growth, first_comp, local_comps)[:, None]
+    own_damping = lax.dynamic_slice_in_dim(damping, first_comp, local_comps)[:, None]
+
+    steps = comps // GROUP
+
+    def group_at(part, tables):
+        return (part + tables[0, tables.shape[1] - 1] * (1 - 2 * part)) * steps
+
+    def with_odd(tables):
+        return jnp.concatenate([tables, jnp.broadcast_to(odd, (tables.shape[0], 1)).astype(i32)], axis=1)
+
+    table_wide = with_odd(table_wide)
+    table_back = with_odd(table_back)
+
+    def propagate(part):
+        whole = lambda shape: pl.BlockSpec(shape, lambda s, t: (0,) * len(shape))
+        column = pl.BlockSpec((GROUP, 1), lambda s, t: (group_at(part, t) + s, 0))
+        halo = pl.BlockSpec((2, GROUP, col_count), lambda s, t: (0, group_at(part, t) + s, 0))
+        out_chunk = jax.ShapeDtypeStruct((comps, width), f32)
+        outs = pl.pallas_call(
+            functools.partial(propagate_kernel, steps),
+            grid_spec=pltpu.PrefetchScalarGridSpec(
+                num_scalar_prefetch=1,
+                grid=(steps,),
+                in_specs=[
+                    pl.BlockSpec((GROUP, row_count, col_count), lambda s, t: (group_at(part, t) + s, 0, 0)),
+                    halo, halo, whole(coef.shape), whole(index_wide.shape), column, column,
+                    whole(packed_fields.shape),
+                ],
+                out_specs=[whole((comps, width))] * (2 * CELL_CHUNKS) + [whole((1, cells))],
+                scratch_shapes=[pltpu.VMEM((comps, cells + BLOCK), f32)],
+            ),
+            out_shape=[out_chunk] * (2 * CELL_CHUNKS) + [jax.ShapeDtypeStruct((1, cells), f32)],
+            name="propagate_chunk",
+            compiler_params=params(44),
+            cost_estimate=pl.CostEstimate(
+                flops=60 * comps * row_count * col_count,
+                bytes_accessed=4 * comps * (row_count * col_count + cells), transcendentals=0,
+            ),
+        )(table_wide, energy, low, high, coef, index_wide, speed_east, speed_north, packed_fields)
+        return outs[:CELL_CHUNKS], outs[CELL_CHUNKS : 2 * CELL_CHUNKS], outs[-1]
+
+    pairs = [(i, i ^ 1) for i in range(comp_count)]
+    apart = [(i, i - 2 if i % 2 == 0 else i + 2) for i in range(comp_count)]
+    apart = [(a, b) for a, b in apart if 0 <= b < comp_count]
+    across = [(b, a) for a, b in apart]
+    own, other, received, sums = [], [], [], []
+    from_own, from_received = [], []
+    for part in range(2):
+        kept, sent, level_sum = propagate(part)
+        got = [lax.ppermute(piece, "comp", pairs) for piece in sent]
+        own.append(kept)
+        other.append(sent)
+        received.append(got)
+        sums.append(level_sum)
+        from_own.append([lax.ppermute(piece, "comp", apart) for piece in kept])
+        from_received.append([lax.ppermute(piece, "comp", across) for piece in got])
+
+    def swap(levels):
+        return jnp.where(odd > 0, jnp.roll(levels, half, axis=1), levels)
+
+    mean_level = swap(lax.psum(swap(sums[0] + sums[1]), "comp")) / comp_total
+
+    dia_index, coupling, _ = lax.optimization_barrier((dia_index, coupling, sums[0]))
+    chunk_ids = jnp.arange(8)
+    even_first = 8 * pair_pos - 4 + 2 * chunk_ids
+    odd_first = 8 * pair_pos + 10 - 2 * chunk_ids
+    chunk_first = NTH * jnp.where(odd > 0, odd_first, even_first)
+    margin = 8 * NTH
+    dia_pad = jnp.pad(dia_index, ((0, 0), (margin, margin)), constant_values=-1)
+    coupling_pad = jnp.pad(coupling, (margin, margin))
+    own_ids = jnp.arange(comps)
+    targets, rates = [], []
+    for j in range(1, 7):
+        targets.append(lax.dynamic_slice(dia_pad, (0, chunk_first[j] + margin), (4, comps)))
+        rates.append(lax.dynamic_slice_in_dim(coupling_pad, chunk_first[j] + margin, comps))
+    lookup = []
+    for j in range(1, 7):
+        ids = jnp.concatenate([chunk_first[j + d] + own_ids for d in (-1, 0, 1)])
+        lookup.append((targets[j - 1].reshape(4 * comps)[:, None] == ids[None, :]).astype(jnp.bfloat16))
+    lookup = jnp.stack(lookup)
+    out_ids = jnp.concatenate([chunk_first[j] + own_ids for j in range(2, 6)])
+    spread = []
+    for j in range(1, 7):
+        for pair in range(2):
+            hits = [
+                (out_ids[:, None] == targets[j - 1][2 * pair + q][None, :]).astype(f32) for q in range(2)
+            ]
+            spread.append(hits[0] + hits[1])
+    spread = jnp.concatenate(spread, axis=1).astype(jnp.bfloat16)
+    rates = jnp.concatenate(rates)[:, None]
+
+    lanes = 512 if width % 512 == 0 else width
+    own_parts, back_parts = [], []
+    for c in range(CELL_CHUNKS):
+        levels = [
+            from_received[1][c], from_received[0][c], own[0][c], own[1][c],
+            received[1][c], received[0][c], from_own[0][c], from_own[1][c],
+        ]
+        own_part, back_part = pl.pallas_call(
+            interact_kernel,
+            grid=(width // lanes,),
+            in_specs=[
+                pl.BlockSpec(lookup.shape, lambda s: (0, 0, 0)),
+                pl.BlockSpec(spread.shape, lambda s: (0, 0)),
+                pl.BlockSpec(rates.shape, lambda s: (0, 0)),
+            ] + [pl.BlockSpec((comps, lanes), lambda s: (0, s))] * 8,
+            out_specs=[pl.BlockSpec((2 * comps, lanes), lambda s: (0, s))] * 2,
+            out_shape=[jax.ShapeDtypeStruct((2 * comps, width), f32)] * 2,
+            scratch_shapes=[pltpu.VMEM((12 * comps, lanes), jnp.bfloat16)],
+            name="interact_cells",
+            compiler_params=params(32),
+            cost_estimate=pl.CostEstimate(
+                flops=2 * width * comps * comps * (6 * 12 + 48),
+                bytes_accessed=4 * comps * width * 12, transcendentals=0,
+            ),
+        )(lookup, spread, rates, *levels)
+        own_parts.append(own_part)
+        back_parts.append(lax.ppermute(back_part, "comp", pairs))
+
+    def finish(part, so_far):
+        whole = lambda shape: pl.BlockSpec(shape, lambda s, t: (0,) * len(shape))
+        column = pl.BlockSpec((GROUP, 1), lambda s, t: (group_at(part, t) + s, 0))
+        piece = pl.BlockSpec((GROUP, width), lambda s, t: (s, 0))
+        own_piece = pl.BlockSpec((GROUP, width), lambda s, t: (part * steps + s, 0))
+        back_piece = pl.BlockSpec((GROUP, width), lambda s, t: ((1 - part) * steps + s, 0))
+        inputs = [place, mean_level, packed_fields, own_growth, own_damping]
+        specs = [whole(place.shape), whole(mean_level.shape), whole(packed_fields.shape), column, column]
+        inputs += list(own[part]) + list(other[part]) + own_parts + back_parts
+        specs += [piece] * (2 * CELL_CHUNKS) + [own_piece] * CELL_CHUNKS + [back_piece] * CELL_CHUNKS
+        aliases = {}
+        if so_far is not None:
+            inputs.append(so_far)
+            specs.append(pl.BlockSpec(memory_space=pl.ANY))
+            aliases = {len(inputs): 0}
+        return pl.pallas_call(
+            functools.partial(finish_kernel, CELL_CHUNKS),
+            grid_spec=pltpu.PrefetchScalarGridSpec(
+                num_scalar_prefetch=1,
+                grid=(steps,),
+                in_specs=specs,
+                out_specs=pl.BlockSpec((GROUP, row_count, col_count), lambda s, t: (group_at(part, t) + s, 0, 0)),
+                scratch_shapes=[pltpu.VMEM((GROUP, cells), f32)],
+            ),
+            out_shape=jax.ShapeDtypeStruct(energy.shape, f32),
+            input_output_aliases=aliases,
+            name="finish_chunk",
+            compiler_params=params(40),
+            cost_estimate=pl.CostEstimate(
+                flops=20 * comps * row_count * col_count,
+                bytes_accessed=4 * comps * (row_count * col_count + 2 * cells), transcendentals=0,
+            ),
+        )(table_back, *inputs)
+
+    return finish(1, finish(0, None))
+
+
+def choose_shards(energy, *rest):
+    local_comps, row_count, col_count = energy.shape
+    fits = (
+        local_comps == 4 * NTH and lax.axis_size("comp") % 2 == 0
+        and lax.axis_size("comp") * local_comps == NTH * NF
+        and row_count % 8 == 0 and col_count == 2 * BLOCK
+    )
+    return packed_shards(energy, *rest) if fits else shards(energy, *rest)
+
+
 def solution(mesh):
     placed = (
         P("comp", ("grp", "tile"), None),
@@ -189,7 +660,7 @@
         P(),
     )
     return jax.shard_map(
-        shards,
+        choose_shards,
         mesh=mesh,
         in_specs=placed,
         out_specs=P("comp", ("grp", "tile"), None),

time: 1500 us -> 572 us (0.38)
  blocking collectives: 413 us -> 0 us
  Pallas kernels: 0 us -> 233 us
  waiting for transfers between devices: 408 us -> 201 us
  matrix products: 203 us -> 0.21 us
  other arithmetic: 218 us -> 16.7 us
  local copies, waits for them, and re-layouts: 236 us -> 39.1 us
  starting transfers between devices: 10.4 us -> 59 us
  between operations: 0.55 us -> 22.1 us
    all_to_all x1 -> x0, blocking collectives: 413 us -> none  [shards(): lax.all_to_all(result, 'comp', split_axis=0, concat_axis=1, tiled=True)]
    all_to_all x1 -> x0, waiting for transfers between devices: 408 us -> none  [shards(): lax.all_to_all(propagated, 'comp', split_axis=1, concat_axis=0, tiled=True)]
    pallas_call x0 -> x9, Pallas kernels: none -> 233 us  [the longest x2 115 us: propagate(): pl.pallas_call(functools.partial(propagate_kernel, steps), grid_spec=pltp...]
    dot_general x8 -> x1, matrix products: 203 us -> 0.21 us  [packed_shards(): jnp.dot(sea_blocks.astype(jnp.bfloat16), earlier, preferred_element_type=...]
    ppermute x2 -> x30, waiting for transfers between devices: 0.01 us -> 201 us  [the longest x4 84.7 us: packed_shards(): back_parts.append(lax.ppermute(back_part, 'comp', pairs))]
    mul x8 -> x4, other arithmetic: 133 us -> 0.17 us  [the longest x1 0.12 us: packed_shards(): speeds * jnp.sin(angles)]
    concatenate x4, local copies, waits for them, and re-layouts: 77.3 us -> 2.37 us  [the longest x1 2.21 us: packed_shards(): spread = jnp.concatenate(spread, axis=1).astype(jnp.bfloat16)]
    all_to_all x3 -> x0, local copies, waits for them, and re-layouts: 61.9 us -> none  [the longest x2 40.1 us: shards(): lax.all_to_all(propagated, 'comp', split_axis=1, concat_axis=0, tiled=True)]
  transfers between devices with their start and end apart: 3 -> 31, of which waited for: 1 -> 16; matrix products, arithmetic and copies ran while one was open for 3% -> 6% of each run, Pallas kernels for 0% -> 5%
where the time goes in v1:
time: 572 us; the launch traced here: 571 us
  Pallas kernels  233 us (41%)
  waiting for transfers between devices  201 us (35%)
  starting transfers between devices  59 us (10%)
  local copies, waits for them, and re-layouts  39.1 us (7%)
  between operations  22.1 us (4%)
  other arithmetic  16.7 us (3%)
    pallas_call x2, Pallas kernels, propagate(): pl.pallas_call(functools.partial(propagate_kernel, steps), grid_spec=pltp...  115 us
    pallas_call x2, Pallas kernels, finish(): pl.pallas_call(functools.partial(finish_kernel, CELL_CHUNKS), grid_spec=p...  87.4 us
    ppermute x4, waiting for transfers between devices, packed_shards(): back_parts.append(lax.ppermute(back_part, 'comp', pairs))  84.7 us
    ppermute x8, waiting for transfers between devices, packed_shards(): got = [lax.ppermute(piece, 'comp', pairs) for piece in sent]  71.4 us
    ppermute x8, waiting for transfers between devices, packed_shards(): from_received.append([lax.ppermute(piece, 'comp', across) for piece in got])  44.6 us
    ppermute x8, starting transfers between devices, packed_shards(): from_received.append([lax.ppermute(piece, 'comp', across) for piece in got])  30.3 us
    pallas_call x4, Pallas kernels, packed_shards(): pl.pallas_call(interact_kernel, grid=(width // lanes,), in_specs=[pl.Bloc...  27.3 us
    unnamed x118, local copies, waits for them, and re-layouts  16.6 us
  transfers between devices with their start and end apart: 31, of which 16 were waited for; matrix products, arithmetic and copies ran while one was open for 6% of the time, Pallas kernels for 5%

profile of v1, /device:TPU:0, one launch (start us, length us, event | category | flops | bytes accessed | tf_op | source)
XLA Modules:
  0.0 570.9 jit_solution(14974298409180136644)
XLA Ops:
  30.8 5.6 select_reduce_fusion.index_ref
  51.6 56.6 %propagate_chunk.2 = (f32[72,2048]{1,0:T(8,128)S(1)}, f32[72,2048]{1,0:T(8,128)S(1)}, f32[72,2048]{1,0:T(8,128)S(1)}, f32[72,2048]{1,0:T(8,128)S(1)}, f32[72,204...) custom-call(s32[3,262]{1,0:T(4,128)S(1)} %add_add_fusion.table_ref, ...), custom_call_target="tpu_custom_call" | custom-call | flops 141557760 | bytes 14155776 | tf_op jit(solution)/shard_map/propagate_chunk/pallas_call | solution.py:500
  116.1 58.2 %propagate_chunk.3 = (f32[72,2048]{1,0:T(8,128)S(1)}, f32[72,2048]{1,0:T(8,128)}, f32[72,2048]{1,0:T(8,128)S(1)}, f32[72,2048]{1,0:T(8,128)S(1)}, f32[72,2048]{1...) custom-call(s32[3,262]{1,0:T(4,128)S(1)} %add_add_fusion.table_ref, ...), custom_call_target="tpu_custom_call" | custom-call | flops 141557760 | bytes 14155776 | tf_op jit(solution)/shard_map/propagate_chunk/pallas_call | solution.py:500
  184.3 9.1 %collective-permute-done.2.refs_4_ = f32[72,2048]{1,0:T(8,128)S(1)} collective-permute-done((f32[72,2048]{1,0:T(8,128)}, f32[72,2048]{1,0:T(8,128)S(1)}, u32[]{:S(2)}, u32[]{:S(2)}) %collective-permute-start.2) | collective-permute-done | bytes 589856 | tf_op jit(solution)/shard_map/ppermute | solution.py:531
  194.6 11.8 %collective-permute-done.8.refs_4_ = f32[72,2048]{1,0:T(8,128)} collective-permute-done((f32[72,2048]{1,0:T(8,128)}, f32[72,2048]{1,0:T(8,128)}, u32[]{:S(2)}, u32[]{:S(2)}) %collective-permute-start.8) | collective-permute-done | bytes 589856 | tf_op jit(solution)/shard_map/ppermute | solution.py:531
  207.7 11.4 %collective-permute-done.14.refs_4_ = f32[72,2048]{1,0:T(8,128)S(1)} collective-permute-done((f32[72,2048]{1,0:T(8,128)}, f32[72,2048]{1,0:T(8,128)S(1)}, u32[]{:S(2)}, u32[]{:S(2)}) %collective-permute-start.14) | collective-permute-done | bytes 589856 | tf_op jit(solution)/shard_map/ppermute | solution.py:531
  221.1 10.9 %collective-permute-done.20.refs_4_ = f32[72,2048]{1,0:T(8,128)} collective-permute-done((f32[72,2048]{1,0:T(8,128)}, f32[72,2048]{1,0:T(8,128)}, u32[]{:S(2)}, u32[]{:S(2)}) %collective-permute-start.20) | collective-permute-done | bytes 589856 | tf_op jit(solution)/shard_map/ppermute | solution.py:531
  245.9 11.5 %collective-permute-done.10.refs_5_ = f32[72,2048]{1,0:T(8,128)} collective-permute-done((f32[72,2048]{1,0:T(8,128)}, f32[72,2048]{1,0:T(8,128)}, u32[]{:S(2)}, u32[]{:S(2)}) %collective-permute-start.10) | collective-permute-done | bytes 589856 | tf_op jit(solution)/shard_map/ppermute | solution.py:531
  258.8 11.2 %collective-permute-done.16.refs_5_ = f32[72,2048]{1,0:T(8,128)S(1)} collective-permute-done((f32[72,2048]{1,0:T(8,128)}, f32[72,2048]{1,0:T(8,128)S(1)}, u32[]{:S(2)}, u32[]{:S(2)}) %collective-permute-start.16) | collective-permute-done | bytes 589856 | tf_op jit(solution)/shard_map/ppermute | solution.py:531
  270.0 5.0 collective-permute-start.9
  282.7 5.0 collective-permute-start.15
  302.2 11.3 %collective-permute-done.21.refs_0_ = f32[72,2048]{1,0:T(8,128)} collective-permute-done((f32[72,2048]{1,0:T(8,128)}, f32[72,2048]{1,0:T(8,128)}, u32[]{:S(2)}, u32[]{:S(2)}) %collective-permute-start.21) | collective-permute-done | bytes 589856 | tf_op jit(solution)/shard_map/ppermute | solution.py:537
  315.0 23.9 %collective-permute-done.17.refs_1_ = f32[72,2048]{1,0:T(8,128)} collective-permute-done((f32[72,2048]{1,0:T(8,128)}, f32[72,2048]{1,0:T(8,128)}, u32[]{:S(2)}, u32[]{:S(2)}) %collective-permute-start.17) | collective-permute-done | bytes 589856 | tf_op jit(solution)/shard_map/ppermute | solution.py:537
  343.3 8.2 %collective-permute-done.23.refs_1_ = f32[72,2048]{1,0:T(8,128)} collective-permute-done((f32[72,2048]{1,0:T(8,128)}, f32[72,2048]{1,0:T(8,128)}, u32[]{:S(2)}, u32[]{:S(2)}) %collective-permute-start.23) | collective-permute-done | bytes 589856 | tf_op jit(solution)/shard_map/ppermute | solution.py:537
  360.2 6.9 %interact_cells.7 = (f32[144,2048]{1,0:T(8,128)S(1)}, f32[144,2048]{1,0:T(8,128)S(1)}) custom-call(bf16[6,288,216]{2,1,0:T(8,128)(2,1)S(1)} %stack.96.table_ref, bf16[288,864]{1,0:T(8,128)(2,1)S(1)} %copy-done.21, f32[432,1]{1,0:T(8,128)S(1)} %copy-done.22, f32[72,2048]{1,0:T(8,128)} %collective-permute-done.21.refs_0_, ...), custom_call_target="tpu_custom_call" | custom-call | flops 2548039680 | bytes 7077888 | tf_op jit(solution)/shard_map/interact_cells/pallas_call | solution.py:580
  367.2 6.7 %interact_cells.6 = (f32[144,2048]{1,0:T(8,128)S(1)}, f32[144,2048]{1,0:T(8,128)S(1)}) custom-call(bf16[6,288,216]{2,1,0:T(8,128)(2,1)S(1)} %stack.96.table_ref, bf16[288,864]{1,0:T(8,128)(2,1)S(1)} %copy-done.21, f32[432,1]{1,0:T(8,128)S(1)} %copy-done.22, f32[72,2048]{1,0:T(8,128)} %collective-permute-done.15.refs_0_, ...), custom_call_target="tpu_custom_call" | custom-call | flops 2548039680 | bytes 7077888 | tf_op jit(solution)/shard_map/interact_cells/pallas_call | solution.py:580
  374.1 6.8 %interact_cells.5 = (f32[144,2048]{1,0:T(8,128)S(1)}, f32[144,2048]{1,0:T(8,128)S(1)}) custom-call(bf16[6,288,216]{2,1,0:T(8,128)(2,1)S(1)} %stack.96.table_ref, bf16[288,864]{1,0:T(8,128)(2,1)S(1)} %copy-done.21, f32[432,1]{1,0:T(8,128)S(1)} %copy-done.22, f32[72,2048]{1,0:T(8,128)} %collective-permute-done.9.refs_0_, ...), custom_call_target="tpu_custom_call" | custom-call | flops 2548039680 | bytes 7077888 | tf_op jit(solution)/shard_map/interact_cells/pallas_call | solution.py:580
  383.1 6.8 %interact_cells.4 = (f32[144,2048]{1,0:T(8,128)S(1)}, f32[144,2048]{1,0:T(8,128)S(1)}) custom-call(bf16[6,288,216]{2,1,0:T(8,128)(2,1)S(1)} %stack.96.table_ref, bf16[288,864]{1,0:T(8,128)(2,1)S(1)} %copy-done.21, f32[432,1]{1,0:T(8,128)S(1)} %copy-done.22, f32[72,2048]{1,0:T(8,128)S(1)} %collective-permute-done.3.refs_0_, ...), custom_call_target="tpu_custom_call" | custom-call | flops 2548039680 | bytes 7077888 | tf_op jit(solution)/shard_map/interact_cells/pallas_call | solution.py:580
  391.9 11.0 %collective-permute-done.29.refs_15_ = f32[144,2048]{1,0:T(8,128)S(1)} collective-permute-done((f32[144,2048]{1,0:T(8,128)S(1)}, f32[144,2048]{1,0:T(8,128)S(1)}, u32[]{:S(2)}, u32[]{:S(2)}) %collective-permute-start.29) | collective-permute-done | bytes 1179680 | tf_op jit(solution)/shard_map/ppermute | solution.py:599
  402.9 25.3 %collective-permute-done.28.refs_14_ = f32[144,2048]{1,0:T(8,128)S(1)} collective-permute-done((f32[144,2048]{1,0:T(8,128)S(1)}, f32[144,2048]{1,0:T(8,128)S(1)}, u32[]{:S(2)}, u32[]{:S(2)}) %collective-permute-start.28) | collective-permute-done | bytes 1179680 | tf_op jit(solution)/shard_map/ppermute | solution.py:599
  428.2 25.3 %collective-permute-done.27.refs_13_ = f32[144,2048]{1,0:T(8,128)S(1)} collective-permute-done((f32[144,2048]{1,0:T(8,128)S(1)}, f32[144,2048]{1,0:T(8,128)S(1)}, u32[]{:S(2)}, u32[]{:S(2)}) %collective-permute-start.27) | collective-permute-done | bytes 1179680 | tf_op jit(solution)/shard_map/ppermute | solution.py:599
  453.5 23.1 %collective-permute-done.26.refs_12_ = f32[144,2048]{1,0:T(8,128)S(1)} collective-permute-done((f32[144,2048]{1,0:T(8,128)S(1)}, f32[144,2048]{1,0:T(8,128)S(1)}, u32[]{:S(2)}, u32[]{:S(2)}) %collective-permute-start.26) | collective-permute-done | bytes 1179680 | tf_op jit(solution)/shard_map/ppermute | solution.py:599
  476.7 43.5 %finish_chunk.2.refs_16_ = f32[144,128,256]{2,1,0:T(8,128)} custom-call(s32[3,257]{1,0:T(4,128)S(1)} %concatenate.46.table_ref, s32[256,128]{1,0:T(8,128)S(1)} %get-tuple-element.157.place_ref, f32[1,16384]{1,0:T(1,128)S(1)} %fusion.12.mean_ref, f32[8,16384]{1,0:T(8,128)S(1)} %pack_fields.1.fields_ref, f32[144,1]{1,0:T(8,128)S(1)} %copy.100.growth_ref, ...), custom_call_target="tpu_custom_call" | custom-call | flops 47185920 | bytes 18874368 | tf_op jit(solution)/shard_map/finish_chunk/pallas_call | solution.py:616
  520.1 43.9 %finish_chunk.3 = f32[144,128,256]{2,1,0:T(8,128)} custom-call(s32[3,257]{1,0:T(4,128)S(1)} %concatenate.46.table_ref, s32[256,128]{1,0:T(8,128)S(1)} %get-tuple-element.157.place_ref, f32[1,16384]{1,0:T(1,128)S(1)} %fusion.12.mean_ref, f32[8,16384]{1,0:T(8,128)S(1)} %pack_fields.1.fields_ref, ...), custom_call_target="tpu_custom_call", output_to_operand_aliasing={{}: (22, {})} | custom-call | flops 47185920 | bytes 18874368 | tf_op jit(solution)/shard_map/finish_chunk/pallas_call | solution.py:616
  (264 shorter events, 109.6 us)
Async XLA Ops:
  6.5 292.5 %all-reduce.14.cloned.1.call-start = ((), (), s32[]{:S(2)}) async-start(), calls=%async_computation | async-start | bytes 131072 | tf_op jit(solution)/shard_map/psum | solution.py:542
  9.2 42.5 %collective-permute-start = (f32[2,144,256]{2,1,0:T(8,128)}, f32[2,144,256]{2,1,0:T(8,128)S(1)}, u32[]{:S(2)}, u32[]{:S(2)}) collective-permute-start(f32[2,144,256]{2,1,0:T(8,128)} %bitcast.80), channel_id=1, source_target_pairs={{0,1},{2,3},{4,5},{6,7},{8,9},{10,11},{12,13},{14,15},{16,17},{18,... | collective-permute-start | bytes 884744 | tf_op jit(solution)/shard_map/ppermute | solution.py:410
  12.3 39.4 %collective-permute-start.1 = (f32[2,144,256]{2,1,0:T(8,128)}, f32[2,144,256]{2,1,0:T(8,128)S(1)}, u32[]{:S(2)}, u32[]{:S(2)}) collective-permute-start(f32[2,144,256]{2,1,0:T(8,128)} %bitcast.79), channel_id=1, source_target_pairs={{1,0},{3,2},{5,4},{7,6},{9,8},{11,10},{13,12},{15,14},{17,16},{19,... | collective-permute-start | bytes 884744 | tf_op jit(solution)/shard_map/ppermute | solution.py:411
  179.3 39.7 %collective-permute-start.14 = (f32[72,2048]{1,0:T(8,128)}, f32[72,2048]{1,0:T(8,128)S(1)}, u32[]{:S(2)}, u32[]{:S(2)}) collective-permute-start(f32[72,2048]{1,0:T(8,128)} %get-tuple-element.53.refs_6_), channel_id=1, source_target_pairs={{0,2},{2,0},{4,6},{6,4},{8,10},{10,8},{12,14},{14,12},{1,3},{3,1},... | collective-permute-start | bytes 1769480 | tf_op jit(solution)/shard_map/ppermute | solution.py:531
  181.3 50.7 %collective-permute-start.20 = (f32[72,2048]{1,0:T(8,128)}, f32[72,2048]{1,0:T(8,128)}, u32[]{:S(2)}, u32[]{:S(2)}) collective-permute-start(f32[72,2048]{1,0:T(8,128)} %get-tuple-element.54.refs_7_), channel_id=1, source_target_pairs={{0,2},{2,0},{4,6},{6,4},{8,10},{10,8},{12,14},{14,12},{1,3},{3,1},... | collective-permute-start | bytes 1769480 | tf_op jit(solution)/shard_map/ppermute | solution.py:531
  181.4 52.7 %collective-permute-start.13 = (f32[72,2048]{1,0:T(8,128)}, f32[72,2048]{1,0:T(8,128)S(1)}, u32[]{:S(2)}, u32[]{:S(2)}) collective-permute-start(f32[72,2048]{1,0:T(8,128)} %get-tuple-element.48.refs_3_.refs_1_), channel_id=1, source_target_pairs={{2,6},{4,0},{6,10},{8,4},{10,14},{12,8},{3,7},{5,1},{7,11},{9,5},{... | collective-permute-start | bytes 1769480 | tf_op jit(solution)/shard_map/ppermute | solution.py:536
  193.3 41.9 %collective-permute-start.19 = (f32[72,2048]{1,0:T(8,128)}, f32[72,2048]{1,0:T(8,128)S(1)}, u32[]{:S(2)}, u32[]{:S(2)}) collective-permute-start(f32[72,2048]{1,0:T(8,128)} %copy-done.16), channel_id=1, source_target_pairs={{2,6},{4,0},{6,10},{8,4},{10,14},{12,8},{3,7},{5,1},{7,11},{9,5},{... | collective-permute-start | bytes 1769480 | tf_op jit(solution)/shard_map/ppermute | solution.py:536
  206.4 31.7 %collective-permute-start.25 = (f32[72,2048]{1,0:T(8,128)}, f32[72,2048]{1,0:T(8,128)S(1)}, u32[]{:S(2)}, u32[]{:S(2)}) collective-permute-start(f32[72,2048]{1,0:T(8,128)} %copy-done.18), channel_id=1, source_target_pairs={{2,6},{4,0},{6,10},{8,4},{10,14},{12,8},{3,7},{5,1},{7,11},{9,5},{... | collective-permute-start | bytes 1769480 | tf_op jit(solution)/shard_map/ppermute | solution.py:536
  234.9 35.1 %collective-permute-start.16 = (f32[72,2048]{1,0:T(8,128)}, f32[72,2048]{1,0:T(8,128)S(1)}, u32[]{:S(2)}, u32[]{:S(2)}) collective-permute-start(f32[72,2048]{1,0:T(8,128)} %copy-done.10), channel_id=1, source_target_pairs={{0,2},{2,0},{4,6},{6,4},{8,10},{10,8},{12,14},{14,12},{1,3},{3,1},... | collective-permute-start | bytes 1769480 | tf_op jit(solution)/shard_map/ppermute | solution.py:531
  236.1 46.7 %collective-permute-start.22 = (f32[72,2048]{1,0:T(8,128)}, f32[72,2048]{1,0:T(8,128)}, u32[]{:S(2)}, u32[]{:S(2)}) collective-permute-start(f32[72,2048]{1,0:T(8,128)} %copy-done.12), channel_id=1, source_target_pairs={{0,2},{2,0},{4,6},{6,4},{8,10},{10,8},{12,14},{14,12},{1,3},{3,1},... | collective-permute-start | bytes 1769480 | tf_op jit(solution)/shard_map/ppermute | solution.py:531
  238.9 48.9 %collective-permute-start.12 = (f32[72,2048]{1,0:T(8,128)}, f32[72,2048]{1,0:T(8,128)}, u32[]{:S(2)}, u32[]{:S(2)}) collective-permute-start(f32[72,2048]{1,0:T(8,128)} %copy-done), channel_id=1, source_target_pairs={{2,6},{4,0},{6,10},{8,4},{10,14},{12,8},{3,7},{5,1},{7,11},{9,5},{... | collective-permute-start | bytes 1769480 | tf_op jit(solution)/shard_map/ppermute | solution.py:536
  244.6 46.6 %collective-permute-start.18 = (f32[72,2048]{1,0:T(8,128)}, f32[72,2048]{1,0:T(8,128)}, u32[]{:S(2)}, u32[]{:S(2)}) collective-permute-start(f32[72,2048]{1,0:T(8,128)} %copy-done.2), channel_id=1, source_target_pairs={{2,6},{4,0},{6,10},{8,4},{10,14},{12,8},{3,7},{5,1},{7,11},{9,5},{... | collective-permute-start | bytes 1769480 | tf_op jit(solution)/shard_map/ppermute | solution.py:536
  257.5 37.3 %collective-permute-start.24 = (f32[72,2048]{1,0:T(8,128)}, f32[72,2048]{1,0:T(8,128)}, u32[]{:S(2)}, u32[]{:S(2)}) collective-permute-start(f32[72,2048]{1,0:T(8,128)} %copy-done.4), channel_id=1, source_target_pairs={{2,6},{4,0},{6,10},{8,4},{10,14},{12,8},{3,7},{5,1},{7,11},{9,5},{... | collective-permute-start | bytes 1769480 | tf_op jit(solution)/shard_map/ppermute | solution.py:536
  291.3 82.7 %collective-permute-start.11 = (f32[72,2048]{1,0:T(8,128)}, f32[72,2048]{1,0:T(8,128)}, u32[]{:S(2)}, u32[]{:S(2)}) collective-permute-start(f32[72,2048]{1,0:T(8,128)} %collective-permute-done.10.refs_5_), channel_id=1, source_target_pairs={{6,2},{0,4},{10,6},{4,8},{14,10},{8,12},{7,3},{1,5},{11,7},{5,9},{... | collective-permute-start | bytes 1769480 | tf_op jit(solution)/shard_map/ppermute | solution.py:537
  294.8 44.1 %collective-permute-start.17 = (f32[72,2048]{1,0:T(8,128)}, f32[72,2048]{1,0:T(8,128)}, u32[]{:S(2)}, u32[]{:S(2)}) collective-permute-start(f32[72,2048]{1,0:T(8,128)} %copy-done.33), channel_id=1, source_target_pairs={{6,2},{0,4},{10,6},{4,8},{14,10},{8,12},{7,3},{1,5},{11,7},{5,9},{... | collective-permute-start | bytes 1769480 | tf_op jit(solution)/shard_map/ppermute | solution.py:537
  296.9 54.6 %collective-permute-start.23 = (f32[72,2048]{1,0:T(8,128)}, f32[72,2048]{1,0:T(8,128)}, u32[]{:S(2)}, u32[]{:S(2)}) collective-permute-start(f32[72,2048]{1,0:T(8,128)} %collective-permute-done.22.refs_5_), channel_id=1, source_target_pairs={{6,2},{0,4},{10,6},{4,8},{14,10},{8,12},{7,3},{1,5},{11,7},{5,9},{... | collective-permute-start | bytes 1769480 | tf_op jit(solution)/shard_map/ppermute | solution.py:537
  300.9 80.0 %collective-permute-start.7 = (f32[72,2048]{1,0:T(8,128)S(1)}, f32[72,2048]{1,0:T(8,128)S(1)}, u32[]{:S(2)}, u32[]{:S(2)}) collective-permute-start(f32[72,2048]{1,0:T(8,128)S(1)} %copy-done.15), channel_id=1, source_target_pairs={{2,6},{4,0},{6,10},{8,4},{10,14},{12,8},{3,7},{5,1},{7,11},{9,5},{... | collective-permute-start | bytes 1769480 | tf_op jit(solution)/shard_map/ppermute | solution.py:536
  313.6 69.4 %collective-permute-start.6 = (f32[72,2048]{1,0:T(8,128)S(1)}, f32[72,2048]{1,0:T(8,128)S(1)}, u32[]{:S(2)}, u32[]{:S(2)}) collective-permute-start(f32[72,2048]{1,0:T(8,128)S(1)} %get-tuple-element.58.refs_2_.refs_0_), channel_id=1, source_target_pairs={{2,6},{4,0},{6,10},{8,4},{10,14},{12,8},{3,7},{5,1},{7,11},{9,5},{... | collective-permute-start | bytes 1769480 | tf_op jit(solution)/shard_map/ppermute | solution.py:536
  338.9 44.3 %collective-permute-start.3 = (f32[72,2048]{1,0:T(8,128)}, f32[72,2048]{1,0:T(8,128)S(1)}, u32[]{:S(2)}, u32[]{:S(2)}) collective-permute-start(f32[72,2048]{1,0:T(8,128)} %copy-done.23), channel_id=1, source_target_pairs={{6,2},{0,4},{10,6},{4,8},{14,10},{8,12},{7,3},{1,5},{11,7},{5,9},{... | collective-permute-start | bytes 1769480 | tf_op jit(solution)/shard_map/ppermute | solution.py:537
  351.5 31.6 %collective-permute-start.5 = (f32[72,2048]{1,0:T(8,128)}, f32[72,2048]{1,0:T(8,128)S(1)}, u32[]{:S(2)}, u32[]{:S(2)}) collective-permute-start(f32[72,2048]{1,0:T(8,128)} %collective-permute-done.4.refs_5_), channel_id=1, source_target_pairs={{6,2},{0,4},{10,6},{4,8},{14,10},{8,12},{7,3},{1,5},{11,7},{5,9},{... | collective-permute-start | bytes 1769480 | tf_op jit(solution)/shard_map/ppermute | solution.py:537
  374.0 29.0 %collective-permute-start.29 = (f32[144,2048]{1,0:T(8,128)S(1)}, f32[144,2048]{1,0:T(8,128)S(1)}, u32[]{:S(2)}, u32[]{:S(2)}) collective-permute-start(f32[144,2048]{1,0:T(8,128)S(1)} %get-tuple-element.72), channel_id=1, source_target_pairs={{0,2},{2,0},{4,6},{6,4},{8,10},{10,8},{12,14},{14,12},{1,3},{3,1},... | collective-permute-start | bytes 3538952 | tf_op jit(solution)/shard_map/ppermute | solution.py:599
  380.9 47.3 %collective-permute-start.28 = (f32[144,2048]{1,0:T(8,128)S(1)}, f32[144,2048]{1,0:T(8,128)S(1)}, u32[]{:S(2)}, u32[]{:S(2)}) collective-permute-start(f32[144,2048]{1,0:T(8,128)S(1)} %get-tuple-element.71), channel_id=1, source_target_pairs={{0,2},{2,0},{4,6},{6,4},{8,10},{10,8},{12,14},{14,12},{1,3},{3,1},... | collective-permute-start | bytes 3538952 | tf_op jit(solution)/shard_map/ppermute | solution.py:599
  383.0 70.5 %collective-permute-start.27 = (f32[144,2048]{1,0:T(8,128)S(1)}, f32[144,2048]{1,0:T(8,128)S(1)}, u32[]{:S(2)}, u32[]{:S(2)}) collective-permute-start(f32[144,2048]{1,0:T(8,128)S(1)} %get-tuple-element.70), channel_id=1, source_target_pairs={{0,2},{2,0},{4,6},{6,4},{8,10},{10,8},{12,14},{14,12},{1,3},{3,1},... | collective-permute-start | bytes 3538952 | tf_op jit(solution)/shard_map/ppermute | solution.py:599
  389.9 86.7 %collective-permute-start.26 = (f32[144,2048]{1,0:T(8,128)S(1)}, f32[144,2048]{1,0:T(8,128)S(1)}, u32[]{:S(2)}, u32[]{:S(2)}) collective-permute-start(f32[144,2048]{1,0:T(8,128)S(1)} %get-tuple-element.69), channel_id=1, source_target_pairs={{0,2},{2,0},{4,6},{6,4},{8,10},{10,8},{12,14},{14,12},{1,3},{3,1},... | collective-permute-start | bytes 3538952 | tf_op jit(solution)/shard_map/ppermute | solution.py:599
  (65 other events, 2136.2 us)
Sparse Core Ops, SparseCore 0:
  183.8 72.3 all-reduce.13

commit v2 on v1

--- a/solution.py
+++ b/solution.py
@@ -3,6 +3,7 @@
 
 import jax
 import jax.numpy as jnp
+import numpy as np
 from jax import lax
 from jax.experimental import pallas as pl
 from jax.experimental.pallas import tpu as pltpu
@@ -181,6 +182,9 @@
 GROUP = 24
 CELL_CHUNKS = 4
 MIB = 1024 * 1024
+EDGE = 2
+SEA, OPEN_EAST, FLOW_EAST, OPEN_NORTH, FLOW_NORTH, HALF_SEA, WIND, TURN = range(8)
+PUT, OFFSET, SPILL, NEXT = range(4)
 
 
 def row_of(ref, row):
@@ -201,56 +205,180 @@
     return jnp.where(spill > 0, moved, merged)
 
 
-def pack_fields_kernel(row_count, table_ref, fields_ref, index_ref, out_ref, wide_ref):
-    halves = fields_ref.shape[2] // BLOCK
-    group = 8 // halves
-
-    def step(i, held):
-        index_rows = index_ref[pl.ds(pl.multiple_of(8 * i, 8), 8), :]
-        for r in range(group):
-            row = fields_ref[i * group + r]
-            for h in range(halves):
-                at = r * halves + h
-                b = i * 8 + at
+def prepare_kernel(places, base_ref, speed_ref, sea_ref, east_ref, north_ref, wind_ref, turn_ref, cos_ref, sin_ref,
+                   coef_ref, index_ref, place_ref, table_ref, speed_east_ref, speed_north_ref, field_ref, pick_ref):
+    first_row, odd, first_freq = base_ref[0], base_ref[1], base_ref[2]
+    all_rows, col_count = sea_ref.shape
+    row_count = place_ref.shape[1]
+    tiles = places // BLOCK
+    sea = sea_ref[...].astype(jnp.float32)
+    row = lax.broadcasted_iota(jnp.int32, sea.shape, 0)
+    col = lax.broadcasted_iota(jnp.int32, sea.shape, 1)
+
+    def next_row(field):
+        return jnp.where(row == all_rows - 1, 0.0, pltpu.roll(field, all_rows - 1, 0))
+
+    def next_col(field):
+        return jnp.where(col == col_count - 1, 0.0, pltpu.roll(field, col_count - 1, 1))
+
+    open_east, open_north = sea * next_row(sea), sea * next_col(sea)
+    east, north = east_ref[...], north_ref[...]
+    field_ref[SEA] = sea
+    field_ref[OPEN_EAST] = open_east
+    field_ref[FLOW_EAST] = open_east * (0.5 * (east + next_row(east)))
+    field_ref[OPEN_NORTH] = open_north
+    field_ref[FLOW_NORTH] = open_north * (0.5 * (north + next_col(north)))
+    field_ref[HALF_SEA] = 0.5 * sea
+    field_ref[WIND] = wind_ref[...]
+    field_ref[TURN] = turn_ref[...]
+    coef_ref[0:EDGE] = jnp.zeros((EDGE, 8, col_count), jnp.float32)
+    coef_ref[EDGE + all_rows :] = jnp.zeros((EDGE, 8, col_count), jnp.float32)
+
+    @pl.loop(0, all_rows // 8)
+    def _(i):
+        rows = field_ref[:, pl.ds(pl.multiple_of(8 * i, 8), 8), :]
+        coef_ref[pl.ds(8 * i + EDGE, 8)] = jnp.swapaxes(rows, 0, 1)
+
+    freqs = cos_ref.shape[0] // NTH
+    for f in range(freqs):
+        circle = slice(f * NTH, (f + 1) * NTH)
+        speed_east_ref[circle, :] = cos_ref[circle, :] * speed_ref[first_freq + f]
+        speed_north_ref[circle, :] = sin_ref[circle, :] * speed_ref[first_freq + f]
+
+    bf16, f32 = jnp.bfloat16, jnp.float32
+    tile_sea = sea_ref[pl.ds(pl.multiple_of(first_row, 8), row_count), :].astype(f32)
+    square = (BLOCK, BLOCK)
+    down, over = lax.broadcasted_iota(jnp.int32, square, 0), lax.broadcasted_iota(jnp.int32, square, 1)
+    before = (down < over).astype(f32).astype(bf16)
+    ones = jnp.ones(square, bf16)
+    row_square = (row_count, row_count)
+    above = lax.broadcasted_iota(jnp.int32, row_square, 1) < lax.broadcasted_iota(jnp.int32, row_square, 0)
+    above = above.astype(f32).astype(bf16)
+    parts = [tile_sea[:, :BLOCK], tile_sea[:, BLOCK:]]
+    numbers = [jnp.dot(p.astype(bf16), ones, preferred_element_type=f32) for p in parts]
+    in_row = numbers[0] + numbers[1]
+    starts = [jnp.dot(above, in_row.astype(bf16), preferred_element_type=f32)]
+    starts.append(starts[0] + numbers[0])
+    total = jnp.sum(in_row, axis=0, keepdims=True).astype(jnp.int32)
+
+    def turned_tile(tile):
+        return jnp.where(tile >= tiles, tiles, jnp.bitwise_and(tile + odd * (tiles // 2), tiles - 1))
+
+    index_ref[...] = jnp.zeros(index_ref.shape, jnp.int32)
+    wide = (8, 2 * BLOCK)
+    wide_lane = lax.broadcasted_iota(jnp.int32, wide, 1)
+    wide_row = lax.broadcasted_iota(jnp.int32, wide, 0)
+    columns = []
+    for h in range(2):
+        rank = jnp.dot(parts[h].astype(bf16), before, preferred_element_type=f32).astype(jnp.int32)
+        start = starts[h].astype(jnp.int32)
+        offset = jnp.bitwise_and(start, BLOCK - 1)
+        is_sea = parts[h] > 0.0
+        place = jnp.where(is_sea, rank + offset, -1)
+        place_ref[h] = place
+        slot = jnp.where(is_sea, jnp.bitwise_and(place, BLOCK - 1), -1).astype(f32).T
+        from_lane = down[:, :row_count].astype(f32)
+
+        @pl.loop(0, BLOCK // 8)
+        def _(i):
+            found = []
+            for k in range(8):
+                lane = (8 * i + k).astype(f32)
+                found.append(jnp.sum(jnp.where(slot == lane, from_lane, 0.0), axis=0, keepdims=True))
+            pick_ref[pl.ds(pl.multiple_of(8 * i, 8), 8), :] = jnp.concatenate(found, axis=0)
+
+        index_ref[h, EDGE : EDGE + row_count, :] = pick_ref[...].T.astype(jnp.int32)
+        start_row = starts[h].T[0:8, :].astype(jnp.int32)
+        end_row = (starts[h] + numbers[h]).T[0:8, :].astype(jnp.int32)
+        tile = lax.shift_right_logical(start_row, 7)
+        offset_row = jnp.bitwise_and(start_row, BLOCK - 1)
+        spill = jnp.where(offset_row + (end_row - start_row) >= BLOCK, 1, 0)
+        columns += [turned_tile(tile), offset_row, spill, jnp.minimum(turned_tile(tile + 1), tiles - 1)]
+    empty = jnp.where(jnp.bitwise_and(wide_row, 3) == PUT, tiles, 0)
+    merged = jnp.zeros((8, row_count), jnp.int32)
+    for k, column in enumerate(columns):
+        merged = jnp.where(wide_row[:, :row_count] == k, column, merged)
+    merged = jnp.concatenate([merged, jnp.zeros((8, 2 * BLOCK - row_count), jnp.int32)], axis=1)
+    merged = pltpu.roll(merged, EDGE, 1)
+    inside = (wide_lane >= EDGE) & (wide_lane < EDGE + row_count)
+    end_offset = jnp.bitwise_and(total, BLOCK - 1)
+    end_tile = jnp.where(end_offset == 0, tiles, turned_tile(lax.shift_right_logical(total, 7)))
+    end_tile = jnp.concatenate([end_tile, end_tile], axis=1)
+    result = jnp.where(inside, merged, empty)
+    table_ref[...] = jnp.where((wide_lane == EDGE + row_count + EDGE) & (wide_row == PUT), end_tile, result)
+
+
+def pack_fields_kernel(row_count, base_ref, table_ref, coef_ref, index_ref, out_ref, wide_ref):
+    def some_rows(first, count, held):
+        picks = [index_ref[h, pl.ds(first, count), :] for h in range(2)]
+        for at in range(count):
+            row = first + at
+            fields = coef_ref[base_ref[0] + row]
+            for h in range(2):
                 held = pack_block(
-                    row[:, h * BLOCK : (h + 1) * BLOCK], index_rows[at : at + 1, :],
-                    table_ref[1, b], table_ref[2, b], table_ref[0, b], wide_ref, slice(None), held,
+                    fields[:, h * BLOCK : (h + 1) * BLOCK], picks[h][at : at + 1, :], table_ref[4 * h + OFFSET, row],
+                    table_ref[4 * h + SPILL, row], table_ref[4 * h + PUT, row], wide_ref, slice(None), held,
                 )
         return held
 
-    held = lax.fori_loop(0, row_count // group, step, jnp.zeros((8, BLOCK), jnp.float32))
-    last = table_ref[0, row_count * halves]
+    held = jnp.zeros((8, BLOCK), jnp.float32)
+    held = lax.fori_loop(
+        0, row_count // 8, lambda i, held: some_rows(pl.multiple_of(8 * i, 8), 8, held), held
+    )
+    held = some_rows(row_count, EDGE, held)
+    last = table_ref[PUT, row_count + 2 * EDGE]
     wide_ref[:, pl.ds(pl.multiple_of(last * BLOCK, BLOCK), BLOCK)] = held
     out_ref[...] = wide_ref[:, : out_ref.shape[1]]
 
 
-def propagate_kernel(steps, table_ref, energy_ref, low_ref, high_ref, coef_ref, index_ref, east_ref, north_ref,
-                     fields_ref, *refs):
-    wide_ref, sum_ref, outs = refs[-1], refs[-2], refs[:-2]
+def propagate_kernel(part, steps, base_ref, table_ref, energy_ref, low_ref, high_ref, coef_ref, index_ref, east_ref,
+                     north_ref, fields_ref, *refs):
+    wide_ref, rows_ref, sems = refs[-3:]
+    sum_ref, outs = refs[-4], refs[:-4]
     step_id = pl.program_id(0)
     row_count, col_count = energy_ref.shape[1:]
-    halves = col_count // BLOCK
+    first_row = base_ref[0]
+    first_comp = (part + base_ref[1] * (1 - 2 * part)) * steps * GROUP
     lane = lax.broadcasted_iota(jnp.int32, (8, col_count), 1)
     first_lane, last_lane = lane == 0, lane == col_count - 1
 
-    def cell_row(at, coef, index_rows, first, fresh, state, east, north, rows):
+    def fetch(step):
+        comps = pl.ds(first_comp + step * GROUP, GROUP)
+
+        @pl.loop(0, row_count, unroll=4)
+        def _(r):
+            pltpu.make_async_copy(energy_ref.at[comps, r, :], rows_ref.at[step % 2, r], sems.at[step % 2]).start()
+
+    @pl.when(step_id == 0)
+    def _():
+        fetch(0)
+
+    @pl.when(step_id + 1 < steps)
+    def _():
+        fetch(step_id + 1)
+
+    slot = step_id % 2
+    pltpu.make_async_copy(rows_ref.at[slot], rows_ref.at[slot], sems.at[slot]).wait()
+
+    def cell_row(row, picks, fresh, state, east, north, rows):
         here, ahead, bend_here, flux_low, held = state
-        new = fresh * row_of(coef, 0)
+        coef = coef_ref.at[first_row + row]
+        new = fresh * row_of(coef_ref.at[first_row + row + EDGE], SEA)
         slope = ahead - here
         bend_ahead = (new - ahead) - slope
-        flux = upwind(east * row_of(coef, 1) + row_of(coef, 2), here, ahead, slope, bend_here, bend_ahead)
+        flux = upwind(east * row_of(coef, OPEN_EAST) + row_of(coef, FLOW_EAST), here, ahead, slope, bend_here,
+                      bend_ahead)
         right = jnp.where(last_lane, 0.0, pltpu.roll(here, col_count - 1, 1))
         left = jnp.where(first_lane, 0.0, pltpu.roll(here, 1, 1))
         slope_right = right - here
         bend = slope_right - (here - left)
-        cross = upwind(north * row_of(coef, 3) + row_of(coef, 4), here, right, slope_right, bend,
+        cross = upwind(north * row_of(coef, OPEN_NORTH) + row_of(coef, FLOW_NORTH), here, right, slope_right, bend,
                        pltpu.roll(bend, col_count - 1, 1))
-        moved = row_of(coef, 5) * ((here + here) - (flux - flux_low) - (cross - pltpu.roll(cross, 1, 1)))
-        for h in range(halves):
-            b = first + at * halves + h
+        moved = row_of(coef, HALF_SEA) * ((here + here) - (flux - flux_low) - (cross - pltpu.roll(cross, 1, 1)))
+        for h in range(2):
             held = pack_block(
-                moved[:, h * BLOCK : (h + 1) * BLOCK], index_rows[at * halves + h],
-                table_ref[1, b], table_ref[2, b], table_ref[0, b], wide_ref, rows, held,
+                moved[:, h * BLOCK : (h + 1) * BLOCK], picks[h], table_ref[4 * h + OFFSET, row],
+                table_ref[4 * h + SPILL, row], table_ref[4 * h + PUT, row], wide_ref, rows, held,
             )
         return ahead, new, bend_ahead, flux, held
 
@@ -258,29 +386,26 @@
     def _(g):
         local = pl.ds(pl.multiple_of(g * 8, 8), 8)
         rows = pl.ds(pl.multiple_of(step_id * GROUP + g * 8, 8), 8)
-        east = jnp.broadcast_to(east_ref[local, :], (8, col_count))
-        north = jnp.broadcast_to(north_ref[local, :], (8, col_count))
-        here = low_ref[0, local, :] * coef_ref[row_count + 2, 0:1, :]
-        ahead = low_ref[1, local, :] * coef_ref[row_count + 3, 0:1, :]
+        east = jnp.concatenate([east_ref[local, :]] * 2, axis=1)
+        north = jnp.concatenate([north_ref[local, :]] * 2, axis=1)
+        here = low_ref[0, local, :] * row_of(coef_ref.at[first_row], SEA)
+        ahead = low_ref[1, local, :] * row_of(coef_ref.at[first_row + 1], SEA)
         zero = jnp.zeros_like(here)
         state = (here, ahead, zero, zero, jnp.zeros((8, BLOCK), jnp.float32))
 
         def eight(i, state):
-            fresh = jnp.swapaxes(energy_ref[local, pl.ds(pl.multiple_of(8 * i, 8), 8), :], 0, 1)
-            picks = index_ref[pl.ds(pl.multiple_of(8 * halves * i, 8), 8 * halves), :]
-            index_rows = [picks[b : b + 1, :] for b in range(8 * halves)]
+            picks = [index_ref[h, pl.ds(pl.multiple_of(8 * i, 8), 8), :] for h in range(2)]
             for at in range(8):
-                state = cell_row(at, coef_ref.at[8 * i + at], index_rows, 8 * halves * i, fresh[at], state,
-                                 east, north, rows)
+                state = cell_row(8 * i + at, [p[at : at + 1, :] for p in picks],
+                                 rows_ref[slot, 8 * i + at, local, :], state, east, north, rows)
             return state
 
         state = lax.fori_loop(0, row_count // 8, eight, state)
-        first = row_count * halves
-        index_rows = [index_ref[first + b : first + b + 1, :] for b in range(2 * halves)]
-        for at in range(2):
-            state = cell_row(at, coef_ref.at[row_count + at], index_rows, first, high_ref[at, local, :], state,
+        picks = [index_ref[h, row_count : row_count + EDGE, :] for h in range(2)]
+        for at in range(EDGE):
+            state = cell_row(row_count + at, [p[at : at + 1, :] for p in picks], high_ref[at, local, :], state,
                              east, north, rows)
-        last = table_ref[0, first + 2 * halves]
+        last = table_ref[PUT, row_count + 2 * EDGE]
         wide_ref[rows, pl.ds(pl.multiple_of(last * BLOCK, BLOCK), BLOCK)] = state[-1]
 
     @pl.when(step_id == steps - 1)
@@ -296,7 +421,7 @@
                 source = pl.ds(pl.multiple_of(o * width + i * tile_width, tile_width), tile_width)
                 target = pl.ds(pl.multiple_of(i * tile_width, tile_width), tile_width)
                 level = wide_ref[:, source]
-                rate = fields_ref[1:2, source]
+                rate = fields_ref[TURN : TURN + 1, source]
                 forward = jnp.maximum(rate, 0.0)
                 backward = jnp.minimum(rate, 0.0)
                 after = pltpu.roll(level, comps - 1, 0)
@@ -338,12 +463,11 @@
     back_ref[...] += spread[2 * comps :, :]
 
 
-def finish_kernel(chunks, table_ref, place_ref, mean_ref, fields_ref, growth_ref, damping_ref, *refs):
+def finish_kernel(chunks, base_ref, table_ref, place_ref, mean_ref, fields_ref, growth_ref, damping_ref, *refs):
     turned, own, back = refs[: 2 * chunks], refs[2 * chunks : 3 * chunks], refs[3 * chunks : 4 * chunks]
     out_ref, wide_ref = refs[-2], refs[-1]
     width = own[0].shape[1]
-    col_count = out_ref.shape[2]
-    halves = col_count // BLOCK
+    tiles = wide_ref.shape[1] // BLOCK
     tile_width = 2 * BLOCK
     for o in range(2 * chunks):
         extra = own[o] if o < chunks else back[o - chunks]
@@ -352,8 +476,11 @@
         def _(i):
             source = pl.ds(pl.multiple_of(i * tile_width, tile_width), tile_width)
             target = pl.ds(pl.multiple_of(o * width + i * tile_width, tile_width), tile_width)
-            scale = 1.0 + growth_ref[...] * fields_ref[0:1, target] - damping_ref[...] * mean_ref[0:1, target]
+            scale = (1.0 + growth_ref[...] * fields_ref[WIND : WIND + 1, target]
+                     - damping_ref[...] * mean_ref[0:1, target])
             wide_ref[:, target] = turned[o][:, source] * scale + extra[:, source]
+
+    lane = lax.broadcasted_iota(jnp.int32, (8, BLOCK), 1)
 
     @pl.loop(0, GROUP // 8)
     def _(g):
@@ -361,26 +488,30 @@
 
         @pl.loop(0, out_ref.shape[1] // 8)
         def _(i):
-            places = place_ref[pl.ds(pl.multiple_of(8 * halves * i, 8), 8 * halves), :]
+            places = [place_ref[h, pl.ds(pl.multiple_of(8 * i, 8), 8), :] for h in range(2)]
             grid_rows = []
             for r in range(8):
                 parts = []
-                for h in range(halves):
-                    at = r * halves + h
-                    b = 8 * halves * i + at
-                    place = jnp.broadcast_to(places[at : at + 1, :], (8, BLOCK))
-                    lane = jnp.bitwise_and(place, BLOCK - 1)
-                    low = wide_ref[local, pl.ds(pl.multiple_of(table_ref[1, b] * BLOCK, BLOCK), BLOCK)]
-                    high = wide_ref[local, pl.ds(pl.multiple_of(table_ref[2, b] * BLOCK, BLOCK), BLOCK)]
-                    low = jnp.take_along_axis(low, lane, axis=1)
-                    high = jnp.take_along_axis(high, lane, axis=1)
-                    parts.append(jnp.where(place >= BLOCK, high, jnp.where(place >= 0, low, 0.0)))
+                for h in range(2):
+                    row = 8 * i + r + EDGE
+                    place = jnp.broadcast_to(places[h][r : r + 1, :], (8, BLOCK))
+                    first = jnp.minimum(table_ref[4 * h + PUT, row], tiles - 1)
+                    second = table_ref[4 * h + NEXT, row]
+                    low = wide_ref[local, pl.ds(pl.multiple_of(first * BLOCK, BLOCK), BLOCK)]
+                    high = wide_ref[local, pl.ds(pl.multiple_of(second * BLOCK, BLOCK), BLOCK)]
+                    near = jnp.where(lane >= table_ref[4 * h + OFFSET, row], low, high)
+                    level = jnp.take_along_axis(near, jnp.bitwise_and(place, BLOCK - 1), axis=1)
+                    parts.append(jnp.where(place >= 0, level, 0.0))
                 grid_rows.append(jnp.concatenate(parts, axis=1))
             out_ref[local, pl.ds(pl.multiple_of(8 * i, 8), 8), :] = jnp.swapaxes(jnp.stack(grid_rows), 0, 1)
 
 
 def params(limit):
     return pltpu.CompilerParams(vmem_limit_bytes=limit * MIB)
+
+
+def after(value, *others):
+    return lax.optimization_barrier((value,) + others)[0]
 
 
 def packed_shards(energy, sea_mask, current_u, current_v, wind_forcing, refraction, group_speed, growth, damping,
@@ -398,150 +529,120 @@
     cells = row_count * col_count // 2
     half = cells // 2
     width = half // CELL_CHUNKS
-    halves = col_count // BLOCK
-    blocks = row_count * halves
-    tiles = cells // BLOCK
     f32, i32 = jnp.float32, jnp.int32
-
-    low, high = [], []
+    base = jnp.stack([first_row, odd, comp_pos * (local_comps // NTH)]).astype(i32)
+
     tile_count = lax.axis_size("tile")
     forward = [(i, i + 1) for i in range(tile_count - 1)]
     backward = [(target, source) for source, target in forward]
-    low = lax.ppermute(jnp.swapaxes(energy[:, -2:, :], 0, 1), "tile", forward)
-    high = lax.ppermute(jnp.swapaxes(energy[:, :2, :], 0, 1), "tile", backward)
-
-    window = (row_count + 4, col_count)
-
-    def rows_of(field):
-        return lax.dynamic_slice(jnp.pad(field, ((2, 2), (0, 0))), (first_row, 0), window)
-
-    sea = rows_of(sea_mask.astype(f32))
-    east = rows_of(current_u)
-    north = rows_of(current_v)
-    sea_up = jnp.pad(sea[1:], ((0, 1), (0, 0)))
-    east_up = jnp.pad(east[1:], ((0, 1), (0, 0)))
-    open_east = sea * sea_up
-    flow_east = open_east * (0.5 * (east + east_up))
-    open_north = sea * jnp.pad(sea[:, 1:], ((0, 0), (0, 1)))
-    flow_north = open_north * (0.5 * (north + jnp.pad(north[:, 1:], ((0, 0), (0, 1)))))
-    sea_new = jnp.concatenate([sea[2:], sea[:2]], axis=0)
-    coef = jnp.stack([sea_new, open_east, flow_east, open_north, flow_north, 0.5 * sea, sea, sea], axis=1)
-
-    sea_blocks = sea[2:-2].reshape(blocks, BLOCK)
-    lane = jnp.arange(BLOCK)
-    earlier = (lane[:, None] < lane[None, :]).astype(jnp.bfloat16)
-    rank = jnp.dot(sea_blocks.astype(jnp.bfloat16), earlier, preferred_element_type=f32).astype(i32)
-    number = jnp.sum(sea_blocks, axis=1).astype(i32)
-    block_ids = jnp.arange(blocks + 1)
-    start = jnp.sum(jnp.where(block_ids[None, :blocks] < block_ids[:, None], number[None, :], 0), axis=1)
-    offset = start % BLOCK
-    tile_of = start // BLOCK
-    is_sea = sea_blocks > 0.0
-    place = jnp.where(is_sea, rank + offset[:blocks, None], -1)
-    slot = jnp.where(is_sea, place % BLOCK, -1)
-    index = jnp.sum(jnp.where(slot[:, :, None] == lane[None, None, :], lane[None, :, None], 0), axis=1)
-
-    def turned_tile(tile):
-        return jnp.where(tile >= tiles, tiles, (tile + odd * (tiles // 2)) % tiles)
-
-    put = turned_tile(tile_of)
-    put = put.at[blocks].set(jnp.where(offset[blocks] == 0, tiles, put[blocks]))
-    spill = (offset[:blocks] + number >= BLOCK).astype(i32)
-    get_low = jnp.minimum(put[:blocks], tiles - 1)
-    get_high = jnp.minimum(turned_tile(tile_of[:blocks] + 1), tiles - 1)
-    table = jnp.stack([put, offset, jnp.pad(spill, (0, 1))])
-    edge = 2 * halves
-    table_wide = jnp.concatenate(
-        [jnp.broadcast_to(jnp.array([[tiles], [0], [0]], i32), (3, edge)), table], axis=1
-    )
-    index_wide = jnp.pad(index, ((edge, edge), (0, 0)))
-    table_back = jnp.stack([put[:blocks], get_low, get_high])
-
-    tile_wind = lax.dynamic_slice(wind_forcing, (first_row, 0), (row_count, col_count))
-    tile_turn = lax.dynamic_slice(refraction, (first_row, 0), (row_count, col_count))
-    fields = jnp.stack([tile_wind, tile_turn] * 4, axis=1)
+    low = lax.ppermute(jnp.swapaxes(energy[:, -EDGE:, :], 0, 1), "tile", forward)
+    high = lax.ppermute(jnp.swapaxes(energy[:, :EDGE, :], 0, 1), "tile", backward)
+
+    all_rows = sea_mask.shape[0]
+    angles = np.float32(2.0 * math.pi / NTH) * (np.arange(local_comps) % NTH).astype(np.float32)
+    cosines = np.broadcast_to(np.cos(angles)[:, None], (local_comps, BLOCK)).astype(np.float32)
+    sines = np.broadcast_to(np.sin(angles)[:, None], (local_comps, BLOCK)).astype(np.float32)
+    vmem = pl.BlockSpec(memory_space=pltpu.VMEM)
+    padded_rows = row_count + 8
+    coef, index, place, table, speed_east, speed_north = pl.pallas_call(
+        functools.partial(prepare_kernel, cells),
+        grid_spec=pltpu.PrefetchScalarGridSpec(
+            num_scalar_prefetch=2,
+            grid=(),
+            in_specs=[vmem] * 7,
+            out_specs=[vmem] * 6,
+            scratch_shapes=[pltpu.VMEM((8, all_rows, col_count), f32), pltpu.VMEM((BLOCK, row_count), f32)],
+        ),
+        out_shape=[
+            jax.ShapeDtypeStruct((all_rows + 2 * EDGE, 8, col_count), f32),
+            jax.ShapeDtypeStruct((2, padded_rows, BLOCK), i32),
+            jax.ShapeDtypeStruct((2, row_count, BLOCK), i32),
+            jax.ShapeDtypeStruct((8, 2 * BLOCK), i32),
+            jax.ShapeDtypeStruct((local_comps, BLOCK), f32),
+            jax.ShapeDtypeStruct((local_comps, BLOCK), f32),
+        ],
+        name="prepare",
+        compiler_params=params(24),
+    )(base, group_speed, sea_mask, current_u, current_v, wind_forcing, refraction, cosines, sines)
     packed_fields = pl.pallas_call(
         functools.partial(pack_fields_kernel, row_count),
         grid_spec=pltpu.PrefetchScalarGridSpec(
-            num_scalar_prefetch=1,
+            num_scalar_prefetch=2,
             grid=(),
-            in_specs=[pl.BlockSpec(memory_space=pltpu.VMEM)] * 2,
-            out_specs=pl.BlockSpec(memory_space=pltpu.VMEM),
+            in_specs=[vmem] * 2,
+            out_specs=vmem,
             scratch_shapes=[pltpu.VMEM((8, cells + BLOCK), f32)],
         ),
         out_shape=jax.ShapeDtypeStruct((8, cells), f32),
         name="pack_fields",
         compiler_params=params(16),
-    )(table, fields, index)
-
-    angles = (2.0 * math.pi / NTH) * (jnp.arange(comp_total) % NTH).astype(f32)
-    speeds = jnp.repeat(group_speed, NTH)
-    speed_east = lax.dynamic_slice_in_dim(speeds * jnp.cos(angles), first_comp, local_comps)[:, None]
-    speed_north = lax.dynamic_slice_in_dim(speeds * jnp.sin(angles), first_comp, local_comps)[:, None]
-    own_growth = lax.dynamic_slice_in_dim(growth, first_comp, local_comps)[:, None]
-    own_damping = lax.dynamic_slice_in_dim(damping, first_comp, local_comps)[:, None]
+    )(base, table, coef, index)
 
     steps = comps // GROUP
 
-    def group_at(part, tables):
-        return (part + tables[0, tables.shape[1] - 1] * (1 - 2 * part)) * steps
-
-    def with_odd(tables):
-        return jnp.concatenate([tables, jnp.broadcast_to(odd, (tables.shape[0], 1)).astype(i32)], axis=1)
-
-    table_wide = with_odd(table_wide)
-    table_back = with_odd(table_back)
-
-    def propagate(part):
-        whole = lambda shape: pl.BlockSpec(shape, lambda s, t: (0,) * len(shape))
-        column = pl.BlockSpec((GROUP, 1), lambda s, t: (group_at(part, t) + s, 0))
-        halo = pl.BlockSpec((2, GROUP, col_count), lambda s, t: (0, group_at(part, t) + s, 0))
+    def group_at(part, base_ref):
+        return (part + base_ref[1] * (1 - 2 * part)) * steps
+
+    def whole(shape):
+        return pl.BlockSpec(shape, lambda s, b, t: (0,) * len(shape))
+
+    def column(part, lanes):
+        return pl.BlockSpec((GROUP, lanes), lambda s, b, t: (group_at(part, b) + s, 0))
+
+    def propagate(part, table):
+        halo = pl.BlockSpec((EDGE, GROUP, col_count), lambda s, b, t: (0, group_at(part, b) + s, 0))
         out_chunk = jax.ShapeDtypeStruct((comps, width), f32)
         outs = pl.pallas_call(
-            functools.partial(propagate_kernel, steps),
+            functools.partial(propagate_kernel, part, steps),
             grid_spec=pltpu.PrefetchScalarGridSpec(
-                num_scalar_prefetch=1,
+                num_scalar_prefetch=2,
                 grid=(steps,),
                 in_specs=[
-                    pl.BlockSpec((GROUP, row_count, col_count), lambda s, t: (group_at(part, t) + s, 0, 0)),
-                    halo, halo, whole(coef.shape), whole(index_wide.shape), column, column,
-                    whole(packed_fields.shape),
+                    pl.BlockSpec(memory_space=pl.ANY), halo, halo, whole(coef.shape), whole(index.shape),
+                    column(part, BLOCK), column(part, BLOCK), whole(packed_fields.shape),
                 ],
                 out_specs=[whole((comps, width))] * (2 * CELL_CHUNKS) + [whole((1, cells))],
-                scratch_shapes=[pltpu.VMEM((comps, cells + BLOCK), f32)],
+                scratch_shapes=[
+                    pltpu.VMEM((comps, cells + BLOCK), f32),
+                    pltpu.VMEM((2, row_count, GROUP, col_count), f32),
+                    pltpu.SemaphoreType.DMA((2,)),
+                ],
             ),
             out_shape=[out_chunk] * (2 * CELL_CHUNKS) + [jax.ShapeDtypeStruct((1, cells), f32)],
             name="propagate_chunk",
             compiler_params=params(44),
             cost_estimate=pl.CostEstimate(
-                flops=60 * comps * row_count * col_count,
-                bytes_accessed=4 * comps * (row_count * col_count + cells), transcendentals=0,
+                flops=60 * comps * row_count * col_count, bytes_accessed=100 * MIB, transcendentals=0,
             ),
-        )(table_wide, energy, low, high, coef, index_wide, speed_east, speed_north, packed_fields)
-        return outs[:CELL_CHUNKS], outs[CELL_CHUNKS : 2 * CELL_CHUNKS], outs[-1]
+        )(base, table, energy, low, high, coef, index, speed_east, speed_north, packed_fields)
+        return list(outs[:CELL_CHUNKS]), list(outs[CELL_CHUNKS : 2 * CELL_CHUNKS]), outs[-1]
 
     pairs = [(i, i ^ 1) for i in range(comp_count)]
     apart = [(i, i - 2 if i % 2 == 0 else i + 2) for i in range(comp_count)]
     apart = [(a, b) for a, b in apart if 0 <= b < comp_count]
     across = [(b, a) for a, b in apart]
-    own, other, received, sums = [], [], [], []
-    from_own, from_received = [], []
-    for part in range(2):
-        kept, sent, level_sum = propagate(part)
-        got = [lax.ppermute(piece, "comp", pairs) for piece in sent]
-        own.append(kept)
-        other.append(sent)
-        received.append(got)
-        sums.append(level_sum)
-        from_own.append([lax.ppermute(piece, "comp", apart) for piece in kept])
-        from_received.append([lax.ppermute(piece, "comp", across) for piece in got])
+    chunk_range = range(CELL_CHUNKS)
+    kept_0, sent_0, sums_0 = propagate(0, table)
+    got_0 = [lax.ppermute(piece, "comp", pairs) for piece in sent_0]
+    from_own_0 = [lax.ppermute(piece, "comp", apart) for piece in kept_0]
+    kept_1, sent_1, sums_1 = propagate(1, after(table, sums_0))
+    from_got_0 = [lax.ppermute(piece, "comp", across) for piece in got_0]
+    got_1, from_own_1 = [], []
+    for c in chunk_range:
+        waits = [got_0[c]] + ([got_1[c - 2]] if c >= 2 else [])
+        got_1.append(lax.ppermute(after(sent_1[c], *waits), "comp", pairs))
+        from_own_1.append(lax.ppermute(after(kept_1[c], from_own_0[c]), "comp", apart))
 
     def swap(levels):
         return jnp.where(odd > 0, jnp.roll(levels, half, axis=1), levels)
 
-    mean_level = swap(lax.psum(swap(sums[0] + sums[1]), "comp")) / comp_total
-
-    dia_index, coupling, _ = lax.optimization_barrier((dia_index, coupling, sums[0]))
+    mean_level = swap(lax.psum(swap(sums_0 + sums_1), "comp")) / comp_total
+
+    dia_index, coupling, growth, damping, _ = lax.optimization_barrier(
+        (dia_index, coupling, growth, damping, sums_0)
+    )
+    own_growth = lax.dynamic_slice_in_dim(growth, first_comp, local_comps)[:, None]
+    own_damping = lax.dynamic_slice_in_dim(damping, first_comp, local_comps)[:, None]
     chunk_ids = jnp.arange(8)
     even_first = 8 * pair_pos - 4 + 2 * chunk_ids
     odd_first = 8 * pair_pos + 10 - 2 * chunk_ids
@@ -572,10 +673,10 @@
 
     lanes = 512 if width % 512 == 0 else width
     own_parts, back_parts = [], []
-    for c in range(CELL_CHUNKS):
+    for c in chunk_range:
+        from_got_1 = lax.ppermute(after(got_1[c], *own_parts[c - 2 : c - 1]) if c >= 2 else got_1[c], "comp", across)
         levels = [
-            from_received[1][c], from_received[0][c], own[0][c], own[1][c],
-            received[1][c], received[0][c], from_own[0][c], from_own[1][c],
+            from_got_1, from_got_0[c], kept_0[c], kept_1[c], got_1[c], got_0[c], from_own_0[c], from_own_1[c],
         ]
         own_part, back_part = pl.pallas_call(
             interact_kernel,
@@ -592,34 +693,34 @@
             compiler_params=params(32),
             cost_estimate=pl.CostEstimate(
                 flops=2 * width * comps * comps * (6 * 12 + 48),
-                bytes_accessed=4 * comps * width * 12, transcendentals=0,
+                bytes_accessed=20 * MIB, transcendentals=0,
             ),
         )(lookup, spread, rates, *levels)
         own_parts.append(own_part)
-        back_parts.append(lax.ppermute(back_part, "comp", pairs))
+        wait = got_1[c + 2] if c + 2 < CELL_CHUNKS else back_parts[c - 2]
+        back_parts.append(lax.ppermute(after(back_part, wait), "comp", pairs))
 
     def finish(part, so_far):
-        whole = lambda shape: pl.BlockSpec(shape, lambda s, t: (0,) * len(shape))
-        column = pl.BlockSpec((GROUP, 1), lambda s, t: (group_at(part, t) + s, 0))
-        piece = pl.BlockSpec((GROUP, width), lambda s, t: (s, 0))
-        own_piece = pl.BlockSpec((GROUP, width), lambda s, t: (part * steps + s, 0))
-        back_piece = pl.BlockSpec((GROUP, width), lambda s, t: ((1 - part) * steps + s, 0))
+        piece = pl.BlockSpec((GROUP, width), lambda s, b, t: (s, 0))
+        own_piece = pl.BlockSpec((GROUP, width), lambda s, b, t: (part * steps + s, 0))
+        back_piece = pl.BlockSpec((GROUP, width), lambda s, b, t: ((1 - part) * steps + s, 0))
         inputs = [place, mean_level, packed_fields, own_growth, own_damping]
-        specs = [whole(place.shape), whole(mean_level.shape), whole(packed_fields.shape), column, column]
-        inputs += list(own[part]) + list(other[part]) + own_parts + back_parts
+        specs = [whole(place.shape), whole(mean_level.shape), whole(packed_fields.shape), column(part, 1),
+                 column(part, 1)]
+        inputs += [kept_0, kept_1][part] + [sent_0, sent_1][part] + own_parts + back_parts
         specs += [piece] * (2 * CELL_CHUNKS) + [own_piece] * CELL_CHUNKS + [back_piece] * CELL_CHUNKS
         aliases = {}
         if so_far is not None:
             inputs.append(so_far)
             specs.append(pl.BlockSpec(memory_space=pl.ANY))
-            aliases = {len(inputs): 0}
+            aliases = {len(inputs) + 1: 0}
         return pl.pallas_call(
             functools.partial(finish_kernel, CELL_CHUNKS),
             grid_spec=pltpu.PrefetchScalarGridSpec(
-                num_scalar_prefetch=1,
+                num_scalar_prefetch=2,
                 grid=(steps,),
                 in_specs=specs,
-                out_specs=pl.BlockSpec((GROUP, row_count, col_count), lambda s, t: (group_at(part, t) + s, 0, 0)),
+                out_specs=pl.BlockSpec((GROUP, row_count, col_count), lambda s, b, t: (group_at(part, b) + s, 0, 0)),
                 scratch_shapes=[pltpu.VMEM((GROUP, cells), f32)],
             ),
             out_shape=jax.ShapeDtypeStruct(energy.shape, f32),
@@ -628,9 +729,9 @@
             compiler_params=params(40),
             cost_estimate=pl.CostEstimate(
                 flops=20 * comps * row_count * col_count,
-                bytes_accessed=4 * comps * (row_count * col_count + 2 * cells), transcendentals=0,
+                bytes_accessed=100 * MIB, transcendentals=0,
             ),
-        )(table_back, *inputs)
+        )(base, table, *inputs)
 
     return finish(1, finish(0, None))
 

time: 572 us -> 505 us (0.88)
  waiting for transfers between devices: 201 us -> 110 us
  local copies, waits for them, and re-layouts: 39.1 us -> 54.5 us
  starting transfers between devices: 59 us -> 69.2 us
  other arithmetic: 16.7 us -> 9.14 us
    ppermute x30, waiting for transfers between devices: 201 us -> 82.7 us  [the longest x4 49.4 us: packed_shards(): back_parts.append(lax.ppermute(after(back_part, wait), 'comp', pairs))]
    psum x1, waiting for transfers between devices: 0.01 us -> 27.4 us  [packed_shards(): mean_level = swap(lax.psum(swap(sums_0 + sums_1), 'comp')) / comp_total]
    unnamed x118 -> x198, local copies, waits for them, and re-layouts: 16.6 us -> 41.3 us
    another operation x13 -> x0, local copies, waits for them, and re-layouts: 11 us -> none  [the longest x8 9.15 us: packed_shards(): jnp.stack([sea_new, open_east, flow_east, open_north, flow_north, 0.5 * s...]
    ppermute x30, starting transfers between devices: 59 us -> 69.2 us  [the longest x4 18.8 us: packed_shards(): from_got_0 = [lax.ppermute(piece, 'comp', across) for piece in got_0]]
    reduce_sum x3 -> x0, other arithmetic: 5.88 us -> none  [the longest x1 5.62 us: packed_shards(): jnp.sum(jnp.where(slot[:, :, None] == lane[None, None, :], lane[None, :,...]
    pallas_call x2 -> x3, Pallas kernels: 115 us -> 120 us  [the longest x2 116 us: propagate(): pl.pallas_call(functools.partial(propagate_kernel, part, steps), grid_spe...]
  transfers between devices with their start and end apart: 31 -> 31, of which waited for: 16 -> 8; matrix products, arithmetic and copies ran while one was open for 6% -> 3% of each run, Pallas kernels for 5% -> 19%
where the time goes in v2:
time: 505 us; the launch traced here: 503 us
  Pallas kernels  238 us (47%)
  waiting for transfers between devices  110 us (22%)
  starting transfers between devices  69.2 us (14%)
  local copies, waits for them, and re-layouts  54.5 us (11%)
  between operations  21.9 us (4%)
  other arithmetic  9.14 us (2%)
    pallas_call x2, Pallas kernels, propagate(): pl.pallas_call(functools.partial(propagate_kernel, part, steps), grid_spe...  116 us
    pallas_call x2, Pallas kernels, finish(): pl.pallas_call(functools.partial(finish_kernel, CELL_CHUNKS), grid_spec=p...  86.2 us
    ppermute x4, waiting for transfers between devices, packed_shards(): back_parts.append(lax.ppermute(after(back_part, wait), 'comp', pairs))  49.4 us
    unnamed x198, local copies, waits for them, and re-layouts  41.3 us
    pallas_call x4, Pallas kernels, packed_shards(): pl.pallas_call(interact_kernel, grid=(width // lanes,), in_specs=[pl.Bloc...  28.5 us
    psum x1, waiting for transfers between devices, packed_shards(): mean_level = swap(lax.psum(swap(sums_0 + sums_1), 'comp')) / comp_total  27.4 us
    ppermute x4, starting transfers between devices, packed_shards(): from_got_0 = [lax.ppermute(piece, 'comp', across) for piece in got_0]  18.8 us
    ppermute x4, waiting for transfers between devices, packed_shards(): lax.ppermute(after(got_1[c], *own_parts[c - 2:c - 1]) if c >= 2 else got_...  17.8 us
  transfers between devices with their start and end apart: 31, of which 8 were waited for; matrix products, arithmetic and copies ran while one was open for 3% of the time, Pallas kernels for 19%

profile of v2, /device:TPU:0, one launch (start us, length us, event | category | flops | bytes accessed | tf_op | source)
XLA Modules:
  0.0 502.5 jit_solution(403861644336325995)
XLA Ops:
  31.1 4.3 prepare.1
  35.4 2.6 pack_fields.1.fields_ref
  40.1 57.7 %propagate_chunk.2 = (f32[72,2048]{1,0:T(8,128)S(1)}, f32[72,2048]{1,0:T(8,128)S(1)}, f32[72,2048]{1,0:T(8,128)}, f32[72,2048]{1,0:T(8,128)S(1)}, f32[72,2048]{1...) custom-call(s32[3]{0:T(128)S(1)} %pad_add_fusion.7.base_ref, ...), custom_call_target="tpu_custom_call" | custom-call | flops 141557760 | bytes 104857600 | tf_op jit(solution)/shard_map/propagate_chunk/pallas_call | solution.py:595
  115.9 58.4 %propagate_chunk.3 = (f32[72,2048]{1,0:T(8,128)}, f32[72,2048]{1,0:T(8,128)S(1)}, f32[72,2048]{1,0:T(8,128)S(1)}, f32[72,2048]{1,0:T(8,128)}, f32[72,2048]{1,0:T...) custom-call(s32[3]{0:T(128)S(1)} %pad_add_fusion.7.base_ref, ...), custom_call_target="tpu_custom_call" | custom-call | flops 141557760 | bytes 104857600 | tf_op jit(solution)/shard_map/propagate_chunk/pallas_call | solution.py:595
  177.3 6.5 %collective-permute-start.9 = (f32[72,2048]{1,0:T(8,128)S(1)}, f32[72,2048]{1,0:T(8,128)S(1)}, u32[]{:S(2)}, u32[]{:S(2)}) collective-permute-start(f32[72,2048]{1,0:T(8,128)S(1)} %get-tuple-element.83.refs_5_), channel_id=1, source_target_pairs={{0,2},{2,0},{4,6},{6,4},{8,10},{10,8},{12,14},{14,12},{1,3},{3,1},... | collective-permute-start | bytes 1769480 | tf_op jit(solution)/shard_map/ppermute | solution.py:633
  185.4 8.6 %collective-permute-done.12.refs_6_ = f32[72,2048]{1,0:T(8,128)S(1)} collective-permute-done((f32[72,2048]{1,0:T(8,128)S(1)}, f32[72,2048]{1,0:T(8,128)S(1)}, u32[]{:S(2)}, u32[]{:S(2)}) %collective-permute-start.12) | collective-permute-done | bytes 589856 | tf_op jit(solution)/shard_map/ppermute | solution.py:627
  197.4 7.4 %collective-permute-start.3 = (f32[72,2048]{1,0:T(8,128)S(1)}, f32[72,2048]{1,0:T(8,128)}, u32[]{:S(2)}, u32[]{:S(2)}) collective-permute-start(f32[72,2048]{1,0:T(8,128)S(1)} %get-tuple-element.78.refs_4_), channel_id=1, source_target_pairs={{0,2},{2,0},{4,6},{6,4},{8,10},{10,8},{12,14},{14,12},{1,3},{3,1},... | collective-permute-start | bytes 1769480 | tf_op jit(solution)/shard_map/ppermute | solution.py:633
  210.1 2.7 collective-permute-start.10
  216.5 5.8 %collective-permute-done.11.refs_1_ = f32[72,2048]{1,0:T(8,128)S(1)} collective-permute-done((f32[72,2048]{1,0:T(8,128)S(1)}, f32[72,2048]{1,0:T(8,128)S(1)}, u32[]{:S(2)}, u32[]{:S(2)}) %collective-permute-start.11) | collective-permute-done | bytes 589856 | tf_op jit(solution)/shard_map/ppermute | solution.py:629
  226.4 4.9 collective-permute-start.5
  245.8 7.2 %interact_cells.5 = (f32[144,2048]{1,0:T(8,128)S(1)}, f32[144,2048]{1,0:T(8,128)}) custom-call(bf16[6,288,216]{2,1,0:T(8,128)(2,1)S(1)} %stack.28.table_ref, bf16[288,864]{1,0:T(8,128)(2,1)S(1)} %copy-done.29, f32[432,1]{1,0:T(8,128)S(1)} %copy-done.41, f32[72,2048]{1,0:T(8,128)} %collective-permute-done.10.refs_0_, f32[72,2048]{1,0:T(8,128)S(1)} %copy-done.62, ...), custom_call_target="tpu_custom_call" | custom-call | flops 2548039680 | bytes 20971520 | tf_op jit(solution)/shard_map/interact_cells/pallas_call | solution.py:681
  252.9 5.9 %collective-permute-start.23 = (f32[72,2048]{1,0:T(8,128)}, f32[72,2048]{1,0:T(8,128)}, u32[]{:S(2)}, u32[]{:S(2)}) collective-permute-start(f32[72,2048]{1,0:T(8,128)} %collective-permute-done.20.refs_5_), channel_id=1, source_target_pairs={{6,2},{0,4},{10,6},{4,8},{14,10},{8,12},{7,3},{1,5},{11,7},{5,9},{... | collective-permute-start | bytes 1769480 | tf_op jit(solution)/shard_map/ppermute | solution.py:629
  258.9 5.0 collective-permute-start.4
  268.6 17.1 %collective-permute-done.4.refs_0_ = f32[72,2048]{1,0:T(8,128)} collective-permute-done((f32[72,2048]{1,0:T(8,128)}, f32[72,2048]{1,0:T(8,128)}, u32[]{:S(2)}, u32[]{:S(2)}) %collective-permute-start.4) | collective-permute-done | bytes 589856 | tf_op jit(solution)/shard_map/ppermute | solution.py:677
  290.0 7.5 %interact_cells.4 = (f32[144,2048]{1,0:T(8,128)S(1)}, f32[144,2048]{1,0:T(8,128)}) custom-call(bf16[6,288,216]{2,1,0:T(8,128)(2,1)S(1)} %stack.28.table_ref, bf16[288,864]{1,0:T(8,128)(2,1)S(1)} %copy-done.30, f32[432,1]{1,0:T(8,128)S(1)} %copy-done.42, f32[72,2048]{1,0:T(8,128)} %collective-permute-done.4.refs_0_, ...), custom_call_target="tpu_custom_call" | custom-call | flops 2548039680 | bytes 20971520 | tf_op jit(solution)/shard_map/interact_cells/pallas_call | solution.py:681
  298.5 5.8 %collective-permute-start.17 = (f32[72,2048]{1,0:T(8,128)}, f32[72,2048]{1,0:T(8,128)}, u32[]{:S(2)}, u32[]{:S(2)}) collective-permute-start(f32[72,2048]{1,0:T(8,128)} %collective-permute-done.14.refs_5_), channel_id=1, source_target_pairs={{6,2},{0,4},{10,6},{4,8},{14,10},{8,12},{7,3},{1,5},{11,7},{5,9},{... | collective-permute-start | bytes 1769480 | tf_op jit(solution)/shard_map/ppermute | solution.py:629
  304.3 4.0 collective-permute-start.16
  310.3 27.4 %all-reduce.4.cloned.1.call-done = f32[1,16384]{1,0:T(1,128)} async-done(((f32[1,16384]{1,0:T(1,128)}), f32[1,16384]{1,0:T(1,128)}) %all-reduce.4.cloned.1.call-update) | async-done | bytes 65552 | tf_op jit(solution)/shard_map/psum | solution.py:639
  342.7 6.9 %interact_cells.7 = (f32[144,2048]{1,0:T(8,128)S(1)}, f32[144,2048]{1,0:T(8,128)S(1)}) custom-call(bf16[6,288,216]{2,1,0:T(8,128)(2,1)S(1)} %stack.28.table_ref, bf16[288,864]{1,0:T(8,128)(2,1)S(1)} %copy-done.31, f32[432,1]{1,0:T(8,128)S(1)} %copy-done.43, f32[72,2048]{1,0:T(8,128)} %collective-permute-done.22.refs_0_, ...), custom_call_target="tpu_custom_call" | custom-call | flops 2548039680 | bytes 20971520 | tf_op jit(solution)/shard_map/interact_cells/pallas_call | solution.py:681
  349.7 7.0 %interact_cells.6 = (f32[144,2048]{1,0:T(8,128)S(1)}, f32[144,2048]{1,0:T(8,128)S(1)}) custom-call(bf16[6,288,216]{2,1,0:T(8,128)(2,1)S(1)} %stack.28.table_ref, bf16[288,864]{1,0:T(8,128)(2,1)S(1)} %copy-done.31, f32[432,1]{1,0:T(8,128)S(1)} %copy-done.43, f32[72,2048]{1,0:T(8,128)} %collective-permute-done.16.refs_0_, ...), custom_call_target="tpu_custom_call" | custom-call | flops 2548039680 | bytes 20971520 | tf_op jit(solution)/shard_map/interact_cells/pallas_call | solution.py:681
  358.9 26.8 %collective-permute-done.28.refs_14_ = f32[144,2048]{1,0:T(8,128)S(1)} collective-permute-done((f32[144,2048]{1,0:T(8,128)S(1)}, f32[144,2048]{1,0:T(8,128)S(1)}, u32[]{:S(2)}, u32[]{:S(2)}) %collective-permute-start.28) | collective-permute-done | bytes 1179680 | tf_op jit(solution)/shard_map/ppermute | solution.py:701
  385.6 22.7 %collective-permute-done.29.refs_15_ = f32[144,2048]{1,0:T(8,128)S(1)} collective-permute-done((f32[144,2048]{1,0:T(8,128)S(1)}, f32[144,2048]{1,0:T(8,128)S(1)}, u32[]{:S(2)}, u32[]{:S(2)}) %collective-permute-start.29) | collective-permute-done | bytes 1179680 | tf_op jit(solution)/shard_map/ppermute | solution.py:701
  409.4 42.9 %finish_chunk.2.refs_16_ = f32[144,128,256]{2,1,0:T(8,128)} custom-call(s32[3]{0:T(128)S(1)} %pad_add_fusion.7.base_ref, s32[8,256]{1,0:T(8,128)S(1)} %get-tuple-element.63.table_ref, s32[2,128,128]{2,1,0:T(8,128)S(1)} %get-tuple-element.57.place_ref, f32[1,16384]{1,0:T(1,128)S(1)} %fusion.mean_ref, f32[8,16384]{1,0:T(8,128)S(1)} %pack_fields.1.fields_ref, ...), custom_call_target="tpu_custom_call" | custom-call | flops 47185920 | bytes 104857600 | tf_op jit(solution)/shard_map/finish_chunk/pallas_call | solution.py:717
  452.4 43.3 %finish_chunk.3 = f32[144,128,256]{2,1,0:T(8,128)} custom-call(s32[3]{0:T(128)S(1)} %pad_add_fusion.7.base_ref, s32[8,256]{1,0:T(8,128)S(1)} %get-tuple-element.63.table_ref, s32[2,128,128]{2,1,0:T(8,128)S(1)} %get-tuple-element.57.place_ref, f32[1,16384]{1,0:T(1,128)S(1)} %fusion.mean_ref, ...), custom_call_target="tpu_custom_call", output_to_operand_aliasing={{}: (23, {})} | custom-call | flops 47185920 | bytes 104857600 | tf_op jit(solution)/shard_map/finish_chunk/pallas_call | solution.py:717
  (291 shorter events, 92.5 us)
Async XLA Ops:
  6.5 331.2 %all-reduce.4.cloned.1.call-start = ((), (), s32[]{:S(2)}) async-start(), calls=%async_computation | async-start | bytes 131072 | tf_op jit(solution)/shard_map/psum | solution.py:639
  9.2 30.9 %collective-permute-start = (f32[2,144,256]{2,1,0:T(8,128)}, f32[2,144,256]{2,1,0:T(8,128)S(1)}, u32[]{:S(2)}, u32[]{:S(2)}) collective-permute-start(f32[2,144,256]{2,1,0:T(8,128)} %bitcast.67), channel_id=1, source_target_pairs={{0,1},{2,3},{4,5},{6,7},{8,9},{10,11},{12,13},{14,15},{16,17},{18,... | collective-permute-start | bytes 884744 | tf_op jit(solution)/shard_map/ppermute | solution.py:538
  108.2 69.1 %collective-permute-start.2 = (f32[72,2048]{1,0:T(8,128)}, f32[72,2048]{1,0:T(8,128)}, u32[]{:S(2)}, u32[]{:S(2)}) collective-permute-start(f32[72,2048]{1,0:T(8,128)} %copy-done.12), channel_id=1, source_target_pairs={{0,2},{2,0},{4,6},{6,4},{8,10},{10,8},{12,14},{14,12},{1,3},{3,1},... | collective-permute-start | bytes 1769480 | tf_op jit(solution)/shard_map/ppermute | solution.py:626
  110.6 65.3 %collective-permute-start.8 = (f32[72,2048]{1,0:T(8,128)}, f32[72,2048]{1,0:T(8,128)S(1)}, u32[]{:S(2)}, u32[]{:S(2)}) collective-permute-start(f32[72,2048]{1,0:T(8,128)} %copy-done.14), channel_id=1, source_target_pairs={{0,2},{2,0},{4,6},{6,4},{8,10},{10,8},{12,14},{14,12},{1,3},{3,1},... | collective-permute-start | bytes 1769480 | tf_op jit(solution)/shard_map/ppermute | solution.py:626
  110.6 85.5 %collective-permute-start.14 = (f32[72,2048]{1,0:T(8,128)}, f32[72,2048]{1,0:T(8,128)}, u32[]{:S(2)}, u32[]{:S(2)}) collective-permute-start(f32[72,2048]{1,0:T(8,128)} %copy-done.16), channel_id=1, source_target_pairs={{0,2},{2,0},{4,6},{6,4},{8,10},{10,8},{12,14},{14,12},{1,3},{3,1},... | collective-permute-start | bytes 1769480 | tf_op jit(solution)/shard_map/ppermute | solution.py:626
  112.6 84.8 %collective-permute-start.20 = (f32[72,2048]{1,0:T(8,128)}, f32[72,2048]{1,0:T(8,128)}, u32[]{:S(2)}, u32[]{:S(2)}) collective-permute-start(f32[72,2048]{1,0:T(8,128)} %copy-done.18), channel_id=1, source_target_pairs={{0,2},{2,0},{4,6},{6,4},{8,10},{10,8},{12,14},{14,12},{1,3},{3,1},... | collective-permute-start | bytes 1769480 | tf_op jit(solution)/shard_map/ppermute | solution.py:626
  112.6 93.0 %collective-permute-start.6 = (f32[72,2048]{1,0:T(8,128)}, f32[72,2048]{1,0:T(8,128)S(1)}, u32[]{:S(2)}, u32[]{:S(2)}) collective-permute-start(f32[72,2048]{1,0:T(8,128)} %copy-done.2), channel_id=1, source_target_pairs={{2,6},{4,0},{6,10},{8,4},{10,14},{12,8},{3,7},{5,1},{7,11},{9,5},{... | collective-permute-start | bytes 1769480 | tf_op jit(solution)/shard_map/ppermute | solution.py:627
  177.3 32.7 %collective-permute-start.9 = (f32[72,2048]{1,0:T(8,128)S(1)}, f32[72,2048]{1,0:T(8,128)S(1)}, u32[]{:S(2)}, u32[]{:S(2)}) collective-permute-start(f32[72,2048]{1,0:T(8,128)S(1)} %get-tuple-element.83.refs_5_), channel_id=1, source_target_pairs={{0,2},{2,0},{4,6},{6,4},{8,10},{10,8},{12,14},{14,12},{1,3},{3,1},... | collective-permute-start | bytes 1769480 | tf_op jit(solution)/shard_map/ppermute | solution.py:633
  196.1 29.5 %collective-permute-start.13 = (f32[72,2048]{1,0:T(8,128)S(1)}, f32[72,2048]{1,0:T(8,128)S(1)}, u32[]{:S(2)}, u32[]{:S(2)}) collective-permute-start(f32[72,2048]{1,0:T(8,128)S(1)} %get-tuple-element.85.refs_3_.refs_1_), channel_id=1, source_target_pairs={{2,6},{4,0},{6,10},{8,4},{10,14},{12,8},{3,7},{5,1},{7,11},{9,5},{... | collective-permute-start | bytes 1769480 | tf_op jit(solution)/shard_map/ppermute | solution.py:634
  197.4 33.9 %collective-permute-start.3 = (f32[72,2048]{1,0:T(8,128)S(1)}, f32[72,2048]{1,0:T(8,128)}, u32[]{:S(2)}, u32[]{:S(2)}) collective-permute-start(f32[72,2048]{1,0:T(8,128)S(1)} %get-tuple-element.78.refs_4_), channel_id=1, source_target_pairs={{0,2},{2,0},{4,6},{6,4},{8,10},{10,8},{12,14},{14,12},{1,3},{3,1},... | collective-permute-start | bytes 1769480 | tf_op jit(solution)/shard_map/ppermute | solution.py:633
  215.3 43.6 %collective-permute-start.18 = (f32[72,2048]{1,0:T(8,128)}, f32[72,2048]{1,0:T(8,128)}, u32[]{:S(2)}, u32[]{:S(2)}) collective-permute-start(f32[72,2048]{1,0:T(8,128)} %get-tuple-element.90.refs_2_), channel_id=1, source_target_pairs={{2,6},{4,0},{6,10},{8,4},{10,14},{12,8},{3,7},{5,1},{7,11},{9,5},{... | collective-permute-start | bytes 1769480 | tf_op jit(solution)/shard_map/ppermute | solution.py:627
  223.3 40.6 %collective-permute-start.7 = (f32[72,2048]{1,0:T(8,128)}, f32[72,2048]{1,0:T(8,128)}, u32[]{:S(2)}, u32[]{:S(2)}) collective-permute-start(f32[72,2048]{1,0:T(8,128)} %get-tuple-element.80.refs_3_.refs_0_), channel_id=1, source_target_pairs={{2,6},{4,0},{6,10},{8,4},{10,14},{12,8},{3,7},{5,1},{7,11},{9,5},{... | collective-permute-start | bytes 1769480 | tf_op jit(solution)/shard_map/ppermute | solution.py:634
  226.4 32.5 %collective-permute-start.5 = (f32[72,2048]{1,0:T(8,128)}, f32[72,2048]{1,0:T(8,128)}, u32[]{:S(2)}, u32[]{:S(2)}) collective-permute-start(f32[72,2048]{1,0:T(8,128)} %collective-permute-done.2.refs_5_), channel_id=1, source_target_pairs={{6,2},{0,4},{10,6},{4,8},{14,10},{8,12},{7,3},{1,5},{11,7},{5,9},{... | collective-permute-start | bytes 1769480 | tf_op jit(solution)/shard_map/ppermute | solution.py:629
  235.0 73.3 %collective-permute-start.25 = (f32[72,2048]{1,0:T(8,128)}, f32[72,2048]{1,0:T(8,128)}, u32[]{:S(2)}, u32[]{:S(2)}) collective-permute-start(f32[72,2048]{1,0:T(8,128)} %get-tuple-element.97.refs_3_), channel_id=1, source_target_pairs={{2,6},{4,0},{6,10},{8,4},{10,14},{12,8},{3,7},{5,1},{7,11},{9,5},{... | collective-permute-start | bytes 1769480 | tf_op jit(solution)/shard_map/ppermute | solution.py:634
  252.9 51.4 %collective-permute-start.23 = (f32[72,2048]{1,0:T(8,128)}, f32[72,2048]{1,0:T(8,128)}, u32[]{:S(2)}, u32[]{:S(2)}) collective-permute-start(f32[72,2048]{1,0:T(8,128)} %collective-permute-done.20.refs_5_), channel_id=1, source_target_pairs={{6,2},{0,4},{10,6},{4,8},{14,10},{8,12},{7,3},{1,5},{11,7},{5,9},{... | collective-permute-start | bytes 1769480 | tf_op jit(solution)/shard_map/ppermute | solution.py:629
  258.9 39.7 %collective-permute-start.15 = (f32[72,2048]{1,0:T(8,128)}, f32[72,2048]{1,0:T(8,128)}, u32[]{:S(2)}, u32[]{:S(2)}) collective-permute-start(f32[72,2048]{1,0:T(8,128)} %get-tuple-element.88.refs_6_), channel_id=1, source_target_pairs={{0,2},{2,0},{4,6},{6,4},{8,10},{10,8},{12,14},{14,12},{1,3},{3,1},... | collective-permute-start | bytes 1769480 | tf_op jit(solution)/shard_map/ppermute | solution.py:633
  263.9 44.4 %collective-permute-start.22 = (f32[72,2048]{1,0:T(8,128)}, f32[72,2048]{1,0:T(8,128)}, u32[]{:S(2)}, u32[]{:S(2)}) collective-permute-start(f32[72,2048]{1,0:T(8,128)} %collective-permute-done.21.refs_4_), channel_id=1, source_target_pairs={{6,2},{0,4},{10,6},{4,8},{14,10},{8,12},{7,3},{1,5},{11,7},{5,9},{... | collective-permute-start | bytes 1769480 | tf_op jit(solution)/shard_map/ppermute | solution.py:677
  285.7 63.9 %collective-permute-start.19 = (f32[72,2048]{1,0:T(8,128)}, f32[72,2048]{1,0:T(8,128)}, u32[]{:S(2)}, u32[]{:S(2)}) collective-permute-start(f32[72,2048]{1,0:T(8,128)} %copy-done.23), channel_id=1, source_target_pairs={{2,6},{4,0},{6,10},{8,4},{10,14},{12,8},{3,7},{5,1},{7,11},{9,5},{... | collective-permute-start | bytes 1769480 | tf_op jit(solution)/shard_map/ppermute | solution.py:634
  298.5 51.1 %collective-permute-start.17 = (f32[72,2048]{1,0:T(8,128)}, f32[72,2048]{1,0:T(8,128)}, u32[]{:S(2)}, u32[]{:S(2)}) collective-permute-start(f32[72,2048]{1,0:T(8,128)} %collective-permute-done.14.refs_5_), channel_id=1, source_target_pairs={{6,2},{0,4},{10,6},{4,8},{14,10},{8,12},{7,3},{1,5},{11,7},{5,9},{... | collective-permute-start | bytes 1769480 | tf_op jit(solution)/shard_map/ppermute | solution.py:629
  304.3 45.3 %collective-permute-start.16 = (f32[72,2048]{1,0:T(8,128)}, f32[72,2048]{1,0:T(8,128)}, u32[]{:S(2)}, u32[]{:S(2)}) collective-permute-start(f32[72,2048]{1,0:T(8,128)} %collective-permute-done.15.refs_4_), channel_id=1, source_target_pairs={{6,2},{0,4},{10,6},{4,8},{14,10},{8,12},{7,3},{1,5},{11,7},{5,9},{... | collective-permute-start | bytes 1769480 | tf_op jit(solution)/shard_map/ppermute | solution.py:677
  308.3 48.3 %collective-permute-start.26 = (f32[144,2048]{1,0:T(8,128)}, f32[144,2048]{1,0:T(8,128)}, u32[]{:S(2)}, u32[]{:S(2)}) collective-permute-start(f32[144,2048]{1,0:T(8,128)} %get-tuple-element.100), channel_id=1, source_target_pairs={{0,2},{2,0},{4,6},{6,4},{8,10},{10,8},{12,14},{14,12},{1,3},{3,1},... | collective-permute-start | bytes 3538952 | tf_op jit(solution)/shard_map/ppermute | solution.py:701
  308.3 50.0 %collective-permute-start.27 = (f32[144,2048]{1,0:T(8,128)}, f32[144,2048]{1,0:T(8,128)}, u32[]{:S(2)}, u32[]{:S(2)}) collective-permute-start(f32[144,2048]{1,0:T(8,128)} %get-tuple-element.102), channel_id=1, source_target_pairs={{0,2},{2,0},{4,6},{6,4},{8,10},{10,8},{12,14},{14,12},{1,3},{3,1},... | collective-permute-start | bytes 3538952 | tf_op jit(solution)/shard_map/ppermute | solution.py:701
  356.7 29.0 %collective-permute-start.28 = (f32[144,2048]{1,0:T(8,128)S(1)}, f32[144,2048]{1,0:T(8,128)S(1)}, u32[]{:S(2)}, u32[]{:S(2)}) collective-permute-start(f32[144,2048]{1,0:T(8,128)S(1)} %get-tuple-element.104), channel_id=1, source_target_pairs={{0,2},{2,0},{4,6},{6,4},{8,10},{10,8},{12,14},{14,12},{1,3},{3,1},... | collective-permute-start | bytes 3538952 | tf_op jit(solution)/shard_map/ppermute | solution.py:701
  358.3 50.0 %collective-permute-start.29 = (f32[144,2048]{1,0:T(8,128)S(1)}, f32[144,2048]{1,0:T(8,128)S(1)}, u32[]{:S(2)}, u32[]{:S(2)}) collective-permute-start(f32[144,2048]{1,0:T(8,128)S(1)} %get-tuple-element.106), channel_id=1, source_target_pairs={{0,2},{2,0},{4,6},{6,4},{8,10},{10,8},{12,14},{14,12},{1,3},{3,1},... | collective-permute-start | bytes 3538952 | tf_op jit(solution)/shard_map/ppermute | solution.py:701
  (105 other events, 2333.4 us)
Sparse Core Ops, SparseCore 0:
  268.7 68.9 all-reduce.3

commit v3 on v2

--- a/solution.py
+++ b/solution.py
@@ -182,9 +182,10 @@
 GROUP = 24
 CELL_CHUNKS = 4
 MIB = 1024 * 1024
+VMEM_MIB = 60
 EDGE = 2
 SEA, OPEN_EAST, FLOW_EAST, OPEN_NORTH, FLOW_NORTH, HALF_SEA, WIND, TURN = range(8)
-PUT, OFFSET, SPILL, NEXT = range(4)
+KEEP, SPILL, IS_SEA = BLOCK, 2 * BLOCK, 2 * BLOCK
 
 
 def row_of(ref, row):
@@ -197,12 +198,29 @@
     return courant * ((here + ahead) - courant * slope_here - (1.0 / 3.0 - square * (1.0 / 3.0)) * bend)
 
 
-def pack_block(block, index, offset, spill, tile, out_ref, rows, held):
-    lanes = lax.broadcasted_iota(jnp.int32, block.shape, 1)
-    moved = jnp.take_along_axis(block, jnp.broadcast_to(index, block.shape), axis=1)
-    merged = jnp.where(lanes >= offset, moved, held)
-    out_ref[rows, pl.ds(pl.multiple_of(tile * BLOCK, BLOCK), BLOCK)] = merged
-    return jnp.where(spill > 0, moved, merged)
+def pick_lanes(block, index):
+    return jnp.take_along_axis(block, index, axis=1, mode="promise_in_bounds")
+
+
+def tile_at(tile):
+    return pl.ds(pl.multiple_of(tile * BLOCK, BLOCK), BLOCK)
+
+
+def has(code, flag):
+    return jnp.bitwise_and(code, flag) != 0
+
+
+def pack_block(blocks, code, tile, out_ref, firsts, held):
+    code = jnp.broadcast_to(code, (8, BLOCK))
+    index = jnp.bitwise_and(code, BLOCK - 1)
+    keep, spill = has(code, KEEP), has(code, SPILL)
+    result = []
+    for block, first, old in zip(blocks, firsts, held):
+        moved = pick_lanes(block, index)
+        merged = jnp.where(keep, moved, old)
+        out_ref[pl.ds(first, 8), tile_at(tile)] = merged
+        result.append(jnp.where(spill, moved, merged))
+    return tuple(result)
 
 
 def prepare_kernel(places, base_ref, speed_ref, sea_ref, east_ref, north_ref, wind_ref, turn_ref, cos_ref, sin_ref,
@@ -264,19 +282,16 @@
     def turned_tile(tile):
         return jnp.where(tile >= tiles, tiles, jnp.bitwise_and(tile + odd * (tiles // 2), tiles - 1))
 
-    index_ref[...] = jnp.zeros(index_ref.shape, jnp.int32)
-    wide = (8, 2 * BLOCK)
-    wide_lane = lax.broadcasted_iota(jnp.int32, wide, 1)
-    wide_row = lax.broadcasted_iota(jnp.int32, wide, 0)
     columns = []
     for h in range(2):
         rank = jnp.dot(parts[h].astype(bf16), before, preferred_element_type=f32).astype(jnp.int32)
         start = starts[h].astype(jnp.int32)
         offset = jnp.bitwise_and(start, BLOCK - 1)
+        keep = jnp.where(over[:row_count] >= offset, KEEP, 0)
+        slot = jnp.bitwise_and(rank + offset, BLOCK - 1)
         is_sea = parts[h] > 0.0
-        place = jnp.where(is_sea, rank + offset, -1)
-        place_ref[h] = place
-        slot = jnp.where(is_sea, jnp.bitwise_and(place, BLOCK - 1), -1).astype(f32).T
+        place_ref[h] = slot + keep + jnp.where(is_sea, IS_SEA, 0)
+        slot = jnp.where(is_sea, slot, -1).astype(f32).T
         from_lane = down[:, :row_count].astype(f32)
 
         @pl.loop(0, BLOCK // 8)
@@ -287,51 +302,34 @@
                 found.append(jnp.sum(jnp.where(slot == lane, from_lane, 0.0), axis=0, keepdims=True))
             pick_ref[pl.ds(pl.multiple_of(8 * i, 8), 8), :] = jnp.concatenate(found, axis=0)
 
-        index_ref[h, EDGE : EDGE + row_count, :] = pick_ref[...].T.astype(jnp.int32)
-        start_row = starts[h].T[0:8, :].astype(jnp.int32)
-        end_row = (starts[h] + numbers[h]).T[0:8, :].astype(jnp.int32)
-        tile = lax.shift_right_logical(start_row, 7)
-        offset_row = jnp.bitwise_and(start_row, BLOCK - 1)
-        spill = jnp.where(offset_row + (end_row - start_row) >= BLOCK, 1, 0)
-        columns += [turned_tile(tile), offset_row, spill, jnp.minimum(turned_tile(tile + 1), tiles - 1)]
-    empty = jnp.where(jnp.bitwise_and(wide_row, 3) == PUT, tiles, 0)
-    merged = jnp.zeros((8, row_count), jnp.int32)
-    for k, column in enumerate(columns):
-        merged = jnp.where(wide_row[:, :row_count] == k, column, merged)
-    merged = jnp.concatenate([merged, jnp.zeros((8, 2 * BLOCK - row_count), jnp.int32)], axis=1)
-    merged = pltpu.roll(merged, EDGE, 1)
-    inside = (wide_lane >= EDGE) & (wide_lane < EDGE + row_count)
-    end_offset = jnp.bitwise_and(total, BLOCK - 1)
-    end_tile = jnp.where(end_offset == 0, tiles, turned_tile(lax.shift_right_logical(total, 7)))
-    end_tile = jnp.concatenate([end_tile, end_tile], axis=1)
-    result = jnp.where(inside, merged, empty)
-    table_ref[...] = jnp.where((wide_lane == EDGE + row_count + EDGE) & (wide_row == PUT), end_tile, result)
+        spill = jnp.where(offset + numbers[h].astype(jnp.int32) >= BLOCK, SPILL, 0)
+        index_ref[h] = pick_ref[...].T.astype(jnp.int32) + keep + spill
+        columns.append(turned_tile(lax.shift_right_logical(starts[h].T[0:8, :].astype(jnp.int32), 7)))
+    row_id = lax.broadcasted_iota(jnp.int32, (8, row_count), 0)
+    end_tile = jnp.where(
+        jnp.bitwise_and(total, BLOCK - 1) == 0, tiles, turned_tile(lax.shift_right_logical(total, 7))
+    )
+    end_tile = jnp.broadcast_to(end_tile, (8, BLOCK))
+    table_ref[...] = jnp.concatenate([jnp.where(row_id == 0, columns[0], columns[1]), end_tile], axis=1)
 
 
 def pack_fields_kernel(row_count, base_ref, table_ref, coef_ref, index_ref, out_ref, wide_ref):
-    def some_rows(first, count, held):
-        picks = [index_ref[h, pl.ds(first, count), :] for h in range(2)]
-        for at in range(count):
-            row = first + at
-            fields = coef_ref[base_ref[0] + row]
+    def eight(i, held):
+        codes = [index_ref[h, pl.ds(pl.multiple_of(8 * i, 8), 8), :] for h in range(2)]
+        for at in range(8):
+            row = 8 * i + at
+            fields = coef_ref[base_ref[0] + EDGE + row]
             for h in range(2):
-                held = pack_block(
-                    fields[:, h * BLOCK : (h + 1) * BLOCK], picks[h][at : at + 1, :], table_ref[4 * h + OFFSET, row],
-                    table_ref[4 * h + SPILL, row], table_ref[4 * h + PUT, row], wide_ref, slice(None), held,
-                )
+                block = fields[:, h * BLOCK : (h + 1) * BLOCK]
+                held = pack_block([block], codes[h][at : at + 1, :], table_ref[h, row], wide_ref, [0], held)
         return held
 
-    held = jnp.zeros((8, BLOCK), jnp.float32)
-    held = lax.fori_loop(
-        0, row_count // 8, lambda i, held: some_rows(pl.multiple_of(8 * i, 8), 8, held), held
-    )
-    held = some_rows(row_count, EDGE, held)
-    last = table_ref[PUT, row_count + 2 * EDGE]
-    wide_ref[:, pl.ds(pl.multiple_of(last * BLOCK, BLOCK), BLOCK)] = held
+    held = lax.fori_loop(0, row_count // 8, eight, (jnp.zeros((8, BLOCK), jnp.float32),))
+    wide_ref[:, tile_at(table_ref[0, row_count])] = held[0]
     out_ref[...] = wide_ref[:, : out_ref.shape[1]]
 
 
-def propagate_kernel(part, steps, base_ref, table_ref, energy_ref, low_ref, high_ref, coef_ref, index_ref, east_ref,
+def propagate_kernel(part, steps, base_ref, table_ref, energy_ref, halo_ref, coef_ref, index_ref, east_ref,
                      north_ref, fields_ref, *refs):
     wide_ref, rows_ref, sems = refs[-3:]
     sum_ref, outs = refs[-4], refs[:-4]
@@ -339,8 +337,8 @@
     row_count, col_count = energy_ref.shape[1:]
     first_row = base_ref[0]
     first_comp = (part + base_ref[1] * (1 - 2 * part)) * steps * GROUP
-    lane = lax.broadcasted_iota(jnp.int32, (8, col_count), 1)
-    first_lane, last_lane = lane == 0, lane == col_count - 1
+    lane = lax.broadcasted_iota(jnp.int32, (8, BLOCK), 1)
+    first_lane, last_lane = lane == 0, lane == BLOCK - 1
 
     def fetch(step):
         comps = pl.ds(first_comp + step * GROUP, GROUP)
@@ -360,53 +358,80 @@
     slot = step_id % 2
     pltpu.make_async_copy(rows_ref.at[slot], rows_ref.at[slot], sems.at[slot]).wait()
 
-    def cell_row(row, picks, fresh, state, east, north, rows):
-        here, ahead, bend_here, flux_low, held = state
-        coef = coef_ref.at[first_row + row]
-        new = fresh * row_of(coef_ref.at[first_row + row + EDGE], SEA)
-        slope = ahead - here
-        bend_ahead = (new - ahead) - slope
-        flux = upwind(east * row_of(coef, OPEN_EAST) + row_of(coef, FLOW_EAST), here, ahead, slope, bend_here,
-                      bend_ahead)
-        right = jnp.where(last_lane, 0.0, pltpu.roll(here, col_count - 1, 1))
-        left = jnp.where(first_lane, 0.0, pltpu.roll(here, 1, 1))
-        slope_right = right - here
-        bend = slope_right - (here - left)
-        cross = upwind(north * row_of(coef, OPEN_NORTH) + row_of(coef, FLOW_NORTH), here, right, slope_right, bend,
-                       pltpu.roll(bend, col_count - 1, 1))
-        moved = row_of(coef, HALF_SEA) * ((here + here) - (flux - flux_low) - (cross - pltpu.roll(cross, 1, 1)))
+    def halves(row):
+        return row[:, :BLOCK], row[:, BLOCK:]
+
+    def masked(row, at):
+        sea_row = halves(coef_ref.at[first_row + at][SEA : SEA + 1, :])
+        return tuple(part * sea for part, sea in zip(halves(row), sea_row))
+
+    def cell_row(at, new, state, east, north):
+        here, ahead, bend_here, flux_low = state
+        coef = [halves(row_of(coef_ref.at[first_row + at], k)) for k in range(HALF_SEA + 1)]
+        to_right = [pltpu.roll(part, BLOCK - 1, 1) for part in here]
+        to_left = [pltpu.roll(part, 1, 1) for part in here]
+        right = (jnp.where(last_lane, to_right[1], to_right[0]), jnp.where(last_lane, 0.0, to_right[1]))
+        left = (jnp.where(first_lane, 0.0, to_left[0]), jnp.where(first_lane, to_left[0], to_left[1]))
+        slope_right = [right[h] - here[h] for h in range(2)]
+        bend = [slope_right[h] - (here[h] - left[h]) for h in range(2)]
+        bend_roll = [pltpu.roll(part, BLOCK - 1, 1) for part in bend]
+        bend_right = (jnp.where(last_lane, bend_roll[1], bend_roll[0]), bend_roll[1])
+        cross, flux, bend_ahead = [], [], []
         for h in range(2):
-            held = pack_block(
-                moved[:, h * BLOCK : (h + 1) * BLOCK], picks[h], table_ref[4 * h + OFFSET, row],
-                table_ref[4 * h + SPILL, row], table_ref[4 * h + PUT, row], wide_ref, rows, held,
-            )
-        return ahead, new, bend_ahead, flux, held
+            cross.append(upwind(north * coef[OPEN_NORTH][h] + coef[FLOW_NORTH][h], here[h], right[h],
+                                slope_right[h], bend[h], bend_right[h]))
+            slope = ahead[h] - here[h]
+            bend_ahead.append((new[h] - ahead[h]) - slope)
+            flux.append(upwind(east * coef[OPEN_EAST][h] + coef[FLOW_EAST][h], here[h], ahead[h], slope,
+                               bend_here[h], bend_ahead[h]))
+        cross_roll = [pltpu.roll(part, 1, 1) for part in cross]
+        cross_low = (jnp.where(first_lane, cross_roll[1], cross_roll[0]),
+                     jnp.where(first_lane, cross_roll[0], cross_roll[1]))
+        moved = [
+            coef[HALF_SEA][h] * ((here[h] + here[h]) - (flux[h] - flux_low[h]) - (cross[h] - cross_low[h]))
+            for h in range(2)
+        ]
+        return (ahead, new, tuple(bend_ahead), tuple(flux)), jnp.concatenate(moved, axis=1)
 
     @pl.loop(0, GROUP // 8)
     def _(g):
         local = pl.ds(pl.multiple_of(g * 8, 8), 8)
-        rows = pl.ds(pl.multiple_of(step_id * GROUP + g * 8, 8), 8)
-        east = jnp.concatenate([east_ref[local, :]] * 2, axis=1)
-        north = jnp.concatenate([north_ref[local, :]] * 2, axis=1)
-        here = low_ref[0, local, :] * row_of(coef_ref.at[first_row], SEA)
-        ahead = low_ref[1, local, :] * row_of(coef_ref.at[first_row + 1], SEA)
-        zero = jnp.zeros_like(here)
-        state = (here, ahead, zero, zero, jnp.zeros((8, BLOCK), jnp.float32))
+        east, north = east_ref[local, :], north_ref[local, :]
+        zero = (jnp.zeros((8, BLOCK), jnp.float32),) * 2
+        state = (masked(halo_ref[local, 0, :], 0), masked(halo_ref[local, 1, :], 1), zero, zero)
 
         def eight(i, state):
-            picks = [index_ref[h, pl.ds(pl.multiple_of(8 * i, 8), 8), :] for h in range(2)]
-            for at in range(8):
-                state = cell_row(8 * i + at, [p[at : at + 1, :] for p in picks],
-                                 rows_ref[slot, 8 * i + at, local, :], state, east, north, rows)
+            fresh = [rows_ref[slot, 8 * i + k, local, :] for k in range(8)]
+            done = []
+            for k in range(8):
+                new = masked(fresh[k], 8 * i + k + EDGE)
+                state, moved = cell_row(8 * i + k, new, state, east, north)
+                done.append(moved)
+            for k in range(8):
+                rows_ref[slot, jnp.maximum(8 * i + k - EDGE, 0), local, :] = done[k]
             return state
 
         state = lax.fori_loop(0, row_count // 8, eight, state)
-        picks = [index_ref[h, row_count : row_count + EDGE, :] for h in range(2)]
-        for at in range(EDGE):
-            state = cell_row(row_count + at, [p[at : at + 1, :] for p in picks], high_ref[at, local, :], state,
-                             east, north, rows)
-        last = table_ref[PUT, row_count + 2 * EDGE]
-        wide_ref[rows, pl.ds(pl.multiple_of(last * BLOCK, BLOCK), BLOCK)] = state[-1]
+        for k in range(EDGE):
+            new = masked(halo_ref[local, k, :], row_count + EDGE + k)
+            state, moved = cell_row(row_count + k, new, state, east, north)
+            rows_ref[slot, row_count - EDGE + k, local, :] = moved
+
+    group_rows = [pl.multiple_of(step_id * GROUP + 8 * k, 8) for k in range(GROUP // 8)]
+
+    def pack_eight(i, held):
+        codes = [index_ref[h, pl.ds(pl.multiple_of(8 * i, 8), 8), :] for h in range(2)]
+        for k in range(8):
+            for h in range(2):
+                lanes = slice(h * BLOCK, (h + 1) * BLOCK)
+                blocks = [rows_ref[slot, 8 * i + k, 8 * n : 8 * n + 8, lanes] for n in range(GROUP // 8)]
+                held = pack_block(blocks, codes[h][k : k + 1, :], table_ref[h, 8 * i + k], wide_ref, group_rows, held)
+        return held
+
+    empty = (jnp.zeros((8, BLOCK), jnp.float32),) * (GROUP // 8)
+    held = lax.fori_loop(0, row_count // 8, pack_eight, empty)
+    for first, block in zip(group_rows, held):
+        wide_ref[pl.ds(first, 8), tile_at(table_ref[0, row_count])] = block
 
     @pl.when(step_id == steps - 1)
     def _():
@@ -436,7 +461,7 @@
 
 
 def interact_kernel(table_ref, spread_ref, coupling_ref, *refs):
-    window, own_ref, back_ref, delta_ref = refs[:8], refs[8], refs[9], refs[10]
+    window, (own_ref, back_0_ref, back_1_ref, delta_ref) = refs[:8], refs[8:]
     comps = window[0].shape[0]
     kept = []
     for j in range(1, 7):
@@ -455,12 +480,16 @@
         delta_ref[(j - 1) * 2 * comps : j * 2 * comps, :] = both
         if 2 <= j <= 5:
             part = -2.0 * (deltas[0] + deltas[1])
-            target = own_ref if j <= 3 else back_ref
-            at = (j % 2) * comps
-            target[at : at + comps, :] = part
+            if j <= 3:
+                own_ref[(j - 2) * comps : (j - 1) * comps, :] = part
+            elif j == 4:
+                back_1_ref[...] = part
+            else:
+                back_0_ref[...] = part
     spread = jnp.dot(spread_ref[...], delta_ref[...], preferred_element_type=jnp.float32)
     own_ref[...] += spread[: 2 * comps, :]
-    back_ref[...] += spread[2 * comps :, :]
+    back_1_ref[...] += spread[2 * comps : 3 * comps, :]
+    back_0_ref[...] += spread[3 * comps :, :]
 
 
 def finish_kernel(chunks, base_ref, table_ref, place_ref, mean_ref, fields_ref, growth_ref, damping_ref, *refs):
@@ -469,6 +498,8 @@
     width = own[0].shape[1]
     tiles = wide_ref.shape[1] // BLOCK
     tile_width = 2 * BLOCK
+    growth = jnp.broadcast_to(growth_ref[...], (GROUP, tile_width))
+    damping = jnp.broadcast_to(damping_ref[...], (GROUP, tile_width))
     for o in range(2 * chunks):
         extra = own[o] if o < chunks else back[o - chunks]
 
@@ -476,34 +507,29 @@
         def _(i):
             source = pl.ds(pl.multiple_of(i * tile_width, tile_width), tile_width)
             target = pl.ds(pl.multiple_of(o * width + i * tile_width, tile_width), tile_width)
-            scale = (1.0 + growth_ref[...] * fields_ref[WIND : WIND + 1, target]
-                     - damping_ref[...] * mean_ref[0:1, target])
+            scale = 1.0 + growth * fields_ref[WIND : WIND + 1, target] - damping * mean_ref[0:1, target]
             wide_ref[:, target] = turned[o][:, source] * scale + extra[:, source]
 
-    lane = lax.broadcasted_iota(jnp.int32, (8, BLOCK), 1)
-
-    @pl.loop(0, GROUP // 8)
-    def _(g):
-        local = pl.ds(pl.multiple_of(g * 8, 8), 8)
-
-        @pl.loop(0, out_ref.shape[1] // 8)
-        def _(i):
-            places = [place_ref[h, pl.ds(pl.multiple_of(8 * i, 8), 8), :] for h in range(2)]
-            grid_rows = []
-            for r in range(8):
-                parts = []
-                for h in range(2):
-                    row = 8 * i + r + EDGE
-                    place = jnp.broadcast_to(places[h][r : r + 1, :], (8, BLOCK))
-                    first = jnp.minimum(table_ref[4 * h + PUT, row], tiles - 1)
-                    second = table_ref[4 * h + NEXT, row]
-                    low = wide_ref[local, pl.ds(pl.multiple_of(first * BLOCK, BLOCK), BLOCK)]
-                    high = wide_ref[local, pl.ds(pl.multiple_of(second * BLOCK, BLOCK), BLOCK)]
-                    near = jnp.where(lane >= table_ref[4 * h + OFFSET, row], low, high)
-                    level = jnp.take_along_axis(near, jnp.bitwise_and(place, BLOCK - 1), axis=1)
-                    parts.append(jnp.where(place >= 0, level, 0.0))
-                grid_rows.append(jnp.concatenate(parts, axis=1))
-            out_ref[local, pl.ds(pl.multiple_of(8 * i, 8), 8), :] = jnp.swapaxes(jnp.stack(grid_rows), 0, 1)
+    @pl.loop(0, out_ref.shape[1] // 8)
+    def _(i):
+        codes = [place_ref[h, pl.ds(pl.multiple_of(8 * i, 8), 8), :] for h in range(2)]
+        done = [[] for _ in range(GROUP // 8)]
+        for r in range(8):
+            parts = [[] for _ in range(GROUP // 8)]
+            for h in range(2):
+                code = jnp.broadcast_to(codes[h][r : r + 1, :], (8, BLOCK))
+                index = jnp.bitwise_and(code, BLOCK - 1)
+                keep, is_sea = has(code, KEEP), has(code, IS_SEA)
+                tile = table_ref[h, 8 * i + r]
+                first, second = jnp.minimum(tile, tiles - 1), jnp.bitwise_and(tile + 1, tiles - 1)
+                for k in range(GROUP // 8):
+                    rows = slice(8 * k, 8 * k + 8)
+                    near = jnp.where(keep, wide_ref[rows, tile_at(first)], wide_ref[rows, tile_at(second)])
+                    parts[k].append(jnp.where(is_sea, pick_lanes(near, index), 0.0))
+            for k in range(GROUP // 8):
+                done[k].append(jnp.concatenate(parts[k], axis=1))
+        for k in range(GROUP // 8):
+            out_ref[8 * k : 8 * k + 8, pl.ds(pl.multiple_of(8 * i, 8), 8), :] = jnp.swapaxes(jnp.stack(done[k]), 0, 1)
 
 
 def params(limit):
@@ -532,18 +558,15 @@
     f32, i32 = jnp.float32, jnp.int32
     base = jnp.stack([first_row, odd, comp_pos * (local_comps // NTH)]).astype(i32)
 
-    tile_count = lax.axis_size("tile")
-    forward = [(i, i + 1) for i in range(tile_count - 1)]
-    backward = [(target, source) for source, target in forward]
-    low = lax.ppermute(jnp.swapaxes(energy[:, -EDGE:, :], 0, 1), "tile", forward)
-    high = lax.ppermute(jnp.swapaxes(energy[:, :EDGE, :], 0, 1), "tile", backward)
+    edge_first = jnp.where(tile_pos == 0, row_count - EDGE, 0)
+    edge_rows = lax.dynamic_slice_in_dim(energy, edge_first, EDGE, axis=1)
+    halo_rows = lax.ppermute(edge_rows, "tile", [(0, 1), (1, 0)])
 
     all_rows = sea_mask.shape[0]
     angles = np.float32(2.0 * math.pi / NTH) * (np.arange(local_comps) % NTH).astype(np.float32)
     cosines = np.broadcast_to(np.cos(angles)[:, None], (local_comps, BLOCK)).astype(np.float32)
     sines = np.broadcast_to(np.sin(angles)[:, None], (local_comps, BLOCK)).astype(np.float32)
     vmem = pl.BlockSpec(memory_space=pltpu.VMEM)
-    padded_rows = row_count + 8
     coef, index, place, table, speed_east, speed_north = pl.pallas_call(
         functools.partial(prepare_kernel, cells),
         grid_spec=pltpu.PrefetchScalarGridSpec(
@@ -555,14 +578,14 @@
         ),
         out_shape=[
             jax.ShapeDtypeStruct((all_rows + 2 * EDGE, 8, col_count), f32),
-            jax.ShapeDtypeStruct((2, padded_rows, BLOCK), i32),
+            jax.ShapeDtypeStruct((2, row_count, BLOCK), i32),
             jax.ShapeDtypeStruct((2, row_count, BLOCK), i32),
             jax.ShapeDtypeStruct((8, 2 * BLOCK), i32),
             jax.ShapeDtypeStruct((local_comps, BLOCK), f32),
             jax.ShapeDtypeStruct((local_comps, BLOCK), f32),
         ],
         name="prepare",
-        compiler_params=params(24),
+        compiler_params=params(VMEM_MIB),
     )(base, group_speed, sea_mask, current_u, current_v, wind_forcing, refraction, cosines, sines)
     packed_fields = pl.pallas_call(
         functools.partial(pack_fields_kernel, row_count),
@@ -575,7 +598,7 @@
         ),
         out_shape=jax.ShapeDtypeStruct((8, cells), f32),
         name="pack_fields",
-        compiler_params=params(16),
+        compiler_params=params(VMEM_MIB),
     )(base, table, coef, index)
 
     steps = comps // GROUP
@@ -590,7 +613,7 @@
         return pl.BlockSpec((GROUP, lanes), lambda s, b, t: (group_at(part, b) + s, 0))
 
     def propagate(part, table):
-        halo = pl.BlockSpec((EDGE, GROUP, col_count), lambda s, b, t: (0, group_at(part, b) + s, 0))
+        halo = pl.BlockSpec((GROUP, EDGE, col_count), lambda s, b, t: (group_at(part, b) + s, 0, 0))
         out_chunk = jax.ShapeDtypeStruct((comps, width), f32)
         outs = pl.pallas_call(
             functools.partial(propagate_kernel, part, steps),
@@ -598,7 +621,7 @@
                 num_scalar_prefetch=2,
                 grid=(steps,),
                 in_specs=[
-                    pl.BlockSpec(memory_space=pl.ANY), halo, halo, whole(coef.shape), whole(index.shape),
+                    pl.BlockSpec(memory_space=pl.ANY), halo, whole(coef.shape), whole(index.shape),
                     column(part, BLOCK), column(part, BLOCK), whole(packed_fields.shape),
                 ],
                 out_specs=[whole((comps, width))] * (2 * CELL_CHUNKS) + [whole((1, cells))],
@@ -610,11 +633,11 @@
             ),
             out_shape=[out_chunk] * (2 * CELL_CHUNKS) + [jax.ShapeDtypeStruct((1, cells), f32)],
             name="propagate_chunk",
-            compiler_params=params(44),
+            compiler_params=params(VMEM_MIB),
             cost_estimate=pl.CostEstimate(
                 flops=60 * comps * row_count * col_count, bytes_accessed=100 * MIB, transcendentals=0,
             ),
-        )(base, table, energy, low, high, coef, index, speed_east, speed_north, packed_fields)
+        )(base, table, energy, halo_rows, coef, index, speed_east, speed_north, packed_fields)
         return list(outs[:CELL_CHUNKS]), list(outs[CELL_CHUNKS : 2 * CELL_CHUNKS]), outs[-1]
 
     pairs = [(i, i ^ 1) for i in range(comp_count)]
@@ -627,26 +650,27 @@
     from_own_0 = [lax.ppermute(piece, "comp", apart) for piece in kept_0]
     kept_1, sent_1, sums_1 = propagate(1, after(table, sums_0))
     from_got_0 = [lax.ppermute(piece, "comp", across) for piece in got_0]
+    sums = sums_0 + sums_1
+    partner_sums = lax.ppermute(sums, "comp", pairs)
+    partner_sums = jnp.roll(partner_sums, half, axis=1)
     got_1, from_own_1 = [], []
     for c in chunk_range:
-        waits = [got_0[c]] + ([got_1[c - 2]] if c >= 2 else [])
+        waits = [got_0[c]] + ([got_1[c - 2]] if c >= 2 else []) + ([partner_sums] if c == 2 else [])
         got_1.append(lax.ppermute(after(sent_1[c], *waits), "comp", pairs))
         from_own_1.append(lax.ppermute(after(kept_1[c], from_own_0[c]), "comp", apart))
-
-    def swap(levels):
-        return jnp.where(odd > 0, jnp.roll(levels, half, axis=1), levels)
-
-    mean_level = swap(lax.psum(swap(sums_0 + sums_1), "comp")) / comp_total
-
-    dia_index, coupling, growth, damping, _ = lax.optimization_barrier(
-        (dia_index, coupling, growth, damping, sums_0)
+    sums = sums + partner_sums
+    sums = sums_two = sums + lax.ppermute(sums, "comp", [(i, i ^ 2) for i in range(comp_count)])
+    sums = sums + lax.ppermute(sums, "comp", [(i, i ^ 4) for i in range(comp_count)])
+    mean_level = sums / comp_total
+
+    dia_index, coupling, growth, damping, late_odd, late_pair, _ = lax.optimization_barrier(
+        (dia_index, coupling, growth, damping, odd, pair_pos, sums_0)
     )
     own_growth = lax.dynamic_slice_in_dim(growth, first_comp, local_comps)[:, None]
     own_damping = lax.dynamic_slice_in_dim(damping, first_comp, local_comps)[:, None]
-    chunk_ids = jnp.arange(8)
-    even_first = 8 * pair_pos - 4 + 2 * chunk_ids
-    odd_first = 8 * pair_pos + 10 - 2 * chunk_ids
-    chunk_first = NTH * jnp.where(odd > 0, odd_first, even_first)
+    chunk_first = [
+        NTH * jnp.where(late_odd > 0, 8 * late_pair + 10 - 2 * j, 8 * late_pair - 4 + 2 * j) for j in range(8)
+    ]
     margin = 8 * NTH
     dia_pad = jnp.pad(dia_index, ((0, 0), (margin, margin)), constant_values=-1)
     coupling_pad = jnp.pad(coupling, (margin, margin))
@@ -672,13 +696,13 @@
     rates = jnp.concatenate(rates)[:, None]
 
     lanes = 512 if width % 512 == 0 else width
-    own_parts, back_parts = [], []
+    own_parts, parts_0, parts_1 = [], [], []
     for c in chunk_range:
         from_got_1 = lax.ppermute(after(got_1[c], *own_parts[c - 2 : c - 1]) if c >= 2 else got_1[c], "comp", across)
         levels = [
             from_got_1, from_got_0[c], kept_0[c], kept_1[c], got_1[c], got_0[c], from_own_0[c], from_own_1[c],
         ]
-        own_part, back_part = pl.pallas_call(
+        own_part, part_0, part_1 = pl.pallas_call(
             interact_kernel,
             grid=(width // lanes,),
             in_specs=[
@@ -686,29 +710,40 @@
                 pl.BlockSpec(spread.shape, lambda s: (0, 0)),
                 pl.BlockSpec(rates.shape, lambda s: (0, 0)),
             ] + [pl.BlockSpec((comps, lanes), lambda s: (0, s))] * 8,
-            out_specs=[pl.BlockSpec((2 * comps, lanes), lambda s: (0, s))] * 2,
-            out_shape=[jax.ShapeDtypeStruct((2 * comps, width), f32)] * 2,
+            out_specs=[pl.BlockSpec((n * comps, lanes), lambda s: (0, s)) for n in (2, 1, 1)],
+            out_shape=[jax.ShapeDtypeStruct((n * comps, width), f32) for n in (2, 1, 1)],
             scratch_shapes=[pltpu.VMEM((12 * comps, lanes), jnp.bfloat16)],
             name="interact_cells",
-            compiler_params=params(32),
+            compiler_params=params(VMEM_MIB),
             cost_estimate=pl.CostEstimate(
                 flops=2 * width * comps * comps * (6 * 12 + 48),
                 bytes_accessed=20 * MIB, transcendentals=0,
             ),
         )(lookup, spread, rates, *levels)
         own_parts.append(own_part)
-        wait = got_1[c + 2] if c + 2 < CELL_CHUNKS else back_parts[c - 2]
-        back_parts.append(lax.ppermute(after(back_part, wait), "comp", pairs))
+        parts_0.append(part_0)
+        parts_1.append(part_1)
+
+    def send_back(piece, *waits):
+        return lax.ppermute(after(piece, *waits), "comp", pairs)
+
+    back = [[None] * CELL_CHUNKS for _ in range(2)]
+    back[0][0] = send_back(parts_0[0], got_1[2], sums_two)
+    back[1][0] = send_back(parts_1[0], got_1[3])
+    back[0][1] = send_back(parts_0[1], back[0][0], sums)
+    back[0][2] = send_back(parts_0[2], back[1][0])
+    back[0][3] = send_back(parts_0[3], back[0][1])
+    for c in range(1, CELL_CHUNKS):
+        back[1][c] = send_back(parts_1[c], back[0][2])
 
     def finish(part, so_far):
         piece = pl.BlockSpec((GROUP, width), lambda s, b, t: (s, 0))
         own_piece = pl.BlockSpec((GROUP, width), lambda s, b, t: (part * steps + s, 0))
-        back_piece = pl.BlockSpec((GROUP, width), lambda s, b, t: ((1 - part) * steps + s, 0))
         inputs = [place, mean_level, packed_fields, own_growth, own_damping]
         specs = [whole(place.shape), whole(mean_level.shape), whole(packed_fields.shape), column(part, 1),
                  column(part, 1)]
-        inputs += [kept_0, kept_1][part] + [sent_0, sent_1][part] + own_parts + back_parts
-        specs += [piece] * (2 * CELL_CHUNKS) + [own_piece] * CELL_CHUNKS + [back_piece] * CELL_CHUNKS
+        inputs += [kept_0, kept_1][part] + [sent_0, sent_1][part] + own_parts + back[part]
+        specs += [piece] * (2 * CELL_CHUNKS) + [own_piece] * CELL_CHUNKS + [piece] * CELL_CHUNKS
         aliases = {}
         if so_far is not None:
             inputs.append(so_far)
@@ -726,7 +761,7 @@
             out_shape=jax.ShapeDtypeStruct(energy.shape, f32),
             input_output_aliases=aliases,
             name="finish_chunk",
-            compiler_params=params(40),
+            compiler_params=params(VMEM_MIB),
             cost_estimate=pl.CostEstimate(
                 flops=20 * comps * row_count * col_count,
                 bytes_accessed=100 * MIB, transcendentals=0,
@@ -739,9 +774,8 @@
 def choose_shards(energy, *rest):
     local_comps, row_count, col_count = energy.shape
     fits = (
-        local_comps == 4 * NTH and lax.axis_size("comp") % 2 == 0
-        and lax.axis_size("comp") * local_comps == NTH * NF
-        and row_count % 8 == 0 and col_count == 2 * BLOCK
+        local_comps == 4 * NTH and lax.axis_size("comp") == 8 and local_comps * 8 == NTH * NF
+        and lax.axis_size("tile") == 2 and row_count == BLOCK and col_count == 2 * BLOCK
     )
     return packed_shards(energy, *rest) if fits else shards(energy, *rest)
 

time: 505 us -> 367 us (0.73)
  Pallas kernels: 238 us -> 192 us
  local copies, waits for them, and re-layouts: 54.5 us -> 11 us
  waiting for transfers between devices: 110 us -> 78.5 us
  between operations: 21.9 us -> 0.81 us
  starting transfers between devices: 69.2 us -> 76.9 us
    pallas_call x2, Pallas kernels: 86.2 us -> 32 us  [finish(): pl.pallas_call(functools.partial(finish_kernel, CELL_CHUNKS), grid_spec=p...]
    unnamed x198 -> x48, local copies, waits for them, and re-layouts: 41.3 us -> 2.45 us
    psum x1 -> x0, waiting for transfers between devices: 27.4 us -> none  [packed_shards(): mean_level = swap(lax.psum(swap(sums_0 + sums_1), 'comp')) / comp_total]
    ppermute x6 -> x12, waiting for transfers between devices: 49.4 us -> 31 us  [the longest x8 28.1 us: send_back(): return lax.ppermute(after(piece, *waits), 'comp', pairs)]
    ppermute x6 -> x12, starting transfers between devices: 7.76 us -> 25 us  [the longest x8 13.3 us: send_back(): return lax.ppermute(after(piece, *waits), 'comp', pairs)]
    ppermute x4, waiting for transfers between devices: 0.01 us -> 10.8 us  [packed_shards(): got_1.append(lax.ppermute(after(sent_1[c], *waits), 'comp', pairs))]
    ppermute x4, starting transfers between devices: 13.9 us -> 3.94 us  [packed_shards(): got_1.append(lax.ppermute(after(sent_1[c], *waits), 'comp', pairs))]
    ppermute x4, waiting for transfers between devices: 0.01 us -> 6.02 us  [packed_shards(): got_0 = [lax.ppermute(piece, 'comp', pairs) for piece in sent_0]]
  transfers between devices with their start and end apart: 31 -> 36, of which waited for: 8 -> 13; matrix products, arithmetic and copies ran while one was open for 3% -> 4% of each run, Pallas kernels for 19% -> 32%
where the time goes in v3:
time: 367 us; the launch traced here: 366 us
  Pallas kernels  192 us (52%)
  waiting for transfers between devices  78.5 us (21%)
  starting transfers between devices  76.9 us (21%)
  local copies, waits for them, and re-layouts  11 us (3%)
  other arithmetic  7.1 us (2%)
    pallas_call x2, Pallas kernels, propagate(): pl.pallas_call(functools.partial(propagate_kernel, part, steps), grid_spe...  114 us
    pallas_call x4, Pallas kernels, packed_shards(): pl.pallas_call(interact_kernel, grid=(width // lanes,), in_specs=[pl.Bloc...  33.5 us
    pallas_call x2, Pallas kernels, finish(): pl.pallas_call(functools.partial(finish_kernel, CELL_CHUNKS), grid_spec=p...  32 us
    ppermute x8, waiting for transfers between devices, send_back(): return lax.ppermute(after(piece, *waits), 'comp', pairs)  28.1 us
    ppermute x4, waiting for transfers between devices, packed_shards(): lax.ppermute(after(got_1[c], *own_parts[c - 2:c - 1]) if c >= 2 else got_...  20.6 us
    ppermute x4, starting transfers between devices, packed_shards(): from_got_0 = [lax.ppermute(piece, 'comp', across) for piece in got_0]  19.3 us
    ppermute x8, starting transfers between devices, send_back(): return lax.ppermute(after(piece, *waits), 'comp', pairs)  13.3 us
    ppermute x4, starting transfers between devices, packed_shards(): lax.ppermute(after(got_1[c], *own_parts[c - 2:c - 1]) if c >= 2 else got_...  11.8 us
  transfers between devices with their start and end apart: 36, of which 13 were waited for; matrix products, arithmetic and copies ran while one was open for 4% of the time, Pallas kernels for 32%

profile of v3, /device:TPU:0, one launch (start us, length us, event | category | flops | bytes accessed | tf_op | source)
XLA Modules:
  0.0 365.7 jit_solution(10037350638376307306)
XLA Ops:
  2.5 7.0 %prepare.1 = (f32[260,8,256]{2,1,0:T(8,128)}, s32[2,128,128]{2,1,0:T(8,128)}, s32[2,128,128]{2,1,0:T(8,128)}, s32[8,256]{1,0:T(8,128)}, f32[144,128]{1,0:T(8,128)}, /*index=5*/f32[144,128]{1,0:T(8,128)}) custom-call(s32[3]{0:T(128)} %pad_add_fusion.7.base_ref, f32[32]{0:T(128)} %speed_ref.1, s32[256,256]{1,0:T(8,128)} %sea_ref.1, f32[256,256]{1,0:T(8,128)} %east_ref.1, ...), custom_call_target="tpu_custom_call" | custom-call | tf_op jit(solution)/shard_map/prepare/pallas_call | solution.py:570
  9.5 5.1 %pack_fields.1.fields_ref = f32[8,16384]{1,0:T(8,128)} custom-call(s32[3]{0:T(128)} %pad_add_fusion.7.base_ref, s32[8,256]{1,0:T(8,128)} %get-tuple-element.73.table_ref, f32[260,8,256]{2,1,0:T(8,128)} %get-tuple-element.68.coef_ref, s32[2,128,128]{2,1,0:T(8,128)} %get-tuple-element.69.index_ref), custom_call_target="tpu_custom_call" | custom-call | tf_op jit(solution)/shard_map/pack_fields/pallas_call | solution.py:590
  15.3 57.0 %propagate_chunk.2 = (f32[72,2048]{1,0:T(8,128)}, f32[72,2048]{1,0:T(8,128)}, f32[72,2048]{1,0:T(8,128)}, f32[72,2048]{1,0:T(8,128)}, f32[72,2048]{1,0:T(8,128)}...) custom-call(s32[3]{0:T(128)} %pad_add_fusion.7.base_ref, ...), custom_call_target="tpu_custom_call" | custom-call | flops 141557760 | bytes 104857600 | tf_op jit(solution)/shard_map/propagate_chunk/pallas_call | solution.py:618
  79.1 56.9 %propagate_chunk.3 = (f32[72,2048]{1,0:T(8,128)}, f32[72,2048]{1,0:T(8,128)}, f32[72,2048]{1,0:T(8,128)}, f32[72,2048]{1,0:T(8,128)}, f32[72,2048]{1,0:T(8,128)}...) custom-call(s32[3]{0:T(128)} %pad_add_fusion.7.base_ref, ...), custom_call_target="tpu_custom_call" | custom-call | flops 141557760 | bytes 104857600 | tf_op jit(solution)/shard_map/propagate_chunk/pallas_call | solution.py:618
  154.7 6.0 %collective-permute-done.22.refs_5_ = f32[72,2048]{1,0:T(8,128)} collective-permute-done((f32[72,2048]{1,0:T(8,128)S(1)}, f32[72,2048]{1,0:T(8,128)}, u32[]{:S(2)}, u32[]{:S(2)}) %collective-permute-start.22) | collective-permute-done | bytes 589856 | tf_op jit(solution)/shard_map/ppermute | solution.py:649
  162.5 10.8 %collective-permute-done.5.refs_4_ = f32[72,2048]{1,0:T(8,128)S(1)} collective-permute-done((f32[72,2048]{1,0:T(8,128)}, f32[72,2048]{1,0:T(8,128)S(1)}, u32[]{:S(2)}, u32[]{:S(2)}) %collective-permute-start.5) | collective-permute-done | bytes 589856 | tf_op jit(solution)/shard_map/ppermute | solution.py:659
  177.1 3.8 %collective-permute-done.20.refs_6_ = f32[72,2048]{1,0:T(8,128)} collective-permute-done((f32[72,2048]{1,0:T(8,128)S(1)}, f32[72,2048]{1,0:T(8,128)}, u32[]{:S(2)}, u32[]{:S(2)}) %collective-permute-start.20) | collective-permute-done | bytes 589856 | tf_op jit(solution)/shard_map/ppermute | solution.py:650
  186.0 3.9 %collective-permute-done.7.refs_1_ = f32[72,2048]{1,0:T(8,128)} collective-permute-done((f32[72,2048]{1,0:T(8,128)}, f32[72,2048]{1,0:T(8,128)}, u32[]{:S(2)}, u32[]{:S(2)}) %collective-permute-start.7) | collective-permute-done | bytes 589856 | tf_op jit(solution)/shard_map/ppermute | solution.py:652
  194.8 5.4 %collective-permute-start.13 = (f32[72,2048]{1,0:T(8,128)}, f32[72,2048]{1,0:T(8,128)}, u32[]{:S(2)}, u32[]{:S(2)}) collective-permute-start(f32[72,2048]{1,0:T(8,128)} %collective-permute-done.10.refs_5_), channel_id=1, source_target_pairs={{6,2},{0,4},{10,6},{4,8},{14,10},{8,12},{7,3},{1,5},{11,7},{5,9},{... | collective-permute-start | bytes 1769480 | tf_op jit(solution)/shard_map/ppermute | solution.py:652
  208.6 8.4 %interact_cells.4 = (f32[144,2048]{1,0:T(8,128)}, f32[72,2048]{1,0:T(8,128)}, f32[72,2048]{1,0:T(8,128)}) custom-call(bf16[6,288,216]{2,1,0:T(8,128)(2,1)} %stack.28.table_ref, bf16[288,864]{1,0:T(8,128)(2,1)} %concatenate.40.spread_ref, f32[432,1]{1,0:T(8,128)} %copy.47.coupling_ref, f32[72,2048]{1,0:T(8,128)} %collective-permute-done.6.refs_0_, ...), custom_call_target="tpu_custom_call" | custom-call | flops 2548039680 | bytes 20971520 | tf_op jit(solution)/shard_map/interact_cells/pallas_call | solution.py:705
  217.0 4.9 %collective-permute-start.19 = (f32[72,2048]{1,0:T(8,128)}, f32[72,2048]{1,0:T(8,128)}, u32[]{:S(2)}, u32[]{:S(2)}) collective-permute-start(f32[72,2048]{1,0:T(8,128)} %collective-permute-done.16.refs_5_), channel_id=1, source_target_pairs={{6,2},{0,4},{10,6},{4,8},{14,10},{8,12},{7,3},{1,5},{11,7},{5,9},{... | collective-permute-start | bytes 1769480 | tf_op jit(solution)/shard_map/ppermute | solution.py:652
  226.6 6.4 %collective-permute-start.3 = (f32[1,16384]{1,0:T(1,128)S(1)}, f32[1,16384]{1,0:T(1,128)S(1)}, u32[]{:S(2)}, u32[]{:S(2)}) collective-permute-start(f32[1,16384]{1,0:T(1,128)S(1)} %add.253), channel_id=1, source_target_pairs={{0,8},{2,10},{4,12},{6,14},{8,0},{10,2},{12,4},{14,6},{1,9},{3,11}... | collective-permute-start | bytes 196616 | tf_op jit(solution)/shard_map/ppermute | solution.py:663
  232.9 8.4 %interact_cells.5 = (f32[144,2048]{1,0:T(8,128)}, f32[72,2048]{1,0:T(8,128)}, f32[72,2048]{1,0:T(8,128)}) custom-call(bf16[6,288,216]{2,1,0:T(8,128)(2,1)} %stack.28.table_ref, bf16[288,864]{1,0:T(8,128)(2,1)} %concatenate.40.spread_ref, f32[432,1]{1,0:T(8,128)} %copy.47.coupling_ref, f32[72,2048]{1,0:T(8,128)} %collective-permute-done.12.refs_0_, ...), custom_call_target="tpu_custom_call" | custom-call | flops 2548039680 | bytes 20971520 | tf_op jit(solution)/shard_map/interact_cells/pallas_call | solution.py:705
  242.7 5.4 %collective-permute-start.25 = (f32[72,2048]{1,0:T(8,128)}, f32[72,2048]{1,0:T(8,128)}, u32[]{:S(2)}, u32[]{:S(2)}) collective-permute-start(f32[72,2048]{1,0:T(8,128)} %collective-permute-done.22.refs_5_), channel_id=1, source_target_pairs={{6,2},{0,4},{10,6},{4,8},{14,10},{8,12},{7,3},{1,5},{11,7},{5,9},{... | collective-permute-start | bytes 1769480 | tf_op jit(solution)/shard_map/ppermute | solution.py:652
  253.5 19.9 %collective-permute-done.18.refs_0_ = f32[72,2048]{1,0:T(8,128)S(1)} collective-permute-done((f32[72,2048]{1,0:T(8,128)S(1)}, f32[72,2048]{1,0:T(8,128)S(1)}, u32[]{:S(2)}, u32[]{:S(2)}) %collective-permute-start.18) | collective-permute-done | bytes 589856 | tf_op jit(solution)/shard_map/ppermute | solution.py:701
  273.4 4.1 %collective-permute-start.34 = (f32[72,2048]{1,0:T(8,128)}, f32[72,2048]{1,0:T(8,128)S(1)}, u32[]{:S(2)}, u32[]{:S(2)}) collective-permute-start(f32[72,2048]{1,0:T(8,128)} %get-tuple-element.124), channel_id=1, source_target_pairs={{0,2},{2,0},{4,6},{6,4},{8,10},{10,8},{12,14},{14,12},{1,3},{3,1},... | collective-permute-start | bytes 1769480 | tf_op jit(solution)/shard_map/ppermute | solution.py:728
  277.5 8.4 %interact_cells.6 = (f32[144,2048]{1,0:T(8,128)}, f32[72,2048]{1,0:T(8,128)}, f32[72,2048]{1,0:T(8,128)}) custom-call(bf16[6,288,216]{2,1,0:T(8,128)(2,1)} %stack.28.table_ref, bf16[288,864]{1,0:T(8,128)(2,1)} %concatenate.40.spread_ref, f32[432,1]{1,0:T(8,128)} %copy.47.coupling_ref, f32[72,2048]{1,0:T(8,128)} %copy-done.23, ...), custom_call_target="tpu_custom_call" | custom-call | flops 2548039680 | bytes 20971520 | tf_op jit(solution)/shard_map/interact_cells/pallas_call | solution.py:705
  286.8 8.4 %interact_cells.7 = (f32[144,2048]{1,0:T(8,128)}, f32[72,2048]{1,0:T(8,128)}, f32[72,2048]{1,0:T(8,128)}) custom-call(bf16[6,288,216]{2,1,0:T(8,128)(2,1)} %stack.28.table_ref, bf16[288,864]{1,0:T(8,128)(2,1)} %concatenate.40.spread_ref, f32[432,1]{1,0:T(8,128)} %copy.47.coupling_ref, f32[72,2048]{1,0:T(8,128)} %collective-permute-done.24.refs_0_, ...), custom_call_target="tpu_custom_call" | custom-call | flops 2548039680 | bytes 20971520 | tf_op jit(solution)/shard_map/interact_cells/pallas_call | solution.py:705
  296.4 7.6 %collective-permute-done.29.refs_14_ = f32[72,2048]{1,0:T(8,128)S(1)} collective-permute-done((f32[72,2048]{1,0:T(8,128)}, f32[72,2048]{1,0:T(8,128)S(1)}, u32[]{:S(2)}, u32[]{:S(2)}) %collective-permute-start.29) | collective-permute-done | bytes 589856 | tf_op jit(solution)/shard_map/ppermute | solution.py:728
  311.5 5.2 %collective-permute-done.35.refs_15_ = f32[72,2048]{1,0:T(8,128)S(1)} collective-permute-done((f32[72,2048]{1,0:T(8,128)}, f32[72,2048]{1,0:T(8,128)S(1)}, u32[]{:S(2)}, u32[]{:S(2)}) %collective-permute-start.35) | collective-permute-done | bytes 589856 | tf_op jit(solution)/shard_map/ppermute | solution.py:728
  317.5 16.0 %finish_chunk.2.refs_16_ = f32[144,128,256]{2,1,0:T(8,128)} custom-call(s32[3]{0:T(128)} %pad_add_fusion.7.base_ref, s32[8,256]{1,0:T(8,128)} %get-tuple-element.73.table_ref, s32[2,128,128]{2,1,0:T(8,128)} %get-tuple-element.67.place_ref, f32[1,16384]{1,0:T(1,128)} %broadcast_multiply_fusion, f32[8,16384]{1,0:T(8,128)} %pack_fields.1.fields_ref, ...), custom_call_target="tpu_custom_call" | custom-call | flops 47185920 | bytes 104857600 | tf_op jit(solution)/shard_map/finish_chunk/pallas_call | solution.py:752
  333.5 8.5 %collective-permute-done.31.refs_14_ = f32[72,2048]{1,0:T(8,128)S(1)} collective-permute-done((f32[72,2048]{1,0:T(8,128)}, f32[72,2048]{1,0:T(8,128)S(1)}, u32[]{:S(2)}, u32[]{:S(2)}) %collective-permute-start.31) | collective-permute-done | bytes 589856 | tf_op jit(solution)/shard_map/ppermute | solution.py:728
  342.0 6.8 %collective-permute-done.32.refs_15_ = f32[72,2048]{1,0:T(8,128)S(1)} collective-permute-done((f32[72,2048]{1,0:T(8,128)}, f32[72,2048]{1,0:T(8,128)S(1)}, u32[]{:S(2)}, u32[]{:S(2)}) %collective-permute-start.32) | collective-permute-done | bytes 589856 | tf_op jit(solution)/shard_map/ppermute | solution.py:728
  349.6 16.0 %finish_chunk.3 = f32[144,128,256]{2,1,0:T(8,128)} custom-call(s32[3]{0:T(128)} %pad_add_fusion.7.base_ref, s32[8,256]{1,0:T(8,128)} %get-tuple-element.73.table_ref, s32[2,128,128]{2,1,0:T(8,128)} %get-tuple-element.67.place_ref, f32[1,16384]{1,0:T(1,128)} %broadcast_multiply_fusion, ...), custom_call_target="tpu_custom_call", output_to_operand_aliasing={{}: (23, {})} | custom-call | flops 47185920 | bytes 104857600 | tf_op jit(solution)/shard_map/finish_chunk/pallas_call | solution.py:752
  (148 shorter events, 74.9 us)
Async XLA Ops:
  73.1 71.1 %collective-permute-start.4 = (f32[72,2048]{1,0:T(8,128)}, f32[72,2048]{1,0:T(8,128)}, u32[]{:S(2)}, u32[]{:S(2)}) collective-permute-start(f32[72,2048]{1,0:T(8,128)} %get-tuple-element.89.refs_4_), channel_id=1, source_target_pairs={{0,2},{2,0},{4,6},{6,4},{8,10},{10,8},{12,14},{14,12},{1,3},{3,1},... | collective-permute-start | bytes 1769480 | tf_op jit(solution)/shard_map/ppermute | solution.py:649
  75.6 74.4 %collective-permute-start.10 = (f32[72,2048]{1,0:T(8,128)}, f32[72,2048]{1,0:T(8,128)}, u32[]{:S(2)}, u32[]{:S(2)}) collective-permute-start(f32[72,2048]{1,0:T(8,128)} %get-tuple-element.94.refs_5_), channel_id=1, source_target_pairs={{0,2},{2,0},{4,6},{6,4},{8,10},{10,8},{12,14},{14,12},{1,3},{3,1},... | collective-permute-start | bytes 1769480 | tf_op jit(solution)/shard_map/ppermute | solution.py:649
  75.7 77.6 %collective-permute-start.16 = (f32[72,2048]{1,0:T(8,128)}, f32[72,2048]{1,0:T(8,128)}, u32[]{:S(2)}, u32[]{:S(2)}) collective-permute-start(f32[72,2048]{1,0:T(8,128)} %get-tuple-element.99.refs_6_), channel_id=1, source_target_pairs={{0,2},{2,0},{4,6},{6,4},{8,10},{10,8},{12,14},{14,12},{1,3},{3,1},... | collective-permute-start | bytes 1769480 | tf_op jit(solution)/shard_map/ppermute | solution.py:649
  77.7 73.6 %collective-permute-start.8 = (f32[72,2048]{1,0:T(8,128)}, f32[72,2048]{1,0:T(8,128)}, u32[]{:S(2)}, u32[]{:S(2)}) collective-permute-start(f32[72,2048]{1,0:T(8,128)} %get-tuple-element.91.refs_2_.refs_0_), channel_id=1, source_target_pairs={{2,6},{4,0},{6,10},{8,4},{10,14},{12,8},{3,7},{5,1},{7,11},{9,5},{... | collective-permute-start | bytes 1769480 | tf_op jit(solution)/shard_map/ppermute | solution.py:650
  150.0 27.1 %collective-permute-start.14 = (f32[72,2048]{1,0:T(8,128)S(1)}, f32[72,2048]{1,0:T(8,128)}, u32[]{:S(2)}, u32[]{:S(2)}) collective-permute-start(f32[72,2048]{1,0:T(8,128)S(1)} %copy-done.1), channel_id=1, source_target_pairs={{2,6},{4,0},{6,10},{8,4},{10,14},{12,8},{3,7},{5,1},{7,11},{9,5},{... | collective-permute-start | bytes 1769480 | tf_op jit(solution)/shard_map/ppermute | solution.py:650
  151.3 29.6 %collective-permute-start.20 = (f32[72,2048]{1,0:T(8,128)S(1)}, f32[72,2048]{1,0:T(8,128)}, u32[]{:S(2)}, u32[]{:S(2)}) collective-permute-start(f32[72,2048]{1,0:T(8,128)S(1)} %copy-done.2), channel_id=1, source_target_pairs={{2,6},{4,0},{6,10},{8,4},{10,14},{12,8},{3,7},{5,1},{7,11},{9,5},{... | collective-permute-start | bytes 1769480 | tf_op jit(solution)/shard_map/ppermute | solution.py:650
  153.2 40.3 %collective-permute-start.9 = (f32[72,2048]{1,0:T(8,128)}, f32[72,2048]{1,0:T(8,128)}, u32[]{:S(2)}, u32[]{:S(2)}) collective-permute-start(f32[72,2048]{1,0:T(8,128)} %get-tuple-element.92.refs_3_.refs_0_), channel_id=1, source_target_pairs={{2,6},{4,0},{6,10},{8,4},{10,14},{12,8},{3,7},{5,1},{7,11},{9,5},{... | collective-permute-start | bytes 1769480 | tf_op jit(solution)/shard_map/ppermute | solution.py:660
  160.7 34.2 %collective-permute-start.11 = (f32[72,2048]{1,0:T(8,128)}, f32[72,2048]{1,0:T(8,128)}, u32[]{:S(2)}, u32[]{:S(2)}) collective-permute-start(f32[72,2048]{1,0:T(8,128)} %get-tuple-element.95.refs_5_), channel_id=1, source_target_pairs={{0,2},{2,0},{4,6},{6,4},{8,10},{10,8},{12,14},{14,12},{1,3},{3,1},... | collective-permute-start | bytes 1769480 | tf_op jit(solution)/shard_map/ppermute | solution.py:659
  177.1 26.4 %collective-permute-start.17 = (f32[72,2048]{1,0:T(8,128)}, f32[72,2048]{1,0:T(8,128)S(1)}, u32[]{:S(2)}, u32[]{:S(2)}) collective-permute-start(f32[72,2048]{1,0:T(8,128)} %get-tuple-element.100.refs_6_), channel_id=1, source_target_pairs={{0,2},{2,0},{4,6},{6,4},{8,10},{10,8},{12,14},{14,12},{1,3},{3,1},... | collective-permute-start | bytes 1769480 | tf_op jit(solution)/shard_map/ppermute | solution.py:659
  180.9 27.6 %collective-permute-start.6 = (f32[72,2048]{1,0:T(8,128)}, f32[72,2048]{1,0:T(8,128)}, u32[]{:S(2)}, u32[]{:S(2)}) collective-permute-start(f32[72,2048]{1,0:T(8,128)} %copy-done.22), channel_id=1, source_target_pairs={{6,2},{0,4},{10,6},{4,8},{14,10},{8,12},{7,3},{1,5},{11,7},{5,9},{... | collective-permute-start | bytes 1769480 | tf_op jit(solution)/shard_map/ppermute | solution.py:701
  189.9 27.0 %collective-permute-start.26 = (f32[72,2048]{1,0:T(8,128)S(1)}, f32[72,2048]{1,0:T(8,128)}, u32[]{:S(2)}, u32[]{:S(2)}) collective-permute-start(f32[72,2048]{1,0:T(8,128)S(1)} %copy-done.3), channel_id=1, source_target_pairs={{2,6},{4,0},{6,10},{8,4},{10,14},{12,8},{3,7},{5,1},{7,11},{9,5},{... | collective-permute-start | bytes 1769480 | tf_op jit(solution)/shard_map/ppermute | solution.py:650
  193.5 29.6 %collective-permute-start.15 = (f32[72,2048]{1,0:T(8,128)}, f32[72,2048]{1,0:T(8,128)}, u32[]{:S(2)}, u32[]{:S(2)}) collective-permute-start(f32[72,2048]{1,0:T(8,128)} %get-tuple-element.97.refs_3_.refs_1_), channel_id=1, source_target_pairs={{2,6},{4,0},{6,10},{8,4},{10,14},{12,8},{3,7},{5,1},{7,11},{9,5},{... | collective-permute-start | bytes 1769480 | tf_op jit(solution)/shard_map/ppermute | solution.py:660
  194.8 27.1 %collective-permute-start.13 = (f32[72,2048]{1,0:T(8,128)}, f32[72,2048]{1,0:T(8,128)}, u32[]{:S(2)}, u32[]{:S(2)}) collective-permute-start(f32[72,2048]{1,0:T(8,128)} %collective-permute-done.10.refs_5_), channel_id=1, source_target_pairs={{6,2},{0,4},{10,6},{4,8},{14,10},{8,12},{7,3},{1,5},{11,7},{5,9},{... | collective-permute-start | bytes 1769480 | tf_op jit(solution)/shard_map/ppermute | solution.py:652
  208.5 32.8 %collective-permute-start.23 = (f32[72,2048]{1,0:T(8,128)S(1)}, f32[72,2048]{1,0:T(8,128)}, u32[]{:S(2)}, u32[]{:S(2)}) collective-permute-start(f32[72,2048]{1,0:T(8,128)S(1)} %copy-done.7), channel_id=1, source_target_pairs={{0,2},{2,0},{4,6},{6,4},{8,10},{10,8},{12,14},{14,12},{1,3},{3,1},... | collective-permute-start | bytes 1769480 | tf_op jit(solution)/shard_map/ppermute | solution.py:659
  217.0 31.1 %collective-permute-start.19 = (f32[72,2048]{1,0:T(8,128)}, f32[72,2048]{1,0:T(8,128)}, u32[]{:S(2)}, u32[]{:S(2)}) collective-permute-start(f32[72,2048]{1,0:T(8,128)} %collective-permute-done.16.refs_5_), channel_id=1, source_target_pairs={{6,2},{0,4},{10,6},{4,8},{14,10},{8,12},{7,3},{1,5},{11,7},{5,9},{... | collective-permute-start | bytes 1769480 | tf_op jit(solution)/shard_map/ppermute | solution.py:652
  221.9 28.3 %collective-permute-start.21 = (f32[72,2048]{1,0:T(8,128)S(1)}, f32[72,2048]{1,0:T(8,128)}, u32[]{:S(2)}, u32[]{:S(2)}) collective-permute-start(f32[72,2048]{1,0:T(8,128)S(1)} %copy-done.5), channel_id=1, source_target_pairs={{2,6},{4,0},{6,10},{8,4},{10,14},{12,8},{3,7},{5,1},{7,11},{9,5},{... | collective-permute-start | bytes 1769480 | tf_op jit(solution)/shard_map/ppermute | solution.py:660
  223.2 29.5 %collective-permute-start.33 = (f32[72,2048]{1,0:T(8,128)}, f32[72,2048]{1,0:T(8,128)S(1)}, u32[]{:S(2)}, u32[]{:S(2)}) collective-permute-start(f32[72,2048]{1,0:T(8,128)} %get-tuple-element.122), channel_id=1, source_target_pairs={{0,2},{2,0},{4,6},{6,4},{8,10},{10,8},{12,14},{14,12},{1,3},{3,1},... | collective-permute-start | bytes 1769480 | tf_op jit(solution)/shard_map/ppermute | solution.py:728
  241.4 45.4 %collective-permute-start.27 = (f32[72,2048]{1,0:T(8,128)S(1)}, f32[72,2048]{1,0:T(8,128)}, u32[]{:S(2)}, u32[]{:S(2)}) collective-permute-start(f32[72,2048]{1,0:T(8,128)S(1)} %copy-done.6), channel_id=1, source_target_pairs={{2,6},{4,0},{6,10},{8,4},{10,14},{12,8},{3,7},{5,1},{7,11},{9,5},{... | collective-permute-start | bytes 1769480 | tf_op jit(solution)/shard_map/ppermute | solution.py:660
  242.7 44.1 %collective-permute-start.25 = (f32[72,2048]{1,0:T(8,128)}, f32[72,2048]{1,0:T(8,128)}, u32[]{:S(2)}, u32[]{:S(2)}) collective-permute-start(f32[72,2048]{1,0:T(8,128)} %collective-permute-done.22.refs_5_), channel_id=1, source_target_pairs={{6,2},{0,4},{10,6},{4,8},{14,10},{8,12},{7,3},{1,5},{11,7},{5,9},{... | collective-permute-start | bytes 1769480 | tf_op jit(solution)/shard_map/ppermute | solution.py:652
  248.1 38.7 %collective-permute-start.24 = (f32[72,2048]{1,0:T(8,128)}, f32[72,2048]{1,0:T(8,128)}, u32[]{:S(2)}, u32[]{:S(2)}) collective-permute-start(f32[72,2048]{1,0:T(8,128)} %collective-permute-done.23.refs_4_), channel_id=1, source_target_pairs={{6,2},{0,4},{10,6},{4,8},{14,10},{8,12},{7,3},{1,5},{11,7},{5,9},{... | collective-permute-start | bytes 1769480 | tf_op jit(solution)/shard_map/ppermute | solution.py:701
  252.7 33.1 %collective-permute-start.28 = (f32[72,2048]{1,0:T(8,128)}, f32[72,2048]{1,0:T(8,128)S(1)}, u32[]{:S(2)}, u32[]{:S(2)}) collective-permute-start(f32[72,2048]{1,0:T(8,128)} %get-tuple-element.112), channel_id=1, source_target_pairs={{0,2},{2,0},{4,6},{6,4},{8,10},{10,8},{12,14},{14,12},{1,3},{3,1},... | collective-permute-start | bytes 1769480 | tf_op jit(solution)/shard_map/ppermute | solution.py:728
  304.0 29.4 %collective-permute-start.30 = (f32[72,2048]{1,0:T(8,128)}, f32[72,2048]{1,0:T(8,128)S(1)}, u32[]{:S(2)}, u32[]{:S(2)}) collective-permute-start(f32[72,2048]{1,0:T(8,128)} %get-tuple-element.116), channel_id=1, source_target_pairs={{0,2},{2,0},{4,6},{6,4},{8,10},{10,8},{12,14},{14,12},{1,3},{3,1},... | collective-permute-start | bytes 1769480 | tf_op jit(solution)/shard_map/ppermute | solution.py:728
  306.4 35.5 %collective-permute-start.31 = (f32[72,2048]{1,0:T(8,128)}, f32[72,2048]{1,0:T(8,128)S(1)}, u32[]{:S(2)}, u32[]{:S(2)}) collective-permute-start(f32[72,2048]{1,0:T(8,128)} %get-tuple-element.118), channel_id=1, source_target_pairs={{0,2},{2,0},{4,6},{6,4},{8,10},{10,8},{12,14},{14,12},{1,3},{3,1},... | collective-permute-start | bytes 1769480 | tf_op jit(solution)/shard_map/ppermute | solution.py:728
  306.5 42.3 %collective-permute-start.32 = (f32[72,2048]{1,0:T(8,128)}, f32[72,2048]{1,0:T(8,128)S(1)}, u32[]{:S(2)}, u32[]{:S(2)}) collective-permute-start(f32[72,2048]{1,0:T(8,128)} %get-tuple-element.120), channel_id=1, source_target_pairs={{0,2},{2,0},{4,6},{6,4},{8,10},{10,8},{12,14},{14,12},{1,3},{3,1},... | collective-permute-start | bytes 1769480 | tf_op jit(solution)/shard_map/ppermute | solution.py:728
  (36 other events, 1060.4 us)

commit v4 on v3

--- a/solution.py
+++ b/solution.py
@@ -180,6 +180,7 @@
 
 BLOCK = 128
 GROUP = 24
+EARLY = 40
 CELL_CHUNKS = 4
 MIB = 1024 * 1024
 VMEM_MIB = 60
@@ -192,10 +193,9 @@
     return ref[row : row + 1, :]
 
 
-def upwind(courant, here, ahead, slope_here, bend_here, bend_ahead):
-    square = courant * courant
+def upwind(courant, total, slope, bend_here, bend_ahead):
     bend = jnp.where(courant > 0.0, bend_here, bend_ahead)
-    return courant * ((here + ahead) - courant * slope_here - (1.0 / 3.0 - square * (1.0 / 3.0)) * bend)
+    return courant * ((total - bend) - courant * (slope - courant * bend))
 
 
 def pick_lanes(block, index):
@@ -313,50 +313,35 @@
     table_ref[...] = jnp.concatenate([jnp.where(row_id == 0, columns[0], columns[1]), end_tile], axis=1)
 
 
-def pack_fields_kernel(row_count, base_ref, table_ref, coef_ref, index_ref, out_ref, wide_ref):
-    def eight(i, held):
-        codes = [index_ref[h, pl.ds(pl.multiple_of(8 * i, 8), 8), :] for h in range(2)]
-        for at in range(8):
-            row = 8 * i + at
-            fields = coef_ref[base_ref[0] + EDGE + row]
-            for h in range(2):
-                block = fields[:, h * BLOCK : (h + 1) * BLOCK]
-                held = pack_block([block], codes[h][at : at + 1, :], table_ref[h, row], wide_ref, [0], held)
-        return held
-
-    held = lax.fori_loop(0, row_count // 8, eight, (jnp.zeros((8, BLOCK), jnp.float32),))
-    wide_ref[:, tile_at(table_ref[0, row_count])] = held[0]
-    out_ref[...] = wide_ref[:, : out_ref.shape[1]]
-
-
-def propagate_kernel(part, steps, base_ref, table_ref, energy_ref, halo_ref, coef_ref, index_ref, east_ref,
-                     north_ref, fields_ref, *refs):
-    wide_ref, rows_ref, sems = refs[-3:]
-    sum_ref, outs = refs[-4], refs[:-4]
-    step_id = pl.program_id(0)
-    row_count, col_count = energy_ref.shape[1:]
+def propagate_kernel(part, late, pieces, base_ref, table_ref, energy_ref, halo_ref, coef_ref, index_ref, east_ref,
+                     north_ref, *refs):
+    refs = list(refs)
+    with_fields = part == 0 and not late
+    fields_ref = None if with_fields else refs.pop(0)
+    seam_ref = refs.pop(0) if late else None
+    if late:
+        refs.pop(0)
+    piece_refs = [refs.pop(0) for _ in range(2 * pieces)]
+    sum_ref, full_ref = refs.pop(0), refs.pop(0)
+    seam_out_ref = None if late else refs.pop(0)
+    fields_out_ref = refs.pop(0) if with_fields else None
+    rows_ref, wide_ref, result_ref, row_sems, out_sems = refs
+    row_count, comp_count, col_count = rows_ref.shape
+    strips = comp_count // 8
+    sent_rows = piece_refs[0].shape[0]
+    cells = result_ref.shape[1]
     first_row = base_ref[0]
-    first_comp = (part + base_ref[1] * (1 - 2 * part)) * steps * GROUP
+    first_comp = pl.multiple_of((part + base_ref[1] * (1 - 2 * part)) * 2 * NTH + late * EARLY, 8)
     lane = lax.broadcasted_iota(jnp.int32, (8, BLOCK), 1)
     first_lane, last_lane = lane == 0, lane == BLOCK - 1
-
-    def fetch(step):
-        comps = pl.ds(first_comp + step * GROUP, GROUP)
-
-        @pl.loop(0, row_count, unroll=4)
-        def _(r):
-            pltpu.make_async_copy(energy_ref.at[comps, r, :], rows_ref.at[step % 2, r], sems.at[step % 2]).start()
-
-    @pl.when(step_id == 0)
-    def _():
-        fetch(0)
-
-    @pl.when(step_id + 1 < steps)
-    def _():
-        fetch(step_id + 1)
-
-    slot = step_id % 2
-    pltpu.make_async_copy(rows_ref.at[slot], rows_ref.at[slot], sems.at[slot]).wait()
+    third = 1.0 / 3.0
+
+    @pl.loop(0, row_count // 8)
+    def _(i):
+        for k in range(8):
+            row = 8 * i + k
+            source = energy_ref.at[pl.ds(first_comp, comp_count), row, :]
+            pltpu.make_async_copy(source, rows_ref.at[row], row_sems.at[i]).start()
 
     def halves(row):
         return row[:, :BLOCK], row[:, BLOCK:]
@@ -366,107 +351,136 @@
         return tuple(part * sea for part, sea in zip(halves(row), sea_row))
 
     def cell_row(at, new, state, east, north):
-        here, ahead, bend_here, flux_low = state
+        here, ahead, slope_ahead, bend_here, flux_low = state
         coef = [halves(row_of(coef_ref.at[first_row + at], k)) for k in range(HALF_SEA + 1)]
         to_right = [pltpu.roll(part, BLOCK - 1, 1) for part in here]
-        to_left = [pltpu.roll(part, 1, 1) for part in here]
         right = (jnp.where(last_lane, to_right[1], to_right[0]), jnp.where(last_lane, 0.0, to_right[1]))
-        left = (jnp.where(first_lane, 0.0, to_left[0]), jnp.where(first_lane, to_left[0], to_left[1]))
-        slope_right = [right[h] - here[h] for h in range(2)]
-        bend = [slope_right[h] - (here[h] - left[h]) for h in range(2)]
+        slope = [right[h] - here[h] for h in range(2)]
+        slope_roll = [pltpu.roll(part, 1, 1) for part in slope]
+        slope_left = (jnp.where(first_lane, here[0], slope_roll[0]),
+                      jnp.where(first_lane, slope_roll[0], slope_roll[1]))
+        bend = [third * (slope[h] - slope_left[h]) for h in range(2)]
         bend_roll = [pltpu.roll(part, BLOCK - 1, 1) for part in bend]
         bend_right = (jnp.where(last_lane, bend_roll[1], bend_roll[0]), bend_roll[1])
-        cross, flux, bend_ahead = [], [], []
+        cross, flux, slope_next, bend_ahead = [], [], [], []
         for h in range(2):
-            cross.append(upwind(north * coef[OPEN_NORTH][h] + coef[FLOW_NORTH][h], here[h], right[h],
-                                slope_right[h], bend[h], bend_right[h]))
-            slope = ahead[h] - here[h]
-            bend_ahead.append((new[h] - ahead[h]) - slope)
-            flux.append(upwind(east * coef[OPEN_EAST][h] + coef[FLOW_EAST][h], here[h], ahead[h], slope,
+            cross.append(upwind(north * coef[OPEN_NORTH][h] + coef[FLOW_NORTH][h], here[h] + right[h], slope[h],
+                                bend[h], bend_right[h]))
+            slope_next.append(new[h] - ahead[h])
+            bend_ahead.append(third * (slope_next[h] - slope_ahead[h]))
+            flux.append(upwind(east * coef[OPEN_EAST][h] + coef[FLOW_EAST][h], here[h] + ahead[h], slope_ahead[h],
                                bend_here[h], bend_ahead[h]))
         cross_roll = [pltpu.roll(part, 1, 1) for part in cross]
         cross_low = (jnp.where(first_lane, cross_roll[1], cross_roll[0]),
                      jnp.where(first_lane, cross_roll[0], cross_roll[1]))
         moved = [
-            coef[HALF_SEA][h] * ((here[h] + here[h]) - (flux[h] - flux_low[h]) - (cross[h] - cross_low[h]))
+            coef[HALF_SEA][h] * (((here[h] + here[h]) + (flux_low[h] + cross_low[h])) - (flux[h] + cross[h]))
             for h in range(2)
         ]
-        return (ahead, new, tuple(bend_ahead), tuple(flux)), jnp.concatenate(moved, axis=1)
-
-    @pl.loop(0, GROUP // 8)
-    def _(g):
+        return (ahead, new, tuple(slope_next), tuple(bend_ahead), tuple(flux)), jnp.concatenate(moved, axis=1)
+
+    def strip(g, arrive):
         local = pl.ds(pl.multiple_of(g * 8, 8), 8)
-        east, north = east_ref[local, :], north_ref[local, :]
+        comps = pl.ds(pl.multiple_of(first_comp + g * 8, 8), 8)
+        east, north = east_ref[comps, :], north_ref[comps, :]
         zero = (jnp.zeros((8, BLOCK), jnp.float32),) * 2
-        state = (masked(halo_ref[local, 0, :], 0), masked(halo_ref[local, 1, :], 1), zero, zero)
+        here, ahead = masked(halo_ref[comps, 0, :], 0), masked(halo_ref[comps, 1, :], 1)
+        state = (here, ahead, tuple(b - a for a, b in zip(here, ahead)), zero, zero)
 
         def eight(i, state):
-            fresh = [rows_ref[slot, 8 * i + k, local, :] for k in range(8)]
+            if arrive:
+                block = rows_ref.at[pl.ds(8 * i, 8)]
+                pltpu.make_async_copy(block, block, row_sems.at[i]).wait()
+            fresh = [rows_ref[8 * i + k, local, :] for k in range(8)]
             done = []
             for k in range(8):
                 new = masked(fresh[k], 8 * i + k + EDGE)
                 state, moved = cell_row(8 * i + k, new, state, east, north)
                 done.append(moved)
             for k in range(8):
-                rows_ref[slot, jnp.maximum(8 * i + k - EDGE, 0), local, :] = done[k]
+                rows_ref[jnp.maximum(8 * i + k - EDGE, 0), local, :] = done[k]
             return state
 
         state = lax.fori_loop(0, row_count // 8, eight, state)
         for k in range(EDGE):
-            new = masked(halo_ref[local, k, :], row_count + EDGE + k)
+            new = masked(halo_ref[comps, k, :], row_count + EDGE + k)
             state, moved = cell_row(row_count + k, new, state, east, north)
-            rows_ref[slot, row_count - EDGE + k, local, :] = moved
-
-    group_rows = [pl.multiple_of(step_id * GROUP + 8 * k, 8) for k in range(GROUP // 8)]
+            rows_ref[row_count - EDGE + k, local, :] = moved
+
+    strip(0, True)
+
+    @pl.loop(1, strips)
+    def _(g):
+        strip(g, False)
+
+    group_rows = [8 * n for n in range(strips + with_fields)]
 
     def pack_eight(i, held):
         codes = [index_ref[h, pl.ds(pl.multiple_of(8 * i, 8), 8), :] for h in range(2)]
         for k in range(8):
+            row = 8 * i + k
             for h in range(2):
                 lanes = slice(h * BLOCK, (h + 1) * BLOCK)
-                blocks = [rows_ref[slot, 8 * i + k, 8 * n : 8 * n + 8, lanes] for n in range(GROUP // 8)]
-                held = pack_block(blocks, codes[h][k : k + 1, :], table_ref[h, 8 * i + k], wide_ref, group_rows, held)
+                blocks = [rows_ref[row, 8 * n : 8 * n + 8, lanes] for n in range(strips)]
+                if with_fields:
+                    blocks.append(coef_ref[first_row + EDGE + row, :, lanes])
+                held = pack_block(blocks, codes[h][k : k + 1, :], table_ref[h, row], wide_ref, group_rows, held)
         return held
 
-    empty = (jnp.zeros((8, BLOCK), jnp.float32),) * (GROUP // 8)
+    empty = (jnp.zeros((8, BLOCK), jnp.float32),) * len(group_rows)
     held = lax.fori_loop(0, row_count // 8, pack_eight, empty)
     for first, block in zip(group_rows, held):
         wide_ref[pl.ds(first, 8), tile_at(table_ref[0, row_count])] = block
-
-    @pl.when(step_id == steps - 1)
-    def _():
-        comps, width = outs[0].shape
-        tile_width = 2 * BLOCK
-        comp_row = lax.broadcasted_iota(jnp.int32, (comps, tile_width), 0)
-        circle_row = comp_row % NTH
-        for o, out_ref in enumerate(outs):
-
-            @pl.loop(0, width // tile_width)
-            def _(i):
-                source = pl.ds(pl.multiple_of(o * width + i * tile_width, tile_width), tile_width)
-                target = pl.ds(pl.multiple_of(i * tile_width, tile_width), tile_width)
-                level = wide_ref[:, source]
-                rate = fields_ref[TURN : TURN + 1, source]
-                forward = jnp.maximum(rate, 0.0)
-                backward = jnp.minimum(rate, 0.0)
-                after = pltpu.roll(level, comps - 1, 0)
-                before = pltpu.roll(level, 1, 0)
-                for start in range(0, comps, NTH):
-                    end = start + NTH - 1
-                    after = jnp.where(comp_row == end, level[start : start + 1, :], after)
-                    before = jnp.where(comp_row == start, level[end : end + 1, :], before)
-                turned = (1.0 - forward + backward) * level - backward * after + forward * before
-                out_ref[:, target] = turned
-                sum_ref[:, source] = jnp.sum(turned, axis=0, keepdims=True)
+    if with_fields:
+        fields_out_ref[...] = wide_ref[comp_count:, :cells]
+
+    tile_width = 2 * BLOCK
+    height = result_ref.shape[0]
+    comp_row = lax.broadcasted_iota(jnp.int32, (height, tile_width), 0)
+    start = height - NTH if late else 0
+    end = start + NTH - 1
+    in_circle = (comp_row >= start) & (comp_row <= end)
+
+    @pl.loop(0, cells // tile_width)
+    def _(i):
+        source = pl.ds(pl.multiple_of(i * tile_width, tile_width), tile_width)
+        level = wide_ref[:comp_count, source]
+        if late:
+            level = jnp.concatenate([seam_ref[:, source], level], axis=0)
+        if with_fields:
+            rate = wide_ref[comp_count + TURN : comp_count + TURN + 1, source]
+        else:
+            rate = fields_ref[TURN : TURN + 1, source]
+        forward = jnp.maximum(rate, 0.0)
+        backward = jnp.minimum(rate, 0.0)
+        above = jnp.where(comp_row == end, level[start : start + 1, :], pltpu.roll(level, height - 1, 0))
+        below = jnp.where(comp_row == start, level[end : end + 1, :], pltpu.roll(level, 1, 0))
+        turned = (1.0 - forward + backward) * level - backward * above + forward * below
+        result_ref[:, source] = jnp.where(in_circle, turned, level)
+        sum_ref[:, source] = jnp.sum(jnp.where(in_circle, turned, 0.0), axis=0, keepdims=True)
+
+    if not late:
+        seam_out_ref[...] = result_ref[sent_rows:, :]
+    width = cells // (2 * pieces)
+    copies = []
+    for n, piece in enumerate(piece_refs):
+        source = result_ref.at[:sent_rows, n * width : (n + 1) * width]
+        copies.append(pltpu.make_async_copy(source, piece, out_sems.at[n]))
+    rows = pl.ds(EARLY - 8 if late else 0, sent_rows)
+    copies.append(pltpu.make_async_copy(result_ref.at[:sent_rows, :], full_ref.at[rows, :], out_sems.at[2 * pieces]))
+    for copy in copies:
+        copy.start()
+    for copy in copies:
+        copy.wait()
 
 
 def interact_kernel(table_ref, spread_ref, coupling_ref, *refs):
-    window, (own_ref, back_0_ref, back_1_ref, delta_ref) = refs[:8], refs[8:]
+    own_ref, back_0_ref, back_1_ref, delta_ref = refs[16:]
+    window = [jnp.concatenate([refs[2 * j][...], refs[2 * j + 1][...]], axis=0) for j in range(8)]
     comps = window[0].shape[0]
-    kept = []
     for j in range(1, 7):
-        level = window[j][...]
-        around = jnp.concatenate([window[j - 1][...], level, window[j + 1][...]], axis=0).astype(jnp.bfloat16)
+        level = window[j]
+        around = jnp.concatenate([window[j - 1], level, window[j + 1]], axis=0).astype(jnp.bfloat16)
         partner = jnp.dot(table_ref[j - 1], around, preferred_element_type=jnp.float32)
         rate = coupling_ref[(j - 1) * comps : j * comps, :] * level
         plus_part = weight_plus * level
@@ -493,7 +507,7 @@
 
 
 def finish_kernel(chunks, base_ref, table_ref, place_ref, mean_ref, fields_ref, growth_ref, damping_ref, *refs):
-    turned, own, back = refs[: 2 * chunks], refs[2 * chunks : 3 * chunks], refs[3 * chunks : 4 * chunks]
+    turned_ref, own, back = refs[0], refs[1 : 1 + chunks], refs[1 + chunks : 1 + 2 * chunks]
     out_ref, wide_ref = refs[-2], refs[-1]
     width = own[0].shape[1]
     tiles = wide_ref.shape[1] // BLOCK
@@ -508,7 +522,7 @@
             source = pl.ds(pl.multiple_of(i * tile_width, tile_width), tile_width)
             target = pl.ds(pl.multiple_of(o * width + i * tile_width, tile_width), tile_width)
             scale = 1.0 + growth * fields_ref[WIND : WIND + 1, target] - damping * mean_ref[0:1, target]
-            wide_ref[:, target] = turned[o][:, source] * scale + extra[:, source]
+            wide_ref[:, target] = turned_ref[:, target] * scale + extra[:, source]
 
     @pl.loop(0, out_ref.shape[1] // 8)
     def _(i):
@@ -587,20 +601,6 @@
         name="prepare",
         compiler_params=params(VMEM_MIB),
     )(base, group_speed, sea_mask, current_u, current_v, wind_forcing, refraction, cosines, sines)
-    packed_fields = pl.pallas_call(
-        functools.partial(pack_fields_kernel, row_count),
-        grid_spec=pltpu.PrefetchScalarGridSpec(
-            num_scalar_prefetch=2,
-            grid=(),
-            in_specs=[vmem] * 2,
-            out_specs=vmem,
-            scratch_shapes=[pltpu.VMEM((8, cells + BLOCK), f32)],
-        ),
-        out_shape=jax.ShapeDtypeStruct((8, cells), f32),
-        name="pack_fields",
-        compiler_params=params(VMEM_MIB),
-    )(base, table, coef, index)
-
     steps = comps // GROUP
 
     def group_at(part, base_ref):
@@ -612,52 +612,101 @@
     def column(part, lanes):
         return pl.BlockSpec((GROUP, lanes), lambda s, b, t: (group_at(part, b) + s, 0))
 
-    def propagate(part, table):
-        halo = pl.BlockSpec((GROUP, EDGE, col_count), lambda s, b, t: (group_at(part, b) + s, 0, 0))
-        out_chunk = jax.ShapeDtypeStruct((comps, width), f32)
+    def propagate(part, late, table, fields=None, seam=None, full=None):
+        pieces = CELL_CHUNKS if part and late else 1
+        comp_rows = comps - EARLY if late else EARLY
+        sent_rows = comps - EARLY + 8 if late else EARLY - 8
+        height = EARLY
+        anywhere = pl.BlockSpec(memory_space=pl.ANY)
+        with_fields = fields is None
+        inputs = [energy, halo_rows, coef, index, speed_east, speed_north]
+        in_specs = [anywhere] + [vmem] * 5
+        aliases = {}
+        if not with_fields:
+            inputs.append(fields)
+            in_specs.append(vmem)
+        if late:
+            inputs += [seam, full]
+            in_specs += [vmem, anywhere]
+            aliases = {len(inputs) + 1: 2 * pieces + 1}
+        shapes = [(sent_rows, half // pieces)] * (2 * pieces) + [(1, cells), (comps, cells)]
+        out_specs = [anywhere] * (2 * pieces) + [vmem, anywhere]
+        if not late:
+            shapes.append((8, cells))
+            out_specs.append(vmem)
+        if with_fields:
+            shapes.append((8, cells))
+            out_specs.append(vmem)
         outs = pl.pallas_call(
-            functools.partial(propagate_kernel, part, steps),
+            functools.partial(propagate_kernel, part, late, pieces),
             grid_spec=pltpu.PrefetchScalarGridSpec(
                 num_scalar_prefetch=2,
-                grid=(steps,),
-                in_specs=[
-                    pl.BlockSpec(memory_space=pl.ANY), halo, whole(coef.shape), whole(index.shape),
-                    column(part, BLOCK), column(part, BLOCK), whole(packed_fields.shape),
-                ],
-                out_specs=[whole((comps, width))] * (2 * CELL_CHUNKS) + [whole((1, cells))],
+                grid=(),
+                in_specs=in_specs,
+                out_specs=out_specs,
                 scratch_shapes=[
-                    pltpu.VMEM((comps, cells + BLOCK), f32),
-                    pltpu.VMEM((2, row_count, GROUP, col_count), f32),
-                    pltpu.SemaphoreType.DMA((2,)),
+                    pltpu.VMEM((row_count, comp_rows, col_count), f32),
+                    pltpu.VMEM((comp_rows + (8 if with_fields else 0), cells + BLOCK), f32),
+                    pltpu.VMEM((height, cells), f32),
+                    pltpu.SemaphoreType.DMA((row_count // 8,)),
+                    pltpu.SemaphoreType.DMA((2 * pieces + 1,)),
                 ],
             ),
-            out_shape=[out_chunk] * (2 * CELL_CHUNKS) + [jax.ShapeDtypeStruct((1, cells), f32)],
-            name="propagate_chunk",
+            out_shape=[jax.ShapeDtypeStruct(shape, f32) for shape in shapes],
+            input_output_aliases=aliases,
+            name="propagate_late" if late else "propagate_early",
             compiler_params=params(VMEM_MIB),
             cost_estimate=pl.CostEstimate(
-                flops=60 * comps * row_count * col_count, bytes_accessed=100 * MIB, transcendentals=0,
+                flops=60 * comp_rows * row_count * col_count, bytes_accessed=60 * MIB, transcendentals=0,
             ),
-        )(base, table, energy, halo_rows, coef, index, speed_east, speed_north, packed_fields)
-        return list(outs[:CELL_CHUNKS]), list(outs[CELL_CHUNKS : 2 * CELL_CHUNKS]), outs[-1]
+        )(base, table, *inputs)
+        return list(outs[:pieces]), list(outs[pieces : 2 * pieces]), outs[2 * pieces :]
 
     pairs = [(i, i ^ 1) for i in range(comp_count)]
     apart = [(i, i - 2 if i % 2 == 0 else i + 2) for i in range(comp_count)]
     apart = [(a, b) for a, b in apart if 0 <= b < comp_count]
     across = [(b, a) for a, b in apart]
     chunk_range = range(CELL_CHUNKS)
-    kept_0, sent_0, sums_0 = propagate(0, table)
-    got_0 = [lax.ppermute(piece, "comp", pairs) for piece in sent_0]
-    from_own_0 = [lax.ppermute(piece, "comp", apart) for piece in kept_0]
-    kept_1, sent_1, sums_1 = propagate(1, after(table, sums_0))
-    from_got_0 = [lax.ppermute(piece, "comp", across) for piece in got_0]
-    sums = sums_0 + sums_1
+
+    def send(pieces, route, waits):
+        return [lax.ppermute(after(piece, *wait), "comp", route) for piece, wait in zip(pieces, waits)]
+
+    stages = [(0, 0), (0, 1), (1, 0), (1, 1)]
+    kept, sent, got, from_own, from_got, level_sums, full = {}, {}, {}, {}, {}, [], {}
+    fields = seam = before = None
+    part_table = table
+    for stage in stages:
+        part, late = stage
+        kept[stage], sent[stage], extra = propagate(part, late, part_table, fields, seam, full.get(part))
+        level_sums.append(extra[0])
+        full[part] = extra[1]
+        seam = None if late else extra[2]
+        fields = extra[3] if fields is None else fields
+        if stage == stages[-1]:
+            break
+        got[stage] = send(sent[stage], pairs, [[]])
+        from_own[stage] = send(kept[stage], apart, [[]])
+        waits = [from_got[before][0]] if stage == stages[2] else []
+        from_got[stage] = send(got[stage], across, [waits])
+        done = [extra[0]]
+        if before is not None:
+            done.append(got[before][0])
+            if stage == stages[2]:
+                done += [from_got[stages[0]][0], from_own[stages[1]][0]]
+        part_table = after(table, *done)
+        before = stage
+    packed_fields = fields
+    sums_0 = level_sums[0]
+
+    sums = level_sums[0] + level_sums[1] + level_sums[2] + level_sums[3]
     partner_sums = lax.ppermute(sums, "comp", pairs)
     partner_sums = jnp.roll(partner_sums, half, axis=1)
-    got_1, from_own_1 = [], []
+    last, got_1, from_own_1 = stages[-1], [], []
     for c in chunk_range:
-        waits = [got_0[c]] + ([got_1[c - 2]] if c >= 2 else []) + ([partner_sums] if c == 2 else [])
-        got_1.append(lax.ppermute(after(sent_1[c], *waits), "comp", pairs))
-        from_own_1.append(lax.ppermute(after(kept_1[c], from_own_0[c]), "comp", apart))
+        waits = [got[before][0]] + ([got_1[c - 2]] if c >= 2 else []) + ([partner_sums] if c == 2 else [])
+        got_1.append(lax.ppermute(after(sent[last][c], *waits), "comp", pairs))
+        from_own_1.append(lax.ppermute(after(kept[last][c], from_own[before][0]), "comp", apart))
+    got[last], from_own[last], from_got[last] = got_1, from_own_1, []
     sums = sums + partner_sums
     sums = sums_two = sums + lax.ppermute(sums, "comp", [(i, i ^ 2) for i in range(comp_count)])
     sums = sums + lax.ppermute(sums, "comp", [(i, i ^ 4) for i in range(comp_count)])
@@ -697,11 +746,20 @@
 
     lanes = 512 if width % 512 == 0 else width
     own_parts, parts_0, parts_1 = [], [], []
+    groups = [(from_got, 1), (from_got, 0), (kept, 0), (kept, 1), (got, 1), (got, 0), (from_own, 0), (from_own, 1)]
     for c in chunk_range:
-        from_got_1 = lax.ppermute(after(got_1[c], *own_parts[c - 2 : c - 1]) if c >= 2 else got_1[c], "comp", across)
-        levels = [
-            from_got_1, from_got_0[c], kept_0[c], kept_1[c], got_1[c], got_0[c], from_own_0[c], from_own_1[c],
-        ]
+        waits = [from_got[before][0]] + ([from_got[last][c - 2]] if c >= 2 else [])
+        from_got[last].append(lax.ppermute(after(got_1[c], *waits), "comp", across))
+        levels, level_specs = [], []
+        for group, part in groups:
+            for late in range(2):
+                pieces = group[part, late]
+                single = len(pieces) == 1
+                levels.append(pieces[0 if single else c])
+                skipped = c * (width // lanes) if single else 0
+                level_specs.append(
+                    pl.BlockSpec((levels[-1].shape[0], lanes), functools.partial(lambda n, s: (0, n + s), skipped))
+                )
         own_part, part_0, part_1 = pl.pallas_call(
             interact_kernel,
             grid=(width // lanes,),
@@ -709,7 +767,7 @@
                 pl.BlockSpec(lookup.shape, lambda s: (0, 0, 0)),
                 pl.BlockSpec(spread.shape, lambda s: (0, 0)),
                 pl.BlockSpec(rates.shape, lambda s: (0, 0)),
-            ] + [pl.BlockSpec((comps, lanes), lambda s: (0, s))] * 8,
+            ] + level_specs,
             out_specs=[pl.BlockSpec((n * comps, lanes), lambda s: (0, s)) for n in (2, 1, 1)],
             out_shape=[jax.ShapeDtypeStruct((n * comps, width), f32) for n in (2, 1, 1)],
             scratch_shapes=[pltpu.VMEM((12 * comps, lanes), jnp.bfloat16)],
@@ -742,8 +800,9 @@
         inputs = [place, mean_level, packed_fields, own_growth, own_damping]
         specs = [whole(place.shape), whole(mean_level.shape), whole(packed_fields.shape), column(part, 1),
                  column(part, 1)]
-        inputs += [kept_0, kept_1][part] + [sent_0, sent_1][part] + own_parts + back[part]
-        specs += [piece] * (2 * CELL_CHUNKS) + [own_piece] * CELL_CHUNKS + [piece] * CELL_CHUNKS
+        inputs += [full[part]] + own_parts + back[part]
+        specs.append(pl.BlockSpec((GROUP, cells), lambda s, b, t: (s, 0)))
+        specs += [own_piece] * CELL_CHUNKS + [piece] * CELL_CHUNKS
         aliases = {}
         if so_far is not None:
             inputs.append(so_far)

time: 367 us -> 382 us (1.041)
  Pallas kernels: 192 us -> 214 us
  starting transfers between devices: 76.9 us -> 65.2 us
    pallas_call x3 -> x4, Pallas kernels: 119 us -> 142 us  [propagate(): pl.pallas_call(functools.partial(propagate_kernel, part, late, pieces), g...]
    ppermute x8, starting transfers between devices: 13.3 us -> 7.37 us  [send_back(): return lax.ppermute(after(piece, *waits), 'comp', pairs)]
    ppermute x24 -> x21, starting transfers between devices: 51.9 us -> 47.8 us  [the longest x9 22.9 us: send(): lax.ppermute(after(piece, *wait), 'comp', route)]
    ppermute x24 -> x21, waiting for transfers between devices: 47.4 us -> 45.7 us  [the longest x9 39.9 us: send(): lax.ppermute(after(piece, *wait), 'comp', route)]
  transfers between devices with their start and end apart: 36 -> 33, of which waited for: 13 -> 11; matrix products, arithmetic and copies ran while one was open for 4% -> 4% of each run, Pallas kernels for 32% -> 42%
where the time goes in v4:
time: 382 us; the launch traced here: 380 us
  Pallas kernels  214 us (56%)
  waiting for transfers between devices  77.1 us (20%)
  starting transfers between devices  65.2 us (17%)
  local copies, waits for them, and re-layouts  14.3 us (4%)
  other arithmetic  9.32 us (2%)
    pallas_call x4, Pallas kernels, propagate(): pl.pallas_call(functools.partial(propagate_kernel, part, late, pieces), g...  142 us
    ppermute x9, waiting for transfers between devices, send(): lax.ppermute(after(piece, *wait), 'comp', route)  39.9 us
    pallas_call x2, Pallas kernels, finish(): pl.pallas_call(functools.partial(finish_kernel, CELL_CHUNKS), grid_spec=p...  32.4 us
    pallas_call x4, Pallas kernels, packed_shards(): pl.pallas_call(interact_kernel, grid=(width // lanes,), in_specs=[pl.Bloc...  32.3 us
    ppermute x8, waiting for transfers between devices, send_back(): return lax.ppermute(after(piece, *waits), 'comp', pairs)  31.4 us
    ppermute x9, starting transfers between devices, send(): lax.ppermute(after(piece, *wait), 'comp', route)  22.9 us
    ppermute x4, starting transfers between devices, packed_shards(): from_got[last].append(lax.ppermute(after(got_1[c], *waits), 'comp', across))  14.9 us
  transfers between devices with their start and end apart: 33, of which 11 were waited for; matrix products, arithmetic and copies ran while one was open for 4% of the time, Pallas kernels for 42%

profile of v4, /device:TPU:0, one launch (start us, length us, event | category | flops | bytes accessed | tf_op | source)
XLA Modules:
  0.0 380.2 jit_solution(2626706021682462890)
XLA Ops:
  2.5 7.0 %prepare.1 = (f32[260,8,256]{2,1,0:T(8,128)}, s32[2,128,128]{2,1,0:T(8,128)}, s32[2,128,128]{2,1,0:T(8,128)}, s32[8,256]{1,0:T(8,128)}, f32[144,128]{1,0:T(8,128)}, /*index=5*/f32[144,128]{1,0:T(8,128)}) custom-call(s32[3]{0:T(128)} %pad_add_fusion.7.base_ref, f32[32]{0:T(128)} %speed_ref.1, s32[256,256]{1,0:T(8,128)} %sea_ref.1, f32[256,256]{1,0:T(8,128)} %east_ref.1, ...), custom_call_target="tpu_custom_call" | custom-call | tf_op jit(solution)/shard_map/prepare/pallas_call | solution.py:584
  10.3 38.5 %propagate_early.2 = (f32[32,8192]{1,0:T(8,128)}, f32[32,8192]{1,0:T(8,128)}, f32[1,16384]{1,0:T(1,128)}, f32[72,16384]{1,0:T(8,128)}, f32[8,16384]{1,0:T(8,128)}, /*index=5*/f32[8,16384]{1,0:T(8,128)}) custom-call(s32[3]{0:T(128)} %pad_add_fusion.7.base_ref, s32[8,256]{1,0:T(8,128)} %get-tuple-element.95.table_ref, f32[144,128,256]{2,1,0:T(8,128)} %energy_ref.7, ...), custom_call_target="tpu_custom_call" | custom-call | flops 78643200 | bytes 62914560 | tf_op jit(solution)/shard_map/propagate_early/pallas_call | solution.py:640
  53.3 32.6 %propagate_late.2 = (f32[40,8192]{1,0:T(8,128)}, f32[40,8192]{1,0:T(8,128)}, f32[1,16384]{1,0:T(1,128)}, f32[72,16384]{1,0:T(8,128)}) custom-call(s32[3]{0:T(128)} %pad_add_fusion.7.base_ref, s32[8,256]{1,0:T(8,128)} %get-tuple-element.95.table_ref, f32[144,128,256]{2,1,0:T(8,128)} %energy_ref.7, ...), custom_call_target="tpu_custom_call", output_to_operand_aliasing={{3}: (10, {})} | custom-call | flops 62914560 | bytes 62914560 | tf_op jit(solution)/shard_map/propagate_late/pallas_call | solution.py:640
  85.9 3.8 %collective-permute-start.2 = (f32[40,8192]{1,0:T(8,128)}, f32[40,8192]{1,0:T(8,128)S(1)}, u32[]{:S(2)}, u32[]{:S(2)}) collective-permute-start(f32[40,8192]{1,0:T(8,128)} %get-tuple-element.93), channel_id=1, source_target_pairs={{0,2},{2,0},{4,6},{6,4},{8,10},{10,8},{12,14},{14,12},{1,3},{3,1},... | collective-permute-start | bytes 3932168 | tf_op jit(solution)/shard_map/ppermute | solution.py:672
  91.4 5.5 %collective-permute-start.3 = (f32[32,8192]{1,0:T(8,128)}, f32[32,8192]{1,0:T(8,128)}, u32[]{:S(2)}, u32[]{:S(2)}) collective-permute-start(f32[32,8192]{1,0:T(8,128)} %collective-permute-done.1.refs_10_), channel_id=1, source_target_pairs={{6,2},{0,4},{10,6},{4,8},{14,10},{8,12},{7,3},{1,5},{11,7},{5,9},{... | collective-permute-start | bytes 3145736 | tf_op jit(solution)/shard_map/ppermute | solution.py:672
  100.0 38.0 %propagate_early.3 = (f32[32,8192]{1,0:T(8,128)}, f32[32,8192]{1,0:T(8,128)}, f32[1,16384]{1,0:T(1,128)}, f32[72,16384]{1,0:T(8,128)}, f32[8,16384]{1,0:T(8,128)}) custom-call(s32[3]{0:T(128)} %pad_add_fusion.7.base_ref, s32[8,256]{1,0:T(8,128)} %get-tuple-element.95.table_ref, f32[144,128,256]{2,1,0:T(8,128)} %energy_ref.7, f32[144,2,256]{2,1,0:T(2,128)} %copy-done.4, ...), custom_call_target="tpu_custom_call" | custom-call | flops 78643200 | bytes 62914560 | tf_op jit(solution)/shard_map/propagate_early/pallas_call | solution.py:640
  139.4 32.8 %propagate_late.3 = (f32[40,2048]{1,0:T(8,128)}, f32[40,2048]{1,0:T(8,128)}, f32[40,2048]{1,0:T(8,128)}, f32[40,2048]{1,0:T(8,128)}, f32[40,2048]{1,0:T(8,128)},...) custom-call(s32[3]{0:T(128)} %pad_add_fusion.7.base_ref, ...), custom_call_target="tpu_custom_call", output_to_operand_aliasing={{9}: (10, {})} | custom-call | flops 62914560 | bytes 62914560 | tf_op jit(solution)/shard_map/propagate_late/pallas_call | solution.py:640
  184.2 22.2 %collective-permute-done.9.refs_3_ = f32[40,8192]{1,0:T(8,128)S(1)} collective-permute-done((f32[40,8192]{1,0:T(8,128)S(1)}, f32[40,8192]{1,0:T(8,128)S(1)}, u32[]{:S(2)}, u32[]{:S(2)}) %collective-permute-start.9) | collective-permute-done | bytes 1310752 | tf_op jit(solution)/shard_map/ppermute | solution.py:672
  206.4 4.4 %collective-permute-start.10 = (f32[32,8192]{1,0:T(8,128)}, f32[32,8192]{1,0:T(8,128)S(1)}, u32[]{:S(2)}, u32[]{:S(2)}) collective-permute-start(f32[32,8192]{1,0:T(8,128)} %collective-permute-done.8.refs_8_), channel_id=1, source_target_pairs={{6,2},{0,4},{10,6},{4,8},{14,10},{8,12},{7,3},{1,5},{11,7},{5,9},{... | collective-permute-start | bytes 3145736 | tf_op jit(solution)/shard_map/ppermute | solution.py:672
  213.9 17.7 %collective-permute-done.10.refs_0_ = f32[32,8192]{1,0:T(8,128)S(1)} collective-permute-done((f32[32,8192]{1,0:T(8,128)}, f32[32,8192]{1,0:T(8,128)S(1)}, u32[]{:S(2)}, u32[]{:S(2)}) %collective-permute-start.10) | collective-permute-done | bytes 1048608 | tf_op jit(solution)/shard_map/ppermute | solution.py:672
  231.6 5.0 %collective-permute-start.12 = (f32[40,2048]{1,0:T(8,128)}, f32[40,2048]{1,0:T(8,128)}, u32[]{:S(2)}, u32[]{:S(2)}) collective-permute-start(f32[40,2048]{1,0:T(8,128)} %collective-permute-done.11.refs_9_), channel_id=1, source_target_pairs={{6,2},{0,4},{10,6},{4,8},{14,10},{8,12},{7,3},{1,5},{11,7},{5,9},{... | collective-permute-start | bytes 983048 | tf_op jit(solution)/shard_map/ppermute | solution.py:752
  247.2 4.1 %collective-permute-start.7 = (f32[1,16384]{1,0:T(1,128)S(1)}, f32[1,16384]{1,0:T(1,128)S(1)}, u32[]{:S(2)}, u32[]{:S(2)}) collective-permute-start(f32[1,16384]{1,0:T(1,128)S(1)} %add.261), channel_id=1, source_target_pairs={{0,8},{2,10},{4,12},{6,14},{8,0},{10,2},{12,4},{14,6},{1,9},{3,11}... | collective-permute-start | bytes 196616 | tf_op jit(solution)/shard_map/ppermute | solution.py:712
  251.3 8.1 %interact_cells.4 = (f32[144,2048]{1,0:T(8,128)}, f32[72,2048]{1,0:T(8,128)}, f32[72,2048]{1,0:T(8,128)}) custom-call(bf16[6,288,216]{2,1,0:T(8,128)(2,1)} %stack.28.table_ref, bf16[288,864]{1,0:T(8,128)(2,1)} %concatenate.40.spread_ref, f32[432,1]{1,0:T(8,128)} %copy.49.coupling_ref, f32[32,8192]{1,0:T(8,128)} %copy-done.3, ...), custom_call_target="tpu_custom_call" | custom-call | flops 2548039680 | bytes 20971520 | tf_op jit(solution)/shard_map/interact_cells/pallas_call | solution.py:763
  269.0 8.1 %interact_cells.5 = (f32[144,2048]{1,0:T(8,128)}, f32[72,2048]{1,0:T(8,128)}, f32[72,2048]{1,0:T(8,128)}) custom-call(bf16[6,288,216]{2,1,0:T(8,128)(2,1)} %stack.28.table_ref, bf16[288,864]{1,0:T(8,128)(2,1)} %concatenate.40.spread_ref, f32[432,1]{1,0:T(8,128)} %copy.49.coupling_ref, f32[32,8192]{1,0:T(8,128)} %copy-done.3, f32[40,2048]{1,0:T(8,128)} %copy-done.17, ...), custom_call_target="tpu_custom_call" | custom-call | flops 2548039680 | bytes 20971520 | tf_op jit(solution)/shard_map/interact_cells/pallas_call | solution.py:763
  277.0 4.0 %collective-permute-done.30.refs_5_ = f32[72,2048]{1,0:T(8,128)S(1)} collective-permute-done((f32[72,2048]{1,0:T(8,128)}, f32[72,2048]{1,0:T(8,128)S(1)}, u32[]{:S(2)}, u32[]{:S(2)}) %collective-permute-start.30) | collective-permute-done | bytes 589856 | tf_op jit(solution)/shard_map/ppermute | solution.py:786
  282.6 8.1 %interact_cells.6 = (f32[144,2048]{1,0:T(8,128)}, f32[72,2048]{1,0:T(8,128)}, f32[72,2048]{1,0:T(8,128)}) custom-call(bf16[6,288,216]{2,1,0:T(8,128)(2,1)} %stack.28.table_ref, bf16[288,864]{1,0:T(8,128)(2,1)} %concatenate.40.spread_ref, f32[432,1]{1,0:T(8,128)} %copy.49.coupling_ref, f32[32,8192]{1,0:T(8,128)} %copy-done.3, f32[40,2048]{1,0:T(8,128)} %copy-done.16, ...), custom_call_target="tpu_custom_call" | custom-call | flops 2548039680 | bytes 20971520 | tf_op jit(solution)/shard_map/interact_cells/pallas_call | solution.py:763
  295.0 4.8 %collective-permute-start.23 = (f32[40,2048]{1,0:T(8,128)}, f32[40,2048]{1,0:T(8,128)S(1)}, u32[]{:S(2)}, u32[]{:S(2)}) collective-permute-start(f32[40,2048]{1,0:T(8,128)} %collective-permute-done.22.refs_9_), channel_id=1, source_target_pairs={{6,2},{0,4},{10,6},{4,8},{14,10},{8,12},{7,3},{1,5},{11,7},{5,9},{... | collective-permute-start | bytes 983048 | tf_op jit(solution)/shard_map/ppermute | solution.py:752
  305.4 8.1 %interact_cells.7 = (f32[144,2048]{1,0:T(8,128)}, f32[72,2048]{1,0:T(8,128)}, f32[72,2048]{1,0:T(8,128)}) custom-call(bf16[6,288,216]{2,1,0:T(8,128)(2,1)} %stack.28.table_ref, bf16[288,864]{1,0:T(8,128)(2,1)} %concatenate.40.spread_ref, f32[432,1]{1,0:T(8,128)} %copy.49.coupling_ref, f32[32,8192]{1,0:T(8,128)} %copy-done.3, f32[40,2048]{1,0:T(8,128)} %copy-done.19, ...), custom_call_target="tpu_custom_call" | custom-call | flops 2548039680 | bytes 20971520 | tf_op jit(solution)/shard_map/interact_cells/pallas_call | solution.py:763
  313.5 3.2 collective-permute-start.32
  324.1 7.5 %collective-permute-done.32.refs_8_ = f32[72,2048]{1,0:T(8,128)S(1)} collective-permute-done((f32[72,2048]{1,0:T(8,128)}, f32[72,2048]{1,0:T(8,128)S(1)}, u32[]{:S(2)}, u32[]{:S(2)}) %collective-permute-start.32) | collective-permute-done | bytes 589856 | tf_op jit(solution)/shard_map/ppermute | solution.py:786
  332.4 16.2 %finish_chunk.2.refs_9_ = f32[144,128,256]{2,1,0:T(8,128)} custom-call(s32[3]{0:T(128)} %pad_add_fusion.7.base_ref, s32[8,256]{1,0:T(8,128)} %get-tuple-element.95.table_ref, s32[2,128,128]{2,1,0:T(8,128)} %get-tuple-element.79.place_ref, f32[1,16384]{1,0:T(1,128)} %broadcast_multiply_fusion, f32[8,16384]{1,0:T(8,128)} %get-tuple-element.86.refs_0_.fields_ref, ...), custom_call_target="tpu_custom_call" | custom-call | flops 47185920 | bytes 104857600 | tf_op jit(solution)/shard_map/finish_chunk/pallas_call | solution.py:811
  348.7 8.2 %collective-permute-done.28.refs_7_ = f32[72,2048]{1,0:T(8,128)S(1)} collective-permute-done((f32[72,2048]{1,0:T(8,128)}, f32[72,2048]{1,0:T(8,128)S(1)}, u32[]{:S(2)}, u32[]{:S(2)}) %collective-permute-start.28) | collective-permute-done | bytes 589856 | tf_op jit(solution)/shard_map/ppermute | solution.py:786
  356.8 6.3 %collective-permute-done.29.refs_8_ = f32[72,2048]{1,0:T(8,128)S(1)} collective-permute-done((f32[72,2048]{1,0:T(8,128)}, f32[72,2048]{1,0:T(8,128)S(1)}, u32[]{:S(2)}, u32[]{:S(2)}) %collective-permute-start.29) | collective-permute-done | bytes 589856 | tf_op jit(solution)/shard_map/ppermute | solution.py:786
  364.0 16.2 %finish_chunk.3 = f32[144,128,256]{2,1,0:T(8,128)} custom-call(s32[3]{0:T(128)} %pad_add_fusion.7.base_ref, s32[8,256]{1,0:T(8,128)} %get-tuple-element.95.table_ref, s32[2,128,128]{2,1,0:T(8,128)} %get-tuple-element.79.place_ref, f32[1,16384]{1,0:T(1,128)} %broadcast_multiply_fusion, ...), custom_call_target="tpu_custom_call", output_to_operand_aliasing={{}: (16, {})} | custom-call | flops 47185920 | bytes 104857600 | tf_op jit(solution)/shard_map/finish_chunk/pallas_call | solution.py:811
  (145 shorter events, 69.0 us)
Async XLA Ops:
  48.9 42.5 %collective-permute-start.1 = (f32[32,8192]{1,0:T(8,128)}, f32[32,8192]{1,0:T(8,128)}, u32[]{:S(2)}, u32[]{:S(2)}) collective-permute-start(f32[32,8192]{1,0:T(8,128)} %get-tuple-element.90), channel_id=1, source_target_pairs={{0,2},{2,0},{4,6},{6,4},{8,10},{10,8},{12,14},{14,12},{1,3},{3,1},... | collective-permute-start | bytes 3145736 | tf_op jit(solution)/shard_map/ppermute | solution.py:672
  52.0 186.8 %collective-permute-start.13 = (f32[32,8192]{1,0:T(8,128)}, f32[32,8192]{1,0:T(8,128)}, u32[]{:S(2)}, u32[]{:S(2)}) collective-permute-start(f32[32,8192]{1,0:T(8,128)} %get-tuple-element.111.refs_4_), channel_id=1, source_target_pairs={{2,6},{4,0},{6,10},{8,4},{10,14},{12,8},{3,7},{5,1},{7,11},{9,5},{... | collective-permute-start | bytes 3145736 | tf_op jit(solution)/shard_map/ppermute | solution.py:672
  85.9 52.2 %collective-permute-start.2 = (f32[40,8192]{1,0:T(8,128)}, f32[40,8192]{1,0:T(8,128)S(1)}, u32[]{:S(2)}, u32[]{:S(2)}) collective-permute-start(f32[40,8192]{1,0:T(8,128)} %get-tuple-element.93), channel_id=1, source_target_pairs={{0,2},{2,0},{4,6},{6,4},{8,10},{10,8},{12,14},{14,12},{1,3},{3,1},... | collective-permute-start | bytes 3932168 | tf_op jit(solution)/shard_map/ppermute | solution.py:672
  89.7 49.7 %collective-permute-start.4 = (f32[40,8192]{1,0:T(8,128)}, f32[40,8192]{1,0:T(8,128)S(1)}, u32[]{:S(2)}, u32[]{:S(2)}) collective-permute-start(f32[40,8192]{1,0:T(8,128)} %get-tuple-element.94.refs_5_), channel_id=1, source_target_pairs={{2,6},{4,0},{6,10},{8,4},{10,14},{12,8},{3,7},{5,1},{7,11},{9,5},{... | collective-permute-start | bytes 3932168 | tf_op jit(solution)/shard_map/ppermute | solution.py:672
  91.4 48.0 %collective-permute-start.3 = (f32[32,8192]{1,0:T(8,128)}, f32[32,8192]{1,0:T(8,128)}, u32[]{:S(2)}, u32[]{:S(2)}) collective-permute-start(f32[32,8192]{1,0:T(8,128)} %collective-permute-done.1.refs_10_), channel_id=1, source_target_pairs={{6,2},{0,4},{10,6},{4,8},{14,10},{8,12},{7,3},{1,5},{11,7},{5,9},{... | collective-permute-start | bytes 3145736 | tf_op jit(solution)/shard_map/ppermute | solution.py:672
  138.0 42.0 %collective-permute-start.8 = (f32[32,8192]{1,0:T(8,128)}, f32[32,8192]{1,0:T(8,128)}, u32[]{:S(2)}, u32[]{:S(2)}) collective-permute-start(f32[32,8192]{1,0:T(8,128)} %get-tuple-element.106), channel_id=1, source_target_pairs={{0,2},{2,0},{4,6},{6,4},{8,10},{10,8},{12,14},{14,12},{1,3},{3,1},... | collective-permute-start | bytes 3145736 | tf_op jit(solution)/shard_map/ppermute | solution.py:672
  138.1 42.0 %collective-permute-start.14 = (f32[32,8192]{1,0:T(8,128)}, f32[32,8192]{1,0:T(8,128)}, u32[]{:S(2)}, u32[]{:S(2)}) collective-permute-start(f32[32,8192]{1,0:T(8,128)} %get-tuple-element.112.refs_6_), channel_id=1, source_target_pairs={{2,6},{4,0},{6,10},{8,4},{10,14},{12,8},{3,7},{5,1},{7,11},{9,5},{... | collective-permute-start | bytes 3145736 | tf_op jit(solution)/shard_map/ppermute | solution.py:672
  177.4 29.0 %collective-permute-start.9 = (f32[40,8192]{1,0:T(8,128)S(1)}, f32[40,8192]{1,0:T(8,128)S(1)}, u32[]{:S(2)}, u32[]{:S(2)}) collective-permute-start(f32[40,8192]{1,0:T(8,128)S(1)} %collective-permute-done.2.refs_11_), channel_id=1, source_target_pairs={{6,2},{0,4},{10,6},{4,8},{14,10},{8,12},{7,3},{1,5},{11,7},{5,9},{... | collective-permute-start | bytes 3932168 | tf_op jit(solution)/shard_map/ppermute | solution.py:672
  180.0 31.7 %collective-permute-start.11 = (f32[40,2048]{1,0:T(8,128)}, f32[40,2048]{1,0:T(8,128)}, u32[]{:S(2)}, u32[]{:S(2)}) collective-permute-start(f32[40,2048]{1,0:T(8,128)} %get-tuple-element.109), channel_id=1, source_target_pairs={{0,2},{2,0},{4,6},{6,4},{8,10},{10,8},{12,14},{14,12},{1,3},{3,1},... | collective-permute-start | bytes 983048 | tf_op jit(solution)/shard_map/ppermute | solution.py:707
  180.1 57.3 %collective-permute-start.16 = (f32[40,2048]{1,0:T(8,128)}, f32[40,2048]{1,0:T(8,128)}, u32[]{:S(2)}, u32[]{:S(2)}) collective-permute-start(f32[40,2048]{1,0:T(8,128)} %get-tuple-element.117), channel_id=1, source_target_pairs={{0,2},{2,0},{4,6},{6,4},{8,10},{10,8},{12,14},{14,12},{1,3},{3,1},... | collective-permute-start | bytes 983048 | tf_op jit(solution)/shard_map/ppermute | solution.py:707
  182.1 63.7 %collective-permute-start.15 = (f32[40,2048]{1,0:T(8,128)}, f32[40,2048]{1,0:T(8,128)}, u32[]{:S(2)}, u32[]{:S(2)}) collective-permute-start(f32[40,2048]{1,0:T(8,128)} %get-tuple-element.114.refs_7_), channel_id=1, source_target_pairs={{2,6},{4,0},{6,10},{8,4},{10,14},{12,8},{3,7},{5,1},{7,11},{9,5},{... | collective-permute-start | bytes 983048 | tf_op jit(solution)/shard_map/ppermute | solution.py:708
  206.4 25.3 %collective-permute-start.10 = (f32[32,8192]{1,0:T(8,128)}, f32[32,8192]{1,0:T(8,128)S(1)}, u32[]{:S(2)}, u32[]{:S(2)}) collective-permute-start(f32[32,8192]{1,0:T(8,128)} %collective-permute-done.8.refs_8_), channel_id=1, source_target_pairs={{6,2},{0,4},{10,6},{4,8},{14,10},{8,12},{7,3},{1,5},{11,7},{5,9},{... | collective-permute-start | bytes 3145736 | tf_op jit(solution)/shard_map/ppermute | solution.py:672
  211.7 29.7 %collective-permute-start.6 = (f32[1,16384]{1,0:T(1,128)S(1)}, f32[1,16384]{1,0:T(1,128)S(1)}, u32[]{:S(2)}, u32[]{:S(2)}) collective-permute-start(f32[1,16384]{1,0:T(1,128)S(1)} %fusion), channel_id=1, source_target_pairs={{0,4},{2,6},{4,0},{6,2},{8,12},{10,14},{12,8},{14,10},{1,5},{3,7},... | collective-permute-start | bytes 196616 | tf_op jit(solution)/shard_map/ppermute | solution.py:711
  237.5 27.2 %collective-permute-start.18 = (f32[40,2048]{1,0:T(8,128)}, f32[40,2048]{1,0:T(8,128)}, u32[]{:S(2)}, u32[]{:S(2)}) collective-permute-start(f32[40,2048]{1,0:T(8,128)} %get-tuple-element.120.refs_7_), channel_id=1, source_target_pairs={{2,6},{4,0},{6,10},{8,4},{10,14},{12,8},{3,7},{5,1},{7,11},{9,5},{... | collective-permute-start | bytes 983048 | tf_op jit(solution)/shard_map/ppermute | solution.py:708
  238.8 20.6 %collective-permute-start.19 = (f32[40,2048]{1,0:T(8,128)}, f32[40,2048]{1,0:T(8,128)}, u32[]{:S(2)}, u32[]{:S(2)}) collective-permute-start(f32[40,2048]{1,0:T(8,128)} %get-tuple-element.123), channel_id=1, source_target_pairs={{0,2},{2,0},{4,6},{6,4},{8,10},{10,8},{12,14},{14,12},{1,3},{3,1},... | collective-permute-start | bytes 983048 | tf_op jit(solution)/shard_map/ppermute | solution.py:707
  241.5 20.9 %collective-permute-start.22 = (f32[40,2048]{1,0:T(8,128)}, f32[40,2048]{1,0:T(8,128)}, u32[]{:S(2)}, u32[]{:S(2)}) collective-permute-start(f32[40,2048]{1,0:T(8,128)} %get-tuple-element.129), channel_id=1, source_target_pairs={{0,2},{2,0},{4,6},{6,4},{8,10},{10,8},{12,14},{14,12},{1,3},{3,1},... | collective-permute-start | bytes 983048 | tf_op jit(solution)/shard_map/ppermute | solution.py:707
  245.9 35.2 %collective-permute-start.21 = (f32[40,2048]{1,0:T(8,128)S(1)}, f32[40,2048]{1,0:T(8,128)S(1)}, u32[]{:S(2)}, u32[]{:S(2)}) collective-permute-start(f32[40,2048]{1,0:T(8,128)S(1)} %copy-done.14), channel_id=1, source_target_pairs={{2,6},{4,0},{6,10},{8,4},{10,14},{12,8},{3,7},{5,1},{7,11},{9,5},{... | collective-permute-start | bytes 983048 | tf_op jit(solution)/shard_map/ppermute | solution.py:708
  262.4 18.7 %collective-permute-start.20 = (f32[40,2048]{1,0:T(8,128)}, f32[40,2048]{1,0:T(8,128)S(1)}, u32[]{:S(2)}, u32[]{:S(2)}) collective-permute-start(f32[40,2048]{1,0:T(8,128)} %collective-permute-done.19.refs_9_), channel_id=1, source_target_pairs={{6,2},{0,4},{10,6},{4,8},{14,10},{8,12},{7,3},{1,5},{11,7},{5,9},{... | collective-permute-start | bytes 983048 | tf_op jit(solution)/shard_map/ppermute | solution.py:752
  264.6 29.1 %collective-permute-start.25 = (f32[72,2048]{1,0:T(8,128)}, f32[72,2048]{1,0:T(8,128)S(1)}, u32[]{:S(2)}, u32[]{:S(2)}) collective-permute-start(f32[72,2048]{1,0:T(8,128)} %get-tuple-element.135), channel_id=1, source_target_pairs={{0,2},{2,0},{4,6},{6,4},{8,10},{10,8},{12,14},{14,12},{1,3},{3,1},... | collective-permute-start | bytes 1769480 | tf_op jit(solution)/shard_map/ppermute | solution.py:786
  281.1 32.5 %collective-permute-start.31 = (f32[72,2048]{1,0:T(8,128)}, f32[72,2048]{1,0:T(8,128)S(1)}, u32[]{:S(2)}, u32[]{:S(2)}) collective-permute-start(f32[72,2048]{1,0:T(8,128)} %get-tuple-element.148), channel_id=1, source_target_pairs={{0,2},{2,0},{4,6},{6,4},{8,10},{10,8},{12,14},{14,12},{1,3},{3,1},... | collective-permute-start | bytes 1769480 | tf_op jit(solution)/shard_map/ppermute | solution.py:786
  293.7 25.3 %collective-permute-start.26 = (f32[72,2048]{1,0:T(8,128)}, f32[72,2048]{1,0:T(8,128)S(1)}, u32[]{:S(2)}, u32[]{:S(2)}) collective-permute-start(f32[72,2048]{1,0:T(8,128)} %get-tuple-element.138), channel_id=1, source_target_pairs={{0,2},{2,0},{4,6},{6,4},{8,10},{10,8},{12,14},{14,12},{1,3},{3,1},... | collective-permute-start | bytes 1769480 | tf_op jit(solution)/shard_map/ppermute | solution.py:786
  319.0 29.7 %collective-permute-start.27 = (f32[72,2048]{1,0:T(8,128)}, f32[72,2048]{1,0:T(8,128)S(1)}, u32[]{:S(2)}, u32[]{:S(2)}) collective-permute-start(f32[72,2048]{1,0:T(8,128)} %get-tuple-element.139), channel_id=1, source_target_pairs={{0,2},{2,0},{4,6},{6,4},{8,10},{10,8},{12,14},{14,12},{1,3},{3,1},... | collective-permute-start | bytes 1769480 | tf_op jit(solution)/shard_map/ppermute | solution.py:786
  319.0 37.8 %collective-permute-start.28 = (f32[72,2048]{1,0:T(8,128)}, f32[72,2048]{1,0:T(8,128)S(1)}, u32[]{:S(2)}, u32[]{:S(2)}) collective-permute-start(f32[72,2048]{1,0:T(8,128)} %get-tuple-element.141), channel_id=1, source_target_pairs={{0,2},{2,0},{4,6},{6,4},{8,10},{10,8},{12,14},{14,12},{1,3},{3,1},... | collective-permute-start | bytes 1769480 | tf_op jit(solution)/shard_map/ppermute | solution.py:786
  321.0 42.1 %collective-permute-start.29 = (f32[72,2048]{1,0:T(8,128)}, f32[72,2048]{1,0:T(8,128)S(1)}, u32[]{:S(2)}, u32[]{:S(2)}) collective-permute-start(f32[72,2048]{1,0:T(8,128)} %get-tuple-element.143), channel_id=1, source_target_pairs={{0,2},{2,0},{4,6},{6,4},{8,10},{10,8},{12,14},{14,12},{1,3},{3,1},... | collective-permute-start | bytes 1769480 | tf_op jit(solution)/shard_map/ppermute | solution.py:786
  (34 other events, 664.7 us)

commit v5 on v4

--- a/solution.py
+++ b/solution.py
@@ -189,10 +189,6 @@
 KEEP, SPILL, IS_SEA = BLOCK, 2 * BLOCK, 2 * BLOCK
 
 
-def row_of(ref, row):
-    return ref[row : row + 1, :]
-
-
 def upwind(courant, total, slope, bend_here, bend_ahead):
     bend = jnp.where(courant > 0.0, bend_here, bend_ahead)
     return courant * ((total - bend) - courant * (slope - courant * bend))
@@ -325,7 +321,7 @@
     sum_ref, full_ref = refs.pop(0), refs.pop(0)
     seam_out_ref = None if late else refs.pop(0)
     fields_out_ref = refs.pop(0) if with_fields else None
-    rows_ref, wide_ref, result_ref, row_sems, out_sems = refs
+    rows_ref, spread_ref, wide_ref, result_ref, row_sems, out_sems = refs
     row_count, comp_count, col_count = rows_ref.shape
     strips = comp_count // 8
     sent_rows = piece_refs[0].shape[0]
@@ -346,13 +342,18 @@
     def halves(row):
         return row[:, :BLOCK], row[:, BLOCK:]
 
+    @pl.loop(0, row_count + 2 * EDGE)
+    def _(r):
+        coef = coef_ref[first_row + r]
+        for k in range(HALF_SEA + 1):
+            spread_ref[r, k] = jnp.broadcast_to(coef[k : k + 1, :], coef.shape)
+
     def masked(row, at):
-        sea_row = halves(coef_ref.at[first_row + at][SEA : SEA + 1, :])
-        return tuple(part * sea for part, sea in zip(halves(row), sea_row))
+        return tuple(part * sea for part, sea in zip(halves(row), halves(spread_ref[at, SEA])))
 
     def cell_row(at, new, state, east, north):
         here, ahead, slope_ahead, bend_here, flux_low = state
-        coef = [halves(row_of(coef_ref.at[first_row + at], k)) for k in range(HALF_SEA + 1)]
+        coef = [None] + [halves(spread_ref[at, k]) for k in range(1, HALF_SEA + 1)]
         to_right = [pltpu.roll(part, BLOCK - 1, 1) for part in here]
         right = (jnp.where(last_lane, to_right[1], to_right[0]), jnp.where(last_lane, 0.0, to_right[1]))
         slope = [right[h] - here[h] for h in range(2)]
@@ -439,7 +440,9 @@
     comp_row = lax.broadcasted_iota(jnp.int32, (height, tile_width), 0)
     start = height - NTH if late else 0
     end = start + NTH - 1
-    in_circle = (comp_row >= start) & (comp_row <= end)
+    mixed = slice(0, 8) if late else slice(height - 8, height)
+    mixed_row = comp_row[mixed]
+    in_circle = (mixed_row >= start) & (mixed_row <= end)
 
     @pl.loop(0, cells // tile_width)
     def _(i):
@@ -453,11 +456,28 @@
             rate = fields_ref[TURN : TURN + 1, source]
         forward = jnp.maximum(rate, 0.0)
         backward = jnp.minimum(rate, 0.0)
-        above = jnp.where(comp_row == end, level[start : start + 1, :], pltpu.roll(level, height - 1, 0))
-        below = jnp.where(comp_row == start, level[end : end + 1, :], pltpu.roll(level, 1, 0))
-        turned = (1.0 - forward + backward) * level - backward * above + forward * below
-        result_ref[:, source] = jnp.where(in_circle, turned, level)
-        sum_ref[:, source] = jnp.sum(jnp.where(in_circle, turned, 0.0), axis=0, keepdims=True)
+        stay = (1.0 - forward) + backward
+        above = pltpu.roll(level, height - 1, 0)
+        below = pltpu.roll(level, 1, 0)
+
+        def with_row(rolled, row, value):
+            tile = slice(row - row % 8, row - row % 8 + 8)
+            fixed = jnp.where(comp_row[tile] == row, value, rolled[tile])
+            parts = [rolled[: tile.start], fixed, rolled[tile.stop :]]
+            return jnp.concatenate([part for part in parts if part.shape[0]], axis=0)
+
+        above = with_row(above, end, level[start : start + 1, :])
+        below = with_row(below, start, level[end : end + 1, :])
+        turned = stay * level - backward * above + forward * below
+        partial = jnp.where(in_circle, turned[mixed], 0.0)
+        for first in range(0, height, 8):
+            rows = slice(first, first + 8)
+            if first == mixed.start:
+                result_ref[rows, source] = jnp.where(in_circle, turned[rows], level[rows])
+            else:
+                result_ref[rows, source] = turned[rows]
+                partial += turned[rows]
+        sum_ref[:, source] = jnp.sum(partial, axis=0, keepdims=True)
 
     if not late:
         seam_out_ref[...] = result_ref[sent_rows:, :]
@@ -646,6 +666,7 @@
                 out_specs=out_specs,
                 scratch_shapes=[
                     pltpu.VMEM((row_count, comp_rows, col_count), f32),
+                    pltpu.VMEM((row_count + 2 * EDGE, HALF_SEA + 1, 8, col_count), f32),
                     pltpu.VMEM((comp_rows + (8 if with_fields else 0), cells + BLOCK), f32),
                     pltpu.VMEM((height, cells), f32),
                     pltpu.SemaphoreType.DMA((row_count // 8,)),

time: 382 us -> 386 us (1.010)
  Pallas kernels: 214 us -> 218 us
    pallas_call x4, Pallas kernels: 142 us -> 146 us  [propagate(): pl.pallas_call(functools.partial(propagate_kernel, part, late, pieces), g...]
where the time goes in v5:
time: 386 us; the launch traced here: 384 us
  Pallas kernels  218 us (56%)
  waiting for transfers between devices  77.1 us (20%)
  starting transfers between devices  65.2 us (17%)
  local copies, waits for them, and re-layouts  14.3 us (4%)
  other arithmetic  9.32 us (2%)
    pallas_call x4, Pallas kernels, propagate(): pl.pallas_call(functools.partial(propagate_kernel, part, late, pieces), g...  146 us
    ppermute x9, waiting for transfers between devices, send(): lax.ppermute(after(piece, *wait), 'comp', route)  39.9 us
    pallas_call x2, Pallas kernels, finish(): pl.pallas_call(functools.partial(finish_kernel, CELL_CHUNKS), grid_spec=p...  32.4 us
    pallas_call x4, Pallas kernels, packed_shards(): pl.pallas_call(interact_kernel, grid=(width // lanes,), in_specs=[pl.Bloc...  32.3 us
    ppermute x8, waiting for transfers between devices, send_back(): return lax.ppermute(after(piece, *waits), 'comp', pairs)  31.4 us
    ppermute x9, starting transfers between devices, send(): lax.ppermute(after(piece, *wait), 'comp', route)  22.9 us
    ppermute x4, starting transfers between devices, packed_shards(): from_got[last].append(lax.ppermute(after(got_1[c], *waits), 'comp', across))  14.9 us
  transfers between devices with their start and end apart: 33, of which 11 were waited for; matrix products, arithmetic and copies ran while one was open for 4% of the time, Pallas kernels for 42%

profile of v5, /device:TPU:0, one launch (start us, length us, event | category | flops | bytes accessed | tf_op | source)
XLA Modules:
  0.0 384.1 jit_solution(2303363795780722086)
XLA Ops:
  2.5 7.0 %prepare.1 = (f32[260,8,256]{2,1,0:T(8,128)}, s32[2,128,128]{2,1,0:T(8,128)}, s32[2,128,128]{2,1,0:T(8,128)}, s32[8,256]{1,0:T(8,128)}, f32[144,128]{1,0:T(8,128)}, /*index=5*/f32[144,128]{1,0:T(8,128)}) custom-call(s32[3]{0:T(128)} %pad_add_fusion.7.base_ref, f32[32]{0:T(128)} %speed_ref.1, s32[256,256]{1,0:T(8,128)} %sea_ref.1, f32[256,256]{1,0:T(8,128)} %east_ref.1, ...), custom_call_target="tpu_custom_call" | custom-call | tf_op jit(solution)/shard_map/prepare/pallas_call | solution.py:604
  10.3 39.5 %propagate_early.2 = (f32[32,8192]{1,0:T(8,128)}, f32[32,8192]{1,0:T(8,128)}, f32[1,16384]{1,0:T(1,128)}, f32[72,16384]{1,0:T(8,128)}, f32[8,16384]{1,0:T(8,128)}, /*index=5*/f32[8,16384]{1,0:T(8,128)}) custom-call(s32[3]{0:T(128)} %pad_add_fusion.7.base_ref, s32[8,256]{1,0:T(8,128)} %get-tuple-element.95.table_ref, f32[144,128,256]{2,1,0:T(8,128)} %energy_ref.7, ...), custom_call_target="tpu_custom_call" | custom-call | flops 78643200 | bytes 62914560 | tf_op jit(solution)/shard_map/propagate_early/pallas_call | solution.py:660
  54.2 33.6 %propagate_late.2 = (f32[40,8192]{1,0:T(8,128)}, f32[40,8192]{1,0:T(8,128)}, f32[1,16384]{1,0:T(1,128)}, f32[72,16384]{1,0:T(8,128)}) custom-call(s32[3]{0:T(128)} %pad_add_fusion.7.base_ref, s32[8,256]{1,0:T(8,128)} %get-tuple-element.95.table_ref, f32[144,128,256]{2,1,0:T(8,128)} %energy_ref.7, ...), custom_call_target="tpu_custom_call", output_to_operand_aliasing={{3}: (10, {})} | custom-call | flops 62914560 | bytes 62914560 | tf_op jit(solution)/shard_map/propagate_late/pallas_call | solution.py:660
  87.8 3.8 collective-permute-start.2
  93.3 5.5 %collective-permute-start.3 = (f32[32,8192]{1,0:T(8,128)}, f32[32,8192]{1,0:T(8,128)}, u32[]{:S(2)}, u32[]{:S(2)}) collective-permute-start(f32[32,8192]{1,0:T(8,128)} %collective-permute-done.1.refs_10_), channel_id=1, source_target_pairs={{6,2},{0,4},{10,6},{4,8},{14,10},{8,12},{7,3},{1,5},{11,7},{5,9},{... | collective-permute-start | bytes 3145736 | tf_op jit(solution)/shard_map/ppermute | solution.py:693
  101.9 39.0 %propagate_early.3 = (f32[32,8192]{1,0:T(8,128)}, f32[32,8192]{1,0:T(8,128)}, f32[1,16384]{1,0:T(1,128)}, f32[72,16384]{1,0:T(8,128)}, f32[8,16384]{1,0:T(8,128)}) custom-call(s32[3]{0:T(128)} %pad_add_fusion.7.base_ref, s32[8,256]{1,0:T(8,128)} %get-tuple-element.95.table_ref, f32[144,128,256]{2,1,0:T(8,128)} %energy_ref.7, f32[144,2,256]{2,1,0:T(2,128)} %copy-done.4, ...), custom_call_target="tpu_custom_call" | custom-call | flops 78643200 | bytes 62914560 | tf_op jit(solution)/shard_map/propagate_early/pallas_call | solution.py:660
  142.4 33.8 %propagate_late.3 = (f32[40,2048]{1,0:T(8,128)}, f32[40,2048]{1,0:T(8,128)}, f32[40,2048]{1,0:T(8,128)}, f32[40,2048]{1,0:T(8,128)}, f32[40,2048]{1,0:T(8,128)},...) custom-call(s32[3]{0:T(128)} %pad_add_fusion.7.base_ref, ...), custom_call_target="tpu_custom_call", output_to_operand_aliasing={{9}: (10, {})} | custom-call | flops 62914560 | bytes 62914560 | tf_op jit(solution)/shard_map/propagate_late/pallas_call | solution.py:660
  188.1 22.2 %collective-permute-done.9.refs_3_ = f32[40,8192]{1,0:T(8,128)S(1)} collective-permute-done((f32[40,8192]{1,0:T(8,128)S(1)}, f32[40,8192]{1,0:T(8,128)S(1)}, u32[]{:S(2)}, u32[]{:S(2)}) %collective-permute-start.9) | collective-permute-done | bytes 1310752 | tf_op jit(solution)/shard_map/ppermute | solution.py:693
  210.3 4.4 %collective-permute-start.10 = (f32[32,8192]{1,0:T(8,128)}, f32[32,8192]{1,0:T(8,128)S(1)}, u32[]{:S(2)}, u32[]{:S(2)}) collective-permute-start(f32[32,8192]{1,0:T(8,128)} %collective-permute-done.8.refs_8_), channel_id=1, source_target_pairs={{6,2},{0,4},{10,6},{4,8},{14,10},{8,12},{7,3},{1,5},{11,7},{5,9},{... | collective-permute-start | bytes 3145736 | tf_op jit(solution)/shard_map/ppermute | solution.py:693
  217.8 17.7 %collective-permute-done.10.refs_0_ = f32[32,8192]{1,0:T(8,128)S(1)} collective-permute-done((f32[32,8192]{1,0:T(8,128)}, f32[32,8192]{1,0:T(8,128)S(1)}, u32[]{:S(2)}, u32[]{:S(2)}) %collective-permute-start.10) | collective-permute-done | bytes 1048608 | tf_op jit(solution)/shard_map/ppermute | solution.py:693
  235.5 5.0 %collective-permute-start.12 = (f32[40,2048]{1,0:T(8,128)}, f32[40,2048]{1,0:T(8,128)}, u32[]{:S(2)}, u32[]{:S(2)}) collective-permute-start(f32[40,2048]{1,0:T(8,128)} %collective-permute-done.11.refs_9_), channel_id=1, source_target_pairs={{6,2},{0,4},{10,6},{4,8},{14,10},{8,12},{7,3},{1,5},{11,7},{5,9},{... | collective-permute-start | bytes 983048 | tf_op jit(solution)/shard_map/ppermute | solution.py:773
  251.1 4.1 %collective-permute-start.7 = (f32[1,16384]{1,0:T(1,128)S(1)}, f32[1,16384]{1,0:T(1,128)S(1)}, u32[]{:S(2)}, u32[]{:S(2)}) collective-permute-start(f32[1,16384]{1,0:T(1,128)S(1)} %add.261), channel_id=1, source_target_pairs={{0,8},{2,10},{4,12},{6,14},{8,0},{10,2},{12,4},{14,6},{1,9},{3,11}... | collective-permute-start | bytes 196616 | tf_op jit(solution)/shard_map/ppermute | solution.py:733
  255.2 8.1 %interact_cells.4 = (f32[144,2048]{1,0:T(8,128)}, f32[72,2048]{1,0:T(8,128)}, f32[72,2048]{1,0:T(8,128)}) custom-call(bf16[6,288,216]{2,1,0:T(8,128)(2,1)} %stack.28.table_ref, bf16[288,864]{1,0:T(8,128)(2,1)} %concatenate.40.spread_ref, f32[432,1]{1,0:T(8,128)} %copy.49.coupling_ref, f32[32,8192]{1,0:T(8,128)} %copy-done.3, ...), custom_call_target="tpu_custom_call" | custom-call | flops 2548039680 | bytes 20971520 | tf_op jit(solution)/shard_map/interact_cells/pallas_call | solution.py:784
  272.9 8.1 %interact_cells.5 = (f32[144,2048]{1,0:T(8,128)}, f32[72,2048]{1,0:T(8,128)}, f32[72,2048]{1,0:T(8,128)}) custom-call(bf16[6,288,216]{2,1,0:T(8,128)(2,1)} %stack.28.table_ref, bf16[288,864]{1,0:T(8,128)(2,1)} %concatenate.40.spread_ref, f32[432,1]{1,0:T(8,128)} %copy.49.coupling_ref, f32[32,8192]{1,0:T(8,128)} %copy-done.3, f32[40,2048]{1,0:T(8,128)} %copy-done.17, ...), custom_call_target="tpu_custom_call" | custom-call | flops 2548039680 | bytes 20971520 | tf_op jit(solution)/shard_map/interact_cells/pallas_call | solution.py:784
  281.0 4.0 %collective-permute-done.30.refs_5_ = f32[72,2048]{1,0:T(8,128)S(1)} collective-permute-done((f32[72,2048]{1,0:T(8,128)}, f32[72,2048]{1,0:T(8,128)S(1)}, u32[]{:S(2)}, u32[]{:S(2)}) %collective-permute-start.30) | collective-permute-done | bytes 589856 | tf_op jit(solution)/shard_map/ppermute | solution.py:807
  286.5 8.1 %interact_cells.6 = (f32[144,2048]{1,0:T(8,128)}, f32[72,2048]{1,0:T(8,128)}, f32[72,2048]{1,0:T(8,128)}) custom-call(bf16[6,288,216]{2,1,0:T(8,128)(2,1)} %stack.28.table_ref, bf16[288,864]{1,0:T(8,128)(2,1)} %concatenate.40.spread_ref, f32[432,1]{1,0:T(8,128)} %copy.49.coupling_ref, f32[32,8192]{1,0:T(8,128)} %copy-done.3, f32[40,2048]{1,0:T(8,128)} %copy-done.16, ...), custom_call_target="tpu_custom_call" | custom-call | flops 2548039680 | bytes 20971520 | tf_op jit(solution)/shard_map/interact_cells/pallas_call | solution.py:784
  298.9 4.8 %collective-permute-start.23 = (f32[40,2048]{1,0:T(8,128)}, f32[40,2048]{1,0:T(8,128)S(1)}, u32[]{:S(2)}, u32[]{:S(2)}) collective-permute-start(f32[40,2048]{1,0:T(8,128)} %collective-permute-done.22.refs_9_), channel_id=1, source_target_pairs={{6,2},{0,4},{10,6},{4,8},{14,10},{8,12},{7,3},{1,5},{11,7},{5,9},{... | collective-permute-start | bytes 983048 | tf_op jit(solution)/shard_map/ppermute | solution.py:773
  309.3 8.1 %interact_cells.7 = (f32[144,2048]{1,0:T(8,128)}, f32[72,2048]{1,0:T(8,128)}, f32[72,2048]{1,0:T(8,128)}) custom-call(bf16[6,288,216]{2,1,0:T(8,128)(2,1)} %stack.28.table_ref, bf16[288,864]{1,0:T(8,128)(2,1)} %concatenate.40.spread_ref, f32[432,1]{1,0:T(8,128)} %copy.49.coupling_ref, f32[32,8192]{1,0:T(8,128)} %copy-done.3, f32[40,2048]{1,0:T(8,128)} %copy-done.19, ...), custom_call_target="tpu_custom_call" | custom-call | flops 2548039680 | bytes 20971520 | tf_op jit(solution)/shard_map/interact_cells/pallas_call | solution.py:784
  317.4 3.2 collective-permute-start.32
  328.0 7.5 %collective-permute-done.32.refs_8_ = f32[72,2048]{1,0:T(8,128)S(1)} collective-permute-done((f32[72,2048]{1,0:T(8,128)}, f32[72,2048]{1,0:T(8,128)S(1)}, u32[]{:S(2)}, u32[]{:S(2)}) %collective-permute-start.32) | collective-permute-done | bytes 589856 | tf_op jit(solution)/shard_map/ppermute | solution.py:807
  336.4 16.2 %finish_chunk.2.refs_9_ = f32[144,128,256]{2,1,0:T(8,128)} custom-call(s32[3]{0:T(128)} %pad_add_fusion.7.base_ref, s32[8,256]{1,0:T(8,128)} %get-tuple-element.95.table_ref, s32[2,128,128]{2,1,0:T(8,128)} %get-tuple-element.79.place_ref, f32[1,16384]{1,0:T(1,128)} %broadcast_multiply_fusion, f32[8,16384]{1,0:T(8,128)} %get-tuple-element.86.refs_0_.fields_ref, ...), custom_call_target="tpu_custom_call" | custom-call | flops 47185920 | bytes 104857600 | tf_op jit(solution)/shard_map/finish_chunk/pallas_call | solution.py:832
  352.6 8.2 %collective-permute-done.28.refs_7_ = f32[72,2048]{1,0:T(8,128)S(1)} collective-permute-done((f32[72,2048]{1,0:T(8,128)}, f32[72,2048]{1,0:T(8,128)S(1)}, u32[]{:S(2)}, u32[]{:S(2)}) %collective-permute-start.28) | collective-permute-done | bytes 589856 | tf_op jit(solution)/shard_map/ppermute | solution.py:807
  360.8 6.3 %collective-permute-done.29.refs_8_ = f32[72,2048]{1,0:T(8,128)S(1)} collective-permute-done((f32[72,2048]{1,0:T(8,128)}, f32[72,2048]{1,0:T(8,128)S(1)}, u32[]{:S(2)}, u32[]{:S(2)}) %collective-permute-start.29) | collective-permute-done | bytes 589856 | tf_op jit(solution)/shard_map/ppermute | solution.py:807
  367.9 16.2 %finish_chunk.3 = f32[144,128,256]{2,1,0:T(8,128)} custom-call(s32[3]{0:T(128)} %pad_add_fusion.7.base_ref, s32[8,256]{1,0:T(8,128)} %get-tuple-element.95.table_ref, s32[2,128,128]{2,1,0:T(8,128)} %get-tuple-element.79.place_ref, f32[1,16384]{1,0:T(1,128)} %broadcast_multiply_fusion, ...), custom_call_target="tpu_custom_call", output_to_operand_aliasing={{}: (16, {})} | custom-call | flops 47185920 | bytes 104857600 | tf_op jit(solution)/shard_map/finish_chunk/pallas_call | solution.py:832
  (145 shorter events, 69.0 us)
Async XLA Ops:
  49.9 43.5 %collective-permute-start.1 = (f32[32,8192]{1,0:T(8,128)}, f32[32,8192]{1,0:T(8,128)}, u32[]{:S(2)}, u32[]{:S(2)}) collective-permute-start(f32[32,8192]{1,0:T(8,128)} %get-tuple-element.90), channel_id=1, source_target_pairs={{0,2},{2,0},{4,6},{6,4},{8,10},{10,8},{12,14},{14,12},{1,3},{3,1},... | collective-permute-start | bytes 3145736 | tf_op jit(solution)/shard_map/ppermute | solution.py:693
  52.9 189.7 %collective-permute-start.13 = (f32[32,8192]{1,0:T(8,128)}, f32[32,8192]{1,0:T(8,128)}, u32[]{:S(2)}, u32[]{:S(2)}) collective-permute-start(f32[32,8192]{1,0:T(8,128)} %get-tuple-element.111.refs_4_), channel_id=1, source_target_pairs={{2,6},{4,0},{6,10},{8,4},{10,14},{12,8},{3,7},{5,1},{7,11},{9,5},{... | collective-permute-start | bytes 3145736 | tf_op jit(solution)/shard_map/ppermute | solution.py:693
  87.8 53.2 %collective-permute-start.2 = (f32[40,8192]{1,0:T(8,128)}, f32[40,8192]{1,0:T(8,128)S(1)}, u32[]{:S(2)}, u32[]{:S(2)}) collective-permute-start(f32[40,8192]{1,0:T(8,128)} %get-tuple-element.93), channel_id=1, source_target_pairs={{0,2},{2,0},{4,6},{6,4},{8,10},{10,8},{12,14},{14,12},{1,3},{3,1},... | collective-permute-start | bytes 3932168 | tf_op jit(solution)/shard_map/ppermute | solution.py:693
  91.6 50.7 %collective-permute-start.4 = (f32[40,8192]{1,0:T(8,128)}, f32[40,8192]{1,0:T(8,128)S(1)}, u32[]{:S(2)}, u32[]{:S(2)}) collective-permute-start(f32[40,8192]{1,0:T(8,128)} %get-tuple-element.94.refs_5_), channel_id=1, source_target_pairs={{2,6},{4,0},{6,10},{8,4},{10,14},{12,8},{3,7},{5,1},{7,11},{9,5},{... | collective-permute-start | bytes 3932168 | tf_op jit(solution)/shard_map/ppermute | solution.py:693
  93.3 49.0 %collective-permute-start.3 = (f32[32,8192]{1,0:T(8,128)}, f32[32,8192]{1,0:T(8,128)}, u32[]{:S(2)}, u32[]{:S(2)}) collective-permute-start(f32[32,8192]{1,0:T(8,128)} %collective-permute-done.1.refs_10_), channel_id=1, source_target_pairs={{6,2},{0,4},{10,6},{4,8},{14,10},{8,12},{7,3},{1,5},{11,7},{5,9},{... | collective-permute-start | bytes 3145736 | tf_op jit(solution)/shard_map/ppermute | solution.py:693
  140.9 43.0 %collective-permute-start.8 = (f32[32,8192]{1,0:T(8,128)}, f32[32,8192]{1,0:T(8,128)}, u32[]{:S(2)}, u32[]{:S(2)}) collective-permute-start(f32[32,8192]{1,0:T(8,128)} %get-tuple-element.106), channel_id=1, source_target_pairs={{0,2},{2,0},{4,6},{6,4},{8,10},{10,8},{12,14},{14,12},{1,3},{3,1},... | collective-permute-start | bytes 3145736 | tf_op jit(solution)/shard_map/ppermute | solution.py:693
  141.0 43.0 %collective-permute-start.14 = (f32[32,8192]{1,0:T(8,128)}, f32[32,8192]{1,0:T(8,128)}, u32[]{:S(2)}, u32[]{:S(2)}) collective-permute-start(f32[32,8192]{1,0:T(8,128)} %get-tuple-element.112.refs_6_), channel_id=1, source_target_pairs={{2,6},{4,0},{6,10},{8,4},{10,14},{12,8},{3,7},{5,1},{7,11},{9,5},{... | collective-permute-start | bytes 3145736 | tf_op jit(solution)/shard_map/ppermute | solution.py:693
  181.3 29.0 %collective-permute-start.9 = (f32[40,8192]{1,0:T(8,128)S(1)}, f32[40,8192]{1,0:T(8,128)S(1)}, u32[]{:S(2)}, u32[]{:S(2)}) collective-permute-start(f32[40,8192]{1,0:T(8,128)S(1)} %collective-permute-done.2.refs_11_), channel_id=1, source_target_pairs={{6,2},{0,4},{10,6},{4,8},{14,10},{8,12},{7,3},{1,5},{11,7},{5,9},{... | collective-permute-start | bytes 3932168 | tf_op jit(solution)/shard_map/ppermute | solution.py:693
  183.9 31.7 %collective-permute-start.11 = (f32[40,2048]{1,0:T(8,128)}, f32[40,2048]{1,0:T(8,128)}, u32[]{:S(2)}, u32[]{:S(2)}) collective-permute-start(f32[40,2048]{1,0:T(8,128)} %get-tuple-element.109), channel_id=1, source_target_pairs={{0,2},{2,0},{4,6},{6,4},{8,10},{10,8},{12,14},{14,12},{1,3},{3,1},... | collective-permute-start | bytes 983048 | tf_op jit(solution)/shard_map/ppermute | solution.py:728
  184.0 57.3 %collective-permute-start.16 = (f32[40,2048]{1,0:T(8,128)}, f32[40,2048]{1,0:T(8,128)}, u32[]{:S(2)}, u32[]{:S(2)}) collective-permute-start(f32[40,2048]{1,0:T(8,128)} %get-tuple-element.117), channel_id=1, source_target_pairs={{0,2},{2,0},{4,6},{6,4},{8,10},{10,8},{12,14},{14,12},{1,3},{3,1},... | collective-permute-start | bytes 983048 | tf_op jit(solution)/shard_map/ppermute | solution.py:728
  186.0 63.7 %collective-permute-start.15 = (f32[40,2048]{1,0:T(8,128)}, f32[40,2048]{1,0:T(8,128)}, u32[]{:S(2)}, u32[]{:S(2)}) collective-permute-start(f32[40,2048]{1,0:T(8,128)} %get-tuple-element.114.refs_7_), channel_id=1, source_target_pairs={{2,6},{4,0},{6,10},{8,4},{10,14},{12,8},{3,7},{5,1},{7,11},{9,5},{... | collective-permute-start | bytes 983048 | tf_op jit(solution)/shard_map/ppermute | solution.py:729
  210.3 25.3 %collective-permute-start.10 = (f32[32,8192]{1,0:T(8,128)}, f32[32,8192]{1,0:T(8,128)S(1)}, u32[]{:S(2)}, u32[]{:S(2)}) collective-permute-start(f32[32,8192]{1,0:T(8,128)} %collective-permute-done.8.refs_8_), channel_id=1, source_target_pairs={{6,2},{0,4},{10,6},{4,8},{14,10},{8,12},{7,3},{1,5},{11,7},{5,9},{... | collective-permute-start | bytes 3145736 | tf_op jit(solution)/shard_map/ppermute | solution.py:693
  215.6 29.7 %collective-permute-start.6 = (f32[1,16384]{1,0:T(1,128)S(1)}, f32[1,16384]{1,0:T(1,128)S(1)}, u32[]{:S(2)}, u32[]{:S(2)}) collective-permute-start(f32[1,16384]{1,0:T(1,128)S(1)} %fusion), channel_id=1, source_target_pairs={{0,4},{2,6},{4,0},{6,2},{8,12},{10,14},{12,8},{14,10},{1,5},{3,7},... | collective-permute-start | bytes 196616 | tf_op jit(solution)/shard_map/ppermute | solution.py:732
  241.4 27.2 %collective-permute-start.18 = (f32[40,2048]{1,0:T(8,128)}, f32[40,2048]{1,0:T(8,128)}, u32[]{:S(2)}, u32[]{:S(2)}) collective-permute-start(f32[40,2048]{1,0:T(8,128)} %get-tuple-element.120.refs_7_), channel_id=1, source_target_pairs={{2,6},{4,0},{6,10},{8,4},{10,14},{12,8},{3,7},{5,1},{7,11},{9,5},{... | collective-permute-start | bytes 983048 | tf_op jit(solution)/shard_map/ppermute | solution.py:729
  242.7 20.6 %collective-permute-start.19 = (f32[40,2048]{1,0:T(8,128)}, f32[40,2048]{1,0:T(8,128)}, u32[]{:S(2)}, u32[]{:S(2)}) collective-permute-start(f32[40,2048]{1,0:T(8,128)} %get-tuple-element.123), channel_id=1, source_target_pairs={{0,2},{2,0},{4,6},{6,4},{8,10},{10,8},{12,14},{14,12},{1,3},{3,1},... | collective-permute-start | bytes 983048 | tf_op jit(solution)/shard_map/ppermute | solution.py:728
  245.4 20.9 %collective-permute-start.22 = (f32[40,2048]{1,0:T(8,128)}, f32[40,2048]{1,0:T(8,128)}, u32[]{:S(2)}, u32[]{:S(2)}) collective-permute-start(f32[40,2048]{1,0:T(8,128)} %get-tuple-element.129), channel_id=1, source_target_pairs={{0,2},{2,0},{4,6},{6,4},{8,10},{10,8},{12,14},{14,12},{1,3},{3,1},... | collective-permute-start | bytes 983048 | tf_op jit(solution)/shard_map/ppermute | solution.py:728
  249.8 35.2 %collective-permute-start.21 = (f32[40,2048]{1,0:T(8,128)S(1)}, f32[40,2048]{1,0:T(8,128)S(1)}, u32[]{:S(2)}, u32[]{:S(2)}) collective-permute-start(f32[40,2048]{1,0:T(8,128)S(1)} %copy-done.14), channel_id=1, source_target_pairs={{2,6},{4,0},{6,10},{8,4},{10,14},{12,8},{3,7},{5,1},{7,11},{9,5},{... | collective-permute-start | bytes 983048 | tf_op jit(solution)/shard_map/ppermute | solution.py:729
  266.3 18.7 %collective-permute-start.20 = (f32[40,2048]{1,0:T(8,128)}, f32[40,2048]{1,0:T(8,128)S(1)}, u32[]{:S(2)}, u32[]{:S(2)}) collective-permute-start(f32[40,2048]{1,0:T(8,128)} %collective-permute-done.19.refs_9_), channel_id=1, source_target_pairs={{6,2},{0,4},{10,6},{4,8},{14,10},{8,12},{7,3},{1,5},{11,7},{5,9},{... | collective-permute-start | bytes 983048 | tf_op jit(solution)/shard_map/ppermute | solution.py:773
  268.5 29.1 %collective-permute-start.25 = (f32[72,2048]{1,0:T(8,128)}, f32[72,2048]{1,0:T(8,128)S(1)}, u32[]{:S(2)}, u32[]{:S(2)}) collective-permute-start(f32[72,2048]{1,0:T(8,128)} %get-tuple-element.135), channel_id=1, source_target_pairs={{0,2},{2,0},{4,6},{6,4},{8,10},{10,8},{12,14},{14,12},{1,3},{3,1},... | collective-permute-start | bytes 1769480 | tf_op jit(solution)/shard_map/ppermute | solution.py:807
  285.0 32.5 %collective-permute-start.31 = (f32[72,2048]{1,0:T(8,128)}, f32[72,2048]{1,0:T(8,128)S(1)}, u32[]{:S(2)}, u32[]{:S(2)}) collective-permute-start(f32[72,2048]{1,0:T(8,128)} %get-tuple-element.148), channel_id=1, source_target_pairs={{0,2},{2,0},{4,6},{6,4},{8,10},{10,8},{12,14},{14,12},{1,3},{3,1},... | collective-permute-start | bytes 1769480 | tf_op jit(solution)/shard_map/ppermute | solution.py:807
  297.6 25.3 %collective-permute-start.26 = (f32[72,2048]{1,0:T(8,128)}, f32[72,2048]{1,0:T(8,128)S(1)}, u32[]{:S(2)}, u32[]{:S(2)}) collective-permute-start(f32[72,2048]{1,0:T(8,128)} %get-tuple-element.138), channel_id=1, source_target_pairs={{0,2},{2,0},{4,6},{6,4},{8,10},{10,8},{12,14},{14,12},{1,3},{3,1},... | collective-permute-start | bytes 1769480 | tf_op jit(solution)/shard_map/ppermute | solution.py:807
  322.9 29.7 %collective-permute-start.27 = (f32[72,2048]{1,0:T(8,128)}, f32[72,2048]{1,0:T(8,128)S(1)}, u32[]{:S(2)}, u32[]{:S(2)}) collective-permute-start(f32[72,2048]{1,0:T(8,128)} %get-tuple-element.139), channel_id=1, source_target_pairs={{0,2},{2,0},{4,6},{6,4},{8,10},{10,8},{12,14},{14,12},{1,3},{3,1},... | collective-permute-start | bytes 1769480 | tf_op jit(solution)/shard_map/ppermute | solution.py:807
  322.9 37.8 %collective-permute-start.28 = (f32[72,2048]{1,0:T(8,128)}, f32[72,2048]{1,0:T(8,128)S(1)}, u32[]{:S(2)}, u32[]{:S(2)}) collective-permute-start(f32[72,2048]{1,0:T(8,128)} %get-tuple-element.141), channel_id=1, source_target_pairs={{0,2},{2,0},{4,6},{6,4},{8,10},{10,8},{12,14},{14,12},{1,3},{3,1},... | collective-permute-start | bytes 1769480 | tf_op jit(solution)/shard_map/ppermute | solution.py:807
  324.9 42.1 %collective-permute-start.29 = (f32[72,2048]{1,0:T(8,128)}, f32[72,2048]{1,0:T(8,128)S(1)}, u32[]{:S(2)}, u32[]{:S(2)}) collective-permute-start(f32[72,2048]{1,0:T(8,128)} %get-tuple-element.143), channel_id=1, source_target_pairs={{0,2},{2,0},{4,6},{6,4},{8,10},{10,8},{12,14},{14,12},{1,3},{3,1},... | collective-permute-start | bytes 1769480 | tf_op jit(solution)/shard_map/ppermute | solution.py:807
  (34 other events, 671.5 us)

commit v6 on v5

--- a/solution.py
+++ b/solution.py
@@ -181,6 +181,7 @@
 BLOCK = 128
 GROUP = 24
 EARLY = 40
+BATCH = 4
 CELL_CHUNKS = 4
 MIB = 1024 * 1024
 VMEM_MIB = 60
@@ -329,7 +330,7 @@
     first_row = base_ref[0]
     first_comp = pl.multiple_of((part + base_ref[1] * (1 - 2 * part)) * 2 * NTH + late * EARLY, 8)
     lane = lax.broadcasted_iota(jnp.int32, (8, BLOCK), 1)
-    first_lane, last_lane = lane == 0, lane == BLOCK - 1
+    first_lane, last_lane, last_lanes = lane == 0, lane == BLOCK - 1, lane >= BLOCK - 2
     third = 1.0 / 3.0
 
     @pl.loop(0, row_count // 8)
@@ -342,7 +343,7 @@
     def halves(row):
         return row[:, :BLOCK], row[:, BLOCK:]
 
-    @pl.loop(0, row_count + 2 * EDGE)
+    @pl.loop(0, row_count + 2 * EDGE, unroll=4)
     def _(r):
         coef = coef_ref[first_row + r]
         for k in range(HALF_SEA + 1):
@@ -351,34 +352,56 @@
     def masked(row, at):
         return tuple(part * sea for part, sea in zip(halves(row), halves(spread_ref[at, SEA])))
 
-    def cell_row(at, new, state, east, north):
-        here, ahead, slope_ahead, bend_here, flux_low = state
-        coef = [None] + [halves(spread_ref[at, k]) for k in range(1, HALF_SEA + 1)]
-        to_right = [pltpu.roll(part, BLOCK - 1, 1) for part in here]
-        right = (jnp.where(last_lane, to_right[1], to_right[0]), jnp.where(last_lane, 0.0, to_right[1]))
-        slope = [right[h] - here[h] for h in range(2)]
-        slope_roll = [pltpu.roll(part, 1, 1) for part in slope]
-        slope_left = (jnp.where(first_lane, here[0], slope_roll[0]),
-                      jnp.where(first_lane, slope_roll[0], slope_roll[1]))
-        bend = [third * (slope[h] - slope_left[h]) for h in range(2)]
-        bend_roll = [pltpu.roll(part, BLOCK - 1, 1) for part in bend]
-        bend_right = (jnp.where(last_lane, bend_roll[1], bend_roll[0]), bend_roll[1])
-        cross, flux, slope_next, bend_ahead = [], [], [], []
+    def cell_rows(first, fresh, state, east, north):
+        here, ahead, slope_here, bend_here, flux_low = state
+        count, sides = len(fresh), range(2)
+        level = [here, ahead] + [masked(row, first + k + EDGE) for k, row in enumerate(fresh)]
+        rows = range(count)
+        coef = [[None] + [halves(spread_ref[first + k, f]) for f in range(1, HALF_SEA + 1)] for k in rows]
+        one_right = [[pltpu.roll(part, BLOCK - 1, 1) for part in level[k]] for k in rows]
+        one_left = [[pltpu.roll(part, 1, 1) for part in level[k]] for k in rows]
+        two_right = [[pltpu.roll(part, BLOCK - 2, 1) for part in level[k]] for k in rows]
+        cross = []
+        for k in rows:
+            right = (jnp.where(last_lane, one_right[k][1], one_right[k][0]), jnp.where(last_lane, 0.0, one_right[k][1]))
+            left = (jnp.where(first_lane, 0.0, one_left[k][0]), jnp.where(first_lane, one_left[k][0], one_left[k][1]))
+            next_right = (jnp.where(last_lanes, two_right[k][1], two_right[k][0]),
+                          jnp.where(last_lanes, 0.0, two_right[k][1]))
+            parts = []
+            for h in sides:
+                mid = level[k][h]
+                slope = right[h] - mid
+                bend = third * (slope - (mid - left[h]))
+                bend_right = third * ((next_right[h] - right[h]) - slope)
+                parts.append(upwind(north * coef[k][OPEN_NORTH][h] + coef[k][FLOW_NORTH][h], mid + right[h], slope,
+                                    bend, bend_right))
+            cross.append(parts)
+        cross_roll = [[pltpu.roll(part, 1, 1) for part in cross[k]] for k in rows]
+        slopes = [slope_here] + [tuple(level[k + 1][h] - level[k][h] for h in sides) for k in range(1, count + 1)]
+        bends = [bend_here] + [
+            tuple(third * (slopes[k][h] - slopes[k - 1][h]) for h in sides) for k in range(1, count + 1)
+        ]
+        flux = [flux_low]
+        for k in rows:
+            flux.append(tuple(
+                upwind(east * coef[k][OPEN_EAST][h] + coef[k][FLOW_EAST][h], level[k][h] + level[k + 1][h],
+                       slopes[k][h], bends[k][h], bends[k + 1][h])
+                for h in sides
+            ))
+        done = []
+        for k in rows:
+            cross_low = (jnp.where(first_lane, cross_roll[k][1], cross_roll[k][0]),
+                         jnp.where(first_lane, cross_roll[k][0], cross_roll[k][1]))
+            done.append([
+                coef[k][HALF_SEA][h] * (((level[k][h] + level[k][h]) + (flux[k][h] + cross_low[h]))
+                                        - (flux[k + 1][h] + cross[k][h]))
+                for h in sides
+            ])
+        return (level[count], level[count + 1], slopes[count], bends[count], flux[count]), done
+
+    def store_row(row, local, parts):
         for h in range(2):
-            cross.append(upwind(north * coef[OPEN_NORTH][h] + coef[FLOW_NORTH][h], here[h] + right[h], slope[h],
-                                bend[h], bend_right[h]))
-            slope_next.append(new[h] - ahead[h])
-            bend_ahead.append(third * (slope_next[h] - slope_ahead[h]))
-            flux.append(upwind(east * coef[OPEN_EAST][h] + coef[FLOW_EAST][h], here[h] + ahead[h], slope_ahead[h],
-                               bend_here[h], bend_ahead[h]))
-        cross_roll = [pltpu.roll(part, 1, 1) for part in cross]
-        cross_low = (jnp.where(first_lane, cross_roll[1], cross_roll[0]),
-                     jnp.where(first_lane, cross_roll[0], cross_roll[1]))
-        moved = [
-            coef[HALF_SEA][h] * (((here[h] + here[h]) + (flux_low[h] + cross_low[h])) - (flux[h] + cross[h]))
-            for h in range(2)
-        ]
-        return (ahead, new, tuple(slope_next), tuple(bend_ahead), tuple(flux)), jnp.concatenate(moved, axis=1)
+            rows_ref[row, local, h * BLOCK : (h + 1) * BLOCK] = parts[h]
 
     def strip(g, arrive):
         local = pl.ds(pl.multiple_of(g * 8, 8), 8)
@@ -392,21 +415,18 @@
             if arrive:
                 block = rows_ref.at[pl.ds(8 * i, 8)]
                 pltpu.make_async_copy(block, block, row_sems.at[i]).wait()
-            fresh = [rows_ref[8 * i + k, local, :] for k in range(8)]
-            done = []
-            for k in range(8):
-                new = masked(fresh[k], 8 * i + k + EDGE)
-                state, moved = cell_row(8 * i + k, new, state, east, north)
-                done.append(moved)
-            for k in range(8):
-                rows_ref[jnp.maximum(8 * i + k - EDGE, 0), local, :] = done[k]
+            for first in range(0, 8, BATCH):
+                fresh = [rows_ref[8 * i + first + k, local, :] for k in range(BATCH)]
+                state, done = cell_rows(8 * i + first, fresh, state, east, north)
+                for k in range(BATCH):
+                    store_row(jnp.maximum(8 * i + first + k - EDGE, 0), local, done[k])
             return state
 
         state = lax.fori_loop(0, row_count // 8, eight, state)
+        fresh = [halo_ref[comps, k, :] for k in range(EDGE)]
+        state, done = cell_rows(row_count, fresh, state, east, north)
         for k in range(EDGE):
-            new = masked(halo_ref[comps, k, :], row_count + EDGE + k)
-            state, moved = cell_row(row_count + k, new, state, east, north)
-            rows_ref[row_count - EDGE + k, local, :] = moved
+            store_row(row_count - EDGE + k, local, done[k])
 
     strip(0, True)
 
@@ -444,7 +464,7 @@
     mixed_row = comp_row[mixed]
     in_circle = (mixed_row >= start) & (mixed_row <= end)
 
-    @pl.loop(0, cells // tile_width)
+    @pl.loop(0, cells // tile_width, unroll=2)
     def _(i):
         source = pl.ds(pl.multiple_of(i * tile_width, tile_width), tile_width)
         level = wide_ref[:comp_count, source]
@@ -537,7 +557,7 @@
     for o in range(2 * chunks):
         extra = own[o] if o < chunks else back[o - chunks]
 
-        @pl.loop(0, width // tile_width)
+        @pl.loop(0, width // tile_width, unroll=2)
         def _(i):
             source = pl.ds(pl.multiple_of(i * tile_width, tile_width), tile_width)
             target = pl.ds(pl.multiple_of(o * width + i * tile_width, tile_width), tile_width)

time: 386 us -> 389 us (level)
  no operation moved by 1% of the time
where the time goes in v6:
time: 389 us; the launch traced here: 387 us
  Pallas kernels  220 us (57%)
  waiting for transfers between devices  77.6 us (20%)
  starting transfers between devices  65.2 us (17%)
  local copies, waits for them, and re-layouts  14.3 us (4%)
  other arithmetic  9.32 us (2%)
    pallas_call x4, Pallas kernels, propagate(): pl.pallas_call(functools.partial(propagate_kernel, part, late, pieces), g...  150 us
    ppermute x9, waiting for transfers between devices, send(): lax.ppermute(after(piece, *wait), 'comp', route)  39.9 us
    pallas_call x4, Pallas kernels, packed_shards(): pl.pallas_call(interact_kernel, grid=(width // lanes,), in_specs=[pl.Bloc...  32.3 us
    ppermute x8, waiting for transfers between devices, send_back(): return lax.ppermute(after(piece, *waits), 'comp', pairs)  31.8 us
    pallas_call x2, Pallas kernels, finish(): pl.pallas_call(functools.partial(finish_kernel, CELL_CHUNKS), grid_spec=p...  31.5 us
    ppermute x9, starting transfers between devices, send(): lax.ppermute(after(piece, *wait), 'comp', route)  22.9 us
    ppermute x4, starting transfers between devices, packed_shards(): from_got[last].append(lax.ppermute(after(got_1[c], *waits), 'comp', across))  14.9 us
  transfers between devices with their start and end apart: 33, of which 11 were waited for; matrix products, arithmetic and copies ran while one was open for 4% of the time, Pallas kernels for 42%

profile of v6, /device:TPU:0, one launch (start us, length us, event | category | flops | bytes accessed | tf_op | source)
XLA Modules:
  0.0 387.5 jit_solution(13803431270811428357)
XLA Ops:
  2.5 7.0 %prepare.1 = (f32[260,8,256]{2,1,0:T(8,128)}, s32[2,128,128]{2,1,0:T(8,128)}, s32[2,128,128]{2,1,0:T(8,128)}, s32[8,256]{1,0:T(8,128)}, f32[144,128]{1,0:T(8,128)}, /*index=5*/f32[144,128]{1,0:T(8,128)}) custom-call(s32[3]{0:T(128)} %pad_add_fusion.7.base_ref, f32[32]{0:T(128)} %speed_ref.1, s32[256,256]{1,0:T(8,128)} %sea_ref.1, f32[256,256]{1,0:T(8,128)} %east_ref.1, ...), custom_call_target="tpu_custom_call" | custom-call | tf_op jit(solution)/shard_map/prepare/pallas_call | solution.py:624
  10.3 40.6 %propagate_early.2 = (f32[32,8192]{1,0:T(8,128)}, f32[32,8192]{1,0:T(8,128)}, f32[1,16384]{1,0:T(1,128)}, f32[72,16384]{1,0:T(8,128)}, f32[8,16384]{1,0:T(8,128)}, /*index=5*/f32[8,16384]{1,0:T(8,128)}) custom-call(s32[3]{0:T(128)} %pad_add_fusion.7.base_ref, s32[8,256]{1,0:T(8,128)} %get-tuple-element.95.table_ref, f32[144,128,256]{2,1,0:T(8,128)} %energy_ref.7, ...), custom_call_target="tpu_custom_call" | custom-call | flops 78643200 | bytes 62914560 | tf_op jit(solution)/shard_map/propagate_early/pallas_call | solution.py:680
  55.4 34.4 %propagate_late.2 = (f32[40,8192]{1,0:T(8,128)}, f32[40,8192]{1,0:T(8,128)}, f32[1,16384]{1,0:T(1,128)}, f32[72,16384]{1,0:T(8,128)}) custom-call(s32[3]{0:T(128)} %pad_add_fusion.7.base_ref, s32[8,256]{1,0:T(8,128)} %get-tuple-element.95.table_ref, f32[144,128,256]{2,1,0:T(8,128)} %energy_ref.7, ...), custom_call_target="tpu_custom_call", output_to_operand_aliasing={{3}: (10, {})} | custom-call | flops 62914560 | bytes 62914560 | tf_op jit(solution)/shard_map/propagate_late/pallas_call | solution.py:680
  89.8 3.8 collective-permute-start.2
  95.3 5.5 %collective-permute-start.3 = (f32[32,8192]{1,0:T(8,128)}, f32[32,8192]{1,0:T(8,128)}, u32[]{:S(2)}, u32[]{:S(2)}) collective-permute-start(f32[32,8192]{1,0:T(8,128)} %collective-permute-done.1.refs_10_), channel_id=1, source_target_pairs={{6,2},{0,4},{10,6},{4,8},{14,10},{8,12},{7,3},{1,5},{11,7},{5,9},{... | collective-permute-start | bytes 3145736 | tf_op jit(solution)/shard_map/ppermute | solution.py:713
  103.9 40.0 %propagate_early.3 = (f32[32,8192]{1,0:T(8,128)}, f32[32,8192]{1,0:T(8,128)}, f32[1,16384]{1,0:T(1,128)}, f32[72,16384]{1,0:T(8,128)}, f32[8,16384]{1,0:T(8,128)}) custom-call(s32[3]{0:T(128)} %pad_add_fusion.7.base_ref, s32[8,256]{1,0:T(8,128)} %get-tuple-element.95.table_ref, f32[144,128,256]{2,1,0:T(8,128)} %energy_ref.7, f32[144,2,256]{2,1,0:T(2,128)} %copy-done.4, ...), custom_call_target="tpu_custom_call" | custom-call | flops 78643200 | bytes 62914560 | tf_op jit(solution)/shard_map/propagate_early/pallas_call | solution.py:680
  145.4 34.7 %propagate_late.3 = (f32[40,2048]{1,0:T(8,128)}, f32[40,2048]{1,0:T(8,128)}, f32[40,2048]{1,0:T(8,128)}, f32[40,2048]{1,0:T(8,128)}, f32[40,2048]{1,0:T(8,128)},...) custom-call(s32[3]{0:T(128)} %pad_add_fusion.7.base_ref, ...), custom_call_target="tpu_custom_call", output_to_operand_aliasing={{9}: (10, {})} | custom-call | flops 62914560 | bytes 62914560 | tf_op jit(solution)/shard_map/propagate_late/pallas_call | solution.py:680
  191.9 22.2 %collective-permute-done.9.refs_3_ = f32[40,8192]{1,0:T(8,128)S(1)} collective-permute-done((f32[40,8192]{1,0:T(8,128)S(1)}, f32[40,8192]{1,0:T(8,128)S(1)}, u32[]{:S(2)}, u32[]{:S(2)}) %collective-permute-start.9) | collective-permute-done | bytes 1310752 | tf_op jit(solution)/shard_map/ppermute | solution.py:713
  214.1 4.4 %collective-permute-start.10 = (f32[32,8192]{1,0:T(8,128)}, f32[32,8192]{1,0:T(8,128)S(1)}, u32[]{:S(2)}, u32[]{:S(2)}) collective-permute-start(f32[32,8192]{1,0:T(8,128)} %collective-permute-done.8.refs_8_), channel_id=1, source_target_pairs={{6,2},{0,4},{10,6},{4,8},{14,10},{8,12},{7,3},{1,5},{11,7},{5,9},{... | collective-permute-start | bytes 3145736 | tf_op jit(solution)/shard_map/ppermute | solution.py:713
  221.6 17.7 %collective-permute-done.10.refs_0_ = f32[32,8192]{1,0:T(8,128)S(1)} collective-permute-done((f32[32,8192]{1,0:T(8,128)}, f32[32,8192]{1,0:T(8,128)S(1)}, u32[]{:S(2)}, u32[]{:S(2)}) %collective-permute-start.10) | collective-permute-done | bytes 1048608 | tf_op jit(solution)/shard_map/ppermute | solution.py:713
  239.4 5.0 %collective-permute-start.12 = (f32[40,2048]{1,0:T(8,128)}, f32[40,2048]{1,0:T(8,128)}, u32[]{:S(2)}, u32[]{:S(2)}) collective-permute-start(f32[40,2048]{1,0:T(8,128)} %collective-permute-done.11.refs_9_), channel_id=1, source_target_pairs={{6,2},{0,4},{10,6},{4,8},{14,10},{8,12},{7,3},{1,5},{11,7},{5,9},{... | collective-permute-start | bytes 983048 | tf_op jit(solution)/shard_map/ppermute | solution.py:793
  254.9 4.1 %collective-permute-start.7 = (f32[1,16384]{1,0:T(1,128)S(1)}, f32[1,16384]{1,0:T(1,128)S(1)}, u32[]{:S(2)}, u32[]{:S(2)}) collective-permute-start(f32[1,16384]{1,0:T(1,128)S(1)} %add.261), channel_id=1, source_target_pairs={{0,8},{2,10},{4,12},{6,14},{8,0},{10,2},{12,4},{14,6},{1,9},{3,11}... | collective-permute-start | bytes 196616 | tf_op jit(solution)/shard_map/ppermute | solution.py:753
  259.1 8.1 %interact_cells.4 = (f32[144,2048]{1,0:T(8,128)}, f32[72,2048]{1,0:T(8,128)}, f32[72,2048]{1,0:T(8,128)}) custom-call(bf16[6,288,216]{2,1,0:T(8,128)(2,1)} %stack.28.table_ref, bf16[288,864]{1,0:T(8,128)(2,1)} %concatenate.40.spread_ref, f32[432,1]{1,0:T(8,128)} %copy.49.coupling_ref, f32[32,8192]{1,0:T(8,128)} %copy-done.3, ...), custom_call_target="tpu_custom_call" | custom-call | flops 2548039680 | bytes 20971520 | tf_op jit(solution)/shard_map/interact_cells/pallas_call | solution.py:804
  276.7 8.1 %interact_cells.5 = (f32[144,2048]{1,0:T(8,128)}, f32[72,2048]{1,0:T(8,128)}, f32[72,2048]{1,0:T(8,128)}) custom-call(bf16[6,288,216]{2,1,0:T(8,128)(2,1)} %stack.28.table_ref, bf16[288,864]{1,0:T(8,128)(2,1)} %concatenate.40.spread_ref, f32[432,1]{1,0:T(8,128)} %copy.49.coupling_ref, f32[32,8192]{1,0:T(8,128)} %copy-done.3, f32[40,2048]{1,0:T(8,128)} %copy-done.17, ...), custom_call_target="tpu_custom_call" | custom-call | flops 2548039680 | bytes 20971520 | tf_op jit(solution)/shard_map/interact_cells/pallas_call | solution.py:804
  284.8 4.0 %collective-permute-done.30.refs_5_ = f32[72,2048]{1,0:T(8,128)S(1)} collective-permute-done((f32[72,2048]{1,0:T(8,128)}, f32[72,2048]{1,0:T(8,128)S(1)}, u32[]{:S(2)}, u32[]{:S(2)}) %collective-permute-start.30) | collective-permute-done | bytes 589856 | tf_op jit(solution)/shard_map/ppermute | solution.py:827
  290.3 8.1 %interact_cells.6 = (f32[144,2048]{1,0:T(8,128)}, f32[72,2048]{1,0:T(8,128)}, f32[72,2048]{1,0:T(8,128)}) custom-call(bf16[6,288,216]{2,1,0:T(8,128)(2,1)} %stack.28.table_ref, bf16[288,864]{1,0:T(8,128)(2,1)} %concatenate.40.spread_ref, f32[432,1]{1,0:T(8,128)} %copy.49.coupling_ref, f32[32,8192]{1,0:T(8,128)} %copy-done.3, f32[40,2048]{1,0:T(8,128)} %copy-done.16, ...), custom_call_target="tpu_custom_call" | custom-call | flops 2548039680 | bytes 20971520 | tf_op jit(solution)/shard_map/interact_cells/pallas_call | solution.py:804
  302.8 4.8 %collective-permute-start.23 = (f32[40,2048]{1,0:T(8,128)}, f32[40,2048]{1,0:T(8,128)S(1)}, u32[]{:S(2)}, u32[]{:S(2)}) collective-permute-start(f32[40,2048]{1,0:T(8,128)} %collective-permute-done.22.refs_9_), channel_id=1, source_target_pairs={{6,2},{0,4},{10,6},{4,8},{14,10},{8,12},{7,3},{1,5},{11,7},{5,9},{... | collective-permute-start | bytes 983048 | tf_op jit(solution)/shard_map/ppermute | solution.py:793
  313.2 8.1 %interact_cells.7 = (f32[144,2048]{1,0:T(8,128)}, f32[72,2048]{1,0:T(8,128)}, f32[72,2048]{1,0:T(8,128)}) custom-call(bf16[6,288,216]{2,1,0:T(8,128)(2,1)} %stack.28.table_ref, bf16[288,864]{1,0:T(8,128)(2,1)} %concatenate.40.spread_ref, f32[432,1]{1,0:T(8,128)} %copy.49.coupling_ref, f32[32,8192]{1,0:T(8,128)} %copy-done.3, f32[40,2048]{1,0:T(8,128)} %copy-done.19, ...), custom_call_target="tpu_custom_call" | custom-call | flops 2548039680 | bytes 20971520 | tf_op jit(solution)/shard_map/interact_cells/pallas_call | solution.py:804
  321.3 3.2 collective-permute-start.32
  331.8 7.5 %collective-permute-done.32.refs_8_ = f32[72,2048]{1,0:T(8,128)S(1)} collective-permute-done((f32[72,2048]{1,0:T(8,128)}, f32[72,2048]{1,0:T(8,128)S(1)}, u32[]{:S(2)}, u32[]{:S(2)}) %collective-permute-start.32) | collective-permute-done | bytes 589856 | tf_op jit(solution)/shard_map/ppermute | solution.py:827
  340.2 15.7 %finish_chunk.2.refs_9_ = f32[144,128,256]{2,1,0:T(8,128)} custom-call(s32[3]{0:T(128)} %pad_add_fusion.7.base_ref, s32[8,256]{1,0:T(8,128)} %get-tuple-element.95.table_ref, s32[2,128,128]{2,1,0:T(8,128)} %get-tuple-element.79.place_ref, f32[1,16384]{1,0:T(1,128)} %broadcast_multiply_fusion, f32[8,16384]{1,0:T(8,128)} %get-tuple-element.86.refs_0_.fields_ref, ...), custom_call_target="tpu_custom_call" | custom-call | flops 47185920 | bytes 104857600 | tf_op jit(solution)/shard_map/finish_chunk/pallas_call | solution.py:852
  355.9 8.7 %collective-permute-done.28.refs_7_ = f32[72,2048]{1,0:T(8,128)S(1)} collective-permute-done((f32[72,2048]{1,0:T(8,128)}, f32[72,2048]{1,0:T(8,128)S(1)}, u32[]{:S(2)}, u32[]{:S(2)}) %collective-permute-start.28) | collective-permute-done | bytes 589856 | tf_op jit(solution)/shard_map/ppermute | solution.py:827
  364.6 6.3 %collective-permute-done.29.refs_8_ = f32[72,2048]{1,0:T(8,128)S(1)} collective-permute-done((f32[72,2048]{1,0:T(8,128)}, f32[72,2048]{1,0:T(8,128)S(1)}, u32[]{:S(2)}, u32[]{:S(2)}) %collective-permute-start.29) | collective-permute-done | bytes 589856 | tf_op jit(solution)/shard_map/ppermute | solution.py:827
  371.7 15.7 %finish_chunk.3 = f32[144,128,256]{2,1,0:T(8,128)} custom-call(s32[3]{0:T(128)} %pad_add_fusion.7.base_ref, s32[8,256]{1,0:T(8,128)} %get-tuple-element.95.table_ref, s32[2,128,128]{2,1,0:T(8,128)} %get-tuple-element.79.place_ref, f32[1,16384]{1,0:T(1,128)} %broadcast_multiply_fusion, ...), custom_call_target="tpu_custom_call", output_to_operand_aliasing={{}: (16, {})} | custom-call | flops 47185920 | bytes 104857600 | tf_op jit(solution)/shard_map/finish_chunk/pallas_call | solution.py:852
  (145 shorter events, 69.0 us)
Async XLA Ops:
  51.0 44.3 %collective-permute-start.1 = (f32[32,8192]{1,0:T(8,128)}, f32[32,8192]{1,0:T(8,128)}, u32[]{:S(2)}, u32[]{:S(2)}) collective-permute-start(f32[32,8192]{1,0:T(8,128)} %get-tuple-element.90), channel_id=1, source_target_pairs={{0,2},{2,0},{4,6},{6,4},{8,10},{10,8},{12,14},{14,12},{1,3},{3,1},... | collective-permute-start | bytes 3145736 | tf_op jit(solution)/shard_map/ppermute | solution.py:713
  54.1 192.4 %collective-permute-start.13 = (f32[32,8192]{1,0:T(8,128)}, f32[32,8192]{1,0:T(8,128)}, u32[]{:S(2)}, u32[]{:S(2)}) collective-permute-start(f32[32,8192]{1,0:T(8,128)} %get-tuple-element.111.refs_4_), channel_id=1, source_target_pairs={{2,6},{4,0},{6,10},{8,4},{10,14},{12,8},{3,7},{5,1},{7,11},{9,5},{... | collective-permute-start | bytes 3145736 | tf_op jit(solution)/shard_map/ppermute | solution.py:713
  89.8 54.2 %collective-permute-start.2 = (f32[40,8192]{1,0:T(8,128)}, f32[40,8192]{1,0:T(8,128)S(1)}, u32[]{:S(2)}, u32[]{:S(2)}) collective-permute-start(f32[40,8192]{1,0:T(8,128)} %get-tuple-element.93), channel_id=1, source_target_pairs={{0,2},{2,0},{4,6},{6,4},{8,10},{10,8},{12,14},{14,12},{1,3},{3,1},... | collective-permute-start | bytes 3932168 | tf_op jit(solution)/shard_map/ppermute | solution.py:713
  93.6 51.7 %collective-permute-start.4 = (f32[40,8192]{1,0:T(8,128)}, f32[40,8192]{1,0:T(8,128)S(1)}, u32[]{:S(2)}, u32[]{:S(2)}) collective-permute-start(f32[40,8192]{1,0:T(8,128)} %get-tuple-element.94.refs_5_), channel_id=1, source_target_pairs={{2,6},{4,0},{6,10},{8,4},{10,14},{12,8},{3,7},{5,1},{7,11},{9,5},{... | collective-permute-start | bytes 3932168 | tf_op jit(solution)/shard_map/ppermute | solution.py:713
  95.3 50.0 %collective-permute-start.3 = (f32[32,8192]{1,0:T(8,128)}, f32[32,8192]{1,0:T(8,128)}, u32[]{:S(2)}, u32[]{:S(2)}) collective-permute-start(f32[32,8192]{1,0:T(8,128)} %collective-permute-done.1.refs_10_), channel_id=1, source_target_pairs={{6,2},{0,4},{10,6},{4,8},{14,10},{8,12},{7,3},{1,5},{11,7},{5,9},{... | collective-permute-start | bytes 3145736 | tf_op jit(solution)/shard_map/ppermute | solution.py:713
  143.9 43.9 %collective-permute-start.8 = (f32[32,8192]{1,0:T(8,128)}, f32[32,8192]{1,0:T(8,128)}, u32[]{:S(2)}, u32[]{:S(2)}) collective-permute-start(f32[32,8192]{1,0:T(8,128)} %get-tuple-element.106), channel_id=1, source_target_pairs={{0,2},{2,0},{4,6},{6,4},{8,10},{10,8},{12,14},{14,12},{1,3},{3,1},... | collective-permute-start | bytes 3145736 | tf_op jit(solution)/shard_map/ppermute | solution.py:713
  144.0 43.9 %collective-permute-start.14 = (f32[32,8192]{1,0:T(8,128)}, f32[32,8192]{1,0:T(8,128)}, u32[]{:S(2)}, u32[]{:S(2)}) collective-permute-start(f32[32,8192]{1,0:T(8,128)} %get-tuple-element.112.refs_6_), channel_id=1, source_target_pairs={{2,6},{4,0},{6,10},{8,4},{10,14},{12,8},{3,7},{5,1},{7,11},{9,5},{... | collective-permute-start | bytes 3145736 | tf_op jit(solution)/shard_map/ppermute | solution.py:713
  185.1 29.0 %collective-permute-start.9 = (f32[40,8192]{1,0:T(8,128)S(1)}, f32[40,8192]{1,0:T(8,128)S(1)}, u32[]{:S(2)}, u32[]{:S(2)}) collective-permute-start(f32[40,8192]{1,0:T(8,128)S(1)} %collective-permute-done.2.refs_11_), channel_id=1, source_target_pairs={{6,2},{0,4},{10,6},{4,8},{14,10},{8,12},{7,3},{1,5},{11,7},{5,9},{... | collective-permute-start | bytes 3932168 | tf_op jit(solution)/shard_map/ppermute | solution.py:713
  187.8 31.7 %collective-permute-start.11 = (f32[40,2048]{1,0:T(8,128)}, f32[40,2048]{1,0:T(8,128)}, u32[]{:S(2)}, u32[]{:S(2)}) collective-permute-start(f32[40,2048]{1,0:T(8,128)} %get-tuple-element.109), channel_id=1, source_target_pairs={{0,2},{2,0},{4,6},{6,4},{8,10},{10,8},{12,14},{14,12},{1,3},{3,1},... | collective-permute-start | bytes 983048 | tf_op jit(solution)/shard_map/ppermute | solution.py:748
  187.9 57.3 %collective-permute-start.16 = (f32[40,2048]{1,0:T(8,128)}, f32[40,2048]{1,0:T(8,128)}, u32[]{:S(2)}, u32[]{:S(2)}) collective-permute-start(f32[40,2048]{1,0:T(8,128)} %get-tuple-element.117), channel_id=1, source_target_pairs={{0,2},{2,0},{4,6},{6,4},{8,10},{10,8},{12,14},{14,12},{1,3},{3,1},... | collective-permute-start | bytes 983048 | tf_op jit(solution)/shard_map/ppermute | solution.py:748
  189.9 63.7 %collective-permute-start.15 = (f32[40,2048]{1,0:T(8,128)}, f32[40,2048]{1,0:T(8,128)}, u32[]{:S(2)}, u32[]{:S(2)}) collective-permute-start(f32[40,2048]{1,0:T(8,128)} %get-tuple-element.114.refs_7_), channel_id=1, source_target_pairs={{2,6},{4,0},{6,10},{8,4},{10,14},{12,8},{3,7},{5,1},{7,11},{9,5},{... | collective-permute-start | bytes 983048 | tf_op jit(solution)/shard_map/ppermute | solution.py:749
  214.1 25.3 %collective-permute-start.10 = (f32[32,8192]{1,0:T(8,128)}, f32[32,8192]{1,0:T(8,128)S(1)}, u32[]{:S(2)}, u32[]{:S(2)}) collective-permute-start(f32[32,8192]{1,0:T(8,128)} %collective-permute-done.8.refs_8_), channel_id=1, source_target_pairs={{6,2},{0,4},{10,6},{4,8},{14,10},{8,12},{7,3},{1,5},{11,7},{5,9},{... | collective-permute-start | bytes 3145736 | tf_op jit(solution)/shard_map/ppermute | solution.py:713
  219.5 29.7 %collective-permute-start.6 = (f32[1,16384]{1,0:T(1,128)S(1)}, f32[1,16384]{1,0:T(1,128)S(1)}, u32[]{:S(2)}, u32[]{:S(2)}) collective-permute-start(f32[1,16384]{1,0:T(1,128)S(1)} %fusion), channel_id=1, source_target_pairs={{0,4},{2,6},{4,0},{6,2},{8,12},{10,14},{12,8},{14,10},{1,5},{3,7},... | collective-permute-start | bytes 196616 | tf_op jit(solution)/shard_map/ppermute | solution.py:752
  245.2 27.2 %collective-permute-start.18 = (f32[40,2048]{1,0:T(8,128)}, f32[40,2048]{1,0:T(8,128)}, u32[]{:S(2)}, u32[]{:S(2)}) collective-permute-start(f32[40,2048]{1,0:T(8,128)} %get-tuple-element.120.refs_7_), channel_id=1, source_target_pairs={{2,6},{4,0},{6,10},{8,4},{10,14},{12,8},{3,7},{5,1},{7,11},{9,5},{... | collective-permute-start | bytes 983048 | tf_op jit(solution)/shard_map/ppermute | solution.py:749
  246.5 20.6 %collective-permute-start.19 = (f32[40,2048]{1,0:T(8,128)}, f32[40,2048]{1,0:T(8,128)}, u32[]{:S(2)}, u32[]{:S(2)}) collective-permute-start(f32[40,2048]{1,0:T(8,128)} %get-tuple-element.123), channel_id=1, source_target_pairs={{0,2},{2,0},{4,6},{6,4},{8,10},{10,8},{12,14},{14,12},{1,3},{3,1},... | collective-permute-start | bytes 983048 | tf_op jit(solution)/shard_map/ppermute | solution.py:748
  249.2 20.9 %collective-permute-start.22 = (f32[40,2048]{1,0:T(8,128)}, f32[40,2048]{1,0:T(8,128)}, u32[]{:S(2)}, u32[]{:S(2)}) collective-permute-start(f32[40,2048]{1,0:T(8,128)} %get-tuple-element.129), channel_id=1, source_target_pairs={{0,2},{2,0},{4,6},{6,4},{8,10},{10,8},{12,14},{14,12},{1,3},{3,1},... | collective-permute-start | bytes 983048 | tf_op jit(solution)/shard_map/ppermute | solution.py:748
  253.6 35.2 %collective-permute-start.21 = (f32[40,2048]{1,0:T(8,128)S(1)}, f32[40,2048]{1,0:T(8,128)S(1)}, u32[]{:S(2)}, u32[]{:S(2)}) collective-permute-start(f32[40,2048]{1,0:T(8,128)S(1)} %copy-done.14), channel_id=1, source_target_pairs={{2,6},{4,0},{6,10},{8,4},{10,14},{12,8},{3,7},{5,1},{7,11},{9,5},{... | collective-permute-start | bytes 983048 | tf_op jit(solution)/shard_map/ppermute | solution.py:749
  270.1 18.7 %collective-permute-start.20 = (f32[40,2048]{1,0:T(8,128)}, f32[40,2048]{1,0:T(8,128)S(1)}, u32[]{:S(2)}, u32[]{:S(2)}) collective-permute-start(f32[40,2048]{1,0:T(8,128)} %collective-permute-done.19.refs_9_), channel_id=1, source_target_pairs={{6,2},{0,4},{10,6},{4,8},{14,10},{8,12},{7,3},{1,5},{11,7},{5,9},{... | collective-permute-start | bytes 983048 | tf_op jit(solution)/shard_map/ppermute | solution.py:793
  272.4 29.1 %collective-permute-start.25 = (f32[72,2048]{1,0:T(8,128)}, f32[72,2048]{1,0:T(8,128)S(1)}, u32[]{:S(2)}, u32[]{:S(2)}) collective-permute-start(f32[72,2048]{1,0:T(8,128)} %get-tuple-element.135), channel_id=1, source_target_pairs={{0,2},{2,0},{4,6},{6,4},{8,10},{10,8},{12,14},{14,12},{1,3},{3,1},... | collective-permute-start | bytes 1769480 | tf_op jit(solution)/shard_map/ppermute | solution.py:827
  288.8 32.5 %collective-permute-start.31 = (f32[72,2048]{1,0:T(8,128)}, f32[72,2048]{1,0:T(8,128)S(1)}, u32[]{:S(2)}, u32[]{:S(2)}) collective-permute-start(f32[72,2048]{1,0:T(8,128)} %get-tuple-element.148), channel_id=1, source_target_pairs={{0,2},{2,0},{4,6},{6,4},{8,10},{10,8},{12,14},{14,12},{1,3},{3,1},... | collective-permute-start | bytes 1769480 | tf_op jit(solution)/shard_map/ppermute | solution.py:827
  301.4 25.3 %collective-permute-start.26 = (f32[72,2048]{1,0:T(8,128)}, f32[72,2048]{1,0:T(8,128)S(1)}, u32[]{:S(2)}, u32[]{:S(2)}) collective-permute-start(f32[72,2048]{1,0:T(8,128)} %get-tuple-element.138), channel_id=1, source_target_pairs={{0,2},{2,0},{4,6},{6,4},{8,10},{10,8},{12,14},{14,12},{1,3},{3,1},... | collective-permute-start | bytes 1769480 | tf_op jit(solution)/shard_map/ppermute | solution.py:827
  326.7 29.2 %collective-permute-start.27 = (f32[72,2048]{1,0:T(8,128)}, f32[72,2048]{1,0:T(8,128)S(1)}, u32[]{:S(2)}, u32[]{:S(2)}) collective-permute-start(f32[72,2048]{1,0:T(8,128)} %get-tuple-element.139), channel_id=1, source_target_pairs={{0,2},{2,0},{4,6},{6,4},{8,10},{10,8},{12,14},{14,12},{1,3},{3,1},... | collective-permute-start | bytes 1769480 | tf_op jit(solution)/shard_map/ppermute | solution.py:827
  326.7 37.8 %collective-permute-start.28 = (f32[72,2048]{1,0:T(8,128)}, f32[72,2048]{1,0:T(8,128)S(1)}, u32[]{:S(2)}, u32[]{:S(2)}) collective-permute-start(f32[72,2048]{1,0:T(8,128)} %get-tuple-element.141), channel_id=1, source_target_pairs={{0,2},{2,0},{4,6},{6,4},{8,10},{10,8},{12,14},{14,12},{1,3},{3,1},... | collective-permute-start | bytes 1769480 | tf_op jit(solution)/shard_map/ppermute | solution.py:827
  328.8 42.1 %collective-permute-start.29 = (f32[72,2048]{1,0:T(8,128)}, f32[72,2048]{1,0:T(8,128)S(1)}, u32[]{:S(2)}, u32[]{:S(2)}) collective-permute-start(f32[72,2048]{1,0:T(8,128)} %get-tuple-element.143), channel_id=1, source_target_pairs={{0,2},{2,0},{4,6},{6,4},{8,10},{10,8},{12,14},{14,12},{1,3},{3,1},... | collective-permute-start | bytes 1769480 | tf_op jit(solution)/shard_map/ppermute | solution.py:827
  (34 other events, 678.2 us)

commit v7 on v6

--- a/solution.py
+++ b/solution.py
@@ -322,7 +322,7 @@
     sum_ref, full_ref = refs.pop(0), refs.pop(0)
     seam_out_ref = None if late else refs.pop(0)
     fields_out_ref = refs.pop(0) if with_fields else None
-    rows_ref, spread_ref, wide_ref, result_ref, row_sems, out_sems = refs
+    energy_vmem, rows_ref, spread_ref, wide_ref, result_ref, strip_sems, out_sems = refs
     row_count, comp_count, col_count = rows_ref.shape
     strips = comp_count // 8
     sent_rows = piece_refs[0].shape[0]
@@ -330,15 +330,16 @@
     first_row = base_ref[0]
     first_comp = pl.multiple_of((part + base_ref[1] * (1 - 2 * part)) * 2 * NTH + late * EARLY, 8)
     lane = lax.broadcasted_iota(jnp.int32, (8, BLOCK), 1)
-    first_lane, last_lane, last_lanes = lane == 0, lane == BLOCK - 1, lane >= BLOCK - 2
+    first_lane, last_lane = lane == 0, lane == BLOCK - 1
     third = 1.0 / 3.0
 
-    @pl.loop(0, row_count // 8)
-    def _(i):
-        for k in range(8):
-            row = 8 * i + k
-            source = energy_ref.at[pl.ds(first_comp, comp_count), row, :]
-            pltpu.make_async_copy(source, rows_ref.at[row], row_sems.at[i]).start()
+    def arrival(g):
+        target = energy_vmem.at[pl.ds(pl.multiple_of(8 * g, 8), 8)]
+        source = energy_ref.at[pl.ds(pl.multiple_of(first_comp + 8 * g, 8), 8)]
+        return pltpu.make_async_copy(source, target, strip_sems.at[g])
+
+    for g in range(strips):
+        arrival(g).start()
 
     def halves(row):
         return row[:, :BLOCK], row[:, BLOCK:]
@@ -359,23 +360,25 @@
         rows = range(count)
         coef = [[None] + [halves(spread_ref[first + k, f]) for f in range(1, HALF_SEA + 1)] for k in rows]
         one_right = [[pltpu.roll(part, BLOCK - 1, 1) for part in level[k]] for k in rows]
-        one_left = [[pltpu.roll(part, 1, 1) for part in level[k]] for k in rows]
-        two_right = [[pltpu.roll(part, BLOCK - 2, 1) for part in level[k]] for k in rows]
+        right = [
+            (jnp.where(last_lane, one[1], one[0]), jnp.where(last_lane, 0.0, one[1])) for one in one_right
+        ]
+        slope = [[right[k][h] - level[k][h] for h in sides] for k in rows]
+        slope_roll = [[pltpu.roll(part, 1, 1) for part in slope[k]] for k in rows]
+        bend = [
+            (third * (slope[k][0] - jnp.where(first_lane, level[k][0], slope_roll[k][0])),
+             third * (slope[k][1] - jnp.where(first_lane, slope_roll[k][0], slope_roll[k][1])))
+            for k in rows
+        ]
+        bend_roll = [[pltpu.roll(part, BLOCK - 1, 1) for part in bend[k]] for k in rows]
         cross = []
         for k in rows:
-            right = (jnp.where(last_lane, one_right[k][1], one_right[k][0]), jnp.where(last_lane, 0.0, one_right[k][1]))
-            left = (jnp.where(first_lane, 0.0, one_left[k][0]), jnp.where(first_lane, one_left[k][0], one_left[k][1]))
-            next_right = (jnp.where(last_lanes, two_right[k][1], two_right[k][0]),
-                          jnp.where(last_lanes, 0.0, two_right[k][1]))
-            parts = []
-            for h in sides:
-                mid = level[k][h]
-                slope = right[h] - mid
-                bend = third * (slope - (mid - left[h]))
-                bend_right = third * ((next_right[h] - right[h]) - slope)
-                parts.append(upwind(north * coef[k][OPEN_NORTH][h] + coef[k][FLOW_NORTH][h], mid + right[h], slope,
-                                    bend, bend_right))
-            cross.append(parts)
+            bend_right = (jnp.where(last_lane, bend_roll[k][1], bend_roll[k][0]), bend_roll[k][1])
+            cross.append([
+                upwind(north * coef[k][OPEN_NORTH][h] + coef[k][FLOW_NORTH][h], level[k][h] + right[k][h],
+                       slope[k][h], bend[k][h], bend_right[h])
+                for h in sides
+            ])
         cross_roll = [[pltpu.roll(part, 1, 1) for part in cross[k]] for k in rows]
         slopes = [slope_here] + [tuple(level[k + 1][h] - level[k][h] for h in sides) for k in range(1, count + 1)]
         bends = [bend_here] + [
@@ -403,7 +406,9 @@
         for h in range(2):
             rows_ref[row, local, h * BLOCK : (h + 1) * BLOCK] = parts[h]
 
-    def strip(g, arrive):
+    @pl.loop(0, strips)
+    def _(g):
+        arrival(g).wait()
         local = pl.ds(pl.multiple_of(g * 8, 8), 8)
         comps = pl.ds(pl.multiple_of(first_comp + g * 8, 8), 8)
         east, north = east_ref[comps, :], north_ref[comps, :]
@@ -412,11 +417,9 @@
         state = (here, ahead, tuple(b - a for a, b in zip(here, ahead)), zero, zero)
 
         def eight(i, state):
-            if arrive:
-                block = rows_ref.at[pl.ds(8 * i, 8)]
-                pltpu.make_async_copy(block, block, row_sems.at[i]).wait()
+            block = jnp.swapaxes(energy_vmem[local, pl.ds(pl.multiple_of(8 * i, 8), 8), :], 0, 1)
             for first in range(0, 8, BATCH):
-                fresh = [rows_ref[8 * i + first + k, local, :] for k in range(BATCH)]
+                fresh = [block[first + k] for k in range(BATCH)]
                 state, done = cell_rows(8 * i + first, fresh, state, east, north)
                 for k in range(BATCH):
                     store_row(jnp.maximum(8 * i + first + k - EDGE, 0), local, done[k])
@@ -427,12 +430,6 @@
         state, done = cell_rows(row_count, fresh, state, east, north)
         for k in range(EDGE):
             store_row(row_count - EDGE + k, local, done[k])
-
-    strip(0, True)
-
-    @pl.loop(1, strips)
-    def _(g):
-        strip(g, False)
 
     group_rows = [8 * n for n in range(strips + with_fields)]
 
@@ -685,11 +682,12 @@
                 in_specs=in_specs,
                 out_specs=out_specs,
                 scratch_shapes=[
+                    pltpu.VMEM((comp_rows, row_count, col_count), f32),
                     pltpu.VMEM((row_count, comp_rows, col_count), f32),
                     pltpu.VMEM((row_count + 2 * EDGE, HALF_SEA + 1, 8, col_count), f32),
                     pltpu.VMEM((comp_rows + (8 if with_fields else 0), cells + BLOCK), f32),
                     pltpu.VMEM((height, cells), f32),
-                    pltpu.SemaphoreType.DMA((row_count // 8,)),
+                    pltpu.SemaphoreType.DMA((comp_rows // 8,)),
                     pltpu.SemaphoreType.DMA((2 * pieces + 1,)),
                 ],
             ),

time: 389 us -> 382 us (0.982)
  Pallas kernels: 220 us -> 213 us
    pallas_call x4, Pallas kernels: 150 us -> 142 us  [propagate(): pl.pallas_call(functools.partial(propagate_kernel, part, late, pieces), g...]
where the time goes in v7:
time: 382 us; the launch traced here: 380 us
  Pallas kernels  213 us (56%)
  waiting for transfers between devices  77.4 us (20%)
  starting transfers between devices  65.2 us (17%)
  local copies, waits for them, and re-layouts  14.3 us (4%)
  other arithmetic  9.32 us (2%)
    pallas_call x4, Pallas kernels, propagate(): pl.pallas_call(functools.partial(propagate_kernel, part, late, pieces), g...  142 us
    ppermute x9, waiting for transfers between devices, send(): lax.ppermute(after(piece, *wait), 'comp', route)  39.9 us
    pallas_call x4, Pallas kernels, packed_shards(): pl.pallas_call(interact_kernel, grid=(width // lanes,), in_specs=[pl.Bloc...  32.3 us
    ppermute x8, waiting for transfers between devices, send_back(): return lax.ppermute(after(piece, *waits), 'comp', pairs)  31.7 us
    pallas_call x2, Pallas kernels, finish(): pl.pallas_call(functools.partial(finish_kernel, CELL_CHUNKS), grid_spec=p...  31.5 us
    ppermute x9, starting transfers between devices, send(): lax.ppermute(after(piece, *wait), 'comp', route)  22.9 us
    ppermute x4, starting transfers between devices, packed_shards(): from_got[last].append(lax.ppermute(after(got_1[c], *waits), 'comp', across))  14.9 us
  transfers between devices with their start and end apart: 33, of which 11 were waited for; matrix products, arithmetic and copies ran while one was open for 4% of the time, Pallas kernels for 42%

profile of v7, /device:TPU:0, one launch (start us, length us, event | category | flops | bytes accessed | tf_op | source)
XLA Modules:
  0.0 379.7 jit_solution(8813496442639532877)
XLA Ops:
  2.5 7.0 %prepare.1 = (f32[260,8,256]{2,1,0:T(8,128)}, s32[2,128,128]{2,1,0:T(8,128)}, s32[2,128,128]{2,1,0:T(8,128)}, s32[8,256]{1,0:T(8,128)}, f32[144,128]{1,0:T(8,128)}, /*index=5*/f32[144,128]{1,0:T(8,128)}) custom-call(s32[3]{0:T(128)} %pad_add_fusion.7.base_ref, f32[32]{0:T(128)} %speed_ref.1, s32[256,256]{1,0:T(8,128)} %sea_ref.1, f32[256,256]{1,0:T(8,128)} %east_ref.1, ...), custom_call_target="tpu_custom_call" | custom-call | tf_op jit(solution)/shard_map/prepare/pallas_call | solution.py:621
  10.3 38.5 %propagate_early.2 = (f32[32,8192]{1,0:T(8,128)}, f32[32,8192]{1,0:T(8,128)}, f32[1,16384]{1,0:T(1,128)}, f32[72,16384]{1,0:T(8,128)}, f32[8,16384]{1,0:T(8,128)}, /*index=5*/f32[8,16384]{1,0:T(8,128)}) custom-call(s32[3]{0:T(128)} %pad_add_fusion.7.base_ref, s32[8,256]{1,0:T(8,128)} %get-tuple-element.95.table_ref, f32[144,128,256]{2,1,0:T(8,128)} %energy_ref.7, ...), custom_call_target="tpu_custom_call" | custom-call | flops 78643200 | bytes 62914560 | tf_op jit(solution)/shard_map/propagate_early/pallas_call | solution.py:677
  53.3 32.7 %propagate_late.2 = (f32[40,8192]{1,0:T(8,128)}, f32[40,8192]{1,0:T(8,128)}, f32[1,16384]{1,0:T(1,128)}, f32[72,16384]{1,0:T(8,128)}) custom-call(s32[3]{0:T(128)} %pad_add_fusion.7.base_ref, s32[8,256]{1,0:T(8,128)} %get-tuple-element.95.table_ref, f32[144,128,256]{2,1,0:T(8,128)} %energy_ref.7, ...), custom_call_target="tpu_custom_call", output_to_operand_aliasing={{3}: (10, {})} | custom-call | flops 62914560 | bytes 62914560 | tf_op jit(solution)/shard_map/propagate_late/pallas_call | solution.py:677
  86.0 3.8 %collective-permute-start.2 = (f32[40,8192]{1,0:T(8,128)}, f32[40,8192]{1,0:T(8,128)S(1)}, u32[]{:S(2)}, u32[]{:S(2)}) collective-permute-start(f32[40,8192]{1,0:T(8,128)} %get-tuple-element.93), channel_id=1, source_target_pairs={{0,2},{2,0},{4,6},{6,4},{8,10},{10,8},{12,14},{14,12},{1,3},{3,1},... | collective-permute-start | bytes 3932168 | tf_op jit(solution)/shard_map/ppermute | solution.py:711
  91.5 5.5 %collective-permute-start.3 = (f32[32,8192]{1,0:T(8,128)}, f32[32,8192]{1,0:T(8,128)}, u32[]{:S(2)}, u32[]{:S(2)}) collective-permute-start(f32[32,8192]{1,0:T(8,128)} %collective-permute-done.1.refs_10_), channel_id=1, source_target_pairs={{6,2},{0,4},{10,6},{4,8},{14,10},{8,12},{7,3},{1,5},{11,7},{5,9},{... | collective-permute-start | bytes 3145736 | tf_op jit(solution)/shard_map/ppermute | solution.py:711
  100.1 38.0 %propagate_early.3 = (f32[32,8192]{1,0:T(8,128)}, f32[32,8192]{1,0:T(8,128)}, f32[1,16384]{1,0:T(1,128)}, f32[72,16384]{1,0:T(8,128)}, f32[8,16384]{1,0:T(8,128)}) custom-call(s32[3]{0:T(128)} %pad_add_fusion.7.base_ref, s32[8,256]{1,0:T(8,128)} %get-tuple-element.95.table_ref, f32[144,128,256]{2,1,0:T(8,128)} %energy_ref.7, f32[144,2,256]{2,1,0:T(2,128)} %copy-done.4, ...), custom_call_target="tpu_custom_call" | custom-call | flops 78643200 | bytes 62914560 | tf_op jit(solution)/shard_map/propagate_early/pallas_call | solution.py:677
  139.6 32.9 %propagate_late.3 = (f32[40,2048]{1,0:T(8,128)}, f32[40,2048]{1,0:T(8,128)}, f32[40,2048]{1,0:T(8,128)}, f32[40,2048]{1,0:T(8,128)}, f32[40,2048]{1,0:T(8,128)},...) custom-call(s32[3]{0:T(128)} %pad_add_fusion.7.base_ref, ...), custom_call_target="tpu_custom_call", output_to_operand_aliasing={{9}: (10, {})} | custom-call | flops 62914560 | bytes 62914560 | tf_op jit(solution)/shard_map/propagate_late/pallas_call | solution.py:677
  184.4 22.2 %collective-permute-done.9.refs_3_ = f32[40,8192]{1,0:T(8,128)S(1)} collective-permute-done((f32[40,8192]{1,0:T(8,128)S(1)}, f32[40,8192]{1,0:T(8,128)S(1)}, u32[]{:S(2)}, u32[]{:S(2)}) %collective-permute-start.9) | collective-permute-done | bytes 1310752 | tf_op jit(solution)/shard_map/ppermute | solution.py:711
  206.5 4.4 %collective-permute-start.10 = (f32[32,8192]{1,0:T(8,128)}, f32[32,8192]{1,0:T(8,128)S(1)}, u32[]{:S(2)}, u32[]{:S(2)}) collective-permute-start(f32[32,8192]{1,0:T(8,128)} %collective-permute-done.8.refs_8_), channel_id=1, source_target_pairs={{6,2},{0,4},{10,6},{4,8},{14,10},{8,12},{7,3},{1,5},{11,7},{5,9},{... | collective-permute-start | bytes 3145736 | tf_op jit(solution)/shard_map/ppermute | solution.py:711
  214.1 17.7 %collective-permute-done.10.refs_0_ = f32[32,8192]{1,0:T(8,128)S(1)} collective-permute-done((f32[32,8192]{1,0:T(8,128)}, f32[32,8192]{1,0:T(8,128)S(1)}, u32[]{:S(2)}, u32[]{:S(2)}) %collective-permute-start.10) | collective-permute-done | bytes 1048608 | tf_op jit(solution)/shard_map/ppermute | solution.py:711
  231.8 5.0 %collective-permute-start.12 = (f32[40,2048]{1,0:T(8,128)}, f32[40,2048]{1,0:T(8,128)}, u32[]{:S(2)}, u32[]{:S(2)}) collective-permute-start(f32[40,2048]{1,0:T(8,128)} %collective-permute-done.11.refs_9_), channel_id=1, source_target_pairs={{6,2},{0,4},{10,6},{4,8},{14,10},{8,12},{7,3},{1,5},{11,7},{5,9},{... | collective-permute-start | bytes 983048 | tf_op jit(solution)/shard_map/ppermute | solution.py:791
  247.4 4.1 %collective-permute-start.7 = (f32[1,16384]{1,0:T(1,128)S(1)}, f32[1,16384]{1,0:T(1,128)S(1)}, u32[]{:S(2)}, u32[]{:S(2)}) collective-permute-start(f32[1,16384]{1,0:T(1,128)S(1)} %add.261), channel_id=1, source_target_pairs={{0,8},{2,10},{4,12},{6,14},{8,0},{10,2},{12,4},{14,6},{1,9},{3,11}... | collective-permute-start | bytes 196616 | tf_op jit(solution)/shard_map/ppermute | solution.py:751
  251.5 8.1 %interact_cells.4 = (f32[144,2048]{1,0:T(8,128)}, f32[72,2048]{1,0:T(8,128)}, f32[72,2048]{1,0:T(8,128)}) custom-call(bf16[6,288,216]{2,1,0:T(8,128)(2,1)} %stack.28.table_ref, bf16[288,864]{1,0:T(8,128)(2,1)} %concatenate.40.spread_ref, f32[432,1]{1,0:T(8,128)} %copy.49.coupling_ref, f32[32,8192]{1,0:T(8,128)} %copy-done.3, ...), custom_call_target="tpu_custom_call" | custom-call | flops 2548039680 | bytes 20971520 | tf_op jit(solution)/shard_map/interact_cells/pallas_call | solution.py:802
  269.2 8.1 %interact_cells.5 = (f32[144,2048]{1,0:T(8,128)}, f32[72,2048]{1,0:T(8,128)}, f32[72,2048]{1,0:T(8,128)}) custom-call(bf16[6,288,216]{2,1,0:T(8,128)(2,1)} %stack.28.table_ref, bf16[288,864]{1,0:T(8,128)(2,1)} %concatenate.40.spread_ref, f32[432,1]{1,0:T(8,128)} %copy.49.coupling_ref, f32[32,8192]{1,0:T(8,128)} %copy-done.3, f32[40,2048]{1,0:T(8,128)} %copy-done.17, ...), custom_call_target="tpu_custom_call" | custom-call | flops 2548039680 | bytes 20971520 | tf_op jit(solution)/shard_map/interact_cells/pallas_call | solution.py:802
  277.2 3.8 %collective-permute-done.30.refs_5_ = f32[72,2048]{1,0:T(8,128)S(1)} collective-permute-done((f32[72,2048]{1,0:T(8,128)}, f32[72,2048]{1,0:T(8,128)S(1)}, u32[]{:S(2)}, u32[]{:S(2)}) %collective-permute-start.30) | collective-permute-done | bytes 589856 | tf_op jit(solution)/shard_map/ppermute | solution.py:825
  282.6 8.1 %interact_cells.6 = (f32[144,2048]{1,0:T(8,128)}, f32[72,2048]{1,0:T(8,128)}, f32[72,2048]{1,0:T(8,128)}) custom-call(bf16[6,288,216]{2,1,0:T(8,128)(2,1)} %stack.28.table_ref, bf16[288,864]{1,0:T(8,128)(2,1)} %concatenate.40.spread_ref, f32[432,1]{1,0:T(8,128)} %copy.49.coupling_ref, f32[32,8192]{1,0:T(8,128)} %copy-done.3, f32[40,2048]{1,0:T(8,128)} %copy-done.16, ...), custom_call_target="tpu_custom_call" | custom-call | flops 2548039680 | bytes 20971520 | tf_op jit(solution)/shard_map/interact_cells/pallas_call | solution.py:802
  295.0 5.0 %collective-permute-start.23 = (f32[40,2048]{1,0:T(8,128)}, f32[40,2048]{1,0:T(8,128)S(1)}, u32[]{:S(2)}, u32[]{:S(2)}) collective-permute-start(f32[40,2048]{1,0:T(8,128)} %collective-permute-done.22.refs_9_), channel_id=1, source_target_pairs={{6,2},{0,4},{10,6},{4,8},{14,10},{8,12},{7,3},{1,5},{11,7},{5,9},{... | collective-permute-start | bytes 983048 | tf_op jit(solution)/shard_map/ppermute | solution.py:791
  305.4 8.1 %interact_cells.7 = (f32[144,2048]{1,0:T(8,128)}, f32[72,2048]{1,0:T(8,128)}, f32[72,2048]{1,0:T(8,128)}) custom-call(bf16[6,288,216]{2,1,0:T(8,128)(2,1)} %stack.28.table_ref, bf16[288,864]{1,0:T(8,128)(2,1)} %concatenate.40.spread_ref, f32[432,1]{1,0:T(8,128)} %copy.49.coupling_ref, f32[32,8192]{1,0:T(8,128)} %copy-done.3, f32[40,2048]{1,0:T(8,128)} %copy-done.19, ...), custom_call_target="tpu_custom_call" | custom-call | flops 2548039680 | bytes 20971520 | tf_op jit(solution)/shard_map/interact_cells/pallas_call | solution.py:802
  313.5 3.2 collective-permute-start.32
  324.1 7.5 %collective-permute-done.32.refs_8_ = f32[72,2048]{1,0:T(8,128)S(1)} collective-permute-done((f32[72,2048]{1,0:T(8,128)}, f32[72,2048]{1,0:T(8,128)S(1)}, u32[]{:S(2)}, u32[]{:S(2)}) %collective-permute-start.32) | collective-permute-done | bytes 589856 | tf_op jit(solution)/shard_map/ppermute | solution.py:825
  332.5 15.7 %finish_chunk.2.refs_9_ = f32[144,128,256]{2,1,0:T(8,128)} custom-call(s32[3]{0:T(128)} %pad_add_fusion.7.base_ref, s32[8,256]{1,0:T(8,128)} %get-tuple-element.95.table_ref, s32[2,128,128]{2,1,0:T(8,128)} %get-tuple-element.79.place_ref, f32[1,16384]{1,0:T(1,128)} %broadcast_multiply_fusion, f32[8,16384]{1,0:T(8,128)} %get-tuple-element.86.refs_0_.fields_ref, ...), custom_call_target="tpu_custom_call" | custom-call | flops 47185920 | bytes 104857600 | tf_op jit(solution)/shard_map/finish_chunk/pallas_call | solution.py:850
  348.2 8.7 %collective-permute-done.28.refs_7_ = f32[72,2048]{1,0:T(8,128)S(1)} collective-permute-done((f32[72,2048]{1,0:T(8,128)}, f32[72,2048]{1,0:T(8,128)S(1)}, u32[]{:S(2)}, u32[]{:S(2)}) %collective-permute-start.28) | collective-permute-done | bytes 589856 | tf_op jit(solution)/shard_map/ppermute | solution.py:825
  356.9 6.3 %collective-permute-done.29.refs_8_ = f32[72,2048]{1,0:T(8,128)S(1)} collective-permute-done((f32[72,2048]{1,0:T(8,128)}, f32[72,2048]{1,0:T(8,128)S(1)}, u32[]{:S(2)}, u32[]{:S(2)}) %collective-permute-start.29) | collective-permute-done | bytes 589856 | tf_op jit(solution)/shard_map/ppermute | solution.py:825
  364.0 15.7 %finish_chunk.3 = f32[144,128,256]{2,1,0:T(8,128)} custom-call(s32[3]{0:T(128)} %pad_add_fusion.7.base_ref, s32[8,256]{1,0:T(8,128)} %get-tuple-element.95.table_ref, s32[2,128,128]{2,1,0:T(8,128)} %get-tuple-element.79.place_ref, f32[1,16384]{1,0:T(1,128)} %broadcast_multiply_fusion, ...), custom_call_target="tpu_custom_call", output_to_operand_aliasing={{}: (16, {})} | custom-call | flops 47185920 | bytes 104857600 | tf_op jit(solution)/shard_map/finish_chunk/pallas_call | solution.py:850
  (145 shorter events, 68.8 us)
Async XLA Ops:
  48.9 42.6 %collective-permute-start.1 = (f32[32,8192]{1,0:T(8,128)}, f32[32,8192]{1,0:T(8,128)}, u32[]{:S(2)}, u32[]{:S(2)}) collective-permute-start(f32[32,8192]{1,0:T(8,128)} %get-tuple-element.90), channel_id=1, source_target_pairs={{0,2},{2,0},{4,6},{6,4},{8,10},{10,8},{12,14},{14,12},{1,3},{3,1},... | collective-permute-start | bytes 3145736 | tf_op jit(solution)/shard_map/ppermute | solution.py:711
  52.0 186.9 %collective-permute-start.13 = (f32[32,8192]{1,0:T(8,128)}, f32[32,8192]{1,0:T(8,128)}, u32[]{:S(2)}, u32[]{:S(2)}) collective-permute-start(f32[32,8192]{1,0:T(8,128)} %get-tuple-element.111.refs_4_), channel_id=1, source_target_pairs={{2,6},{4,0},{6,10},{8,4},{10,14},{12,8},{3,7},{5,1},{7,11},{9,5},{... | collective-permute-start | bytes 3145736 | tf_op jit(solution)/shard_map/ppermute | solution.py:711
  86.0 52.1 %collective-permute-start.2 = (f32[40,8192]{1,0:T(8,128)}, f32[40,8192]{1,0:T(8,128)S(1)}, u32[]{:S(2)}, u32[]{:S(2)}) collective-permute-start(f32[40,8192]{1,0:T(8,128)} %get-tuple-element.93), channel_id=1, source_target_pairs={{0,2},{2,0},{4,6},{6,4},{8,10},{10,8},{12,14},{14,12},{1,3},{3,1},... | collective-permute-start | bytes 3932168 | tf_op jit(solution)/shard_map/ppermute | solution.py:711
  89.8 49.7 %collective-permute-start.4 = (f32[40,8192]{1,0:T(8,128)}, f32[40,8192]{1,0:T(8,128)S(1)}, u32[]{:S(2)}, u32[]{:S(2)}) collective-permute-start(f32[40,8192]{1,0:T(8,128)} %get-tuple-element.94.refs_5_), channel_id=1, source_target_pairs={{2,6},{4,0},{6,10},{8,4},{10,14},{12,8},{3,7},{5,1},{7,11},{9,5},{... | collective-permute-start | bytes 3932168 | tf_op jit(solution)/shard_map/ppermute | solution.py:711
  91.5 48.0 %collective-permute-start.3 = (f32[32,8192]{1,0:T(8,128)}, f32[32,8192]{1,0:T(8,128)}, u32[]{:S(2)}, u32[]{:S(2)}) collective-permute-start(f32[32,8192]{1,0:T(8,128)} %collective-permute-done.1.refs_10_), channel_id=1, source_target_pairs={{6,2},{0,4},{10,6},{4,8},{14,10},{8,12},{7,3},{1,5},{11,7},{5,9},{... | collective-permute-start | bytes 3145736 | tf_op jit(solution)/shard_map/ppermute | solution.py:711
  138.1 42.1 %collective-permute-start.8 = (f32[32,8192]{1,0:T(8,128)}, f32[32,8192]{1,0:T(8,128)}, u32[]{:S(2)}, u32[]{:S(2)}) collective-permute-start(f32[32,8192]{1,0:T(8,128)} %get-tuple-element.106), channel_id=1, source_target_pairs={{0,2},{2,0},{4,6},{6,4},{8,10},{10,8},{12,14},{14,12},{1,3},{3,1},... | collective-permute-start | bytes 3145736 | tf_op jit(solution)/shard_map/ppermute | solution.py:711
  138.2 42.1 %collective-permute-start.14 = (f32[32,8192]{1,0:T(8,128)}, f32[32,8192]{1,0:T(8,128)}, u32[]{:S(2)}, u32[]{:S(2)}) collective-permute-start(f32[32,8192]{1,0:T(8,128)} %get-tuple-element.112.refs_6_), channel_id=1, source_target_pairs={{2,6},{4,0},{6,10},{8,4},{10,14},{12,8},{3,7},{5,1},{7,11},{9,5},{... | collective-permute-start | bytes 3145736 | tf_op jit(solution)/shard_map/ppermute | solution.py:711
  177.6 29.0 %collective-permute-start.9 = (f32[40,8192]{1,0:T(8,128)S(1)}, f32[40,8192]{1,0:T(8,128)S(1)}, u32[]{:S(2)}, u32[]{:S(2)}) collective-permute-start(f32[40,8192]{1,0:T(8,128)S(1)} %collective-permute-done.2.refs_11_), channel_id=1, source_target_pairs={{6,2},{0,4},{10,6},{4,8},{14,10},{8,12},{7,3},{1,5},{11,7},{5,9},{... | collective-permute-start | bytes 3932168 | tf_op jit(solution)/shard_map/ppermute | solution.py:711
  180.2 31.7 %collective-permute-start.11 = (f32[40,2048]{1,0:T(8,128)}, f32[40,2048]{1,0:T(8,128)}, u32[]{:S(2)}, u32[]{:S(2)}) collective-permute-start(f32[40,2048]{1,0:T(8,128)} %get-tuple-element.109), channel_id=1, source_target_pairs={{0,2},{2,0},{4,6},{6,4},{8,10},{10,8},{12,14},{14,12},{1,3},{3,1},... | collective-permute-start | bytes 983048 | tf_op jit(solution)/shard_map/ppermute | solution.py:746
  180.3 57.3 %collective-permute-start.16 = (f32[40,2048]{1,0:T(8,128)}, f32[40,2048]{1,0:T(8,128)}, u32[]{:S(2)}, u32[]{:S(2)}) collective-permute-start(f32[40,2048]{1,0:T(8,128)} %get-tuple-element.117), channel_id=1, source_target_pairs={{0,2},{2,0},{4,6},{6,4},{8,10},{10,8},{12,14},{14,12},{1,3},{3,1},... | collective-permute-start | bytes 983048 | tf_op jit(solution)/shard_map/ppermute | solution.py:746
  182.3 63.7 %collective-permute-start.15 = (f32[40,2048]{1,0:T(8,128)}, f32[40,2048]{1,0:T(8,128)}, u32[]{:S(2)}, u32[]{:S(2)}) collective-permute-start(f32[40,2048]{1,0:T(8,128)} %get-tuple-element.114.refs_7_), channel_id=1, source_target_pairs={{2,6},{4,0},{6,10},{8,4},{10,14},{12,8},{3,7},{5,1},{7,11},{9,5},{... | collective-permute-start | bytes 983048 | tf_op jit(solution)/shard_map/ppermute | solution.py:747
  206.5 25.3 %collective-permute-start.10 = (f32[32,8192]{1,0:T(8,128)}, f32[32,8192]{1,0:T(8,128)S(1)}, u32[]{:S(2)}, u32[]{:S(2)}) collective-permute-start(f32[32,8192]{1,0:T(8,128)} %collective-permute-done.8.refs_8_), channel_id=1, source_target_pairs={{6,2},{0,4},{10,6},{4,8},{14,10},{8,12},{7,3},{1,5},{11,7},{5,9},{... | collective-permute-start | bytes 3145736 | tf_op jit(solution)/shard_map/ppermute | solution.py:711
  211.9 29.7 %collective-permute-start.6 = (f32[1,16384]{1,0:T(1,128)S(1)}, f32[1,16384]{1,0:T(1,128)S(1)}, u32[]{:S(2)}, u32[]{:S(2)}) collective-permute-start(f32[1,16384]{1,0:T(1,128)S(1)} %fusion), channel_id=1, source_target_pairs={{0,4},{2,6},{4,0},{6,2},{8,12},{10,14},{12,8},{14,10},{1,5},{3,7},... | collective-permute-start | bytes 196616 | tf_op jit(solution)/shard_map/ppermute | solution.py:750
  237.6 27.0 %collective-permute-start.18 = (f32[40,2048]{1,0:T(8,128)}, f32[40,2048]{1,0:T(8,128)}, u32[]{:S(2)}, u32[]{:S(2)}) collective-permute-start(f32[40,2048]{1,0:T(8,128)} %get-tuple-element.120.refs_7_), channel_id=1, source_target_pairs={{2,6},{4,0},{6,10},{8,4},{10,14},{12,8},{3,7},{5,1},{7,11},{9,5},{... | collective-permute-start | bytes 983048 | tf_op jit(solution)/shard_map/ppermute | solution.py:747
  239.0 20.6 %collective-permute-start.19 = (f32[40,2048]{1,0:T(8,128)}, f32[40,2048]{1,0:T(8,128)}, u32[]{:S(2)}, u32[]{:S(2)}) collective-permute-start(f32[40,2048]{1,0:T(8,128)} %get-tuple-element.123), channel_id=1, source_target_pairs={{0,2},{2,0},{4,6},{6,4},{8,10},{10,8},{12,14},{14,12},{1,3},{3,1},... | collective-permute-start | bytes 983048 | tf_op jit(solution)/shard_map/ppermute | solution.py:746
  241.6 20.9 %collective-permute-start.22 = (f32[40,2048]{1,0:T(8,128)}, f32[40,2048]{1,0:T(8,128)}, u32[]{:S(2)}, u32[]{:S(2)}) collective-permute-start(f32[40,2048]{1,0:T(8,128)} %get-tuple-element.129), channel_id=1, source_target_pairs={{0,2},{2,0},{4,6},{6,4},{8,10},{10,8},{12,14},{14,12},{1,3},{3,1},... | collective-permute-start | bytes 983048 | tf_op jit(solution)/shard_map/ppermute | solution.py:746
  246.1 35.0 %collective-permute-start.21 = (f32[40,2048]{1,0:T(8,128)S(1)}, f32[40,2048]{1,0:T(8,128)S(1)}, u32[]{:S(2)}, u32[]{:S(2)}) collective-permute-start(f32[40,2048]{1,0:T(8,128)S(1)} %copy-done.14), channel_id=1, source_target_pairs={{2,6},{4,0},{6,10},{8,4},{10,14},{12,8},{3,7},{5,1},{7,11},{9,5},{... | collective-permute-start | bytes 983048 | tf_op jit(solution)/shard_map/ppermute | solution.py:747
  262.6 18.5 %collective-permute-start.20 = (f32[40,2048]{1,0:T(8,128)}, f32[40,2048]{1,0:T(8,128)S(1)}, u32[]{:S(2)}, u32[]{:S(2)}) collective-permute-start(f32[40,2048]{1,0:T(8,128)} %collective-permute-done.19.refs_9_), channel_id=1, source_target_pairs={{6,2},{0,4},{10,6},{4,8},{14,10},{8,12},{7,3},{1,5},{11,7},{5,9},{... | collective-permute-start | bytes 983048 | tf_op jit(solution)/shard_map/ppermute | solution.py:791
  264.6 29.1 %collective-permute-start.25 = (f32[72,2048]{1,0:T(8,128)}, f32[72,2048]{1,0:T(8,128)S(1)}, u32[]{:S(2)}, u32[]{:S(2)}) collective-permute-start(f32[72,2048]{1,0:T(8,128)} %get-tuple-element.135), channel_id=1, source_target_pairs={{0,2},{2,0},{4,6},{6,4},{8,10},{10,8},{12,14},{14,12},{1,3},{3,1},... | collective-permute-start | bytes 1769480 | tf_op jit(solution)/shard_map/ppermute | solution.py:825
  281.1 32.4 %collective-permute-start.31 = (f32[72,2048]{1,0:T(8,128)}, f32[72,2048]{1,0:T(8,128)S(1)}, u32[]{:S(2)}, u32[]{:S(2)}) collective-permute-start(f32[72,2048]{1,0:T(8,128)} %get-tuple-element.148), channel_id=1, source_target_pairs={{0,2},{2,0},{4,6},{6,4},{8,10},{10,8},{12,14},{14,12},{1,3},{3,1},... | collective-permute-start | bytes 1769480 | tf_op jit(solution)/shard_map/ppermute | solution.py:825
  293.7 25.3 %collective-permute-start.26 = (f32[72,2048]{1,0:T(8,128)}, f32[72,2048]{1,0:T(8,128)S(1)}, u32[]{:S(2)}, u32[]{:S(2)}) collective-permute-start(f32[72,2048]{1,0:T(8,128)} %get-tuple-element.138), channel_id=1, source_target_pairs={{0,2},{2,0},{4,6},{6,4},{8,10},{10,8},{12,14},{14,12},{1,3},{3,1},... | collective-permute-start | bytes 1769480 | tf_op jit(solution)/shard_map/ppermute | solution.py:825
  319.0 29.2 %collective-permute-start.27 = (f32[72,2048]{1,0:T(8,128)}, f32[72,2048]{1,0:T(8,128)S(1)}, u32[]{:S(2)}, u32[]{:S(2)}) collective-permute-start(f32[72,2048]{1,0:T(8,128)} %get-tuple-element.139), channel_id=1, source_target_pairs={{0,2},{2,0},{4,6},{6,4},{8,10},{10,8},{12,14},{14,12},{1,3},{3,1},... | collective-permute-start | bytes 1769480 | tf_op jit(solution)/shard_map/ppermute | solution.py:825
  319.0 37.8 %collective-permute-start.28 = (f32[72,2048]{1,0:T(8,128)}, f32[72,2048]{1,0:T(8,128)S(1)}, u32[]{:S(2)}, u32[]{:S(2)}) collective-permute-start(f32[72,2048]{1,0:T(8,128)} %get-tuple-element.141), channel_id=1, source_target_pairs={{0,2},{2,0},{4,6},{6,4},{8,10},{10,8},{12,14},{14,12},{1,3},{3,1},... | collective-permute-start | bytes 1769480 | tf_op jit(solution)/shard_map/ppermute | solution.py:825
  321.0 42.1 %collective-permute-start.29 = (f32[72,2048]{1,0:T(8,128)}, f32[72,2048]{1,0:T(8,128)S(1)}, u32[]{:S(2)}, u32[]{:S(2)}) collective-permute-start(f32[72,2048]{1,0:T(8,128)} %get-tuple-element.143), channel_id=1, source_target_pairs={{0,2},{2,0},{4,6},{6,4},{8,10},{10,8},{12,14},{14,12},{1,3},{3,1},... | collective-permute-start | bytes 1769480 | tf_op jit(solution)/shard_map/ppermute | solution.py:825
  (34 other events, 665.5 us)

commit v8 on v7

--- a/solution.py
+++ b/solution.py
@@ -313,14 +313,14 @@
 def propagate_kernel(part, late, pieces, base_ref, table_ref, energy_ref, halo_ref, coef_ref, index_ref, east_ref,
                      north_ref, *refs):
     refs = list(refs)
-    with_fields = part == 0 and not late
+    with_fields = part == 0 and late == 0
     fields_ref = None if with_fields else refs.pop(0)
     seam_ref = refs.pop(0) if late else None
     if late:
         refs.pop(0)
     piece_refs = [refs.pop(0) for _ in range(2 * pieces)]
     sum_ref, full_ref = refs.pop(0), refs.pop(0)
-    seam_out_ref = None if late else refs.pop(0)
+    seam_out_ref = refs.pop(0) if late == 0 else None
     fields_out_ref = refs.pop(0) if with_fields else None
     energy_vmem, rows_ref, spread_ref, wide_ref, result_ref, strip_sems, out_sems = refs
     row_count, comp_count, col_count = rows_ref.shape
@@ -328,7 +328,7 @@
     sent_rows = piece_refs[0].shape[0]
     cells = result_ref.shape[1]
     first_row = base_ref[0]
-    first_comp = pl.multiple_of((part + base_ref[1] * (1 - 2 * part)) * 2 * NTH + late * EARLY, 8)
+    first_comp = pl.multiple_of((part + base_ref[1] * (1 - 2 * part)) * 2 * NTH + (EARLY if late else 0), 8)
     lane = lax.broadcasted_iota(jnp.int32, (8, BLOCK), 1)
     first_lane, last_lane = lane == 0, lane == BLOCK - 1
     third = 1.0 / 3.0
@@ -455,11 +455,9 @@
     tile_width = 2 * BLOCK
     height = result_ref.shape[0]
     comp_row = lax.broadcasted_iota(jnp.int32, (height, tile_width), 0)
-    start = height - NTH if late else 0
-    end = start + NTH - 1
-    mixed = slice(0, 8) if late else slice(height - 8, height)
-    mixed_row = comp_row[mixed]
-    in_circle = (mixed_row >= start) & (mixed_row <= end)
+    starts = {0: [0], 1: [height - NTH], None: [0, NTH]}[late]
+    mixed = {0: slice(height - 8, height), 1: slice(0, 8), None: slice(0, 0)}[late]
+    in_circle = (comp_row[:8] + mixed.start >= starts[0]) & (comp_row[:8] + mixed.start < starts[0] + NTH)
 
     @pl.loop(0, cells // tile_width, unroll=2)
     def _(i):
@@ -483,20 +481,23 @@
             parts = [rolled[: tile.start], fixed, rolled[tile.stop :]]
             return jnp.concatenate([part for part in parts if part.shape[0]], axis=0)
 
-        above = with_row(above, end, level[start : start + 1, :])
-        below = with_row(below, start, level[end : end + 1, :])
+        for start in starts:
+            end = start + NTH - 1
+            above = with_row(above, end, level[start : start + 1, :])
+            below = with_row(below, start, level[end : end + 1, :])
         turned = stay * level - backward * above + forward * below
-        partial = jnp.where(in_circle, turned[mixed], 0.0)
+        partial = jnp.zeros((8, tile_width), jnp.float32)
         for first in range(0, height, 8):
             rows = slice(first, first + 8)
-            if first == mixed.start:
+            if rows == mixed:
                 result_ref[rows, source] = jnp.where(in_circle, turned[rows], level[rows])
+                partial += jnp.where(in_circle, turned[rows], 0.0)
             else:
                 result_ref[rows, source] = turned[rows]
                 partial += turned[rows]
         sum_ref[:, source] = jnp.sum(partial, axis=0, keepdims=True)
 
-    if not late:
+    if late == 0:
         seam_out_ref[...] = result_ref[sent_rows:, :]
     width = cells // (2 * pieces)
     copies = []
@@ -511,9 +512,13 @@
         copy.wait()
 
 
-def interact_kernel(table_ref, spread_ref, coupling_ref, *refs):
-    own_ref, back_0_ref, back_1_ref, delta_ref = refs[16:]
-    window = [jnp.concatenate([refs[2 * j][...], refs[2 * j + 1][...]], axis=0) for j in range(8)]
+def interact_kernel(counts, table_ref, spread_ref, coupling_ref, *refs):
+    own_ref, back_0_ref, back_1_ref, delta_ref = refs[sum(counts) :]
+    window = []
+    for j, count in enumerate(counts):
+        first = sum(counts[:j])
+        parts = [ref[...] for ref in refs[first : first + count]]
+        window.append(parts[0] if count == 1 else jnp.concatenate(parts, axis=0))
     comps = window[0].shape[0]
     for j in range(1, 7):
         level = window[j]
@@ -650,10 +655,10 @@
         return pl.BlockSpec((GROUP, lanes), lambda s, b, t: (group_at(part, b) + s, 0))
 
     def propagate(part, late, table, fields=None, seam=None, full=None):
-        pieces = CELL_CHUNKS if part and late else 1
-        comp_rows = comps - EARLY if late else EARLY
-        sent_rows = comps - EARLY + 8 if late else EARLY - 8
-        height = EARLY
+        pieces = CELL_CHUNKS if part else 1
+        comp_rows = {0: EARLY, 1: comps - EARLY, None: comps}[late]
+        sent_rows = {0: EARLY - 8, 1: comps - EARLY + 8, None: comps}[late]
+        height = comps if late is None else EARLY
         anywhere = pl.BlockSpec(memory_space=pl.ANY)
         with_fields = fields is None
         inputs = [energy, halo_rows, coef, index, speed_east, speed_north]
@@ -668,7 +673,7 @@
             aliases = {len(inputs) + 1: 2 * pieces + 1}
         shapes = [(sent_rows, half // pieces)] * (2 * pieces) + [(1, cells), (comps, cells)]
         out_specs = [anywhere] * (2 * pieces) + [vmem, anywhere]
-        if not late:
+        if late == 0:
             shapes.append((8, cells))
             out_specs.append(vmem)
         if with_fields:
@@ -693,7 +698,7 @@
             ),
             out_shape=[jax.ShapeDtypeStruct(shape, f32) for shape in shapes],
             input_output_aliases=aliases,
-            name="propagate_late" if late else "propagate_early",
+            name={0: "propagate_early", 1: "propagate_late", None: "propagate_whole"}[late],
             compiler_params=params(VMEM_MIB),
             cost_estimate=pl.CostEstimate(
                 flops=60 * comp_rows * row_count * col_count, bytes_accessed=60 * MIB, transcendentals=0,
@@ -710,7 +715,7 @@
     def send(pieces, route, waits):
         return [lax.ppermute(after(piece, *wait), "comp", route) for piece, wait in zip(pieces, waits)]
 
-    stages = [(0, 0), (0, 1), (1, 0), (1, 1)]
+    stages = [(0, 0), (0, 1), (1, None)]
     kept, sent, got, from_own, from_got, level_sums, full = {}, {}, {}, {}, {}, [], {}
     fields = seam = before = None
     part_table = table
@@ -719,25 +724,23 @@
         kept[stage], sent[stage], extra = propagate(part, late, part_table, fields, seam, full.get(part))
         level_sums.append(extra[0])
         full[part] = extra[1]
-        seam = None if late else extra[2]
+        seam = extra[2] if late == 0 else None
         fields = extra[3] if fields is None else fields
         if stage == stages[-1]:
             break
         got[stage] = send(sent[stage], pairs, [[]])
         from_own[stage] = send(kept[stage], apart, [[]])
-        waits = [from_got[before][0]] if stage == stages[2] else []
+        waits = [from_got[before][0]] if before is not None else []
         from_got[stage] = send(got[stage], across, [waits])
         done = [extra[0]]
         if before is not None:
             done.append(got[before][0])
-            if stage == stages[2]:
-                done += [from_got[stages[0]][0], from_own[stages[1]][0]]
         part_table = after(table, *done)
         before = stage
     packed_fields = fields
     sums_0 = level_sums[0]
 
-    sums = level_sums[0] + level_sums[1] + level_sums[2] + level_sums[3]
+    sums = level_sums[0] + level_sums[1] + level_sums[2]
     partner_sums = lax.ppermute(sums, "comp", pairs)
     partner_sums = jnp.roll(partner_sums, half, axis=1)
     last, got_1, from_own_1 = stages[-1], [], []
@@ -789,9 +792,10 @@
     for c in chunk_range:
         waits = [from_got[before][0]] + ([from_got[last][c - 2]] if c >= 2 else [])
         from_got[last].append(lax.ppermute(after(got_1[c], *waits), "comp", across))
-        levels, level_specs = [], []
+        levels, level_specs, counts = [], [], []
         for group, part in groups:
-            for late in range(2):
+            counts.append(1 if part else 2)
+            for late in [None] if part else [0, 1]:
                 pieces = group[part, late]
                 single = len(pieces) == 1
                 levels.append(pieces[0 if single else c])
@@ -800,7 +804,7 @@
                     pl.BlockSpec((levels[-1].shape[0], lanes), functools.partial(lambda n, s: (0, n + s), skipped))
                 )
         own_part, part_0, part_1 = pl.pallas_call(
-            interact_kernel,
+            functools.partial(interact_kernel, tuple(counts)),
             grid=(width // lanes,),
             in_specs=[
                 pl.BlockSpec(lookup.shape, lambda s: (0, 0, 0)),

time: 382 us -> 364 us (0.953)
  Pallas kernels: 213 us -> 205 us
  starting transfers between devices: 65.2 us -> 57.7 us
    ppermute x9 -> x6, waiting for transfers between devices: 39.9 us -> 12.7 us  [send(): lax.ppermute(after(piece, *wait), 'comp', route)]
    ppermute x4, waiting for transfers between devices: 0.01 us -> 8.8 us  [packed_shards(): got_1.append(lax.ppermute(after(sent[last][c], *waits), 'comp', pairs))]
    pallas_call x4 -> x3, Pallas kernels: 142 us -> 134 us  [propagate(): pl.pallas_call(functools.partial(propagate_kernel, part, late, pieces), g...]
    ppermute x1, waiting for transfers between devices: 0.01 us -> 7.63 us  [packed_shards(): lax.ppermute(sums, 'comp', [(i, i ^ 2) for i in range(comp_count)])]
    ppermute x9 -> x6, starting transfers between devices: 22.9 us -> 16 us  [send(): lax.ppermute(after(piece, *wait), 'comp', route)]
    ppermute x8, waiting for transfers between devices: 31.7 us -> 37.9 us  [send_back(): return lax.ppermute(after(piece, *waits), 'comp', pairs)]
    ppermute x4, waiting for transfers between devices: 2.92 us -> 9.02 us  [packed_shards(): lax.ppermute(after(kept[last][c], from_own[before][0]), 'comp', apart)]
  transfers between devices with their start and end apart: 33 -> 30, of which waited for: 11 -> 10; matrix products, arithmetic and copies ran while one was open for 4% -> 3% of each run, Pallas kernels for 42% -> 42%
where the time goes in v8:
time: 364 us; the launch traced here: 363 us
  Pallas kernels  205 us (56%)
  waiting for transfers between devices  77.3 us (21%)
  starting transfers between devices  57.7 us (16%)
  local copies, waits for them, and re-layouts  16.2 us (4%)
  other arithmetic  5.83 us (2%)
    pallas_call x3, Pallas kernels, propagate(): pl.pallas_call(functools.partial(propagate_kernel, part, late, pieces), g...  134 us
    ppermute x8, waiting for transfers between devices, send_back(): return lax.ppermute(after(piece, *waits), 'comp', pairs)  37.9 us
    pallas_call x4, Pallas kernels, packed_shards(): pl.pallas_call(functools.partial(interact_kernel, tuple(counts)), grid=(w...  32.9 us
    pallas_call x2, Pallas kernels, finish(): pl.pallas_call(functools.partial(finish_kernel, CELL_CHUNKS), grid_spec=p...  31.5 us
    ppermute x4, starting transfers between devices, packed_shards(): from_got[last].append(lax.ppermute(after(got_1[c], *waits), 'comp', across))  16.8 us
    ppermute x6, starting transfers between devices, send(): lax.ppermute(after(piece, *wait), 'comp', route)  16 us
    ppermute x6, waiting for transfers between devices, send(): lax.ppermute(after(piece, *wait), 'comp', route)  12.7 us
    ppermute x4, waiting for transfers between devices, packed_shards(): lax.ppermute(after(kept[last][c], from_own[before][0]), 'comp', apart)  9.02 us
  transfers between devices with their start and end apart: 30, of which 10 were waited for; matrix products, arithmetic and copies ran while one was open for 3% of the time, Pallas kernels for 42%

profile of v8, /device:TPU:0, one launch (start us, length us, event | category | flops | bytes accessed | tf_op | source)
XLA Modules:
  0.0 362.8 jit_solution(10041806612844978257)
XLA Ops:
  2.5 7.0 %prepare.1 = (f32[260,8,256]{2,1,0:T(8,128)}, s32[2,128,128]{2,1,0:T(8,128)}, s32[2,128,128]{2,1,0:T(8,128)}, s32[8,256]{1,0:T(8,128)}, f32[144,128]{1,0:T(8,128)}, /*index=5*/f32[144,128]{1,0:T(8,128)}) custom-call(s32[3]{0:T(128)} %pad_add_fusion.7.base_ref, f32[32]{0:T(128)} %speed_ref.1, s32[256,256]{1,0:T(8,128)} %sea_ref.1, f32[256,256]{1,0:T(8,128)} %east_ref.1, ...), custom_call_target="tpu_custom_call" | custom-call | tf_op jit(solution)/shard_map/prepare/pallas_call | solution.py:626
  10.2 38.5 %propagate_early.1 = (f32[32,8192]{1,0:T(8,128)}, f32[32,8192]{1,0:T(8,128)}, f32[1,16384]{1,0:T(1,128)}, f32[72,16384]{1,0:T(8,128)}, f32[8,16384]{1,0:T(8,128)}, /*index=5*/f32[8,16384]{1,0:T(8,128)}) custom-call(s32[3]{0:T(128)} %pad_add_fusion.7.base_ref, s32[8,256]{1,0:T(8,128)} %get-tuple-element.85.table_ref, f32[144,128,256]{2,1,0:T(8,128)} %energy_ref.5, ...), custom_call_target="tpu_custom_call" | custom-call | flops 78643200 | bytes 62914560 | tf_op jit(solution)/shard_map/propagate_early/pallas_call | solution.py:682
  53.2 32.7 %propagate_late.1 = (f32[40,8192]{1,0:T(8,128)}, f32[40,8192]{1,0:T(8,128)}, f32[1,16384]{1,0:T(1,128)}, f32[72,16384]{1,0:T(8,128)}) custom-call(s32[3]{0:T(128)} %pad_add_fusion.7.base_ref, s32[8,256]{1,0:T(8,128)} %get-tuple-element.85.table_ref, f32[144,128,256]{2,1,0:T(8,128)} %energy_ref.5, ...), custom_call_target="tpu_custom_call", output_to_operand_aliasing={{3}: (10, {})} | custom-call | flops 62914560 | bytes 62914560 | tf_op jit(solution)/shard_map/propagate_late/pallas_call | solution.py:682
  85.9 3.8 %collective-permute-start.5 = (f32[40,8192]{1,0:T(8,128)}, f32[40,8192]{1,0:T(8,128)S(1)}, u32[]{:S(2)}, u32[]{:S(2)}) collective-permute-start(f32[40,8192]{1,0:T(8,128)} %get-tuple-element.95), channel_id=1, source_target_pairs={{0,2},{2,0},{4,6},{6,4},{8,10},{10,8},{12,14},{14,12},{1,3},{3,1},... | collective-permute-start | bytes 3932168 | tf_op jit(solution)/shard_map/ppermute | solution.py:716
  92.2 5.6 %collective-permute-start.7 = (f32[32,8192]{1,0:T(8,128)}, f32[32,8192]{1,0:T(8,128)}, u32[]{:S(2)}, u32[]{:S(2)}) collective-permute-start(f32[32,8192]{1,0:T(8,128)} %collective-permute-done.1.refs_7_), channel_id=1, source_target_pairs={{6,2},{0,4},{10,6},{4,8},{14,10},{8,12},{7,3},{1,5},{11,7},{5,9},{... | collective-permute-start | bytes 3145736 | tf_op jit(solution)/shard_map/ppermute | solution.py:716
  97.7 62.5 %propagate_whole.1 = (f32[72,2048]{1,0:T(8,128)}, f32[72,2048]{1,0:T(8,128)}, f32[72,2048]{1,0:T(8,128)}, f32[72,2048]{1,0:T(8,128)}, f32[72,2048]{1,0:T(8,128)}...) custom-call(s32[3]{0:T(128)} %pad_add_fusion.7.base_ref, ...), custom_call_target="tpu_custom_call" | custom-call | flops 141557760 | bytes 62914560 | tf_op jit(solution)/shard_map/propagate_whole/pallas_call | solution.py:682
  170.3 8.8 %collective-permute-done.6.refs_6_ = f32[72,2048]{1,0:T(8,128)} collective-permute-done((f32[72,2048]{1,0:T(8,128)}, f32[72,2048]{1,0:T(8,128)}, u32[]{:S(2)}, u32[]{:S(2)}) %collective-permute-start.6) | collective-permute-done | bytes 589856 | tf_op jit(solution)/shard_map/ppermute | solution.py:749
  179.1 12.7 %collective-permute-done.8.refs_2_ = f32[40,8192]{1,0:T(8,128)S(1)} collective-permute-done((f32[40,8192]{1,0:T(8,128)S(1)}, f32[40,8192]{1,0:T(8,128)S(1)}, u32[]{:S(2)}, u32[]{:S(2)}) %collective-permute-start.8) | collective-permute-done | bytes 1310752 | tf_op jit(solution)/shard_map/ppermute | solution.py:716
  192.9 5.2 %collective-permute-start.9 = (f32[72,2048]{1,0:T(8,128)}, f32[72,2048]{1,0:T(8,128)}, u32[]{:S(2)}, u32[]{:S(2)}) collective-permute-start(f32[72,2048]{1,0:T(8,128)} %collective-permute-done.6.refs_6_), channel_id=1, source_target_pairs={{6,2},{0,4},{10,6},{4,8},{14,10},{8,12},{7,3},{1,5},{11,7},{5,9},{... | collective-permute-start | bytes 1769480 | tf_op jit(solution)/shard_map/ppermute | solution.py:794
  201.7 7.6 %collective-permute-done.3 = f32[1,16384]{1,0:T(1,128)S(1)} collective-permute-done((f32[1,16384]{1,0:T(1,128)S(1)}, f32[1,16384]{1,0:T(1,128)S(1)}, u32[]{:S(2)}, u32[]{:S(2)}) %collective-permute-start.3) | collective-permute-done | bytes 65568 | tf_op jit(solution)/shard_map/ppermute | solution.py:753
  209.3 5.2 %collective-permute-start.14 = (f32[72,2048]{1,0:T(8,128)}, f32[72,2048]{1,0:T(8,128)}, u32[]{:S(2)}, u32[]{:S(2)}) collective-permute-start(f32[72,2048]{1,0:T(8,128)} %collective-permute-done.13.refs_6_), channel_id=1, source_target_pairs={{6,2},{0,4},{10,6},{4,8},{14,10},{8,12},{7,3},{1,5},{11,7},{5,9},{... | collective-permute-start | bytes 1769480 | tf_op jit(solution)/shard_map/ppermute | solution.py:794
  224.1 8.3 %interact_cells.4 = (f32[144,2048]{1,0:T(8,128)}, f32[72,2048]{1,0:T(8,128)}, f32[72,2048]{1,0:T(8,128)}) custom-call(bf16[6,288,216]{2,1,0:T(8,128)(2,1)} %stack.28.table_ref, bf16[288,864]{1,0:T(8,128)(2,1)} %concatenate.40.spread_ref, f32[432,1]{1,0:T(8,128)} %copy.48.coupling_ref, f32[72,2048]{1,0:T(8,128)} %collective-permute-done.9.refs_0_, ...), custom_call_target="tpu_custom_call" | custom-call | flops 2548039680 | bytes 20971520 | tf_op jit(solution)/shard_map/interact_cells/pallas_call | solution.py:806
  240.8 9.0 %collective-permute-done.15.refs_11_ = f32[72,2048]{1,0:T(8,128)S(1)} collective-permute-done((f32[72,2048]{1,0:T(8,128)S(1)}, f32[72,2048]{1,0:T(8,128)S(1)}, u32[]{:S(2)}, u32[]{:S(2)}) %collective-permute-start.15) | collective-permute-done | bytes 589856 | tf_op jit(solution)/shard_map/ppermute | solution.py:750
  251.1 8.7 %collective-permute-done.27.refs_5_ = f32[72,2048]{1,0:T(8,128)S(1)} collective-permute-done((f32[72,2048]{1,0:T(8,128)}, f32[72,2048]{1,0:T(8,128)S(1)}, u32[]{:S(2)}, u32[]{:S(2)}) %collective-permute-start.27) | collective-permute-done | bytes 589856 | tf_op jit(solution)/shard_map/ppermute | solution.py:829
  260.6 3.7 %collective-permute-start.20 = (f32[72,2048]{1,0:T(8,128)}, f32[72,2048]{1,0:T(8,128)S(1)}, u32[]{:S(2)}, u32[]{:S(2)}) collective-permute-start(f32[72,2048]{1,0:T(8,128)} %collective-permute-done.19.refs_6_), channel_id=1, source_target_pairs={{6,2},{0,4},{10,6},{4,8},{14,10},{8,12},{7,3},{1,5},{11,7},{5,9},{... | collective-permute-start | bytes 1769480 | tf_op jit(solution)/shard_map/ppermute | solution.py:794
  264.3 8.2 %interact_cells.5 = (f32[144,2048]{1,0:T(8,128)}, f32[72,2048]{1,0:T(8,128)}, f32[72,2048]{1,0:T(8,128)}) custom-call(bf16[6,288,216]{2,1,0:T(8,128)(2,1)} %stack.28.table_ref, bf16[288,864]{1,0:T(8,128)(2,1)} %concatenate.40.spread_ref, f32[432,1]{1,0:T(8,128)} %copy.48.coupling_ref, f32[72,2048]{1,0:T(8,128)} %collective-permute-done.14.refs_0_, ...), custom_call_target="tpu_custom_call" | custom-call | flops 2548039680 | bytes 20971520 | tf_op jit(solution)/shard_map/interact_cells/pallas_call | solution.py:806
  274.1 8.2 %interact_cells.6 = (f32[144,2048]{1,0:T(8,128)}, f32[72,2048]{1,0:T(8,128)}, f32[72,2048]{1,0:T(8,128)}) custom-call(bf16[6,288,216]{2,1,0:T(8,128)(2,1)} %stack.28.table_ref, bf16[288,864]{1,0:T(8,128)(2,1)} %concatenate.40.spread_ref, f32[432,1]{1,0:T(8,128)} %copy.48.coupling_ref, f32[72,2048]{1,0:T(8,128)} %copy-done.10, ...), custom_call_target="tpu_custom_call" | custom-call | flops 2548039680 | bytes 20971520 | tf_op jit(solution)/shard_map/interact_cells/pallas_call | solution.py:806
  285.3 8.2 %interact_cells.7 = (f32[144,2048]{1,0:T(8,128)}, f32[72,2048]{1,0:T(8,128)}, f32[72,2048]{1,0:T(8,128)}) custom-call(bf16[6,288,216]{2,1,0:T(8,128)(2,1)} %stack.28.table_ref, bf16[288,864]{1,0:T(8,128)(2,1)} %concatenate.40.spread_ref, f32[432,1]{1,0:T(8,128)} %copy.48.coupling_ref, f32[72,2048]{1,0:T(8,128)} %copy-done.9, ...), custom_call_target="tpu_custom_call" | custom-call | flops 2548039680 | bytes 20971520 | tf_op jit(solution)/shard_map/interact_cells/pallas_call | solution.py:806
  294.3 4.5 %collective-permute-done.23.refs_7_ = f32[72,2048]{1,0:T(8,128)S(1)} collective-permute-done((f32[72,2048]{1,0:T(8,128)}, f32[72,2048]{1,0:T(8,128)S(1)}, u32[]{:S(2)}, u32[]{:S(2)}) %collective-permute-start.23) | collective-permute-done | bytes 589856 | tf_op jit(solution)/shard_map/ppermute | solution.py:829
  305.0 6.5 %collective-permute-done.29.refs_8_ = f32[72,2048]{1,0:T(8,128)S(1)} collective-permute-done((f32[72,2048]{1,0:T(8,128)}, f32[72,2048]{1,0:T(8,128)S(1)}, u32[]{:S(2)}, u32[]{:S(2)}) %collective-permute-start.29) | collective-permute-done | bytes 589856 | tf_op jit(solution)/shard_map/ppermute | solution.py:829
  312.3 15.7 %finish_chunk.2.refs_9_ = f32[144,128,256]{2,1,0:T(8,128)} custom-call(s32[3]{0:T(128)} %pad_add_fusion.7.base_ref, s32[8,256]{1,0:T(8,128)} %get-tuple-element.85.table_ref, s32[2,128,128]{2,1,0:T(8,128)} %get-tuple-element.73.place_ref, f32[1,16384]{1,0:T(1,128)} %broadcast_multiply_fusion, f32[8,16384]{1,0:T(8,128)} %get-tuple-element.80.refs_0_.fields_ref, ...), custom_call_target="tpu_custom_call" | custom-call | flops 47185920 | bytes 104857600 | tf_op jit(solution)/shard_map/finish_chunk/pallas_call | solution.py:854
  328.1 8.7 %collective-permute-done.25.refs_7_ = f32[72,2048]{1,0:T(8,128)S(1)} collective-permute-done((f32[72,2048]{1,0:T(8,128)}, f32[72,2048]{1,0:T(8,128)S(1)}, u32[]{:S(2)}, u32[]{:S(2)}) %collective-permute-start.25) | collective-permute-done | bytes 589856 | tf_op jit(solution)/shard_map/ppermute | solution.py:829
  336.8 9.4 %collective-permute-done.26.refs_8_ = f32[72,2048]{1,0:T(8,128)S(1)} collective-permute-done((f32[72,2048]{1,0:T(8,128)}, f32[72,2048]{1,0:T(8,128)S(1)}, u32[]{:S(2)}, u32[]{:S(2)}) %collective-permute-start.26) | collective-permute-done | bytes 589856 | tf_op jit(solution)/shard_map/ppermute | solution.py:829
  347.1 15.7 %finish_chunk.3 = f32[144,128,256]{2,1,0:T(8,128)} custom-call(s32[3]{0:T(128)} %pad_add_fusion.7.base_ref, s32[8,256]{1,0:T(8,128)} %get-tuple-element.85.table_ref, s32[2,128,128]{2,1,0:T(8,128)} %get-tuple-element.73.place_ref, f32[1,16384]{1,0:T(1,128)} %broadcast_multiply_fusion, ...), custom_call_target="tpu_custom_call", output_to_operand_aliasing={{}: (16, {})} | custom-call | flops 47185920 | bytes 104857600 | tf_op jit(solution)/shard_map/finish_chunk/pallas_call | solution.py:854
  (156 shorter events, 57.5 us)
Async XLA Ops:
  49.4 42.8 %collective-permute-start.1 = (f32[32,8192]{1,0:T(8,128)}, f32[32,8192]{1,0:T(8,128)}, u32[]{:S(2)}, u32[]{:S(2)}) collective-permute-start(f32[32,8192]{1,0:T(8,128)} %get-tuple-element.84), channel_id=1, source_target_pairs={{0,2},{2,0},{4,6},{6,4},{8,10},{10,8},{12,14},{14,12},{1,3},{3,1},... | collective-permute-start | bytes 3145736 | tf_op jit(solution)/shard_map/ppermute | solution.py:716
  51.9 148.8 %collective-permute-start.10 = (f32[32,8192]{1,0:T(8,128)}, f32[32,8192]{1,0:T(8,128)}, u32[]{:S(2)}, u32[]{:S(2)}) collective-permute-start(f32[32,8192]{1,0:T(8,128)} %get-tuple-element.99.refs_3_), channel_id=1, source_target_pairs={{2,6},{4,0},{6,10},{8,4},{10,14},{12,8},{3,7},{5,1},{7,11},{9,5},{... | collective-permute-start | bytes 3145736 | tf_op jit(solution)/shard_map/ppermute | solution.py:716
  85.9 75.6 %collective-permute-start.5 = (f32[40,8192]{1,0:T(8,128)}, f32[40,8192]{1,0:T(8,128)S(1)}, u32[]{:S(2)}, u32[]{:S(2)}) collective-permute-start(f32[40,8192]{1,0:T(8,128)} %get-tuple-element.95), channel_id=1, source_target_pairs={{0,2},{2,0},{4,6},{6,4},{8,10},{10,8},{12,14},{14,12},{1,3},{3,1},... | collective-permute-start | bytes 3932168 | tf_op jit(solution)/shard_map/ppermute | solution.py:716
  89.7 76.6 %collective-permute-start.11 = (f32[40,8192]{1,0:T(8,128)}, f32[40,8192]{1,0:T(8,128)S(1)}, u32[]{:S(2)}, u32[]{:S(2)}) collective-permute-start(f32[40,8192]{1,0:T(8,128)} %get-tuple-element.100.refs_4_), channel_id=1, source_target_pairs={{2,6},{4,0},{6,10},{8,4},{10,14},{12,8},{3,7},{5,1},{7,11},{9,5},{... | collective-permute-start | bytes 3932168 | tf_op jit(solution)/shard_map/ppermute | solution.py:716
  92.2 71.4 %collective-permute-start.7 = (f32[32,8192]{1,0:T(8,128)}, f32[32,8192]{1,0:T(8,128)}, u32[]{:S(2)}, u32[]{:S(2)}) collective-permute-start(f32[32,8192]{1,0:T(8,128)} %collective-permute-done.1.refs_7_), channel_id=1, source_target_pairs={{6,2},{0,4},{10,6},{4,8},{14,10},{8,12},{7,3},{1,5},{11,7},{5,9},{... | collective-permute-start | bytes 3145736 | tf_op jit(solution)/shard_map/ppermute | solution.py:716
  161.5 17.6 %collective-permute-start.6 = (f32[72,2048]{1,0:T(8,128)}, f32[72,2048]{1,0:T(8,128)}, u32[]{:S(2)}, u32[]{:S(2)}) collective-permute-start(f32[72,2048]{1,0:T(8,128)} %get-tuple-element.96), channel_id=1, source_target_pairs={{0,2},{2,0},{4,6},{6,4},{8,10},{10,8},{12,14},{14,12},{1,3},{3,1},... | collective-permute-start | bytes 1769480 | tf_op jit(solution)/shard_map/ppermute | solution.py:749
  163.6 28.3 %collective-permute-start.8 = (f32[40,8192]{1,0:T(8,128)S(1)}, f32[40,8192]{1,0:T(8,128)S(1)}, u32[]{:S(2)}, u32[]{:S(2)}) collective-permute-start(f32[40,8192]{1,0:T(8,128)S(1)} %collective-permute-done.5.refs_8_), channel_id=1, source_target_pairs={{6,2},{0,4},{10,6},{4,8},{14,10},{8,12},{7,3},{1,5},{11,7},{5,9},{... | collective-permute-start | bytes 3932168 | tf_op jit(solution)/shard_map/ppermute | solution.py:716
  166.4 53.8 %collective-permute-start.12 = (f32[72,2048]{1,0:T(8,128)}, f32[72,2048]{1,0:T(8,128)}, u32[]{:S(2)}, u32[]{:S(2)}) collective-permute-start(f32[72,2048]{1,0:T(8,128)} %get-tuple-element.102.refs_5_), channel_id=1, source_target_pairs={{2,6},{4,0},{6,10},{8,4},{10,14},{12,8},{3,7},{5,1},{7,11},{9,5},{... | collective-permute-start | bytes 1769480 | tf_op jit(solution)/shard_map/ppermute | solution.py:750
  167.7 31.9 %collective-permute-start.13 = (f32[72,2048]{1,0:T(8,128)}, f32[72,2048]{1,0:T(8,128)}, u32[]{:S(2)}, u32[]{:S(2)}) collective-permute-start(f32[72,2048]{1,0:T(8,128)} %get-tuple-element.105), channel_id=1, source_target_pairs={{0,2},{2,0},{4,6},{6,4},{8,10},{10,8},{12,14},{14,12},{1,3},{3,1},... | collective-permute-start | bytes 1769480 | tf_op jit(solution)/shard_map/ppermute | solution.py:749
  192.9 29.9 %collective-permute-start.9 = (f32[72,2048]{1,0:T(8,128)}, f32[72,2048]{1,0:T(8,128)}, u32[]{:S(2)}, u32[]{:S(2)}) collective-permute-start(f32[72,2048]{1,0:T(8,128)} %collective-permute-done.6.refs_6_), channel_id=1, source_target_pairs={{6,2},{0,4},{10,6},{4,8},{14,10},{8,12},{7,3},{1,5},{11,7},{5,9},{... | collective-permute-start | bytes 1769480 | tf_op jit(solution)/shard_map/ppermute | solution.py:794
  199.6 32.8 %collective-permute-start.19 = (f32[72,2048]{1,0:T(8,128)}, f32[72,2048]{1,0:T(8,128)}, u32[]{:S(2)}, u32[]{:S(2)}) collective-permute-start(f32[72,2048]{1,0:T(8,128)} %get-tuple-element.117), channel_id=1, source_target_pairs={{0,2},{2,0},{4,6},{6,4},{8,10},{10,8},{12,14},{14,12},{1,3},{3,1},... | collective-permute-start | bytes 1769480 | tf_op jit(solution)/shard_map/ppermute | solution.py:749
  200.7 33.0 %collective-permute-start.16 = (f32[72,2048]{1,0:T(8,128)}, f32[72,2048]{1,0:T(8,128)}, u32[]{:S(2)}, u32[]{:S(2)}) collective-permute-start(f32[72,2048]{1,0:T(8,128)} %get-tuple-element.111), channel_id=1, source_target_pairs={{0,2},{2,0},{4,6},{6,4},{8,10},{10,8},{12,14},{14,12},{1,3},{3,1},... | collective-permute-start | bytes 1769480 | tf_op jit(solution)/shard_map/ppermute | solution.py:749
  209.3 30.7 %collective-permute-start.14 = (f32[72,2048]{1,0:T(8,128)}, f32[72,2048]{1,0:T(8,128)}, u32[]{:S(2)}, u32[]{:S(2)}) collective-permute-start(f32[72,2048]{1,0:T(8,128)} %collective-permute-done.13.refs_6_), channel_id=1, source_target_pairs={{6,2},{0,4},{10,6},{4,8},{14,10},{8,12},{7,3},{1,5},{11,7},{5,9},{... | collective-permute-start | bytes 1769480 | tf_op jit(solution)/shard_map/ppermute | solution.py:794
  222.8 49.7 %collective-permute-start.18 = (f32[72,2048]{1,0:T(8,128)S(1)}, f32[72,2048]{1,0:T(8,128)S(1)}, u32[]{:S(2)}, u32[]{:S(2)}) collective-permute-start(f32[72,2048]{1,0:T(8,128)S(1)} %copy-done.5), channel_id=1, source_target_pairs={{2,6},{4,0},{6,10},{8,4},{10,14},{12,8},{3,7},{5,1},{7,11},{9,5},{... | collective-permute-start | bytes 1769480 | tf_op jit(solution)/shard_map/ppermute | solution.py:750
  233.7 48.6 %collective-permute-start.22 = (f32[72,2048]{1,0:T(8,128)}, f32[72,2048]{1,0:T(8,128)}, u32[]{:S(2)}, u32[]{:S(2)}) collective-permute-start(f32[72,2048]{1,0:T(8,128)} %get-tuple-element.123), channel_id=1, source_target_pairs={{0,2},{2,0},{4,6},{6,4},{8,10},{10,8},{12,14},{14,12},{1,3},{3,1},... | collective-permute-start | bytes 1769480 | tf_op jit(solution)/shard_map/ppermute | solution.py:829
  237.2 35.4 %collective-permute-start.17 = (f32[72,2048]{1,0:T(8,128)}, f32[72,2048]{1,0:T(8,128)S(1)}, u32[]{:S(2)}, u32[]{:S(2)}) collective-permute-start(f32[72,2048]{1,0:T(8,128)} %collective-permute-done.16.refs_6_), channel_id=1, source_target_pairs={{6,2},{0,4},{10,6},{4,8},{14,10},{8,12},{7,3},{1,5},{11,7},{5,9},{... | collective-permute-start | bytes 1769480 | tf_op jit(solution)/shard_map/ppermute | solution.py:794
  240.0 19.8 %collective-permute-start.27 = (f32[72,2048]{1,0:T(8,128)}, f32[72,2048]{1,0:T(8,128)S(1)}, u32[]{:S(2)}, u32[]{:S(2)}) collective-permute-start(f32[72,2048]{1,0:T(8,128)} %get-tuple-element.134), channel_id=1, source_target_pairs={{0,2},{2,0},{4,6},{6,4},{8,10},{10,8},{12,14},{14,12},{1,3},{3,1},... | collective-permute-start | bytes 1769480 | tf_op jit(solution)/shard_map/ppermute | solution.py:829
  249.8 33.9 %collective-permute-start.21 = (f32[72,2048]{1,0:T(8,128)S(1)}, f32[72,2048]{1,0:T(8,128)S(1)}, u32[]{:S(2)}, u32[]{:S(2)}) collective-permute-start(f32[72,2048]{1,0:T(8,128)S(1)} %copy-done.4), channel_id=1, source_target_pairs={{2,6},{4,0},{6,10},{8,4},{10,14},{12,8},{3,7},{5,1},{7,11},{9,5},{... | collective-permute-start | bytes 1769480 | tf_op jit(solution)/shard_map/ppermute | solution.py:750
  260.6 23.1 %collective-permute-start.20 = (f32[72,2048]{1,0:T(8,128)}, f32[72,2048]{1,0:T(8,128)S(1)}, u32[]{:S(2)}, u32[]{:S(2)}) collective-permute-start(f32[72,2048]{1,0:T(8,128)} %collective-permute-done.19.refs_6_), channel_id=1, source_target_pairs={{6,2},{0,4},{10,6},{4,8},{14,10},{8,12},{7,3},{1,5},{11,7},{5,9},{... | collective-permute-start | bytes 1769480 | tf_op jit(solution)/shard_map/ppermute | solution.py:794
  272.5 21.0 %collective-permute-start.28 = (f32[72,2048]{1,0:T(8,128)}, f32[72,2048]{1,0:T(8,128)S(1)}, u32[]{:S(2)}, u32[]{:S(2)}) collective-permute-start(f32[72,2048]{1,0:T(8,128)} %get-tuple-element.136), channel_id=1, source_target_pairs={{0,2},{2,0},{4,6},{6,4},{8,10},{10,8},{12,14},{14,12},{1,3},{3,1},... | collective-permute-start | bytes 1769480 | tf_op jit(solution)/shard_map/ppermute | solution.py:829
  293.6 18.0 %collective-permute-start.29 = (f32[72,2048]{1,0:T(8,128)}, f32[72,2048]{1,0:T(8,128)S(1)}, u32[]{:S(2)}, u32[]{:S(2)}) collective-permute-start(f32[72,2048]{1,0:T(8,128)} %get-tuple-element.138), channel_id=1, source_target_pairs={{0,2},{2,0},{4,6},{6,4},{8,10},{10,8},{12,14},{14,12},{1,3},{3,1},... | collective-permute-start | bytes 1769480 | tf_op jit(solution)/shard_map/ppermute | solution.py:829
  298.9 29.2 %collective-permute-start.24 = (f32[72,2048]{1,0:T(8,128)}, f32[72,2048]{1,0:T(8,128)S(1)}, u32[]{:S(2)}, u32[]{:S(2)}) collective-permute-start(f32[72,2048]{1,0:T(8,128)} %get-tuple-element.127), channel_id=1, source_target_pairs={{0,2},{2,0},{4,6},{6,4},{8,10},{10,8},{12,14},{14,12},{1,3},{3,1},... | collective-permute-start | bytes 1769480 | tf_op jit(solution)/shard_map/ppermute | solution.py:829
  300.0 36.8 %collective-permute-start.25 = (f32[72,2048]{1,0:T(8,128)}, f32[72,2048]{1,0:T(8,128)S(1)}, u32[]{:S(2)}, u32[]{:S(2)}) collective-permute-start(f32[72,2048]{1,0:T(8,128)} %get-tuple-element.129), channel_id=1, source_target_pairs={{0,2},{2,0},{4,6},{6,4},{8,10},{10,8},{12,14},{14,12},{1,3},{3,1},... | collective-permute-start | bytes 1769480 | tf_op jit(solution)/shard_map/ppermute | solution.py:829
  300.9 45.3 %collective-permute-start.26 = (f32[72,2048]{1,0:T(8,128)}, f32[72,2048]{1,0:T(8,128)S(1)}, u32[]{:S(2)}, u32[]{:S(2)}) collective-permute-start(f32[72,2048]{1,0:T(8,128)} %get-tuple-element.131), channel_id=1, source_target_pairs={{0,2},{2,0},{4,6},{6,4},{8,10},{10,8},{12,14},{14,12},{1,3},{3,1},... | collective-permute-start | bytes 1769480 | tf_op jit(solution)/shard_map/ppermute | solution.py:829
  (40 other events, 616.8 us)

commit v9 on v8

--- a/solution.py
+++ b/solution.py
@@ -790,7 +790,7 @@
     own_parts, parts_0, parts_1 = [], [], []
     groups = [(from_got, 1), (from_got, 0), (kept, 0), (kept, 1), (got, 1), (got, 0), (from_own, 0), (from_own, 1)]
     for c in chunk_range:
-        waits = [from_got[before][0]] + ([from_got[last][c - 2]] if c >= 2 else [])
+        waits = [from_got[before][0], from_own_1[c]] + ([from_got[last][c - 2]] if c >= 2 else [])
         from_got[last].append(lax.ppermute(after(got_1[c], *waits), "comp", across))
         levels, level_specs, counts = [], [], []
         for group, part in groups:

time: 364 us -> 357 us (0.981)
  waiting for transfers between devices: 77.3 us -> 70.6 us
    ppermute x8, waiting for transfers between devices: 37.9 us -> 29 us  [send_back(): return lax.ppermute(after(piece, *waits), 'comp', pairs)]
    ppermute x4, waiting for transfers between devices: 0.01 us -> 7.55 us  [packed_shards(): from_got[last].append(lax.ppermute(after(got_1[c], *waits), 'comp', across))]
    ppermute x4, waiting for transfers between devices: 8.8 us -> 1.63 us  [packed_shards(): got_1.append(lax.ppermute(after(sent[last][c], *waits), 'comp', pairs))]
    unnamed x68 -> x64, local copies, waits for them, and re-layouts: 7.42 us -> 5.27 us
  transfers between devices with their start and end apart: 30 -> 30, of which waited for: 10 -> 10; matrix products, arithmetic and copies ran while one was open for 3% -> 4% of each run, Pallas kernels for 42% -> 42%
where the time goes in v9:
time: 357 us; the launch traced here: 356 us
  Pallas kernels  205 us (57%)
  waiting for transfers between devices  70.6 us (20%)
  starting transfers between devices  59.3 us (17%)
  local copies, waits for them, and re-layouts  14 us (4%)
  other arithmetic  5.93 us (2%)
    pallas_call x3, Pallas kernels, propagate(): pl.pallas_call(functools.partial(propagate_kernel, part, late, pieces), g...  134 us
    pallas_call x4, Pallas kernels, packed_shards(): pl.pallas_call(functools.partial(interact_kernel, tuple(counts)), grid=(w...  32.9 us
    pallas_call x2, Pallas kernels, finish(): pl.pallas_call(functools.partial(finish_kernel, CELL_CHUNKS), grid_spec=p...  31.5 us
    ppermute x8, waiting for transfers between devices, send_back(): return lax.ppermute(after(piece, *waits), 'comp', pairs)  29 us
    ppermute x6, starting transfers between devices, send(): lax.ppermute(after(piece, *wait), 'comp', route)  18.1 us
    ppermute x4, starting transfers between devices, packed_shards(): from_got[last].append(lax.ppermute(after(got_1[c], *waits), 'comp', across))  16.3 us
    ppermute x6, waiting for transfers between devices, send(): lax.ppermute(after(piece, *wait), 'comp', route)  15.2 us
    ppermute x8, starting transfers between devices, send_back(): return lax.ppermute(after(piece, *waits), 'comp', pairs)  10.5 us
  transfers between devices with their start and end apart: 30, of which 10 were waited for; matrix products, arithmetic and copies ran while one was open for 4% of the time, Pallas kernels for 42%

profile of v9, /device:TPU:0, one launch (start us, length us, event | category | flops | bytes accessed | tf_op | source)
XLA Modules:
  0.0 355.7 jit_solution(16394184837788047127)
XLA Ops:
  2.6 7.0 %prepare.1 = (f32[260,8,256]{2,1,0:T(8,128)}, s32[2,128,128]{2,1,0:T(8,128)}, s32[2,128,128]{2,1,0:T(8,128)}, s32[8,256]{1,0:T(8,128)}, f32[144,128]{1,0:T(8,128)}, /*index=5*/f32[144,128]{1,0:T(8,128)}) custom-call(s32[3]{0:T(128)} %pad_add_fusion.7.base_ref, f32[32]{0:T(128)} %speed_ref.1, s32[256,256]{1,0:T(8,128)} %sea_ref.1, f32[256,256]{1,0:T(8,128)} %east_ref.1, ...), custom_call_target="tpu_custom_call" | custom-call | tf_op jit(solution)/shard_map/prepare/pallas_call | solution.py:626
  10.3 38.5 %propagate_early.1 = (f32[32,8192]{1,0:T(8,128)}, f32[32,8192]{1,0:T(8,128)}, f32[1,16384]{1,0:T(1,128)}, f32[72,16384]{1,0:T(8,128)}, f32[8,16384]{1,0:T(8,128)}, /*index=5*/f32[8,16384]{1,0:T(8,128)}) custom-call(s32[3]{0:T(128)} %pad_add_fusion.7.base_ref, s32[8,256]{1,0:T(8,128)} %get-tuple-element.85.table_ref, f32[144,128,256]{2,1,0:T(8,128)} %energy_ref.5, ...), custom_call_target="tpu_custom_call" | custom-call | flops 78643200 | bytes 62914560 | tf_op jit(solution)/shard_map/propagate_early/pallas_call | solution.py:682
  53.3 32.7 %propagate_late.1 = (f32[40,8192]{1,0:T(8,128)}, f32[40,8192]{1,0:T(8,128)}, f32[1,16384]{1,0:T(1,128)}, f32[72,16384]{1,0:T(8,128)}) custom-call(s32[3]{0:T(128)} %pad_add_fusion.7.base_ref, s32[8,256]{1,0:T(8,128)} %get-tuple-element.85.table_ref, f32[144,128,256]{2,1,0:T(8,128)} %energy_ref.5, ...), custom_call_target="tpu_custom_call", output_to_operand_aliasing={{3}: (10, {})} | custom-call | flops 62914560 | bytes 62914560 | tf_op jit(solution)/shard_map/propagate_late/pallas_call | solution.py:682
  86.0 3.8 %collective-permute-start.5 = (f32[40,8192]{1,0:T(8,128)}, f32[40,8192]{1,0:T(8,128)S(1)}, u32[]{:S(2)}, u32[]{:S(2)}) collective-permute-start(f32[40,8192]{1,0:T(8,128)} %get-tuple-element.95), channel_id=1, source_target_pairs={{0,2},{2,0},{4,6},{6,4},{8,10},{10,8},{12,14},{14,12},{1,3},{3,1},... | collective-permute-start | bytes 3932168 | tf_op jit(solution)/shard_map/ppermute | solution.py:716
  92.3 5.5 %collective-permute-start.7 = (f32[32,8192]{1,0:T(8,128)}, f32[32,8192]{1,0:T(8,128)}, u32[]{:S(2)}, u32[]{:S(2)}) collective-permute-start(f32[32,8192]{1,0:T(8,128)} %collective-permute-done.1.refs_7_), channel_id=1, source_target_pairs={{6,2},{0,4},{10,6},{4,8},{14,10},{8,12},{7,3},{1,5},{11,7},{5,9},{... | collective-permute-start | bytes 3145736 | tf_op jit(solution)/shard_map/ppermute | solution.py:716
  97.9 62.5 %propagate_whole.1 = (f32[72,2048]{1,0:T(8,128)}, f32[72,2048]{1,0:T(8,128)}, f32[72,2048]{1,0:T(8,128)}, f32[72,2048]{1,0:T(8,128)}, f32[72,2048]{1,0:T(8,128)}...) custom-call(s32[3]{0:T(128)} %pad_add_fusion.7.base_ref, ...), custom_call_target="tpu_custom_call" | custom-call | flops 141557760 | bytes 62914560 | tf_op jit(solution)/shard_map/propagate_whole/pallas_call | solution.py:682
  165.2 3.6 %collective-permute-start.8 = (f32[40,8192]{1,0:T(8,128)S(1)}, f32[40,8192]{1,0:T(8,128)S(1)}, u32[]{:S(2)}, u32[]{:S(2)}) collective-permute-start(f32[40,8192]{1,0:T(8,128)S(1)} %collective-permute-done.5.refs_8_), channel_id=1, source_target_pairs={{6,2},{0,4},{10,6},{4,8},{14,10},{8,12},{7,3},{1,5},{11,7},{5,9},{... | collective-permute-start | bytes 3932168 | tf_op jit(solution)/shard_map/ppermute | solution.py:716
  170.2 9.8 %collective-permute-done.10.refs_11_ = f32[72,2048]{1,0:T(8,128)S(1)} collective-permute-done((f32[72,2048]{1,0:T(8,128)}, f32[72,2048]{1,0:T(8,128)S(1)}, u32[]{:S(2)}, u32[]{:S(2)}) %collective-permute-start.10) | collective-permute-done | bytes 589856 | tf_op jit(solution)/shard_map/ppermute | solution.py:750
  180.0 15.2 %collective-permute-done.8.refs_2_ = f32[40,8192]{1,0:T(8,128)S(1)} collective-permute-done((f32[40,8192]{1,0:T(8,128)S(1)}, f32[40,8192]{1,0:T(8,128)S(1)}, u32[]{:S(2)}, u32[]{:S(2)}) %collective-permute-start.8) | collective-permute-done | bytes 1310752 | tf_op jit(solution)/shard_map/ppermute | solution.py:716
  196.2 5.2 %collective-permute-start.11 = (f32[72,2048]{1,0:T(8,128)}, f32[72,2048]{1,0:T(8,128)}, u32[]{:S(2)}, u32[]{:S(2)}) collective-permute-start(f32[72,2048]{1,0:T(8,128)} %collective-permute-done.6.refs_6_), channel_id=1, source_target_pairs={{6,2},{0,4},{10,6},{4,8},{14,10},{8,12},{7,3},{1,5},{11,7},{5,9},{... | collective-permute-start | bytes 1769480 | tf_op jit(solution)/shard_map/ppermute | solution.py:794
  204.8 7.5 %collective-permute-done.3 = f32[1,16384]{1,0:T(1,128)S(1)} collective-permute-done((f32[1,16384]{1,0:T(1,128)S(1)}, f32[1,16384]{1,0:T(1,128)S(1)}, u32[]{:S(2)}, u32[]{:S(2)}) %collective-permute-start.3) | collective-permute-done | bytes 65568 | tf_op jit(solution)/shard_map/ppermute | solution.py:753
  224.3 8.2 %interact_cells.4 = (f32[144,2048]{1,0:T(8,128)}, f32[72,2048]{1,0:T(8,128)}, f32[72,2048]{1,0:T(8,128)}) custom-call(bf16[6,288,216]{2,1,0:T(8,128)(2,1)} %stack.28.table_ref, bf16[288,864]{1,0:T(8,128)(2,1)} %concatenate.40.spread_ref, f32[432,1]{1,0:T(8,128)} %copy.48.coupling_ref, f32[72,2048]{1,0:T(8,128)} %collective-permute-done.11.refs_0_, ...), custom_call_target="tpu_custom_call" | custom-call | flops 2548039680 | bytes 20971520 | tf_op jit(solution)/shard_map/interact_cells/pallas_call | solution.py:806
  232.6 4.6 %collective-permute-start.15 = (f32[72,2048]{1,0:T(8,128)}, f32[72,2048]{1,0:T(8,128)S(1)}, u32[]{:S(2)}, u32[]{:S(2)}) collective-permute-start(f32[72,2048]{1,0:T(8,128)} %collective-permute-done.13.refs_6_), channel_id=1, source_target_pairs={{6,2},{0,4},{10,6},{4,8},{14,10},{8,12},{7,3},{1,5},{11,7},{5,9},{... | collective-permute-start | bytes 1769480 | tf_op jit(solution)/shard_map/ppermute | solution.py:794
  243.6 7.5 %collective-permute-done.15.refs_0_ = f32[72,2048]{1,0:T(8,128)S(1)} collective-permute-done((f32[72,2048]{1,0:T(8,128)}, f32[72,2048]{1,0:T(8,128)S(1)}, u32[]{:S(2)}, u32[]{:S(2)}) %collective-permute-start.15) | collective-permute-done | bytes 589856 | tf_op jit(solution)/shard_map/ppermute | solution.py:794
  251.2 4.5 %collective-permute-start.21 = (f32[72,2048]{1,0:T(8,128)}, f32[72,2048]{1,0:T(8,128)S(1)}, u32[]{:S(2)}, u32[]{:S(2)}) collective-permute-start(f32[72,2048]{1,0:T(8,128)} %collective-permute-done.19.refs_6_), channel_id=1, source_target_pairs={{6,2},{0,4},{10,6},{4,8},{14,10},{8,12},{7,3},{1,5},{11,7},{5,9},{... | collective-permute-start | bytes 1769480 | tf_op jit(solution)/shard_map/ppermute | solution.py:794
  255.7 8.2 %interact_cells.5 = (f32[144,2048]{1,0:T(8,128)}, f32[72,2048]{1,0:T(8,128)}, f32[72,2048]{1,0:T(8,128)}) custom-call(bf16[6,288,216]{2,1,0:T(8,128)(2,1)} %stack.28.table_ref, bf16[288,864]{1,0:T(8,128)(2,1)} %concatenate.40.spread_ref, f32[432,1]{1,0:T(8,128)} %copy.48.coupling_ref, f32[72,2048]{1,0:T(8,128)} %copy-done.9, ...), custom_call_target="tpu_custom_call" | custom-call | flops 2548039680 | bytes 20971520 | tf_op jit(solution)/shard_map/interact_cells/pallas_call | solution.py:806
  267.7 8.3 %interact_cells.6 = (f32[144,2048]{1,0:T(8,128)}, f32[72,2048]{1,0:T(8,128)}, f32[72,2048]{1,0:T(8,128)}) custom-call(bf16[6,288,216]{2,1,0:T(8,128)(2,1)} %stack.28.table_ref, bf16[288,864]{1,0:T(8,128)(2,1)} %concatenate.40.spread_ref, f32[432,1]{1,0:T(8,128)} %copy.48.coupling_ref, f32[72,2048]{1,0:T(8,128)} %copy-done.8, ...), custom_call_target="tpu_custom_call" | custom-call | flops 2548039680 | bytes 20971520 | tf_op jit(solution)/shard_map/interact_cells/pallas_call | solution.py:806
  277.1 8.2 %interact_cells.7 = (f32[144,2048]{1,0:T(8,128)}, f32[72,2048]{1,0:T(8,128)}, f32[72,2048]{1,0:T(8,128)}) custom-call(bf16[6,288,216]{2,1,0:T(8,128)(2,1)} %stack.28.table_ref, bf16[288,864]{1,0:T(8,128)(2,1)} %concatenate.40.spread_ref, f32[432,1]{1,0:T(8,128)} %copy.48.coupling_ref, f32[72,2048]{1,0:T(8,128)} %copy-done.7, ...), custom_call_target="tpu_custom_call" | custom-call | flops 2548039680 | bytes 20971520 | tf_op jit(solution)/shard_map/interact_cells/pallas_call | solution.py:806
  287.2 5.7 %collective-permute-done.23.refs_7_ = f32[72,2048]{1,0:T(8,128)S(1)} collective-permute-done((f32[72,2048]{1,0:T(8,128)}, f32[72,2048]{1,0:T(8,128)S(1)}, u32[]{:S(2)}, u32[]{:S(2)}) %collective-permute-start.23) | collective-permute-done | bytes 589856 | tf_op jit(solution)/shard_map/ppermute | solution.py:829
  300.4 5.2 %collective-permute-done.29.refs_8_ = f32[72,2048]{1,0:T(8,128)S(1)} collective-permute-done((f32[72,2048]{1,0:T(8,128)}, f32[72,2048]{1,0:T(8,128)S(1)}, u32[]{:S(2)}, u32[]{:S(2)}) %collective-permute-start.29) | collective-permute-done | bytes 589856 | tf_op jit(solution)/shard_map/ppermute | solution.py:829
  306.4 15.7 %finish_chunk.2.refs_9_ = f32[144,128,256]{2,1,0:T(8,128)} custom-call(s32[3]{0:T(128)} %pad_add_fusion.7.base_ref, s32[8,256]{1,0:T(8,128)} %get-tuple-element.85.table_ref, s32[2,128,128]{2,1,0:T(8,128)} %get-tuple-element.73.place_ref, f32[1,16384]{1,0:T(1,128)} %broadcast_multiply_fusion, f32[8,16384]{1,0:T(8,128)} %get-tuple-element.80.refs_0_.fields_ref, ...), custom_call_target="tpu_custom_call" | custom-call | flops 47185920 | bytes 104857600 | tf_op jit(solution)/shard_map/finish_chunk/pallas_call | solution.py:854
  322.1 8.7 %collective-permute-done.25.refs_7_ = f32[72,2048]{1,0:T(8,128)S(1)} collective-permute-done((f32[72,2048]{1,0:T(8,128)}, f32[72,2048]{1,0:T(8,128)S(1)}, u32[]{:S(2)}, u32[]{:S(2)}) %collective-permute-start.25) | collective-permute-done | bytes 589856 | tf_op jit(solution)/shard_map/ppermute | solution.py:829
  330.8 8.3 %collective-permute-done.26.refs_8_ = f32[72,2048]{1,0:T(8,128)S(1)} collective-permute-done((f32[72,2048]{1,0:T(8,128)}, f32[72,2048]{1,0:T(8,128)S(1)}, u32[]{:S(2)}, u32[]{:S(2)}) %collective-permute-start.26) | collective-permute-done | bytes 589856 | tf_op jit(solution)/shard_map/ppermute | solution.py:829
  340.0 15.7 %finish_chunk.3 = f32[144,128,256]{2,1,0:T(8,128)} custom-call(s32[3]{0:T(128)} %pad_add_fusion.7.base_ref, s32[8,256]{1,0:T(8,128)} %get-tuple-element.85.table_ref, s32[2,128,128]{2,1,0:T(8,128)} %get-tuple-element.73.place_ref, f32[1,16384]{1,0:T(1,128)} %broadcast_multiply_fusion, ...), custom_call_target="tpu_custom_call", output_to_operand_aliasing={{}: (16, {})} | custom-call | flops 47185920 | bytes 104857600 | tf_op jit(solution)/shard_map/finish_chunk/pallas_call | solution.py:854
  (152 shorter events, 54.7 us)
Async XLA Ops:
  49.5 42.8 %collective-permute-start.1 = (f32[32,8192]{1,0:T(8,128)}, f32[32,8192]{1,0:T(8,128)}, u32[]{:S(2)}, u32[]{:S(2)}) collective-permute-start(f32[32,8192]{1,0:T(8,128)} %get-tuple-element.84), channel_id=1, source_target_pairs={{0,2},{2,0},{4,6},{6,4},{8,10},{10,8},{12,14},{14,12},{1,3},{3,1},... | collective-permute-start | bytes 3145736 | tf_op jit(solution)/shard_map/ppermute | solution.py:716
  52.0 168.4 %collective-permute-start.12 = (f32[32,8192]{1,0:T(8,128)}, f32[32,8192]{1,0:T(8,128)}, u32[]{:S(2)}, u32[]{:S(2)}) collective-permute-start(f32[32,8192]{1,0:T(8,128)} %get-tuple-element.102.refs_3_), channel_id=1, source_target_pairs={{2,6},{4,0},{6,10},{8,4},{10,14},{12,8},{3,7},{5,1},{7,11},{9,5},{... | collective-permute-start | bytes 3145736 | tf_op jit(solution)/shard_map/ppermute | solution.py:716
  86.0 75.5 %collective-permute-start.5 = (f32[40,8192]{1,0:T(8,128)}, f32[40,8192]{1,0:T(8,128)S(1)}, u32[]{:S(2)}, u32[]{:S(2)}) collective-permute-start(f32[40,8192]{1,0:T(8,128)} %get-tuple-element.95), channel_id=1, source_target_pairs={{0,2},{2,0},{4,6},{6,4},{8,10},{10,8},{12,14},{14,12},{1,3},{3,1},... | collective-permute-start | bytes 3932168 | tf_op jit(solution)/shard_map/ppermute | solution.py:716
  89.9 71.7 %collective-permute-start.9 = (f32[40,8192]{1,0:T(8,128)}, f32[40,8192]{1,0:T(8,128)S(1)}, u32[]{:S(2)}, u32[]{:S(2)}) collective-permute-start(f32[40,8192]{1,0:T(8,128)} %get-tuple-element.99.refs_4_), channel_id=1, source_target_pairs={{2,6},{4,0},{6,10},{8,4},{10,14},{12,8},{3,7},{5,1},{7,11},{9,5},{... | collective-permute-start | bytes 3932168 | tf_op jit(solution)/shard_map/ppermute | solution.py:716
  92.3 72.9 %collective-permute-start.7 = (f32[32,8192]{1,0:T(8,128)}, f32[32,8192]{1,0:T(8,128)}, u32[]{:S(2)}, u32[]{:S(2)}) collective-permute-start(f32[32,8192]{1,0:T(8,128)} %collective-permute-done.1.refs_7_), channel_id=1, source_target_pairs={{6,2},{0,4},{10,6},{4,8},{14,10},{8,12},{7,3},{1,5},{11,7},{5,9},{... | collective-permute-start | bytes 3145736 | tf_op jit(solution)/shard_map/ppermute | solution.py:716
  165.2 29.9 %collective-permute-start.8 = (f32[40,8192]{1,0:T(8,128)S(1)}, f32[40,8192]{1,0:T(8,128)S(1)}, u32[]{:S(2)}, u32[]{:S(2)}) collective-permute-start(f32[40,8192]{1,0:T(8,128)S(1)} %collective-permute-done.5.refs_8_), channel_id=1, source_target_pairs={{6,2},{0,4},{10,6},{4,8},{14,10},{8,12},{7,3},{1,5},{11,7},{5,9},{... | collective-permute-start | bytes 3932168 | tf_op jit(solution)/shard_map/ppermute | solution.py:716
  168.9 45.8 %collective-permute-start.14 = (f32[72,2048]{1,0:T(8,128)}, f32[72,2048]{1,0:T(8,128)}, u32[]{:S(2)}, u32[]{:S(2)}) collective-permute-start(f32[72,2048]{1,0:T(8,128)} %get-tuple-element.107.refs_5_), channel_id=1, source_target_pairs={{2,6},{4,0},{6,10},{8,4},{10,14},{12,8},{3,7},{5,1},{7,11},{9,5},{... | collective-permute-start | bytes 1769480 | tf_op jit(solution)/shard_map/ppermute | solution.py:750
  180.0 23.5 %collective-permute-start.13 = (f32[72,2048]{1,0:T(8,128)}, f32[72,2048]{1,0:T(8,128)}, u32[]{:S(2)}, u32[]{:S(2)}) collective-permute-start(f32[72,2048]{1,0:T(8,128)} %get-tuple-element.105), channel_id=1, source_target_pairs={{0,2},{2,0},{4,6},{6,4},{8,10},{10,8},{12,14},{14,12},{1,3},{3,1},... | collective-permute-start | bytes 1769480 | tf_op jit(solution)/shard_map/ppermute | solution.py:749
  196.2 26.8 %collective-permute-start.11 = (f32[72,2048]{1,0:T(8,128)}, f32[72,2048]{1,0:T(8,128)}, u32[]{:S(2)}, u32[]{:S(2)}) collective-permute-start(f32[72,2048]{1,0:T(8,128)} %collective-permute-done.6.refs_6_), channel_id=1, source_target_pairs={{6,2},{0,4},{10,6},{4,8},{14,10},{8,12},{7,3},{1,5},{11,7},{5,9},{... | collective-permute-start | bytes 1769480 | tf_op jit(solution)/shard_map/ppermute | solution.py:794
  203.5 37.3 %collective-permute-start.17 = (f32[72,2048]{1,0:T(8,128)}, f32[72,2048]{1,0:T(8,128)}, u32[]{:S(2)}, u32[]{:S(2)}) collective-permute-start(f32[72,2048]{1,0:T(8,128)} %get-tuple-element.113.refs_5_), channel_id=1, source_target_pairs={{2,6},{4,0},{6,10},{8,4},{10,14},{12,8},{3,7},{5,1},{7,11},{9,5},{... | collective-permute-start | bytes 1769480 | tf_op jit(solution)/shard_map/ppermute | solution.py:750
  212.3 20.3 %collective-permute-start.19 = (f32[72,2048]{1,0:T(8,128)}, f32[72,2048]{1,0:T(8,128)}, u32[]{:S(2)}, u32[]{:S(2)}) collective-permute-start(f32[72,2048]{1,0:T(8,128)} %get-tuple-element.117), channel_id=1, source_target_pairs={{0,2},{2,0},{4,6},{6,4},{8,10},{10,8},{12,14},{14,12},{1,3},{3,1},... | collective-permute-start | bytes 1769480 | tf_op jit(solution)/shard_map/ppermute | solution.py:749
  214.7 24.1 %collective-permute-start.16 = (f32[72,2048]{1,0:T(8,128)}, f32[72,2048]{1,0:T(8,128)}, u32[]{:S(2)}, u32[]{:S(2)}) collective-permute-start(f32[72,2048]{1,0:T(8,128)} %get-tuple-element.111), channel_id=1, source_target_pairs={{0,2},{2,0},{4,6},{6,4},{8,10},{10,8},{12,14},{14,12},{1,3},{3,1},... | collective-permute-start | bytes 1769480 | tf_op jit(solution)/shard_map/ppermute | solution.py:749
  220.4 22.4 %collective-permute-start.4 = (f32[1,16384]{1,0:T(1,128)S(1)}, f32[1,16384]{1,0:T(1,128)S(1)}, u32[]{:S(2)}, u32[]{:S(2)}) collective-permute-start(f32[1,16384]{1,0:T(1,128)S(1)} %add.257), channel_id=1, source_target_pairs={{0,8},{2,10},{4,12},{6,14},{8,0},{10,2},{12,4},{14,6},{1,9},{3,11}... | collective-permute-start | bytes 196616 | tf_op jit(solution)/shard_map/ppermute | solution.py:754
  223.0 20.6 %collective-permute-start.20 = (f32[72,2048]{1,0:T(8,128)S(1)}, f32[72,2048]{1,0:T(8,128)S(1)}, u32[]{:S(2)}, u32[]{:S(2)}) collective-permute-start(f32[72,2048]{1,0:T(8,128)S(1)} %copy-done.4), channel_id=1, source_target_pairs={{2,6},{4,0},{6,10},{8,4},{10,14},{12,8},{3,7},{5,1},{7,11},{9,5},{... | collective-permute-start | bytes 1769480 | tf_op jit(solution)/shard_map/ppermute | solution.py:750
  232.6 18.6 %collective-permute-start.15 = (f32[72,2048]{1,0:T(8,128)}, f32[72,2048]{1,0:T(8,128)S(1)}, u32[]{:S(2)}, u32[]{:S(2)}) collective-permute-start(f32[72,2048]{1,0:T(8,128)} %collective-permute-done.13.refs_6_), channel_id=1, source_target_pairs={{6,2},{0,4},{10,6},{4,8},{14,10},{8,12},{7,3},{1,5},{11,7},{5,9},{... | collective-permute-start | bytes 1769480 | tf_op jit(solution)/shard_map/ppermute | solution.py:794
  238.8 37.2 %collective-permute-start.22 = (f32[72,2048]{1,0:T(8,128)}, f32[72,2048]{1,0:T(8,128)S(1)}, u32[]{:S(2)}, u32[]{:S(2)}) collective-permute-start(f32[72,2048]{1,0:T(8,128)} %get-tuple-element.123), channel_id=1, source_target_pairs={{0,2},{2,0},{4,6},{6,4},{8,10},{10,8},{12,14},{14,12},{1,3},{3,1},... | collective-permute-start | bytes 1769480 | tf_op jit(solution)/shard_map/ppermute | solution.py:829
  240.8 26.1 %collective-permute-start.18 = (f32[72,2048]{1,0:T(8,128)}, f32[72,2048]{1,0:T(8,128)S(1)}, u32[]{:S(2)}, u32[]{:S(2)}) collective-permute-start(f32[72,2048]{1,0:T(8,128)} %collective-permute-done.16.refs_6_), channel_id=1, source_target_pairs={{6,2},{0,4},{10,6},{4,8},{14,10},{8,12},{7,3},{1,5},{11,7},{5,9},{... | collective-permute-start | bytes 1769480 | tf_op jit(solution)/shard_map/ppermute | solution.py:794
  242.8 22.1 %collective-permute-start.27 = (f32[72,2048]{1,0:T(8,128)}, f32[72,2048]{1,0:T(8,128)}, u32[]{:S(2)}, u32[]{:S(2)}) collective-permute-start(f32[72,2048]{1,0:T(8,128)} %get-tuple-element.134), channel_id=1, source_target_pairs={{0,2},{2,0},{4,6},{6,4},{8,10},{10,8},{12,14},{14,12},{1,3},{3,1},... | collective-permute-start | bytes 1769480 | tf_op jit(solution)/shard_map/ppermute | solution.py:829
  251.2 24.9 %collective-permute-start.21 = (f32[72,2048]{1,0:T(8,128)}, f32[72,2048]{1,0:T(8,128)S(1)}, u32[]{:S(2)}, u32[]{:S(2)}) collective-permute-start(f32[72,2048]{1,0:T(8,128)} %collective-permute-done.19.refs_6_), channel_id=1, source_target_pairs={{6,2},{0,4},{10,6},{4,8},{14,10},{8,12},{7,3},{1,5},{11,7},{5,9},{... | collective-permute-start | bytes 1769480 | tf_op jit(solution)/shard_map/ppermute | solution.py:794
  264.9 20.4 %collective-permute-start.28 = (f32[72,2048]{1,0:T(8,128)}, f32[72,2048]{1,0:T(8,128)S(1)}, u32[]{:S(2)}, u32[]{:S(2)}) collective-permute-start(f32[72,2048]{1,0:T(8,128)} %get-tuple-element.136), channel_id=1, source_target_pairs={{0,2},{2,0},{4,6},{6,4},{8,10},{10,8},{12,14},{14,12},{1,3},{3,1},... | collective-permute-start | bytes 1769480 | tf_op jit(solution)/shard_map/ppermute | solution.py:829
  285.3 20.2 %collective-permute-start.29 = (f32[72,2048]{1,0:T(8,128)}, f32[72,2048]{1,0:T(8,128)S(1)}, u32[]{:S(2)}, u32[]{:S(2)}) collective-permute-start(f32[72,2048]{1,0:T(8,128)} %get-tuple-element.138), channel_id=1, source_target_pairs={{0,2},{2,0},{4,6},{6,4},{8,10},{10,8},{12,14},{14,12},{1,3},{3,1},... | collective-permute-start | bytes 1769480 | tf_op jit(solution)/shard_map/ppermute | solution.py:829
  292.9 29.2 %collective-permute-start.24 = (f32[72,2048]{1,0:T(8,128)}, f32[72,2048]{1,0:T(8,128)S(1)}, u32[]{:S(2)}, u32[]{:S(2)}) collective-permute-start(f32[72,2048]{1,0:T(8,128)} %get-tuple-element.127), channel_id=1, source_target_pairs={{0,2},{2,0},{4,6},{6,4},{8,10},{10,8},{12,14},{14,12},{1,3},{3,1},... | collective-permute-start | bytes 1769480 | tf_op jit(solution)/shard_map/ppermute | solution.py:829
  295.3 35.5 %collective-permute-start.25 = (f32[72,2048]{1,0:T(8,128)}, f32[72,2048]{1,0:T(8,128)S(1)}, u32[]{:S(2)}, u32[]{:S(2)}) collective-permute-start(f32[72,2048]{1,0:T(8,128)} %get-tuple-element.129), channel_id=1, source_target_pairs={{0,2},{2,0},{4,6},{6,4},{8,10},{10,8},{12,14},{14,12},{1,3},{3,1},... | collective-permute-start | bytes 1769480 | tf_op jit(solution)/shard_map/ppermute | solution.py:829
  295.3 43.8 %collective-permute-start.26 = (f32[72,2048]{1,0:T(8,128)}, f32[72,2048]{1,0:T(8,128)S(1)}, u32[]{:S(2)}, u32[]{:S(2)}) collective-permute-start(f32[72,2048]{1,0:T(8,128)} %get-tuple-element.131), channel_id=1, source_target_pairs={{0,2},{2,0},{4,6},{6,4},{8,10},{10,8},{12,14},{14,12},{1,3},{3,1},... | collective-permute-start | bytes 1769480 | tf_op jit(solution)/shard_map/ppermute | solution.py:829
  (38 other events, 627.7 us)

commit v10 on v9

--- a/solution.py
+++ b/solution.py
@@ -749,10 +749,6 @@
         got_1.append(lax.ppermute(after(sent[last][c], *waits), "comp", pairs))
         from_own_1.append(lax.ppermute(after(kept[last][c], from_own[before][0]), "comp", apart))
     got[last], from_own[last], from_got[last] = got_1, from_own_1, []
-    sums = sums + partner_sums
-    sums = sums_two = sums + lax.ppermute(sums, "comp", [(i, i ^ 2) for i in range(comp_count)])
-    sums = sums + lax.ppermute(sums, "comp", [(i, i ^ 4) for i in range(comp_count)])
-    mean_level = sums / comp_total
 
     dia_index, coupling, growth, damping, late_odd, late_pair, _ = lax.optimization_barrier(
         (dia_index, coupling, growth, damping, odd, pair_pos, sums_0)
@@ -825,13 +821,18 @@
         parts_0.append(part_0)
         parts_1.append(part_1)
 
+    sums = sums + partner_sums
+    sums = sums + lax.ppermute(after(sums, own_parts[0]), "comp", [(i, i ^ 2) for i in range(comp_count)])
+    sums = sums + lax.ppermute(after(sums, own_parts[2]), "comp", [(i, i ^ 4) for i in range(comp_count)])
+    mean_level = sums / comp_total
+
     def send_back(piece, *waits):
         return lax.ppermute(after(piece, *waits), "comp", pairs)
 
     back = [[None] * CELL_CHUNKS for _ in range(2)]
-    back[0][0] = send_back(parts_0[0], got_1[2], sums_two)
+    back[0][0] = send_back(parts_0[0], got_1[2])
     back[1][0] = send_back(parts_1[0], got_1[3])
-    back[0][1] = send_back(parts_0[1], back[0][0], sums)
+    back[0][1] = send_back(parts_0[1], back[0][0])
     back[0][2] = send_back(parts_0[2], back[1][0])
     back[0][3] = send_back(parts_0[3], back[0][1])
     for c in range(1, CELL_CHUNKS):

time: 357 us -> 391 us (1.095)
  waiting for transfers between devices: 70.6 us -> 106 us
    ppermute x6, waiting for transfers between devices: 15.2 us -> 35.4 us  [send(): lax.ppermute(after(piece, *wait), 'comp', route)]
    ppermute x8, waiting for transfers between devices: 29 us -> 45.3 us  [send_back(): return lax.ppermute(after(piece, *waits), 'comp', pairs)]
    ppermute x4, waiting for transfers between devices: 1.63 us -> 16.6 us  [packed_shards(): got_1.append(lax.ppermute(after(sent[last][c], *waits), 'comp', pairs))]
    ppermute x2, waiting for transfers between devices: 7.47 us -> 0.01 us  [the longest x1 0.01 us: packed_shards(): lax.ppermute(after(sums, own_parts[0]), 'comp', [(i, i ^ 2) for i in rang...]
    ppermute x4, waiting for transfers between devices: 9.83 us -> 3.77 us  [packed_shards(): lax.ppermute(after(kept[last][c], from_own[before][0]), 'comp', apart)]
    ppermute x4, starting transfers between devices: 4.77 us -> 9.81 us  [packed_shards(): got_1.append(lax.ppermute(after(sent[last][c], *waits), 'comp', pairs))]
  transfers between devices with their start and end apart: 30 -> 30, of which waited for: 10 -> 8; matrix products, arithmetic and copies ran while one was open for 4% -> 4% of each run, Pallas kernels for 42% -> 39%
where the time goes in v10:
time: 391 us; the launch traced here: 390 us
  Pallas kernels  205 us (52%)
  waiting for transfers between devices  106 us (27%)
  starting transfers between devices  59.3 us (15%)
  local copies, waits for them, and re-layouts  12.4 us (3%)
  other arithmetic  6.68 us (2%)
    pallas_call x3, Pallas kernels, propagate(): pl.pallas_call(functools.partial(propagate_kernel, part, late, pieces), g...  134 us
    ppermute x8, waiting for transfers between devices, send_back(): return lax.ppermute(after(piece, *waits), 'comp', pairs)  45.3 us
    ppermute x6, waiting for transfers between devices, send(): lax.ppermute(after(piece, *wait), 'comp', route)  35.4 us
    pallas_call x4, Pallas kernels, packed_shards(): pl.pallas_call(functools.partial(interact_kernel, tuple(counts)), grid=(w...  32.9 us
    pallas_call x2, Pallas kernels, finish(): pl.pallas_call(functools.partial(finish_kernel, CELL_CHUNKS), grid_spec=p...  31.5 us
    ppermute x4, starting transfers between devices, packed_shards(): from_got[last].append(lax.ppermute(after(got_1[c], *waits), 'comp', across))  16.7 us
    ppermute x4, waiting for transfers between devices, packed_shards(): got_1.append(lax.ppermute(after(sent[last][c], *waits), 'comp', pairs))  16.6 us
    ppermute x6, starting transfers between devices, send(): lax.ppermute(after(piece, *wait), 'comp', route)  15.4 us
  transfers between devices with their start and end apart: 30, of which 8 were waited for; matrix products, arithmetic and copies ran while one was open for 4% of the time, Pallas kernels for 39%

profile of v10, /device:TPU:0, one launch (start us, length us, event | category | flops | bytes accessed | tf_op | source)
XLA Modules:
  0.0 390.0 jit_solution(7660183005839898366)
XLA Ops:
  2.6 7.0 %prepare.1 = (f32[260,8,256]{2,1,0:T(8,128)}, s32[2,128,128]{2,1,0:T(8,128)}, s32[2,128,128]{2,1,0:T(8,128)}, s32[8,256]{1,0:T(8,128)}, f32[144,128]{1,0:T(8,128)}, /*index=5*/f32[144,128]{1,0:T(8,128)}) custom-call(s32[3]{0:T(128)} %pad_add_fusion.7.base_ref, f32[32]{0:T(128)} %speed_ref.1, s32[256,256]{1,0:T(8,128)} %sea_ref.1, f32[256,256]{1,0:T(8,128)} %east_ref.1, ...), custom_call_target="tpu_custom_call" | custom-call | tf_op jit(solution)/shard_map/prepare/pallas_call | solution.py:626
  10.3 38.5 %propagate_early.1 = (f32[32,8192]{1,0:T(8,128)}, f32[32,8192]{1,0:T(8,128)}, f32[1,16384]{1,0:T(1,128)}, f32[72,16384]{1,0:T(8,128)}, f32[8,16384]{1,0:T(8,128)}, /*index=5*/f32[8,16384]{1,0:T(8,128)}) custom-call(s32[3]{0:T(128)} %pad_add_fusion.7.base_ref, s32[8,256]{1,0:T(8,128)} %get-tuple-element.87.table_ref, f32[144,128,256]{2,1,0:T(8,128)} %energy_ref.5, ...), custom_call_target="tpu_custom_call" | custom-call | flops 78643200 | bytes 62914560 | tf_op jit(solution)/shard_map/propagate_early/pallas_call | solution.py:682
  51.9 32.7 %propagate_late.1 = (f32[40,8192]{1,0:T(8,128)}, f32[40,8192]{1,0:T(8,128)}, f32[1,16384]{1,0:T(1,128)}, f32[72,16384]{1,0:T(8,128)}) custom-call(s32[3]{0:T(128)} %pad_add_fusion.7.base_ref, s32[8,256]{1,0:T(8,128)} %get-tuple-element.87.table_ref, f32[144,128,256]{2,1,0:T(8,128)} %energy_ref.5, ...), custom_call_target="tpu_custom_call", output_to_operand_aliasing={{3}: (10, {})} | custom-call | flops 62914560 | bytes 62914560 | tf_op jit(solution)/shard_map/propagate_late/pallas_call | solution.py:682
  86.3 5.6 %collective-permute-start.5 = (f32[32,8192]{1,0:T(8,128)}, f32[32,8192]{1,0:T(8,128)}, u32[]{:S(2)}, u32[]{:S(2)}) collective-permute-start(f32[32,8192]{1,0:T(8,128)} %collective-permute-done.1.refs_7_), channel_id=1, source_target_pairs={{6,2},{0,4},{10,6},{4,8},{14,10},{8,12},{7,3},{1,5},{11,7},{5,9},{... | collective-permute-start | bytes 3145736 | tf_op jit(solution)/shard_map/ppermute | solution.py:716
  92.5 23.3 %collective-permute-done.3.refs_8_ = f32[40,8192]{1,0:T(8,128)S(1)} collective-permute-done((f32[40,8192]{1,0:T(8,128)}, f32[40,8192]{1,0:T(8,128)S(1)}, u32[]{:S(2)}, u32[]{:S(2)}) %collective-permute-start.3) | collective-permute-done | bytes 1310752 | tf_op jit(solution)/shard_map/ppermute | solution.py:716
  115.8 4.5 %collective-permute-start.6 = (f32[40,8192]{1,0:T(8,128)S(1)}, f32[40,8192]{1,0:T(8,128)}, u32[]{:S(2)}, u32[]{:S(2)}) collective-permute-start(f32[40,8192]{1,0:T(8,128)S(1)} %collective-permute-done.3.refs_8_), channel_id=1, source_target_pairs={{6,2},{0,4},{10,6},{4,8},{14,10},{8,12},{7,3},{1,5},{11,7},{5,9},{... | collective-permute-start | bytes 3932168 | tf_op jit(solution)/shard_map/ppermute | solution.py:716
  121.2 62.5 %propagate_whole.1 = (f32[72,2048]{1,0:T(8,128)}, f32[72,2048]{1,0:T(8,128)}, f32[72,2048]{1,0:T(8,128)}, f32[72,2048]{1,0:T(8,128)}, f32[72,2048]{1,0:T(8,128)}...) custom-call(s32[3]{0:T(128)} %pad_add_fusion.7.base_ref, ...), custom_call_target="tpu_custom_call" | custom-call | flops 141557760 | bytes 62914560 | tf_op jit(solution)/shard_map/propagate_whole/pallas_call | solution.py:682
  186.3 4.6 %collective-permute-start.16 = (f32[72,2048]{1,0:T(8,128)}, f32[72,2048]{1,0:T(8,128)}, u32[]{:S(2)}, u32[]{:S(2)}) collective-permute-start(f32[72,2048]{1,0:T(8,128)} %get-tuple-element.115), channel_id=1, source_target_pairs={{0,2},{2,0},{4,6},{6,4},{8,10},{10,8},{12,14},{14,12},{1,3},{3,1},... | collective-permute-start | bytes 1769480 | tf_op jit(solution)/shard_map/ppermute | solution.py:749
  197.3 8.2 %collective-permute-done.16.refs_6_ = f32[72,2048]{1,0:T(8,128)} collective-permute-done((f32[72,2048]{1,0:T(8,128)}, f32[72,2048]{1,0:T(8,128)}, u32[]{:S(2)}, u32[]{:S(2)}) %collective-permute-start.16) | collective-permute-done | bytes 589856 | tf_op jit(solution)/shard_map/ppermute | solution.py:749
  206.8 8.5 %collective-permute-done.4.refs_6_ = f32[72,2048]{1,0:T(8,128)} collective-permute-done((f32[72,2048]{1,0:T(8,128)}, f32[72,2048]{1,0:T(8,128)}, u32[]{:S(2)}, u32[]{:S(2)}) %collective-permute-start.4) | collective-permute-done | bytes 589856 | tf_op jit(solution)/shard_map/ppermute | solution.py:749
  216.6 5.1 %collective-permute-start.19 = (f32[72,2048]{1,0:T(8,128)}, f32[72,2048]{1,0:T(8,128)}, u32[]{:S(2)}, u32[]{:S(2)}) collective-permute-start(f32[72,2048]{1,0:T(8,128)} %get-tuple-element.121), channel_id=1, source_target_pairs={{0,2},{2,0},{4,6},{6,4},{8,10},{10,8},{12,14},{14,12},{1,3},{3,1},... | collective-permute-start | bytes 1769480 | tf_op jit(solution)/shard_map/ppermute | solution.py:749
  225.1 12.1 %collective-permute-done.10.refs_9_ = f32[32,8192]{1,0:T(8,128)S(1)} collective-permute-done((f32[32,8192]{1,0:T(8,128)}, f32[32,8192]{1,0:T(8,128)S(1)}, u32[]{:S(2)}, u32[]{:S(2)}) %collective-permute-start.10) | collective-permute-done | bytes 1048608 | tf_op jit(solution)/shard_map/ppermute | solution.py:716
  238.6 8.3 %interact_cells.4 = (f32[144,2048]{1,0:T(8,128)}, f32[72,2048]{1,0:T(8,128)}, f32[72,2048]{1,0:T(8,128)}) custom-call(bf16[6,288,216]{2,1,0:T(8,128)(2,1)} %stack.28.table_ref, bf16[288,864]{1,0:T(8,128)(2,1)} %concatenate.40.spread_ref, f32[432,1]{1,0:T(8,128)} %copy.48.coupling_ref, f32[72,2048]{1,0:T(8,128)} %collective-permute-done.9.refs_0_, ...), custom_call_target="tpu_custom_call" | custom-call | flops 2548039680 | bytes 20971520 | tf_op jit(solution)/shard_map/interact_cells/pallas_call | solution.py:802
  246.8 4.6 %collective-permute-start.18 = (f32[72,2048]{1,0:T(8,128)}, f32[72,2048]{1,0:T(8,128)S(1)}, u32[]{:S(2)}, u32[]{:S(2)}) collective-permute-start(f32[72,2048]{1,0:T(8,128)} %collective-permute-done.16.refs_6_), channel_id=1, source_target_pairs={{6,2},{0,4},{10,6},{4,8},{14,10},{8,12},{7,3},{1,5},{11,7},{5,9},{... | collective-permute-start | bytes 1769480 | tf_op jit(solution)/shard_map/ppermute | solution.py:790
  251.5 5.2 %collective-permute-start.14 = (f32[72,2048]{1,0:T(8,128)S(1)}, f32[72,2048]{1,0:T(8,128)}, u32[]{:S(2)}, u32[]{:S(2)}) collective-permute-start(f32[72,2048]{1,0:T(8,128)S(1)} %collective-permute-done.12.refs_6_), channel_id=1, source_target_pairs={{6,2},{0,4},{10,6},{4,8},{14,10},{8,12},{7,3},{1,5},{11,7},{5,9},{... | collective-permute-start | bytes 1769480 | tf_op jit(solution)/shard_map/ppermute | solution.py:790
  260.5 4.9 %collective-permute-done.18.refs_0_ = f32[72,2048]{1,0:T(8,128)S(1)} collective-permute-done((f32[72,2048]{1,0:T(8,128)}, f32[72,2048]{1,0:T(8,128)S(1)}, u32[]{:S(2)}, u32[]{:S(2)}) %collective-permute-start.18) | collective-permute-done | bytes 589856 | tf_op jit(solution)/shard_map/ppermute | solution.py:790
  265.5 4.5 %collective-permute-start.21 = (f32[72,2048]{1,0:T(8,128)}, f32[72,2048]{1,0:T(8,128)S(1)}, u32[]{:S(2)}, u32[]{:S(2)}) collective-permute-start(f32[72,2048]{1,0:T(8,128)} %collective-permute-done.19.refs_6_), channel_id=1, source_target_pairs={{6,2},{0,4},{10,6},{4,8},{14,10},{8,12},{7,3},{1,5},{11,7},{5,9},{... | collective-permute-start | bytes 1769480 | tf_op jit(solution)/shard_map/ppermute | solution.py:790
  270.0 8.2 %interact_cells.6 = (f32[144,2048]{1,0:T(8,128)}, f32[72,2048]{1,0:T(8,128)}, f32[72,2048]{1,0:T(8,128)}) custom-call(bf16[6,288,216]{2,1,0:T(8,128)(2,1)} %stack.28.table_ref, bf16[288,864]{1,0:T(8,128)(2,1)} %concatenate.40.spread_ref, f32[432,1]{1,0:T(8,128)} %copy.48.coupling_ref, f32[72,2048]{1,0:T(8,128)} %copy-done.8, ...), custom_call_target="tpu_custom_call" | custom-call | flops 2548039680 | bytes 20971520 | tf_op jit(solution)/shard_map/interact_cells/pallas_call | solution.py:802
  278.2 8.3 %interact_cells.5 = (f32[144,2048]{1,0:T(8,128)}, f32[72,2048]{1,0:T(8,128)}, f32[72,2048]{1,0:T(8,128)}) custom-call(bf16[6,288,216]{2,1,0:T(8,128)(2,1)} %stack.28.table_ref, bf16[288,864]{1,0:T(8,128)(2,1)} %concatenate.40.spread_ref, f32[432,1]{1,0:T(8,128)} %copy.48.coupling_ref, f32[72,2048]{1,0:T(8,128)} %collective-permute-done.14.refs_0_, ...), custom_call_target="tpu_custom_call" | custom-call | flops 2548039680 | bytes 20971520 | tf_op jit(solution)/shard_map/interact_cells/pallas_call | solution.py:802
  297.3 8.2 %interact_cells.7 = (f32[144,2048]{1,0:T(8,128)}, f32[72,2048]{1,0:T(8,128)}, f32[72,2048]{1,0:T(8,128)}) custom-call(bf16[6,288,216]{2,1,0:T(8,128)(2,1)} %stack.28.table_ref, bf16[288,864]{1,0:T(8,128)(2,1)} %concatenate.40.spread_ref, f32[432,1]{1,0:T(8,128)} %copy.48.coupling_ref, f32[72,2048]{1,0:T(8,128)} %copy-done.7, ...), custom_call_target="tpu_custom_call" | custom-call | flops 2548039680 | bytes 20971520 | tf_op jit(solution)/shard_map/interact_cells/pallas_call | solution.py:802
  309.2 6.5 %collective-permute-done.28.refs_6_ = f32[72,2048]{1,0:T(8,128)S(1)} collective-permute-done((f32[72,2048]{1,0:T(8,128)S(1)}, f32[72,2048]{1,0:T(8,128)S(1)}, u32[]{:S(2)}, u32[]{:S(2)}) %collective-permute-start.28) | collective-permute-done | bytes 589856 | tf_op jit(solution)/shard_map/ppermute | solution.py:830
  317.7 38.8 %collective-permute-done.29.refs_8_ = f32[72,2048]{1,0:T(8,128)S(1)} collective-permute-done((f32[72,2048]{1,0:T(8,128)}, f32[72,2048]{1,0:T(8,128)S(1)}, u32[]{:S(2)}, u32[]{:S(2)}) %collective-permute-start.29) | collective-permute-done | bytes 589856 | tf_op jit(solution)/shard_map/ppermute | solution.py:830
  357.3 15.7 %finish_chunk.2.refs_9_ = f32[144,128,256]{2,1,0:T(8,128)} custom-call(s32[3]{0:T(128)} %pad_add_fusion.7.base_ref, s32[8,256]{1,0:T(8,128)} %get-tuple-element.87.table_ref, s32[2,128,128]{2,1,0:T(8,128)} %get-tuple-element.75.place_ref, f32[1,16384]{1,0:T(1,128)} %add_multiply_fusion.mean_ref, f32[8,16384]{1,0:T(8,128)} %get-tuple-element.82.refs_0_.fields_ref, ...), custom_call_target="tpu_custom_call" | custom-call | flops 47185920 | bytes 104857600 | tf_op jit(solution)/shard_map/finish_chunk/pallas_call | solution.py:855
  374.3 15.7 %finish_chunk.3 = f32[144,128,256]{2,1,0:T(8,128)} custom-call(s32[3]{0:T(128)} %pad_add_fusion.7.base_ref, s32[8,256]{1,0:T(8,128)} %get-tuple-element.87.table_ref, s32[2,128,128]{2,1,0:T(8,128)} %get-tuple-element.75.place_ref, f32[1,16384]{1,0:T(1,128)} %add_multiply_fusion.mean_ref, ...), custom_call_target="tpu_custom_call", output_to_operand_aliasing={{}: (16, {})} | custom-call | flops 47185920 | bytes 104857600 | tf_op jit(solution)/shard_map/finish_chunk/pallas_call | solution.py:855
  (124 shorter events, 48.1 us)
Async XLA Ops:
  48.8 37.5 %collective-permute-start.1 = (f32[32,8192]{1,0:T(8,128)}, f32[32,8192]{1,0:T(8,128)}, u32[]{:S(2)}, u32[]{:S(2)}) collective-permute-start(f32[32,8192]{1,0:T(8,128)} %get-tuple-element.86), channel_id=1, source_target_pairs={{0,2},{2,0},{4,6},{6,4},{8,10},{10,8},{12,14},{14,12},{1,3},{3,1},... | collective-permute-start | bytes 3145736 | tf_op jit(solution)/shard_map/ppermute | solution.py:716
  84.6 31.2 %collective-permute-start.3 = (f32[40,8192]{1,0:T(8,128)}, f32[40,8192]{1,0:T(8,128)S(1)}, u32[]{:S(2)}, u32[]{:S(2)}) collective-permute-start(f32[40,8192]{1,0:T(8,128)} %get-tuple-element.94), channel_id=1, source_target_pairs={{0,2},{2,0},{4,6},{6,4},{8,10},{10,8},{12,14},{14,12},{1,3},{3,1},... | collective-permute-start | bytes 3932168 | tf_op jit(solution)/shard_map/ppermute | solution.py:716
  84.8 98.9 %collective-permute-start.7 = (f32[40,8192]{1,0:T(8,128)}, f32[40,8192]{1,0:T(8,128)S(1)}, u32[]{:S(2)}, u32[]{:S(2)}) collective-permute-start(f32[40,8192]{1,0:T(8,128)} %get-tuple-element.98.refs_4_), channel_id=1, source_target_pairs={{2,6},{4,0},{6,10},{8,4},{10,14},{12,8},{3,7},{5,1},{7,11},{9,5},{... | collective-permute-start | bytes 3932168 | tf_op jit(solution)/shard_map/ppermute | solution.py:716
  86.3 29.5 %collective-permute-start.5 = (f32[32,8192]{1,0:T(8,128)}, f32[32,8192]{1,0:T(8,128)}, u32[]{:S(2)}, u32[]{:S(2)}) collective-permute-start(f32[32,8192]{1,0:T(8,128)} %collective-permute-done.1.refs_7_), channel_id=1, source_target_pairs={{6,2},{0,4},{10,6},{4,8},{14,10},{8,12},{7,3},{1,5},{11,7},{5,9},{... | collective-permute-start | bytes 3145736 | tf_op jit(solution)/shard_map/ppermute | solution.py:716
  115.8 105.9 %collective-permute-start.6 = (f32[40,8192]{1,0:T(8,128)S(1)}, f32[40,8192]{1,0:T(8,128)}, u32[]{:S(2)}, u32[]{:S(2)}) collective-permute-start(f32[40,8192]{1,0:T(8,128)S(1)} %collective-permute-done.3.refs_8_), channel_id=1, source_target_pairs={{6,2},{0,4},{10,6},{4,8},{14,10},{8,12},{7,3},{1,5},{11,7},{5,9},{... | collective-permute-start | bytes 3932168 | tf_op jit(solution)/shard_map/ppermute | solution.py:716
  183.7 38.0 %collective-permute-start.17 = (f32[72,2048]{1,0:T(8,128)}, f32[72,2048]{1,0:T(8,128)}, u32[]{:S(2)}, u32[]{:S(2)}) collective-permute-start(f32[72,2048]{1,0:T(8,128)} %get-tuple-element.117.refs_5_), channel_id=1, source_target_pairs={{2,6},{4,0},{6,10},{8,4},{10,14},{12,8},{3,7},{5,1},{7,11},{9,5},{... | collective-permute-start | bytes 1769480 | tf_op jit(solution)/shard_map/ppermute | solution.py:750
  185.0 31.6 %collective-permute-start.8 = (f32[72,2048]{1,0:T(8,128)}, f32[72,2048]{1,0:T(8,128)}, u32[]{:S(2)}, u32[]{:S(2)}) collective-permute-start(f32[72,2048]{1,0:T(8,128)} %get-tuple-element.99.refs_5_), channel_id=1, source_target_pairs={{2,6},{4,0},{6,10},{8,4},{10,14},{12,8},{3,7},{5,1},{7,11},{9,5},{... | collective-permute-start | bytes 1769480 | tf_op jit(solution)/shard_map/ppermute | solution.py:750
  190.9 24.3 %collective-permute-start.4 = (f32[72,2048]{1,0:T(8,128)}, f32[72,2048]{1,0:T(8,128)}, u32[]{:S(2)}, u32[]{:S(2)}) collective-permute-start(f32[72,2048]{1,0:T(8,128)} %get-tuple-element.95), channel_id=1, source_target_pairs={{0,2},{2,0},{4,6},{6,4},{8,10},{10,8},{12,14},{14,12},{1,3},{3,1},... | collective-permute-start | bytes 1769480 | tf_op jit(solution)/shard_map/ppermute | solution.py:749
  205.5 31.7 %collective-permute-start.10 = (f32[32,8192]{1,0:T(8,128)}, f32[32,8192]{1,0:T(8,128)S(1)}, u32[]{:S(2)}, u32[]{:S(2)}) collective-permute-start(f32[32,8192]{1,0:T(8,128)} %get-tuple-element.101.refs_3_), channel_id=1, source_target_pairs={{2,6},{4,0},{6,10},{8,4},{10,14},{12,8},{3,7},{5,1},{7,11},{9,5},{... | collective-permute-start | bytes 3145736 | tf_op jit(solution)/shard_map/ppermute | solution.py:716
  215.3 36.2 %collective-permute-start.13 = (f32[72,2048]{1,0:T(8,128)}, f32[72,2048]{1,0:T(8,128)}, u32[]{:S(2)}, u32[]{:S(2)}) collective-permute-start(f32[72,2048]{1,0:T(8,128)} %get-tuple-element.107.refs_5_), channel_id=1, source_target_pairs={{2,6},{4,0},{6,10},{8,4},{10,14},{12,8},{3,7},{5,1},{7,11},{9,5},{... | collective-permute-start | bytes 1769480 | tf_op jit(solution)/shard_map/ppermute | solution.py:750
  216.6 30.2 %collective-permute-start.19 = (f32[72,2048]{1,0:T(8,128)}, f32[72,2048]{1,0:T(8,128)}, u32[]{:S(2)}, u32[]{:S(2)}) collective-permute-start(f32[72,2048]{1,0:T(8,128)} %get-tuple-element.121), channel_id=1, source_target_pairs={{0,2},{2,0},{4,6},{6,4},{8,10},{10,8},{12,14},{14,12},{1,3},{3,1},... | collective-permute-start | bytes 1769480 | tf_op jit(solution)/shard_map/ppermute | solution.py:749
  221.7 29.8 %collective-permute-start.12 = (f32[72,2048]{1,0:T(8,128)}, f32[72,2048]{1,0:T(8,128)S(1)}, u32[]{:S(2)}, u32[]{:S(2)}) collective-permute-start(f32[72,2048]{1,0:T(8,128)} %get-tuple-element.105), channel_id=1, source_target_pairs={{0,2},{2,0},{4,6},{6,4},{8,10},{10,8},{12,14},{14,12},{1,3},{3,1},... | collective-permute-start | bytes 1769480 | tf_op jit(solution)/shard_map/ppermute | solution.py:749
  237.2 19.5 %collective-permute-start.2 = (f32[1,16384]{1,0:T(1,128)S(1)}, f32[1,16384]{1,0:T(1,128)S(1)}, u32[]{:S(2)}, u32[]{:S(2)}) collective-permute-start(f32[1,16384]{1,0:T(1,128)S(1)} %add_add_fusion), channel_id=1, source_target_pairs={{0,2},{2,0},{4,6},{6,4},{8,10},{10,8},{12,14},{14,12},{1,3},{3,1},... | collective-permute-start | bytes 196616 | tf_op jit(solution)/shard_map/ppermute | solution.py:744
  237.2 23.3 %collective-permute-start.20 = (f32[72,2048]{1,0:T(8,128)S(1)}, f32[72,2048]{1,0:T(8,128)S(1)}, u32[]{:S(2)}, u32[]{:S(2)}) collective-permute-start(f32[72,2048]{1,0:T(8,128)S(1)} %copy-done.4), channel_id=1, source_target_pairs={{2,6},{4,0},{6,10},{8,4},{10,14},{12,8},{3,7},{5,1},{7,11},{9,5},{... | collective-permute-start | bytes 1769480 | tf_op jit(solution)/shard_map/ppermute | solution.py:750
  251.4 35.1 %collective-permute-start.22 = (f32[72,2048]{1,0:T(8,128)}, f32[72,2048]{1,0:T(8,128)}, u32[]{:S(2)}, u32[]{:S(2)}) collective-permute-start(f32[72,2048]{1,0:T(8,128)} %get-tuple-element.127), channel_id=1, source_target_pairs={{0,2},{2,0},{4,6},{6,4},{8,10},{10,8},{12,14},{14,12},{1,3},{3,1},... | collective-permute-start | bytes 1769480 | tf_op jit(solution)/shard_map/ppermute | solution.py:830
  251.5 26.7 %collective-permute-start.14 = (f32[72,2048]{1,0:T(8,128)S(1)}, f32[72,2048]{1,0:T(8,128)}, u32[]{:S(2)}, u32[]{:S(2)}) collective-permute-start(f32[72,2048]{1,0:T(8,128)S(1)} %collective-permute-done.12.refs_6_), channel_id=1, source_target_pairs={{6,2},{0,4},{10,6},{4,8},{14,10},{8,12},{7,3},{1,5},{11,7},{5,9},{... | collective-permute-start | bytes 1769480 | tf_op jit(solution)/shard_map/ppermute | solution.py:790
  256.8 32.6 %collective-permute-start.27 = (f32[72,2048]{1,0:T(8,128)}, f32[72,2048]{1,0:T(8,128)}, u32[]{:S(2)}, u32[]{:S(2)}) collective-permute-start(f32[72,2048]{1,0:T(8,128)} %get-tuple-element.138), channel_id=1, source_target_pairs={{0,2},{2,0},{4,6},{6,4},{8,10},{10,8},{12,14},{14,12},{1,3},{3,1},... | collective-permute-start | bytes 1769480 | tf_op jit(solution)/shard_map/ppermute | solution.py:830
  265.5 31.0 %collective-permute-start.21 = (f32[72,2048]{1,0:T(8,128)}, f32[72,2048]{1,0:T(8,128)S(1)}, u32[]{:S(2)}, u32[]{:S(2)}) collective-permute-start(f32[72,2048]{1,0:T(8,128)} %collective-permute-done.19.refs_6_), channel_id=1, source_target_pairs={{6,2},{0,4},{10,6},{4,8},{14,10},{8,12},{7,3},{1,5},{11,7},{5,9},{... | collective-permute-start | bytes 1769480 | tf_op jit(solution)/shard_map/ppermute | solution.py:790
  289.4 26.3 %collective-permute-start.28 = (f32[72,2048]{1,0:T(8,128)S(1)}, f32[72,2048]{1,0:T(8,128)S(1)}, u32[]{:S(2)}, u32[]{:S(2)}) collective-permute-start(f32[72,2048]{1,0:T(8,128)S(1)} %copy-done.17), channel_id=1, source_target_pairs={{0,2},{2,0},{4,6},{6,4},{8,10},{10,8},{12,14},{14,12},{1,3},{3,1},... | collective-permute-start | bytes 1769480 | tf_op jit(solution)/shard_map/ppermute | solution.py:830
  294.3 22.7 %collective-permute-start.15 = (f32[1,16384]{1,0:T(1,128)S(1)}, f32[1,16384]{1,0:T(1,128)S(1)}, u32[]{:S(2)}, u32[]{:S(2)}) collective-permute-start(f32[1,16384]{1,0:T(1,128)S(1)} %add.300), channel_id=1, source_target_pairs={{0,8},{2,10},{4,12},{6,14},{8,0},{10,2},{12,4},{14,6},{1,9},{3,11}... | collective-permute-start | bytes 196616 | tf_op jit(solution)/shard_map/ppermute | solution.py:826
  305.5 67.5 %collective-permute-start.24 = (f32[72,2048]{1,0:T(8,128)}, f32[72,2048]{1,0:T(8,128)S(1)}, u32[]{:S(2)}, u32[]{:S(2)}) collective-permute-start(f32[72,2048]{1,0:T(8,128)} %get-tuple-element.131), channel_id=1, source_target_pairs={{0,2},{2,0},{4,6},{6,4},{8,10},{10,8},{12,14},{14,12},{1,3},{3,1},... | collective-permute-start | bytes 1769480 | tf_op jit(solution)/shard_map/ppermute | solution.py:830
  307.2 65.9 %collective-permute-start.25 = (f32[72,2048]{1,0:T(8,128)}, f32[72,2048]{1,0:T(8,128)S(1)}, u32[]{:S(2)}, u32[]{:S(2)}) collective-permute-start(f32[72,2048]{1,0:T(8,128)} %get-tuple-element.133), channel_id=1, source_target_pairs={{0,2},{2,0},{4,6},{6,4},{8,10},{10,8},{12,14},{14,12},{1,3},{3,1},... | collective-permute-start | bytes 1769480 | tf_op jit(solution)/shard_map/ppermute | solution.py:830
  307.6 65.4 %collective-permute-start.26 = (f32[72,2048]{1,0:T(8,128)}, f32[72,2048]{1,0:T(8,128)S(1)}, u32[]{:S(2)}, u32[]{:S(2)}) collective-permute-start(f32[72,2048]{1,0:T(8,128)} %get-tuple-element.135), channel_id=1, source_target_pairs={{0,2},{2,0},{4,6},{6,4},{8,10},{10,8},{12,14},{14,12},{1,3},{3,1},... | collective-permute-start | bytes 1769480 | tf_op jit(solution)/shard_map/ppermute | solution.py:830
  315.7 40.8 %collective-permute-start.29 = (f32[72,2048]{1,0:T(8,128)}, f32[72,2048]{1,0:T(8,128)S(1)}, u32[]{:S(2)}, u32[]{:S(2)}) collective-permute-start(f32[72,2048]{1,0:T(8,128)} %get-tuple-element.142), channel_id=1, source_target_pairs={{0,2},{2,0},{4,6},{6,4},{8,10},{10,8},{12,14},{14,12},{1,3},{3,1},... | collective-permute-start | bytes 1769480 | tf_op jit(solution)/shard_map/ppermute | solution.py:830
  (24 other events, 480.3 us)

commit v11 on v9

--- a/solution.py
+++ b/solution.py
@@ -181,7 +181,7 @@
 BLOCK = 128
 GROUP = 24
 EARLY = 40
-BATCH = 4
+BATCH = 2
 CELL_CHUNKS = 4
 MIB = 1024 * 1024
 VMEM_MIB = 60

time: 357 us -> 357 us (level)
  no operation moved by 1% of the time
where the time goes in v11:
time: 357 us; the launch traced here: 356 us
  Pallas kernels  205 us (57%)
  waiting for transfers between devices  70.6 us (20%)
  starting transfers between devices  59.3 us (17%)
  local copies, waits for them, and re-layouts  14 us (4%)
  other arithmetic  5.93 us (2%)
    pallas_call x3, Pallas kernels, propagate(): pl.pallas_call(functools.partial(propagate_kernel, part, late, pieces), g...  134 us
    pallas_call x4, Pallas kernels, packed_shards(): pl.pallas_call(functools.partial(interact_kernel, tuple(counts)), grid=(w...  32.9 us
    pallas_call x2, Pallas kernels, finish(): pl.pallas_call(functools.partial(finish_kernel, CELL_CHUNKS), grid_spec=p...  31.5 us
    ppermute x8, waiting for transfers between devices, send_back(): return lax.ppermute(after(piece, *waits), 'comp', pairs)  29 us
    ppermute x6, starting transfers between devices, send(): lax.ppermute(after(piece, *wait), 'comp', route)  18.1 us
    ppermute x4, starting transfers between devices, packed_shards(): from_got[last].append(lax.ppermute(after(got_1[c], *waits), 'comp', across))  16.3 us
    ppermute x6, waiting for transfers between devices, send(): lax.ppermute(after(piece, *wait), 'comp', route)  15.2 us
    ppermute x8, starting transfers between devices, send_back(): return lax.ppermute(after(piece, *waits), 'comp', pairs)  10.5 us
  transfers between devices with their start and end apart: 30, of which 10 were waited for; matrix products, arithmetic and copies ran while one was open for 4% of the time, Pallas kernels for 42%

profile of v11, /device:TPU:0, one launch (start us, length us, event | category | flops | bytes accessed | tf_op | source)
XLA Modules:
  0.0 355.7 jit_solution(15807509916840082013)
XLA Ops:
  2.6 7.0 %prepare.1 = (f32[260,8,256]{2,1,0:T(8,128)}, s32[2,128,128]{2,1,0:T(8,128)}, s32[2,128,128]{2,1,0:T(8,128)}, s32[8,256]{1,0:T(8,128)}, f32[144,128]{1,0:T(8,128)}, /*index=5*/f32[144,128]{1,0:T(8,128)}) custom-call(s32[3]{0:T(128)} %pad_add_fusion.7.base_ref, f32[32]{0:T(128)} %speed_ref.1, s32[256,256]{1,0:T(8,128)} %sea_ref.1, f32[256,256]{1,0:T(8,128)} %east_ref.1, ...), custom_call_target="tpu_custom_call" | custom-call | tf_op jit(solution)/shard_map/prepare/pallas_call | solution.py:626
  10.3 38.5 %propagate_early.1 = (f32[32,8192]{1,0:T(8,128)}, f32[32,8192]{1,0:T(8,128)}, f32[1,16384]{1,0:T(1,128)}, f32[72,16384]{1,0:T(8,128)}, f32[8,16384]{1,0:T(8,128)}, /*index=5*/f32[8,16384]{1,0:T(8,128)}) custom-call(s32[3]{0:T(128)} %pad_add_fusion.7.base_ref, s32[8,256]{1,0:T(8,128)} %get-tuple-element.85.table_ref, f32[144,128,256]{2,1,0:T(8,128)} %energy_ref.5, ...), custom_call_target="tpu_custom_call" | custom-call | flops 78643200 | bytes 62914560 | tf_op jit(solution)/shard_map/propagate_early/pallas_call | solution.py:682
  53.3 32.7 %propagate_late.1 = (f32[40,8192]{1,0:T(8,128)}, f32[40,8192]{1,0:T(8,128)}, f32[1,16384]{1,0:T(1,128)}, f32[72,16384]{1,0:T(8,128)}) custom-call(s32[3]{0:T(128)} %pad_add_fusion.7.base_ref, s32[8,256]{1,0:T(8,128)} %get-tuple-element.85.table_ref, f32[144,128,256]{2,1,0:T(8,128)} %energy_ref.5, ...), custom_call_target="tpu_custom_call", output_to_operand_aliasing={{3}: (10, {})} | custom-call | flops 62914560 | bytes 62914560 | tf_op jit(solution)/shard_map/propagate_late/pallas_call | solution.py:682
  86.0 3.8 %collective-permute-start.5 = (f32[40,8192]{1,0:T(8,128)}, f32[40,8192]{1,0:T(8,128)S(1)}, u32[]{:S(2)}, u32[]{:S(2)}) collective-permute-start(f32[40,8192]{1,0:T(8,128)} %get-tuple-element.95), channel_id=1, source_target_pairs={{0,2},{2,0},{4,6},{6,4},{8,10},{10,8},{12,14},{14,12},{1,3},{3,1},... | collective-permute-start | bytes 3932168 | tf_op jit(solution)/shard_map/ppermute | solution.py:716
  92.3 5.5 %collective-permute-start.7 = (f32[32,8192]{1,0:T(8,128)}, f32[32,8192]{1,0:T(8,128)}, u32[]{:S(2)}, u32[]{:S(2)}) collective-permute-start(f32[32,8192]{1,0:T(8,128)} %collective-permute-done.1.refs_7_), channel_id=1, source_target_pairs={{6,2},{0,4},{10,6},{4,8},{14,10},{8,12},{7,3},{1,5},{11,7},{5,9},{... | collective-permute-start | bytes 3145736 | tf_op jit(solution)/shard_map/ppermute | solution.py:716
  97.9 62.5 %propagate_whole.1 = (f32[72,2048]{1,0:T(8,128)}, f32[72,2048]{1,0:T(8,128)}, f32[72,2048]{1,0:T(8,128)}, f32[72,2048]{1,0:T(8,128)}, f32[72,2048]{1,0:T(8,128)}...) custom-call(s32[3]{0:T(128)} %pad_add_fusion.7.base_ref, ...), custom_call_target="tpu_custom_call" | custom-call | flops 141557760 | bytes 62914560 | tf_op jit(solution)/shard_map/propagate_whole/pallas_call | solution.py:682
  165.2 3.6 %collective-permute-start.8 = (f32[40,8192]{1,0:T(8,128)S(1)}, f32[40,8192]{1,0:T(8,128)S(1)}, u32[]{:S(2)}, u32[]{:S(2)}) collective-permute-start(f32[40,8192]{1,0:T(8,128)S(1)} %collective-permute-done.5.refs_8_), channel_id=1, source_target_pairs={{6,2},{0,4},{10,6},{4,8},{14,10},{8,12},{7,3},{1,5},{11,7},{5,9},{... | collective-permute-start | bytes 3932168 | tf_op jit(solution)/shard_map/ppermute | solution.py:716
  170.2 9.8 %collective-permute-done.10.refs_11_ = f32[72,2048]{1,0:T(8,128)S(1)} collective-permute-done((f32[72,2048]{1,0:T(8,128)}, f32[72,2048]{1,0:T(8,128)S(1)}, u32[]{:S(2)}, u32[]{:S(2)}) %collective-permute-start.10) | collective-permute-done | bytes 589856 | tf_op jit(solution)/shard_map/ppermute | solution.py:750
  180.0 15.2 %collective-permute-done.8.refs_2_ = f32[40,8192]{1,0:T(8,128)S(1)} collective-permute-done((f32[40,8192]{1,0:T(8,128)S(1)}, f32[40,8192]{1,0:T(8,128)S(1)}, u32[]{:S(2)}, u32[]{:S(2)}) %collective-permute-start.8) | collective-permute-done | bytes 1310752 | tf_op jit(solution)/shard_map/ppermute | solution.py:716
  196.2 5.2 %collective-permute-start.11 = (f32[72,2048]{1,0:T(8,128)}, f32[72,2048]{1,0:T(8,128)}, u32[]{:S(2)}, u32[]{:S(2)}) collective-permute-start(f32[72,2048]{1,0:T(8,128)} %collective-permute-done.6.refs_6_), channel_id=1, source_target_pairs={{6,2},{0,4},{10,6},{4,8},{14,10},{8,12},{7,3},{1,5},{11,7},{5,9},{... | collective-permute-start | bytes 1769480 | tf_op jit(solution)/shard_map/ppermute | solution.py:794
  204.8 7.5 %collective-permute-done.3 = f32[1,16384]{1,0:T(1,128)S(1)} collective-permute-done((f32[1,16384]{1,0:T(1,128)S(1)}, f32[1,16384]{1,0:T(1,128)S(1)}, u32[]{:S(2)}, u32[]{:S(2)}) %collective-permute-start.3) | collective-permute-done | bytes 65568 | tf_op jit(solution)/shard_map/ppermute | solution.py:753
  224.3 8.2 %interact_cells.4 = (f32[144,2048]{1,0:T(8,128)}, f32[72,2048]{1,0:T(8,128)}, f32[72,2048]{1,0:T(8,128)}) custom-call(bf16[6,288,216]{2,1,0:T(8,128)(2,1)} %stack.28.table_ref, bf16[288,864]{1,0:T(8,128)(2,1)} %concatenate.40.spread_ref, f32[432,1]{1,0:T(8,128)} %copy.48.coupling_ref, f32[72,2048]{1,0:T(8,128)} %collective-permute-done.11.refs_0_, ...), custom_call_target="tpu_custom_call" | custom-call | flops 2548039680 | bytes 20971520 | tf_op jit(solution)/shard_map/interact_cells/pallas_call | solution.py:806
  232.5 4.6 %collective-permute-start.15 = (f32[72,2048]{1,0:T(8,128)}, f32[72,2048]{1,0:T(8,128)S(1)}, u32[]{:S(2)}, u32[]{:S(2)}) collective-permute-start(f32[72,2048]{1,0:T(8,128)} %collective-permute-done.13.refs_6_), channel_id=1, source_target_pairs={{6,2},{0,4},{10,6},{4,8},{14,10},{8,12},{7,3},{1,5},{11,7},{5,9},{... | collective-permute-start | bytes 1769480 | tf_op jit(solution)/shard_map/ppermute | solution.py:794
  243.6 7.5 %collective-permute-done.15.refs_0_ = f32[72,2048]{1,0:T(8,128)S(1)} collective-permute-done((f32[72,2048]{1,0:T(8,128)}, f32[72,2048]{1,0:T(8,128)S(1)}, u32[]{:S(2)}, u32[]{:S(2)}) %collective-permute-start.15) | collective-permute-done | bytes 589856 | tf_op jit(solution)/shard_map/ppermute | solution.py:794
  251.2 4.5 %collective-permute-start.21 = (f32[72,2048]{1,0:T(8,128)}, f32[72,2048]{1,0:T(8,128)S(1)}, u32[]{:S(2)}, u32[]{:S(2)}) collective-permute-start(f32[72,2048]{1,0:T(8,128)} %collective-permute-done.19.refs_6_), channel_id=1, source_target_pairs={{6,2},{0,4},{10,6},{4,8},{14,10},{8,12},{7,3},{1,5},{11,7},{5,9},{... | collective-permute-start | bytes 1769480 | tf_op jit(solution)/shard_map/ppermute | solution.py:794
  255.7 8.2 %interact_cells.5 = (f32[144,2048]{1,0:T(8,128)}, f32[72,2048]{1,0:T(8,128)}, f32[72,2048]{1,0:T(8,128)}) custom-call(bf16[6,288,216]{2,1,0:T(8,128)(2,1)} %stack.28.table_ref, bf16[288,864]{1,0:T(8,128)(2,1)} %concatenate.40.spread_ref, f32[432,1]{1,0:T(8,128)} %copy.48.coupling_ref, f32[72,2048]{1,0:T(8,128)} %copy-done.9, ...), custom_call_target="tpu_custom_call" | custom-call | flops 2548039680 | bytes 20971520 | tf_op jit(solution)/shard_map/interact_cells/pallas_call | solution.py:806
  267.7 8.3 %interact_cells.6 = (f32[144,2048]{1,0:T(8,128)}, f32[72,2048]{1,0:T(8,128)}, f32[72,2048]{1,0:T(8,128)}) custom-call(bf16[6,288,216]{2,1,0:T(8,128)(2,1)} %stack.28.table_ref, bf16[288,864]{1,0:T(8,128)(2,1)} %concatenate.40.spread_ref, f32[432,1]{1,0:T(8,128)} %copy.48.coupling_ref, f32[72,2048]{1,0:T(8,128)} %copy-done.8, ...), custom_call_target="tpu_custom_call" | custom-call | flops 2548039680 | bytes 20971520 | tf_op jit(solution)/shard_map/interact_cells/pallas_call | solution.py:806
  277.1 8.2 %interact_cells.7 = (f32[144,2048]{1,0:T(8,128)}, f32[72,2048]{1,0:T(8,128)}, f32[72,2048]{1,0:T(8,128)}) custom-call(bf16[6,288,216]{2,1,0:T(8,128)(2,1)} %stack.28.table_ref, bf16[288,864]{1,0:T(8,128)(2,1)} %concatenate.40.spread_ref, f32[432,1]{1,0:T(8,128)} %copy.48.coupling_ref, f32[72,2048]{1,0:T(8,128)} %copy-done.7, ...), custom_call_target="tpu_custom_call" | custom-call | flops 2548039680 | bytes 20971520 | tf_op jit(solution)/shard_map/interact_cells/pallas_call | solution.py:806
  287.2 5.7 %collective-permute-done.23.refs_7_ = f32[72,2048]{1,0:T(8,128)S(1)} collective-permute-done((f32[72,2048]{1,0:T(8,128)}, f32[72,2048]{1,0:T(8,128)S(1)}, u32[]{:S(2)}, u32[]{:S(2)}) %collective-permute-start.23) | collective-permute-done | bytes 589856 | tf_op jit(solution)/shard_map/ppermute | solution.py:829
  300.4 5.2 %collective-permute-done.29.refs_8_ = f32[72,2048]{1,0:T(8,128)S(1)} collective-permute-done((f32[72,2048]{1,0:T(8,128)}, f32[72,2048]{1,0:T(8,128)S(1)}, u32[]{:S(2)}, u32[]{:S(2)}) %collective-permute-start.29) | collective-permute-done | bytes 589856 | tf_op jit(solution)/shard_map/ppermute | solution.py:829
  306.4 15.7 %finish_chunk.2.refs_9_ = f32[144,128,256]{2,1,0:T(8,128)} custom-call(s32[3]{0:T(128)} %pad_add_fusion.7.base_ref, s32[8,256]{1,0:T(8,128)} %get-tuple-element.85.table_ref, s32[2,128,128]{2,1,0:T(8,128)} %get-tuple-element.73.place_ref, f32[1,16384]{1,0:T(1,128)} %broadcast_multiply_fusion, f32[8,16384]{1,0:T(8,128)} %get-tuple-element.80.refs_0_.fields_ref, ...), custom_call_target="tpu_custom_call" | custom-call | flops 47185920 | bytes 104857600 | tf_op jit(solution)/shard_map/finish_chunk/pallas_call | solution.py:854
  322.1 8.7 %collective-permute-done.25.refs_7_ = f32[72,2048]{1,0:T(8,128)S(1)} collective-permute-done((f32[72,2048]{1,0:T(8,128)}, f32[72,2048]{1,0:T(8,128)S(1)}, u32[]{:S(2)}, u32[]{:S(2)}) %collective-permute-start.25) | collective-permute-done | bytes 589856 | tf_op jit(solution)/shard_map/ppermute | solution.py:829
  330.8 8.3 %collective-permute-done.26.refs_8_ = f32[72,2048]{1,0:T(8,128)S(1)} collective-permute-done((f32[72,2048]{1,0:T(8,128)}, f32[72,2048]{1,0:T(8,128)S(1)}, u32[]{:S(2)}, u32[]{:S(2)}) %collective-permute-start.26) | collective-permute-done | bytes 589856 | tf_op jit(solution)/shard_map/ppermute | solution.py:829
  340.0 15.7 %finish_chunk.3 = f32[144,128,256]{2,1,0:T(8,128)} custom-call(s32[3]{0:T(128)} %pad_add_fusion.7.base_ref, s32[8,256]{1,0:T(8,128)} %get-tuple-element.85.table_ref, s32[2,128,128]{2,1,0:T(8,128)} %get-tuple-element.73.place_ref, f32[1,16384]{1,0:T(1,128)} %broadcast_multiply_fusion, ...), custom_call_target="tpu_custom_call", output_to_operand_aliasing={{}: (16, {})} | custom-call | flops 47185920 | bytes 104857600 | tf_op jit(solution)/shard_map/finish_chunk/pallas_call | solution.py:854
  (152 shorter events, 54.7 us)
Async XLA Ops:
  49.5 42.8 %collective-permute-start.1 = (f32[32,8192]{1,0:T(8,128)}, f32[32,8192]{1,0:T(8,128)}, u32[]{:S(2)}, u32[]{:S(2)}) collective-permute-start(f32[32,8192]{1,0:T(8,128)} %get-tuple-element.84), channel_id=1, source_target_pairs={{0,2},{2,0},{4,6},{6,4},{8,10},{10,8},{12,14},{14,12},{1,3},{3,1},... | collective-permute-start | bytes 3145736 | tf_op jit(solution)/shard_map/ppermute | solution.py:716
  52.0 168.4 %collective-permute-start.12 = (f32[32,8192]{1,0:T(8,128)}, f32[32,8192]{1,0:T(8,128)}, u32[]{:S(2)}, u32[]{:S(2)}) collective-permute-start(f32[32,8192]{1,0:T(8,128)} %get-tuple-element.102.refs_3_), channel_id=1, source_target_pairs={{2,6},{4,0},{6,10},{8,4},{10,14},{12,8},{3,7},{5,1},{7,11},{9,5},{... | collective-permute-start | bytes 3145736 | tf_op jit(solution)/shard_map/ppermute | solution.py:716
  86.0 75.5 %collective-permute-start.5 = (f32[40,8192]{1,0:T(8,128)}, f32[40,8192]{1,0:T(8,128)S(1)}, u32[]{:S(2)}, u32[]{:S(2)}) collective-permute-start(f32[40,8192]{1,0:T(8,128)} %get-tuple-element.95), channel_id=1, source_target_pairs={{0,2},{2,0},{4,6},{6,4},{8,10},{10,8},{12,14},{14,12},{1,3},{3,1},... | collective-permute-start | bytes 3932168 | tf_op jit(solution)/shard_map/ppermute | solution.py:716
  89.9 71.7 %collective-permute-start.9 = (f32[40,8192]{1,0:T(8,128)}, f32[40,8192]{1,0:T(8,128)S(1)}, u32[]{:S(2)}, u32[]{:S(2)}) collective-permute-start(f32[40,8192]{1,0:T(8,128)} %get-tuple-element.99.refs_4_), channel_id=1, source_target_pairs={{2,6},{4,0},{6,10},{8,4},{10,14},{12,8},{3,7},{5,1},{7,11},{9,5},{... | collective-permute-start | bytes 3932168 | tf_op jit(solution)/shard_map/ppermute | solution.py:716
  92.3 72.9 %collective-permute-start.7 = (f32[32,8192]{1,0:T(8,128)}, f32[32,8192]{1,0:T(8,128)}, u32[]{:S(2)}, u32[]{:S(2)}) collective-permute-start(f32[32,8192]{1,0:T(8,128)} %collective-permute-done.1.refs_7_), channel_id=1, source_target_pairs={{6,2},{0,4},{10,6},{4,8},{14,10},{8,12},{7,3},{1,5},{11,7},{5,9},{... | collective-permute-start | bytes 3145736 | tf_op jit(solution)/shard_map/ppermute | solution.py:716
  165.2 29.9 %collective-permute-start.8 = (f32[40,8192]{1,0:T(8,128)S(1)}, f32[40,8192]{1,0:T(8,128)S(1)}, u32[]{:S(2)}, u32[]{:S(2)}) collective-permute-start(f32[40,8192]{1,0:T(8,128)S(1)} %collective-permute-done.5.refs_8_), channel_id=1, source_target_pairs={{6,2},{0,4},{10,6},{4,8},{14,10},{8,12},{7,3},{1,5},{11,7},{5,9},{... | collective-permute-start | bytes 3932168 | tf_op jit(solution)/shard_map/ppermute | solution.py:716
  168.9 45.8 %collective-permute-start.14 = (f32[72,2048]{1,0:T(8,128)}, f32[72,2048]{1,0:T(8,128)}, u32[]{:S(2)}, u32[]{:S(2)}) collective-permute-start(f32[72,2048]{1,0:T(8,128)} %get-tuple-element.107.refs_5_), channel_id=1, source_target_pairs={{2,6},{4,0},{6,10},{8,4},{10,14},{12,8},{3,7},{5,1},{7,11},{9,5},{... | collective-permute-start | bytes 1769480 | tf_op jit(solution)/shard_map/ppermute | solution.py:750
  180.0 23.5 %collective-permute-start.13 = (f32[72,2048]{1,0:T(8,128)}, f32[72,2048]{1,0:T(8,128)}, u32[]{:S(2)}, u32[]{:S(2)}) collective-permute-start(f32[72,2048]{1,0:T(8,128)} %get-tuple-element.105), channel_id=1, source_target_pairs={{0,2},{2,0},{4,6},{6,4},{8,10},{10,8},{12,14},{14,12},{1,3},{3,1},... | collective-permute-start | bytes 1769480 | tf_op jit(solution)/shard_map/ppermute | solution.py:749
  196.2 26.8 %collective-permute-start.11 = (f32[72,2048]{1,0:T(8,128)}, f32[72,2048]{1,0:T(8,128)}, u32[]{:S(2)}, u32[]{:S(2)}) collective-permute-start(f32[72,2048]{1,0:T(8,128)} %collective-permute-done.6.refs_6_), channel_id=1, source_target_pairs={{6,2},{0,4},{10,6},{4,8},{14,10},{8,12},{7,3},{1,5},{11,7},{5,9},{... | collective-permute-start | bytes 1769480 | tf_op jit(solution)/shard_map/ppermute | solution.py:794
  203.5 37.3 %collective-permute-start.17 = (f32[72,2048]{1,0:T(8,128)}, f32[72,2048]{1,0:T(8,128)}, u32[]{:S(2)}, u32[]{:S(2)}) collective-permute-start(f32[72,2048]{1,0:T(8,128)} %get-tuple-element.113.refs_5_), channel_id=1, source_target_pairs={{2,6},{4,0},{6,10},{8,4},{10,14},{12,8},{3,7},{5,1},{7,11},{9,5},{... | collective-permute-start | bytes 1769480 | tf_op jit(solution)/shard_map/ppermute | solution.py:750
  212.3 20.3 %collective-permute-start.19 = (f32[72,2048]{1,0:T(8,128)}, f32[72,2048]{1,0:T(8,128)}, u32[]{:S(2)}, u32[]{:S(2)}) collective-permute-start(f32[72,2048]{1,0:T(8,128)} %get-tuple-element.117), channel_id=1, source_target_pairs={{0,2},{2,0},{4,6},{6,4},{8,10},{10,8},{12,14},{14,12},{1,3},{3,1},... | collective-permute-start | bytes 1769480 | tf_op jit(solution)/shard_map/ppermute | solution.py:749
  214.7 24.1 %collective-permute-start.16 = (f32[72,2048]{1,0:T(8,128)}, f32[72,2048]{1,0:T(8,128)}, u32[]{:S(2)}, u32[]{:S(2)}) collective-permute-start(f32[72,2048]{1,0:T(8,128)} %get-tuple-element.111), channel_id=1, source_target_pairs={{0,2},{2,0},{4,6},{6,4},{8,10},{10,8},{12,14},{14,12},{1,3},{3,1},... | collective-permute-start | bytes 1769480 | tf_op jit(solution)/shard_map/ppermute | solution.py:749
  220.4 22.4 %collective-permute-start.4 = (f32[1,16384]{1,0:T(1,128)S(1)}, f32[1,16384]{1,0:T(1,128)S(1)}, u32[]{:S(2)}, u32[]{:S(2)}) collective-permute-start(f32[1,16384]{1,0:T(1,128)S(1)} %add.257), channel_id=1, source_target_pairs={{0,8},{2,10},{4,12},{6,14},{8,0},{10,2},{12,4},{14,6},{1,9},{3,11}... | collective-permute-start | bytes 196616 | tf_op jit(solution)/shard_map/ppermute | solution.py:754
  223.0 20.6 %collective-permute-start.20 = (f32[72,2048]{1,0:T(8,128)S(1)}, f32[72,2048]{1,0:T(8,128)S(1)}, u32[]{:S(2)}, u32[]{:S(2)}) collective-permute-start(f32[72,2048]{1,0:T(8,128)S(1)} %copy-done.4), channel_id=1, source_target_pairs={{2,6},{4,0},{6,10},{8,4},{10,14},{12,8},{3,7},{5,1},{7,11},{9,5},{... | collective-permute-start | bytes 1769480 | tf_op jit(solution)/shard_map/ppermute | solution.py:750
  232.5 18.6 %collective-permute-start.15 = (f32[72,2048]{1,0:T(8,128)}, f32[72,2048]{1,0:T(8,128)S(1)}, u32[]{:S(2)}, u32[]{:S(2)}) collective-permute-start(f32[72,2048]{1,0:T(8,128)} %collective-permute-done.13.refs_6_), channel_id=1, source_target_pairs={{6,2},{0,4},{10,6},{4,8},{14,10},{8,12},{7,3},{1,5},{11,7},{5,9},{... | collective-permute-start | bytes 1769480 | tf_op jit(solution)/shard_map/ppermute | solution.py:794
  238.8 37.2 %collective-permute-start.22 = (f32[72,2048]{1,0:T(8,128)}, f32[72,2048]{1,0:T(8,128)S(1)}, u32[]{:S(2)}, u32[]{:S(2)}) collective-permute-start(f32[72,2048]{1,0:T(8,128)} %get-tuple-element.123), channel_id=1, source_target_pairs={{0,2},{2,0},{4,6},{6,4},{8,10},{10,8},{12,14},{14,12},{1,3},{3,1},... | collective-permute-start | bytes 1769480 | tf_op jit(solution)/shard_map/ppermute | solution.py:829
  240.8 26.1 %collective-permute-start.18 = (f32[72,2048]{1,0:T(8,128)}, f32[72,2048]{1,0:T(8,128)S(1)}, u32[]{:S(2)}, u32[]{:S(2)}) collective-permute-start(f32[72,2048]{1,0:T(8,128)} %collective-permute-done.16.refs_6_), channel_id=1, source_target_pairs={{6,2},{0,4},{10,6},{4,8},{14,10},{8,12},{7,3},{1,5},{11,7},{5,9},{... | collective-permute-start | bytes 1769480 | tf_op jit(solution)/shard_map/ppermute | solution.py:794
  242.8 22.1 %collective-permute-start.27 = (f32[72,2048]{1,0:T(8,128)}, f32[72,2048]{1,0:T(8,128)}, u32[]{:S(2)}, u32[]{:S(2)}) collective-permute-start(f32[72,2048]{1,0:T(8,128)} %get-tuple-element.134), channel_id=1, source_target_pairs={{0,2},{2,0},{4,6},{6,4},{8,10},{10,8},{12,14},{14,12},{1,3},{3,1},... | collective-permute-start | bytes 1769480 | tf_op jit(solution)/shard_map/ppermute | solution.py:829
  251.2 24.9 %collective-permute-start.21 = (f32[72,2048]{1,0:T(8,128)}, f32[72,2048]{1,0:T(8,128)S(1)}, u32[]{:S(2)}, u32[]{:S(2)}) collective-permute-start(f32[72,2048]{1,0:T(8,128)} %collective-permute-done.19.refs_6_), channel_id=1, source_target_pairs={{6,2},{0,4},{10,6},{4,8},{14,10},{8,12},{7,3},{1,5},{11,7},{5,9},{... | collective-permute-start | bytes 1769480 | tf_op jit(solution)/shard_map/ppermute | solution.py:794
  264.9 20.4 %collective-permute-start.28 = (f32[72,2048]{1,0:T(8,128)}, f32[72,2048]{1,0:T(8,128)S(1)}, u32[]{:S(2)}, u32[]{:S(2)}) collective-permute-start(f32[72,2048]{1,0:T(8,128)} %get-tuple-element.136), channel_id=1, source_target_pairs={{0,2},{2,0},{4,6},{6,4},{8,10},{10,8},{12,14},{14,12},{1,3},{3,1},... | collective-permute-start | bytes 1769480 | tf_op jit(solution)/shard_map/ppermute | solution.py:829
  285.3 20.2 %collective-permute-start.29 = (f32[72,2048]{1,0:T(8,128)}, f32[72,2048]{1,0:T(8,128)S(1)}, u32[]{:S(2)}, u32[]{:S(2)}) collective-permute-start(f32[72,2048]{1,0:T(8,128)} %get-tuple-element.138), channel_id=1, source_target_pairs={{0,2},{2,0},{4,6},{6,4},{8,10},{10,8},{12,14},{14,12},{1,3},{3,1},... | collective-permute-start | bytes 1769480 | tf_op jit(solution)/shard_map/ppermute | solution.py:829
  292.9 29.2 %collective-permute-start.24 = (f32[72,2048]{1,0:T(8,128)}, f32[72,2048]{1,0:T(8,128)S(1)}, u32[]{:S(2)}, u32[]{:S(2)}) collective-permute-start(f32[72,2048]{1,0:T(8,128)} %get-tuple-element.127), channel_id=1, source_target_pairs={{0,2},{2,0},{4,6},{6,4},{8,10},{10,8},{12,14},{14,12},{1,3},{3,1},... | collective-permute-start | bytes 1769480 | tf_op jit(solution)/shard_map/ppermute | solution.py:829
  295.3 35.5 %collective-permute-start.25 = (f32[72,2048]{1,0:T(8,128)}, f32[72,2048]{1,0:T(8,128)S(1)}, u32[]{:S(2)}, u32[]{:S(2)}) collective-permute-start(f32[72,2048]{1,0:T(8,128)} %get-tuple-element.129), channel_id=1, source_target_pairs={{0,2},{2,0},{4,6},{6,4},{8,10},{10,8},{12,14},{14,12},{1,3},{3,1},... | collective-permute-start | bytes 1769480 | tf_op jit(solution)/shard_map/ppermute | solution.py:829
  295.3 43.8 %collective-permute-start.26 = (f32[72,2048]{1,0:T(8,128)}, f32[72,2048]{1,0:T(8,128)S(1)}, u32[]{:S(2)}, u32[]{:S(2)}) collective-permute-start(f32[72,2048]{1,0:T(8,128)} %get-tuple-element.131), channel_id=1, source_target_pairs={{0,2},{2,0},{4,6},{6,4},{8,10},{10,8},{12,14},{14,12},{1,3},{3,1},... | collective-permute-start | bytes 1769480 | tf_op jit(solution)/shard_map/ppermute | solution.py:829
  (38 other events, 627.7 us)
